TPU v7x, 32 devices: a whole 2x2x4 slice. The times are simulated.
32 devices in a mesh: row: 4 (over z), col: 8 (over y, x, core).
Axes of the slice: x: 2, y: 2, z: 4, core: 2. Of those that a mesh axis runs over, the one named last changes fastest.
Arguments:
- pair: bfloat16 [256, 256, 128], P(('row', 'col')), may hold values from -6 to 6
- residue_mask: int32 [256], replicated, may hold values from 0 to 1, as said below
- ln_gain: float32 [2, 128], replicated, may hold values from 0.5 to 1.5
- ln_shift: float32 [2, 128], replicated, may hold values from -3 to 3
- w_proj: bfloat16 [2, 128, 512], replicated, may hold values from -0.5 to 0.5
- w_bias: bfloat16 [2, 128, 4], replicated, may hold values from -10.606602 to 10.606602
- gate_bias: float32 [2, 128], replicated, may hold values from -4 to 4
- w_out: bfloat16 [2, 128, 128], replicated, may hold values from -0.5 to 0.5
- out_bias: float32 [2, 128], replicated, may hold values from -3 to 3
Outputs:
- starting_update: bfloat16 [64, 256, 128], P(('row', 'col'))
- ending_update: bfloat16 [64, 256, 128], P(('row', 'col'))
Inputs may be any that keep to these rules, and one draw needn't show every extreme that they name: `residue_mask`: residue 0 is always a real residue.
All inputs are finite; a program needn't handle non-finite values.
Results may differ from a plain program's by a relative error of at most 0.0065.
The roundings to bfloat16 on the way count: a program that leaves them out, or rounds other values in their place, can miss the bound.
Values may be sent and summed in bfloat16 or wider, within the bound.
No kernel may reach another device: no remote copies, remote signals or barrier semaphores. Data moves between devices by JAX's collectives and lax.ppermute only.
A program may use at most 128 MiB of HBM per device.

v0:
```python
import jax
import jax.numpy as jnp
from jax import lax
from jax.sharding import PartitionSpec as P

WD = 2


EPS = 1e-05


def layer_norm(values, gain, shift):
    wide = values.astype(jnp.float32)
    center = jnp.mean(wide, -1, keepdims=True)
    spread = jnp.mean(jnp.square(wide - center), -1, keepdims=True)
    return ((wide - center) * lax.rsqrt(spread + EPS) * gain + shift).astype(jnp.bfloat16)


def project(normed, weight, offset, head_count):
    lead = normed.shape[:-1]
    inner = weight.shape[1] // 4
    size = inner // head_count
    full = jnp.dot(normed.reshape(-1, normed.shape[-1]), weight, preferred_element_type=jnp.float32)
    queries = (
        (full[:, :inner] * size ** (-0.5)).astype(jnp.bfloat16).reshape(lead + (head_count, size))
    )
    key_rows = full[:, inner : 2 * inner].astype(jnp.bfloat16).reshape(lead + (head_count, size))
    value_rows = (
        full[:, 2 * inner : 3 * inner].astype(jnp.bfloat16).reshape(lead + (head_count, size))
    )
    gating = jax.nn.sigmoid(full[:, 3 * inner :] + offset).reshape(lead + (inner,))
    return (queries, key_rows, value_rows, gating)


def attend(queries, key_rows, value_rows, gating, bias, live, weight_out, offset_out):
    scores = jnp.einsum(
        "qhd,khd->hqk", queries, key_rows, preferred_element_type=jnp.float32
    ) + bias.astype(jnp.float32)
    scores = jnp.where(live[None, None, :] > 0, scores, jnp.float32(-1000000000.0))
    top = jnp.max(scores, -1, keepdims=True)
    expo = jnp.exp(scores - top)
    weights = (expo / jnp.sum(expo, -1, keepdims=True)).astype(jnp.bfloat16)
    mixed = jnp.einsum("hqk,khd->qhd", weights, value_rows, preferred_element_type=jnp.float32)
    gated = (mixed.reshape(mixed.shape[0], -1) * gating).astype(jnp.bfloat16)
    return (jnp.dot(gated, weight_out, preferred_element_type=jnp.float32) + offset_out).astype(
        jnp.bfloat16
    )


def attend_lines(queries, key_rows, value_rows, gating, bias, live, weight_out, offset_out):
    lines, count = (queries.shape[0], queries.shape[1])
    scores = (
        jnp.einsum("wqhd,wkhd->whqk", queries, key_rows, preferred_element_type=jnp.float32)
        + bias.astype(jnp.float32)[None]
    )
    scores = jnp.where(live[None, None, None, :] > 0, scores, jnp.float32(-1000000000.0))
    top = jnp.max(scores, -1, keepdims=True)
    expo = jnp.exp(scores - top)
    weights = (expo / jnp.sum(expo, -1, keepdims=True)).astype(jnp.bfloat16)
    mixed = jnp.einsum("whqk,wkhd->wqhd", weights, value_rows, preferred_element_type=jnp.float32)
    gated = (mixed.reshape(lines, count, -1) * gating).astype(jnp.bfloat16)
    flat = (
        jnp.dot(gated.reshape(lines * count, -1), weight_out, preferred_element_type=jnp.float32)
        + offset_out
    )
    return flat.astype(jnp.bfloat16).reshape(lines, count, -1)


def local_bias(normed, weight):
    rows, length, channels = normed.shape
    flat = jnp.dot(normed.reshape(-1, channels), weight, preferred_element_type=jnp.float32)
    return jnp.transpose(flat.astype(jnp.bfloat16).reshape(rows, length, -1), (2, 0, 1))


def body(pair, residue_mask, ln_gain, ln_shift, w_proj, w_bias, gate_bias, w_out, out_bias):
    rows, length, channels = pair.shape
    head_count = w_bias.shape[2]
    devices = lax.axis_size("row") * lax.axis_size("col")
    width = WD
    normed_start = layer_norm(pair, ln_gain[0], ln_shift[0])
    normed_end = layer_norm(pair, ln_gain[1], ln_shift[1])
    bias_start = local_bias(normed_start, w_bias[0])
    bias_end = local_bias(normed_end, w_bias[1])
    start_q, start_k, start_v, start_g = project(
        normed_start[:width], w_proj[0], gate_bias[0], head_count
    )
    starting_update = attend_lines(
        start_q,
        start_k,
        start_v,
        start_g,
        lax.all_gather(bias_start, ("row", "col"), axis=1, tiled=True),
        residue_mask,
        w_out[0],
        out_bias[0],
    )
    end_full = None
    picked = pair.reshape(rows, devices, rows, channels)[:, :, :width, :]
    moved = lax.all_to_all(picked, ("row", "col"), split_axis=1, concat_axis=1, tiled=True)
    columns = jnp.transpose(moved, (2, 1, 0, 3)).reshape(width, length, channels)
    end_full = lax.all_gather(bias_end, ("row", "col"), axis=1, tiled=True)
    end_table = jnp.transpose(end_full, (0, 2, 1))
    normed_columns = layer_norm(columns, ln_gain[1], ln_shift[1])
    end_q, end_k, end_v, end_g = project(normed_columns, w_proj[1], gate_bias[1], head_count)

    def end_line(item):
        queries, key_rows, value_rows, gating = item
        return attend(
            queries, key_rows, value_rows, gating, end_table, residue_mask, w_out[1], out_bias[1]
        )

    ending_update = lax.map(end_line, (end_q, end_k, end_v, end_g))
    return (starting_update, ending_update)


def solution(mesh):
    return jax.shard_map(
        body,
        mesh=mesh,
        in_specs=(P(("row", "col"), None, None), P(), P(), P(), P(), P(), P(), P(), P()),
        out_specs=(P(("row", "col"), None, None), P(("row", "col"), None, None)),
        check_vma=False,
    )
```

profile of v0, /device:TPU:0, one launch (start us, length us, event | category | flops | bytes accessed | tf_op | source)
XLA Modules:
  0.0 110.8 jit_solution(2834288533543565941)
XLA Ops:
  0.7 1.2 %slice.105 = bf16[8,32,2,128]{3,2,1,0:T(2,128)(2,1)S(1)} slice(bf16[8,32,8,128]{3,2,1,0:T(8,128)(2,1)} %bitcast.154), slice={[0:8], [0:32], [0:2], [0:128]} | slice | bytes 262144 | tf_op jit(solution)/shard_map/slice | solution.py:98
  1.8 0.7 copy.93
  2.6 7.3 %all-to-all-start = ((bf16[8,32,2,128]{3,2,0,1:T(2,128)(2,1)}), bf16[8,32,2,128]{3,2,0,1:T(2,128)(2,1)S(1)}, u32[]{:S(2)}, u32[]{:S(2)}) async-start(bf16[8,32,2,128]{3,2,0,1:T(2,128)(2,1)} %copy.93), calls=%async_computation | async-start | bytes 262144 | tf_op jit(solution)/shard_map/all_to_all | solution.py:99
  9.9 1.3 %convert_reduce_fusion = f32[8,256]{1,0:T(8,128)S(1)} fusion(bf16[8,256,128]{2,1,0:T(8,128)(2,1)} %param.11), kind=kLoop, calls=%fused_computation.37 | loop fusion | flops 522240 | bytes 532480 | tf_op jit(solution)/shard_map/reduce_sum | solution.py:14
  11.2 1.7 %fusion.38 = f32[8,256]{1,0:T(8,128)S(1)} fusion(bf16[8,256,128]{2,1,0:T(8,128)(2,1)} %param.11, f32[8,256]{1,0:T(8,128)S(1)} %broadcast_multiply_fusion.1), kind=kLoop, calls=%fused_computation.49 | loop fusion | flops 1046528 | bytes 540672 | tf_op jit(solution)/shard_map/reduce_sum | solution.py:15
  12.9 0.8 slice_bitcast_fusion.2
  13.6 0.7 fusion.37
  14.4 0.3 fusion.94
  15.3 43.3 %all_gather.6 = bf16[4,256,256]{2,0,1:T(4,128)(2,1)S(1)} all-gather(bf16[4,8,256]{2,0,1:T(4,128)(2,1)S(1)} %bitcast.164), channel_id=1, replica_groups=mesh['row'=4,'col'=8] {'row','col'}, dimensions={1}, use_global_device_ids=true | all-gather | bytes 540672 | tf_op jit(solution)/shard_map/all_gather | solution.py:92
  58.7 1.3 %copy.88 = f32[4,256,256]{1,2,0:T(8,128)} copy(f32[4,256,256]{2,1,0:T(8,128)S(1)} %copy_convert_fusion) | data formatting | bytes 2097152 | tf_op jit(solution)/shard_map/convert_element_type | solution.py:54
  60.2 3.4 %fusion.95 = (f32[2,4,256]{2,1,0:T(4,128)S(1)}, f32[2,4,256,256]{2,3,1,0:T(8,128)}) fusion(f32[4,256,256]{1,2,0:T(8,128)} %copy.88, pred[256]{0:T(512)(128)(4,1)S(1)} %broadcast_compare_fusion.1, bf16[2,256,4,32]{1,0,3,2:T(2,128)(2,1)S(1)} %reshape.133, bf16[2,256,4,32]{1,0,3,2:T(2,128)(2,1)S(1)} %reshape.132), kind=kOutput, calls=%fused_computation.116 | convolution fusion | flops 35651840 | bytes 3416320 | tf_op jit(solution)/shard_map/sub | solution.py:58
  63.6 1.9 %convolution_bitcast_fusion.1 = f32[2,256,4,32]{1,3,2,0:T(8,128)S(1)} fusion(f32[2,4,256,256]{2,3,1,0:T(8,128)} %get-tuple-element.142, f32[2,4,256]{2,1,0:T(4,128)S(1)} %get-tuple-element.141, bf16[2,256,4,32]{1,0,3,2:T(2,128)(2,1)S(1)} %reshape.131), kind=kOutput, calls=%fused_computation.43 | convolution fusion | flops 34603008 | bytes 2498560 | tf_op jit(solution)/shard_map/whqk,wkhd->wqhd/dot_general | solution.py:60
  66.4 0.9 fusion.33
  67.2 38.0 %all_gather.7 = bf16[4,256,256]{2,1,0:T(8,128)(2,1)S(1)} all-gather(bf16[4,8,256]{2,1,0:T(8,128)(2,1)S(1)} %bitcast.165), channel_id=1, replica_groups=mesh['row'=4,'col'=8] {'row','col'}, dimensions={1}, use_global_device_ids=true | all-gather | bytes 540672 | tf_op jit(solution)/shard_map/all_gather | solution.py:101
  105.4 0.2 fusion.55
  105.9 0.3 fusion.100
  106.9 3.3 %while.10 = (s32[]{:T(128)}, bf16[2,256,128]{2,1,0:T(8,128)(2,1)S(1)}, bf16[2,256,4,32]{1,3,2,0:T(8,128)(2,1)S(1)}, s32[256]{0:T(256)S(1)}, bf16[2,256,4,32]{1,3...) while((s32[]{:T(128)}, ...), condition=%wide.region_9.10_spmd, body=%wide.region_6.9_spmd.sunk | while | flops 61736704 | bytes 5420921 | solution.py:112
  106.9 0.4 fusion.128
  107.3 0.6 fusion.127
  107.9 0.3 fusion.129
  108.5 0.3 fusion.128
  108.9 0.6 fusion.127
  109.6 0.3 fusion.129
  110.2 0.6 copy-done.6
  (62 shorter events, 3.3 us)
Async XLA Ops:
  0.6 13.0 %copy-start = (bf16[8,256,128]{2,1,0:T(8,128)(2,1)S(1)}, bf16[8,256,128]{2,1,0:T(8,128)(2,1)}, u32[]{:S(2)}) copy-start(bf16[8,256,128]{2,1,0:T(8,128)(2,1)} %param.11) | copy-start | bytes 1572868
  0.6 13.8 %copy-start.2 = (bf16[2,128,512]{2,1,0:T(8,128)(2,1)S(1)}, bf16[2,128,512]{2,1,0:T(8,128)(2,1)}, u32[]{:S(2)}) copy-start(bf16[2,128,512]{2,1,0:T(8,128)(2,1)} %param.15) | copy-start | bytes 786436
  2.6 102.7 %all-to-all-start = ((bf16[8,32,2,128]{3,2,0,1:T(2,128)(2,1)}), bf16[8,32,2,128]{3,2,0,1:T(2,128)(2,1)S(1)}, u32[]{:S(2)}, u32[]{:S(2)}) async-start(bf16[8,32,2,128]{3,2,0,1:T(2,128)(2,1)} %copy.93), calls=%async_computation | async-start | bytes 262144 | tf_op jit(solution)/shard_map/all_to_all | solution.py:99
  14.4 0.7 copy-start.3
  15.3 44.7 %copy-start.7 = (s32[256]{0:T(256)S(1)}, s32[256]{0:T(256)}, u32[]{:S(2)}) copy-start(s32[256]{0:T(256)} %param.12) | copy-start | bytes 3076
  65.5 0.7 copy-start.4
  65.5 0.7 copy-start.5
  65.5 0.9 copy-start.1
  110.2 0.7 copy-start.6
where the time goes:
time: 111 us
  blocking collectives  81.4 us (73%)
  matrix products  10.1 us (9%)
  starting transfers between devices  7.3 us (7%)
  local copies, waits for them, and re-layouts  6.52 us (6%)
  other arithmetic  4.49 us (4%)
    all_gather x1, blocking collectives, body(): lax.all_gather(bias_start, ('row', 'col'), axis=1, tiled=True)  43.3 us
    all_gather x1, blocking collectives, body(): end_full = lax.all_gather(bias_end, ('row', 'col'), axis=1, tiled=True)  38 us
    all_to_all x1, starting transfers between devices, body(): lax.all_to_all(picked, ('row', 'col'), split_axis=1, concat_axis=1, tiled...  7.3 us
    sub x1, matrix products, attend_lines(): expo = jnp.exp(scores - top)  3.43 us
  transfers between devices with their start and end apart: 1, of which 0 were waited for; matrix products, arithmetic and copies ran while one was open for 12% of the time, Pallas kernels for 0%

commit v1 on v0

v1 whole, which is shorter than its diff:
```python
import functools

import jax
import jax.numpy as jnp
from jax import lax
from jax.experimental import pallas as pl
from jax.experimental.pallas import tpu as pltpu
from jax.sharding import PartitionSpec as P

WD = 2
EPS = 1e-05
MASKED = -1000000000.0
CHUNK = 256
LANES = 128
VMEM = pl.BlockSpec(memory_space=pltpu.VMEM)
SMEM = pl.BlockSpec(memory_space=pltpu.SMEM)


def params(megabytes):
    return pltpu.CompilerParams(vmem_limit_bytes=megabytes * 1024 * 1024)


def for_each(count, step, unrolled):
    if unrolled:
        for index in range(count):
            step(index)
    else:
        lax.fori_loop(0, count, lambda index, carry: (step(index), carry)[1], 0)


def standardize(wide):
    center = jnp.mean(wide, -1, keepdims=True)
    away = wide - center
    spread = jnp.mean(jnp.square(away), -1, keepdims=True)
    return away * lax.rsqrt(spread + EPS)


def contract(left, right, left_dim, right_dim):
    return lax.dot_general(
        left, right, (((left_dim,), (right_dim,)), ((), ())), preferred_element_type=jnp.float32
    )


def bias_kernel(pair_ref, own_ref, live_ref, gain_ref, shift_ref, weight_ref, bias_ref, pick_ref, wide, rows_out, picked):
    rows, length, channels = pair_ref.shape
    heads = weight_ref.shape[1]
    devices = length // rows
    live = live_ref[...] > 0
    for a in range(rows):
        x = pair_ref[a].astype(jnp.float32)
        wide[a] = x
        z = standardize(x)
        for p in range(2):
            normed = (z * gain_ref[p : p + 1, :] + shift_ref[p : p + 1, :]).astype(jnp.bfloat16)
            bias = contract(weight_ref[p], normed, 1, 1)
            if p == 0:
                bias = jnp.where(live, bias, MASKED)
            else:
                bias = jnp.where(own_ref[a] > 0, bias, MASKED)
            for lane in range(length // LANES):
                part = bias[:, lane * LANES : (lane + 1) * LANES]
                rows_out[lane, pl.ds(p * heads * rows + a, heads, stride=rows), :] = part
        for w in range(WD):
            column = wide[a, pl.ds(w, devices, stride=rows), :]
            picked[pl.ds(w * rows + a, devices, stride=WD * rows), :] = column
    for lane in range(length // LANES):
        bias_ref[:, lane * LANES : (lane + 1) * LANES] = rows_out[lane].astype(jnp.bfloat16)
    pick_ref[...] = picked[...].astype(jnp.bfloat16).reshape(pick_ref.shape)


def local_bias(pair, own, live, gain, shift, weight):
    rows, length, channels = pair.shape
    heads = weight.shape[1]
    devices = length // rows
    return pl.pallas_call(
        bias_kernel,
        out_shape=(
            jax.ShapeDtypeStruct((2 * heads * rows, length), jnp.bfloat16),
            jax.ShapeDtypeStruct((devices, WD * rows, channels), jnp.bfloat16),
        ),
        in_specs=[VMEM, SMEM, VMEM, VMEM, VMEM, VMEM],
        out_specs=(VMEM, VMEM),
        scratch_shapes=[
            pltpu.VMEM((rows, length, channels), jnp.float32),
            pltpu.VMEM((length // LANES, 2 * heads * rows, LANES), jnp.float32),
            pltpu.VMEM((devices * WD * rows, channels), jnp.float32),
        ],
        compiler_params=params(40),
        name="bias",
    )(pair, own, live, gain, shift, weight)


def project_kernel(which, scale, lines_ref, gain_ref, shift_ref, weight_ref, offset_ref, q_ref, k_ref, v_ref, g_ref):
    inner = k_ref.shape[-1]
    length = k_ref.shape[1]
    for w in range(WD):
        if which == 0:
            x = lines_ref[w].astype(jnp.float32)
        else:
            blocks, packed, channels = lines_ref.shape
            x = lines_ref[...].astype(jnp.float32).reshape(blocks, WD, packed // WD, channels)
            x = x[:, w].reshape(length, channels)
        gain, shift = gain_ref[which : which + 1, :], shift_ref[which : which + 1, :]
        normed = (standardize(x) * gain + shift).astype(jnp.bfloat16)
        weight = weight_ref[0]
        q_ref[w] = (contract(weight[:, :inner], normed, 0, 1) * scale).astype(jnp.bfloat16)
        k_ref[w] = contract(normed, weight[:, inner : 2 * inner], 1, 0).astype(jnp.bfloat16)
        v_ref[w] = contract(weight[:, 2 * inner : 3 * inner], normed, 0, 1).astype(jnp.bfloat16)
        g_ref[w] = jax.nn.sigmoid(contract(weight[:, 3 * inner :], normed, 0, 1) + offset_ref[0])


def project(which, lines, length, gain, shift, weight, offset, head_count):
    channels, wide = weight.shape[1:]
    inner = wide // 4
    if which == 0:
        lines_spec = pl.BlockSpec((WD, length, channels), lambda i: (0, 0, 0))
    else:
        lines_spec = pl.BlockSpec(lines.shape, lambda i: (0, 0, 0))
    flat = pl.BlockSpec(gain.shape, lambda i: (0, 0))
    turned = jax.ShapeDtypeStruct((WD, inner, length), jnp.bfloat16)
    out = lambda shape: pl.BlockSpec(shape, lambda i: (0, 0, 0))
    return pl.pallas_call(
        functools.partial(project_kernel, which, (inner // head_count) ** (-0.5)),
        grid=(1,),
        out_shape=(
            turned,
            jax.ShapeDtypeStruct((WD, length, inner), jnp.bfloat16),
            turned,
            jax.ShapeDtypeStruct((WD, inner, length), jnp.float32),
        ),
        in_specs=[
            lines_spec,
            flat,
            flat,
            pl.BlockSpec((1, channels, wide), lambda i: (which, 0, 0)),
            pl.BlockSpec((1, inner, 1), lambda i: (which, 0, 0)),
        ],
        out_specs=(
            out((WD, inner, length)),
            out((WD, length, inner)),
            out((WD, inner, length)),
            out((WD, inner, length)),
        ),
        compiler_params=params(40),
        cost_estimate=pl.CostEstimate(
            flops=2 * WD * length * channels * wide, bytes_accessed=4 * WD * length * wide, transcendentals=0
        ),
        name="project",
    )(lines, gain, shift, weight, offset[:, :, None])


def attend_kernel(
    mine_ref, other_ref, q0, k0, v0, g0, q1, k1, v1, g1, weight_ref, offset_ref, out0, out1, bias, mixed
):
    chips, along, packed, length = mine_ref.shape
    inner = k0.shape[-1]
    rows = length // (2 * chips * along)
    heads = packed // (2 * rows)
    size = inner // heads
    unrolled = length <= CHUNK
    core = lax.rem(lax.axis_index("col"), 2)
    sides = ((q0, k0, v0, g0, out0), (q1, k1, v1, g1, out1))
    owner = lax.broadcasted_iota(jnp.int32, (inner, CHUNK), 0) // size
    for p, (q, k, v, g, out) in enumerate(sides):
        for pack in range(heads // 2):
            first = (p * heads + 2 * pack) * rows

            def unpack(block):
                chip, row = block // along, block % along
                for source, parity in ((mine_ref, core), (other_ref, 1 - core)):
                    at = pl.multiple_of(((row * chips + chip) * 2 + parity) * rows, rows)
                    both = source[chip, row, first : first + 2 * rows, :].astype(jnp.float32)
                    for i in range(2):
                        bias[i, pl.ds(at, rows), :] = both[i * rows : (i + 1) * rows]

            for_each(chips * along, unpack, unrolled)
            for i in range(2):
                h = 2 * pack + i

                def columns(chunk):
                    at = chunk * CHUNK if unrolled else pl.multiple_of(chunk * CHUNK, CHUNK)
                    if p == 0:
                        added = bias[i, pl.ds(at, CHUNK), :].T
                    else:
                        added = bias[i, :, pl.ds(at, CHUNK)]
                    for w in range(WD):
                        queries = jnp.where(owner == h, q[w, :, pl.ds(at, CHUNK)], jnp.bfloat16(0))
                        scores = contract(k[w], queries, 1, 0) + added
                        expo = jnp.exp(scores - jnp.max(scores, 0, keepdims=True))
                        weights = expo * (1.0 / jnp.sum(expo, 0, keepdims=True))
                        part = contract(
                            v[w, h * size : (h + 1) * size, :], weights.astype(jnp.bfloat16), 1, 0
                        )
                        mixed[w, h * size : (h + 1) * size, pl.ds(at, CHUNK)] = part

                for_each(length // CHUNK, columns, unrolled)
        for w in range(WD):
            gated = (mixed[w] * g[w]).astype(jnp.bfloat16)
            full = contract(gated, weight_ref[p], 0, 0) + offset_ref[p : p + 1, :]
            out[w] = full.astype(jnp.bfloat16)


def attend(mine, other, start, end, weight, offset):
    length = mine.shape[-1]
    inner, channels = weight.shape[1:]
    result = jax.ShapeDtypeStruct((WD, length, channels), jnp.bfloat16)
    return pl.pallas_call(
        attend_kernel,
        out_shape=(result, result),
        in_specs=[VMEM] * 12,
        out_specs=(VMEM, VMEM),
        scratch_shapes=[
            pltpu.VMEM((2, length, length), jnp.float32),
            pltpu.VMEM((WD, inner, length), jnp.float32),
        ],
        compiler_params=params(56),
        name="attend",
    )(mine, other, *start, *end, weight, offset)


def place(pieces, positions):
    out = jnp.zeros((len(pieces),) + pieces[0].shape, pieces[0].dtype)
    for piece, position in zip(pieces, positions):
        out = lax.dynamic_update_index_in_dim(out, piece, position, 0)
    return out


def staged_gather(block):
    rows, cols = lax.axis_size("row"), lax.axis_size("col")
    row, col = lax.axis_index("row"), lax.axis_index("col")
    pieces, positions = [block], [row]
    for shift in range(1, rows):
        pieces.append(lax.ppermute(block, "row", [(i, (i + shift) % rows) for i in range(rows)]))
        positions.append((row - shift) % rows)
    along = place(pieces, positions)
    pieces, positions = [along], [col // 2]
    for flip in range(2, cols, 2):
        pieces.append(lax.ppermute(along, "col", [(i, i ^ flip) for i in range(cols)]))
        positions.append((col ^ flip) // 2)
    chips = place(pieces, positions)
    other = lax.ppermute(chips, "col", [(i, i ^ 1) for i in range(cols)])
    return chips, other


def body(pair, residue_mask, ln_gain, ln_shift, w_proj, w_bias, gate_bias, w_out, out_bias):
    rows, length, channels = pair.shape
    heads = w_bias.shape[2]
    cols = lax.axis_size("col")
    device = lax.axis_index("row") * cols + lax.axis_index("col")
    own = lax.dynamic_slice(residue_mask, (device * rows,), (rows,))
    block, picked = local_bias(
        pair, own, residue_mask[None, :], ln_gain, ln_shift, jnp.transpose(w_bias, (0, 2, 1))
    )
    moved = lax.all_to_all(picked, ("row", "col"), split_axis=0, concat_axis=0, tiled=True)
    mine, other = staged_gather(block)
    start = project(0, pair, length, ln_gain, ln_shift, w_proj, gate_bias, heads)
    end = project(1, moved, length, ln_gain, ln_shift, w_proj, gate_bias, heads)
    return attend(mine, other, start, end, w_out, out_bias)


def solution(mesh):
    return jax.shard_map(
        body,
        mesh=mesh,
        in_specs=(P(("row", "col"), None, None), P(), P(), P(), P(), P(), P(), P(), P()),
        out_specs=(P(("row", "col"), None, None), P(("row", "col"), None, None)),
        check_vma=False,
    )
```

time: 111 us -> 47.2 us (0.43)
  blocking collectives: 81.4 us -> 0 us
  waiting for transfers between devices: 0.01 us -> 13.1 us
  Pallas kernels: 0 us -> 10.9 us
  matrix products: 10.1 us -> 0 us
  starting transfers between devices: 7.3 us -> 12.4 us
  other arithmetic: 4.49 us -> 0 us
  local copies, waits for them, and re-layouts: 6.52 us -> 9.53 us
    all_gather x2 -> x0, blocking collectives: 81.4 us -> none  [the longest x1 43.3 us: body(): lax.all_gather(bias_start, ('row', 'col'), axis=1, tiled=True)]
    pallas_call x0 -> x4, Pallas kernels: none -> 10.9 us  [the longest x1 7.84 us: attend(): pl.pallas_call(attend_kernel, out_shape=(result, result), in_specs=[VMEM]...]
    ppermute x0 -> x7, starting transfers between devices: none -> 9.69 us  [the longest x3 6.06 us: staged_gather(): lax.ppermute(block, 'row', [(i, (i + shift) % rows) for i in range(rows)])]
    ppermute x0 -> x7, waiting for transfers between devices: none -> 8.98 us  [the longest x3 4.52 us: staged_gather(): lax.ppermute(block, 'row', [(i, (i + shift) % rows) for i in range(rows)])]
    unnamed x18 -> x36, local copies, waits for them, and re-layouts: 0.94 us -> 9.18 us
    dot_general x12 -> x0, matrix products: 5.53 us -> none  [the longest x1 1.85 us: attend_lines(): jnp.einsum('whqk,wkhd->wqhd', weights, value_rows, preferred_element_type...]
    all_to_all x1, starting transfers between devices: 7.3 us -> 2.72 us  [body(): lax.all_to_all(picked, ('row', 'col'), split_axis=0, concat_axis=0, tiled...]
    sub x3 -> x0, matrix products: 4.55 us -> none  [the longest x1 3.43 us: attend_lines(): expo = jnp.exp(scores - top)]
  transfers between devices with their start and end apart: 1 -> 8, of which waited for: 0 -> 4; matrix products, arithmetic and copies ran while one was open for 12% -> 1% of each run, Pallas kernels for 0% -> 3%
where the time goes in v1:
time: 47.2 us; the launch traced here: 46.9 us
  waiting for transfers between devices  13.1 us (28%)
  starting transfers between devices  12.4 us (26%)
  Pallas kernels  10.9 us (23%)
  local copies, waits for them, and re-layouts  9.53 us (20%)
  between operations  1.01 us (2%)
    unnamed x36, local copies, waits for them, and re-layouts  9.18 us
    pallas_call x1, Pallas kernels, attend(): pl.pallas_call(attend_kernel, out_shape=(result, result), in_specs=[VMEM]...  7.84 us
    ppermute x3, starting transfers between devices, staged_gather(): lax.ppermute(block, 'row', [(i, (i + shift) % rows) for i in range(rows)])  6.06 us
    ppermute x3, waiting for transfers between devices, staged_gather(): lax.ppermute(block, 'row', [(i, (i + shift) % rows) for i in range(rows)])  4.52 us
    ppermute x3, waiting for transfers between devices, staged_gather(): lax.ppermute(along, 'col', [(i, i ^ flip) for i in range(cols)])  4.45 us
    all_to_all x1, waiting for transfers between devices, body(): lax.all_to_all(picked, ('row', 'col'), split_axis=0, concat_axis=0, tiled...  4.11 us
    ppermute x3, starting transfers between devices, staged_gather(): lax.ppermute(along, 'col', [(i, i ^ flip) for i in range(cols)])  3.55 us
    all_to_all x1, starting transfers between devices, body(): lax.all_to_all(picked, ('row', 'col'), split_axis=0, concat_axis=0, tiled...  2.72 us
  transfers between devices with their start and end apart: 8, of which 4 were waited for; matrix products, arithmetic and copies ran while one was open for 1% of the time, Pallas kernels for 3%

profile of v1, /device:TPU:0, one launch (start us, length us, event | category | flops | bytes accessed | tf_op | source)
XLA Modules:
  0.0 46.9 jit_solution(15864486817868178118)
XLA Ops:
  0.6 0.7 %copy-done.14 = s32[256]{0:T(256)S(1)} copy-done((s32[256]{0:T(256)S(1)}, s32[256]{0:T(256)}, u32[]{:S(2)}) %copy-start.14) | copy-done | bytes 1048
  1.4 0.6 %copy-done.13 = bf16[2,128,4]{1,2,0:T(4,128)(2,1)S(1)} copy-done((bf16[2,128,4]{1,2,0:T(4,128)(2,1)S(1)}, bf16[2,128,4]{1,2,0:T(4,128)(2,1)}, u32[]{:S(2)}) %copy-start.13) | copy-done | bytes 2072
  2.1 1.0 %copy-done = bf16[8,256,128]{2,1,0:T(8,128)(2,1)S(1)} copy-done((bf16[8,256,128]{2,1,0:T(8,128)(2,1)S(1)}, bf16[8,256,128]{2,1,0:T(8,128)(2,1)}, u32[]{:S(2)}) %copy-start) | copy-done | bytes 524312
  3.1 1.8 %bias.1 = (bf16[64,256]{1,0:T(8,128)(2,1)S(1)}, bf16[32,16,128]{2,1,0:T(8,128)(2,1)}) custom-call(bf16[8,256,128]{2,1,0:T(8,128)(2,1)S(1)} %copy-done, s32[8]{0:T(128)S(1)} %dynamic_slice.3.own_ref, s32[1,256]{1,0:T(1,128)S(1)} %bitcast.20, f32[2,128]{1,0:T(2,128)S(1)} %copy-done.11, f32[2,128]{1,0:T(2,128)S(1)} %copy-done.12, bf16[2,4,128]{2,1,0:T(4,128)(2,1)S(1)} %bitcast.19), custom_call_target="tpu_custom_call" | custom-call | tf_op jit(solution)/shard_map/bias/pallas_call | solution.py:75
  4.9 5.0 %collective-permute-start.2 = (bf16[64,256]{1,0:T(8,128)(2,1)S(1)}, bf16[64,256]{1,0:T(8,128)(2,1)S(1)}, u32[]{:S(2)}, u32[]{:S(2)}) collective-permute-start(bf16[64,256]{1,0:T(8,128)(2,1)S(1)} %get-tuple-element.12), channel_id=1, source_target_pairs={{0,24},{8,0},{16,8},{24,16},{1,25},{9,1},{17,9},{25,17},{2,26},{10... | collective-permute-start | bytes 98312 | tf_op jit(solution)/shard_map/ppermute | solution.py:233
  10.0 1.0 %collective-permute-start = (bf16[64,256]{1,0:T(8,128)(2,1)S(1)}, bf16[64,256]{1,0:T(8,128)(2,1)S(1)}, u32[]{:S(2)}, u32[]{:S(2)}) collective-permute-start(bf16[64,256]{1,0:T(8,128)(2,1)S(1)} %get-tuple-element.12), channel_id=1, source_target_pairs={{0,8},{8,16},{16,24},{24,0},{1,9},{9,17},{17,25},{25,1},{2,10},{10... | collective-permute-start | bytes 98312 | tf_op jit(solution)/shard_map/ppermute | solution.py:233
  11.2 4.5 %collective-permute-done = bf16[64,256]{1,0:T(8,128)(2,1)S(1)} collective-permute-done((bf16[64,256]{1,0:T(8,128)(2,1)S(1)}, bf16[64,256]{1,0:T(8,128)(2,1)S(1)}, u32[]{:S(2)}, u32[]{:S(2)}) %collective-permute-start) | collective-permute-done | bytes 32800 | tf_op jit(solution)/shard_map/ppermute | solution.py:233
  15.8 2.5 %collective-permute-start.5 = (bf16[4,64,256]{2,1,0:T(8,128)(2,1)S(1)}, bf16[4,64,256]{2,1,0:T(8,128)(2,1)S(1)}, u32[]{:S(2)}, u32[]{:S(2)}) collective-permute-start(bf16[4,64,256]{2,1,0:T(8,128)(2,1)S(1)} %bitcast_dynamic-update-slice_fusion.4), channel_id=1, source_target_pairs={{0,6},{1,7},{2,4},{3,5},{4,2},{5,3},{6,0},{7,1},{8,14},{9,15},{10,... | collective-permute-start | bytes 393224 | tf_op jit(solution)/shard_map/ppermute | solution.py:238
  19.4 4.4 %collective-permute-done.3 = bf16[4,64,256]{2,1,0:T(8,128)(2,1)S(1)} collective-permute-done((bf16[4,64,256]{2,1,0:T(8,128)(2,1)S(1)}, bf16[4,64,256]{2,1,0:T(8,128)(2,1)S(1)}, u32[]{:S(2)}, u32[]{:S(2)}) %collective-permute-start.3) | collective-permute-done | bytes 131104 | tf_op jit(solution)/shard_map/ppermute | solution.py:238
  24.0 2.7 %all-to-all-start = ((bf16[32,16,128]{2,1,0:T(8,128)(2,1)}), bf16[32,16,128]{2,1,0:T(8,128)(2,1)S(1)}, u32[]{:S(2)}, u32[]{:S(2)}) async-start(bf16[32,16,128]{2,1,0:T(8,128)(2,1)} %get-tuple-element.17), calls=%async_computation | async-start | bytes 262144 | tf_op jit(solution)/shard_map/all_to_all | solution.py:254
  26.8 0.7 %copy-done.17 = f32[2,128]{1,0:T(2,128)S(1)} copy-done((f32[2,128]{1,0:T(2,128)S(1)}, f32[2,128]{1,0:T(2,128)}, u32[]{:S(2)}) %copy-start.17) | copy-done | bytes 1048
  27.6 0.6 %project.2 = (bf16[2,128,256]{2,1,0:T(8,128)(2,1)S(1)}, bf16[2,256,128]{2,1,0:T(8,128)(2,1)S(1)}, bf16[2,128,256]{2,1,0:T(8,128)(2,1)S(1)}, f32[2,128,256]{2,1,0:T(8,128)S(1)}) custom-call(bf16[8,256,128]{2,1,0:T(8,128)(2,1)S(1)} %copy-done.1, f32[2,128]{1,0:T(2,128)S(1)} %copy-done.11, f32[2,128]{1,0:T(2,128)S(1)} %copy-done.12, ...), custom_call_target="tpu_custom_call" | custom-call | flops 67108864 | bytes 1048576 | tf_op jit(solution)/shard_map/project/pallas_call | solution.py:122
  28.2 0.7 %copy-done.3 = f32[2,128,256]{2,1,0:T(8,128)} copy-done((f32[2,128,256]{2,1,0:T(8,128)}, f32[2,128,256]{2,1,0:T(8,128)S(1)}, u32[]{:S(2)}) %copy-start.3) | copy-done | bytes 262168
  28.9 0.6 %copy-done.5 = bf16[2,128,256]{2,1,0:T(8,128)(2,1)} copy-done((bf16[2,128,256]{2,1,0:T(8,128)(2,1)}, bf16[2,128,256]{2,1,0:T(8,128)(2,1)S(1)}, u32[]{:S(2)}) %copy-start.5) | copy-done | bytes 131096
  29.6 0.6 %copy-done.6 = bf16[2,256,128]{2,1,0:T(8,128)(2,1)} copy-done((bf16[2,256,128]{2,1,0:T(8,128)(2,1)}, bf16[2,256,128]{2,1,0:T(8,128)(2,1)S(1)}, u32[]{:S(2)}) %copy-start.6) | copy-done | bytes 131096
  30.2 0.6 %copy-done.7 = bf16[2,128,256]{2,1,0:T(8,128)(2,1)} copy-done((bf16[2,128,256]{2,1,0:T(8,128)(2,1)}, bf16[2,128,256]{2,1,0:T(8,128)(2,1)S(1)}, u32[]{:S(2)}) %copy-start.7) | copy-done | bytes 131096
  30.9 4.1 %all-to-all-done.lines_ref = bf16[32,16,128]{2,1,0:T(8,128)(2,1)S(1)} async-done(((bf16[32,16,128]{2,1,0:T(8,128)(2,1)}), bf16[32,16,128]{2,1,0:T(8,128)(2,1)S(1)}, u32[]{:S(2)}, u32[]{:S(2)}) %all-to-all-start) | async-done | bytes 131104 | tf_op jit(solution)/shard_map/all_to_all | solution.py:254
  35.0 0.6 %project.3 = (bf16[2,128,256]{2,1,0:T(8,128)(2,1)S(1)}, bf16[2,256,128]{2,1,0:T(8,128)(2,1)S(1)}, bf16[2,128,256]{2,1,0:T(8,128)(2,1)S(1)}, f32[2,128,256]{2,1,0:T(8,128)S(1)}) custom-call(bf16[32,16,128]{2,1,0:T(8,128)(2,1)S(1)} %all-to-all-done.lines_ref, f32[2,128]{1,0:T(2,128)S(1)} %copy-done.11, f32[2,128]{1,0:T(2,128)S(1)} %copy-done.12, ...), custom_call_target="tpu_custom_call" | custom-call | flops 67108864 | bytes 1048576 | tf_op jit(solution)/shard_map/project/pallas_call | solution.py:122
  35.6 0.7 %copy-done.4 = f32[2,128,256]{2,1,0:T(8,128)} copy-done((f32[2,128,256]{2,1,0:T(8,128)}, f32[2,128,256]{2,1,0:T(8,128)S(1)}, u32[]{:S(2)}) %copy-start.4) | copy-done | bytes 262168
  36.3 0.6 %copy-done.8 = bf16[2,128,256]{2,1,0:T(8,128)(2,1)} copy-done((bf16[2,128,256]{2,1,0:T(8,128)(2,1)}, bf16[2,128,256]{2,1,0:T(8,128)(2,1)S(1)}, u32[]{:S(2)}) %copy-start.8) | copy-done | bytes 131096
  37.0 0.6 %copy-done.9 = bf16[2,256,128]{2,1,0:T(8,128)(2,1)} copy-done((bf16[2,256,128]{2,1,0:T(8,128)(2,1)}, bf16[2,256,128]{2,1,0:T(8,128)(2,1)S(1)}, u32[]{:S(2)}) %copy-start.9) | copy-done | bytes 131096
  37.6 0.6 %copy-done.10 = bf16[2,128,256]{2,1,0:T(8,128)(2,1)} copy-done((bf16[2,128,256]{2,1,0:T(8,128)(2,1)}, bf16[2,128,256]{2,1,0:T(8,128)(2,1)S(1)}, u32[]{:S(2)}) %copy-start.10) | copy-done | bytes 131096
  38.2 0.8 %copy-done.16 = bf16[4,4,64,256]{3,2,1,0:T(8,128)(2,1)} copy-done((bf16[4,4,64,256]{3,2,1,0:T(8,128)(2,1)}, bf16[4,4,64,256]{3,2,1,0:T(8,128)(2,1)S(1)}, u32[]{:S(2)}) %copy-start.16) | copy-done | bytes 524312
  39.1 7.8 %attend.1 = (bf16[2,256,128]{2,1,0:T(8,128)(2,1)}, bf16[2,256,128]{2,1,0:T(8,128)(2,1)}) custom-call(bf16[4,4,64,256]{3,2,1,0:T(8,128)(2,1)} %copy-done.15, bf16[4,4,64,256]{3,2,1,0:T(8,128)(2,1)} %copy-done.16, bf16[2,128,256]{2,1,0:T(8,128)(2,1)} %copy-done.5, bf16[2,256,128]{2,1,0:T(8,128)(2,1)} %copy-done.6, bf16[2,128,256]{2,1,0:T(8,128)(2,1)} %copy-done.7, ...), custom_call_target="tpu_custom_call" | custom-call | tf_op jit(solution)/shard_map/attend/pallas_call | solution.py:207
  (44 shorter events, 1.7 us)
Async XLA Ops:
  0.6 0.7 %copy-start.14 = (s32[256]{0:T(256)S(1)}, s32[256]{0:T(256)}, u32[]{:S(2)}) copy-start(s32[256]{0:T(256)} %param.10) | copy-start | bytes 3076
  1.3 0.7 %copy-start.13 = (bf16[2,128,4]{1,2,0:T(4,128)(2,1)S(1)}, bf16[2,128,4]{1,2,0:T(4,128)(2,1)}, u32[]{:S(2)}) copy-start(bf16[2,128,4]{1,2,0:T(4,128)(2,1)} %param.14) | copy-start | bytes 6148
  1.4 0.7 %copy-start.12 = (f32[2,128]{1,0:T(2,128)S(1)}, f32[2,128]{1,0:T(2,128)}, u32[]{:S(2)}) copy-start(f32[2,128]{1,0:T(2,128)} %shift_ref.5) | copy-start | bytes 3076
  1.4 0.7 %copy-start.11 = (f32[2,128]{1,0:T(2,128)S(1)}, f32[2,128]{1,0:T(2,128)}, u32[]{:S(2)}) copy-start(f32[2,128]{1,0:T(2,128)} %gain_ref.5) | copy-start | bytes 3076
  2.1 1.0 %copy-start = (bf16[8,256,128]{2,1,0:T(8,128)(2,1)S(1)}, bf16[8,256,128]{2,1,0:T(8,128)(2,1)}, u32[]{:S(2)}) copy-start(bf16[8,256,128]{2,1,0:T(8,128)(2,1)} %lines_ref.1) | copy-start | bytes 1572868
  4.9 10.8 %collective-permute-start.2 = (bf16[64,256]{1,0:T(8,128)(2,1)S(1)}, bf16[64,256]{1,0:T(8,128)(2,1)S(1)}, u32[]{:S(2)}, u32[]{:S(2)}) collective-permute-start(bf16[64,256]{1,0:T(8,128)(2,1)S(1)} %get-tuple-element.12), channel_id=1, source_target_pairs={{0,24},{8,0},{16,8},{24,16},{1,25},{9,1},{17,9},{25,17},{2,26},{10... | collective-permute-start | bytes 98312 | tf_op jit(solution)/shard_map/ppermute | solution.py:233
  10.0 5.7 %collective-permute-start.1 = (bf16[64,256]{1,0:T(8,128)(2,1)S(1)}, bf16[64,256]{1,0:T(8,128)(2,1)S(1)}, u32[]{:S(2)}, u32[]{:S(2)}) collective-permute-start(bf16[64,256]{1,0:T(8,128)(2,1)S(1)} %get-tuple-element.12), channel_id=1, source_target_pairs={{0,16},{8,24},{16,0},{24,8},{1,17},{9,25},{17,1},{25,9},{2,18},{10... | collective-permute-start | bytes 98312 | tf_op jit(solution)/shard_map/ppermute | solution.py:233
  10.0 5.7 %collective-permute-start = (bf16[64,256]{1,0:T(8,128)(2,1)S(1)}, bf16[64,256]{1,0:T(8,128)(2,1)S(1)}, u32[]{:S(2)}, u32[]{:S(2)}) collective-permute-start(bf16[64,256]{1,0:T(8,128)(2,1)S(1)} %get-tuple-element.12), channel_id=1, source_target_pairs={{0,8},{8,16},{16,24},{24,0},{1,9},{9,17},{17,25},{25,1},{2,10},{10... | collective-permute-start | bytes 98312 | tf_op jit(solution)/shard_map/ppermute | solution.py:233
  15.8 8.1 %collective-permute-start.5 = (bf16[4,64,256]{2,1,0:T(8,128)(2,1)S(1)}, bf16[4,64,256]{2,1,0:T(8,128)(2,1)S(1)}, u32[]{:S(2)}, u32[]{:S(2)}) collective-permute-start(bf16[4,64,256]{2,1,0:T(8,128)(2,1)S(1)} %bitcast_dynamic-update-slice_fusion.4), channel_id=1, source_target_pairs={{0,6},{1,7},{2,4},{3,5},{4,2},{5,3},{6,0},{7,1},{8,14},{9,15},{10,... | collective-permute-start | bytes 393224 | tf_op jit(solution)/shard_map/ppermute | solution.py:238
  18.3 5.6 %collective-permute-start.4 = (bf16[4,64,256]{2,1,0:T(8,128)(2,1)S(1)}, bf16[4,64,256]{2,1,0:T(8,128)(2,1)S(1)}, u32[]{:S(2)}, u32[]{:S(2)}) collective-permute-start(bf16[4,64,256]{2,1,0:T(8,128)(2,1)S(1)} %bitcast_dynamic-update-slice_fusion.4), channel_id=1, source_target_pairs={{0,4},{1,5},{2,6},{3,7},{4,0},{5,1},{6,2},{7,3},{8,12},{9,13},{10,... | collective-permute-start | bytes 393224 | tf_op jit(solution)/shard_map/ppermute | solution.py:238
  18.8 5.0 %collective-permute-start.3 = (bf16[4,64,256]{2,1,0:T(8,128)(2,1)S(1)}, bf16[4,64,256]{2,1,0:T(8,128)(2,1)S(1)}, u32[]{:S(2)}, u32[]{:S(2)}) collective-permute-start(bf16[4,64,256]{2,1,0:T(8,128)(2,1)S(1)} %bitcast_dynamic-update-slice_fusion.4), channel_id=1, source_target_pairs={{0,2},{1,3},{2,0},{3,1},{4,6},{5,7},{6,4},{7,5},{8,10},{9,11},{10,... | collective-permute-start | bytes 393224 | tf_op jit(solution)/shard_map/ppermute | solution.py:238
  23.8 3.8 %copy-start.1 = (bf16[8,256,128]{2,1,0:T(8,128)(2,1)S(1)}, bf16[8,256,128]{2,1,0:T(8,128)(2,1)}, u32[]{:S(2)}) copy-start(bf16[8,256,128]{2,1,0:T(8,128)(2,1)} %lines_ref.1) | copy-start | bytes 1572868
  23.9 4.3 %copy-start.15 = (bf16[4,4,64,256]{3,2,1,0:T(8,128)(2,1)}, bf16[4,4,64,256]{3,2,1,0:T(8,128)(2,1)S(1)}, u32[]{:S(2)}) copy-start(bf16[4,4,64,256]{3,2,1,0:T(8,128)(2,1)S(1)} %bitcast_dynamic-update-slice_fusion.mine_ref) | copy-start | bytes 1572868
  23.9 3.7 %copy-start.2 = (bf16[2,128,512]{2,1,0:T(8,128)(2,1)S(1)}, bf16[2,128,512]{2,1,0:T(8,128)(2,1)}, u32[]{:S(2)}) copy-start(bf16[2,128,512]{2,1,0:T(8,128)(2,1)} %weight_ref.4) | copy-start | bytes 786436
  23.9 14.3 %collective-permute-start.6 = (bf16[4,4,64,256]{3,2,1,0:T(8,128)(2,1)S(1)}, bf16[4,4,64,256]{3,2,1,0:T(8,128)(2,1)S(1)}, u32[]{:S(2)}, u32[]{:S(2)}) collective-permute-start(bf16[4,4,64,256]{3,2,1,0:T(8,128)(2,1)S(1)} %bitcast_dynamic-update-slice_fusion.mine_ref), channel_id=1, source_target_pairs={{0,1},{1,0},{2,3},{3,2},{4,5},{5,4},{6,7},{7,6},{8,9},{9,8},{10,11... | collective-permute-start | bytes 1572872 | tf_op jit(solution)/shard_map/ppermute | solution.py:241
  24.0 11.0 %all-to-all-start = ((bf16[32,16,128]{2,1,0:T(8,128)(2,1)}), bf16[32,16,128]{2,1,0:T(8,128)(2,1)S(1)}, u32[]{:S(2)}, u32[]{:S(2)}) async-start(bf16[32,16,128]{2,1,0:T(8,128)(2,1)} %get-tuple-element.17), calls=%async_computation | async-start | bytes 262144 | tf_op jit(solution)/shard_map/all_to_all | solution.py:254
  26.7 0.7 %copy-start.17 = (f32[2,128]{1,0:T(2,128)S(1)}, f32[2,128]{1,0:T(2,128)}, u32[]{:S(2)}) copy-start(f32[2,128]{1,0:T(2,128)} %param.15) | copy-start | bytes 3076
  28.2 0.7 %copy-start.3 = (f32[2,128,256]{2,1,0:T(8,128)}, f32[2,128,256]{2,1,0:T(8,128)S(1)}, u32[]{:S(2)}) copy-start(f32[2,128,256]{2,1,0:T(8,128)S(1)} %get-tuple-element.16.g0) | copy-start | bytes 786436
  28.9 0.7 %copy-start.5 = (bf16[2,128,256]{2,1,0:T(8,128)(2,1)}, bf16[2,128,256]{2,1,0:T(8,128)(2,1)S(1)}, u32[]{:S(2)}) copy-start(bf16[2,128,256]{2,1,0:T(8,128)(2,1)S(1)} %get-tuple-element.13.q0) | copy-start | bytes 393220
  29.6 0.7 %copy-start.6 = (bf16[2,256,128]{2,1,0:T(8,128)(2,1)}, bf16[2,256,128]{2,1,0:T(8,128)(2,1)S(1)}, u32[]{:S(2)}) copy-start(bf16[2,256,128]{2,1,0:T(8,128)(2,1)S(1)} %get-tuple-element.14.k0) | copy-start | bytes 393220
  35.6 0.7 %copy-start.4 = (f32[2,128,256]{2,1,0:T(8,128)}, f32[2,128,256]{2,1,0:T(8,128)S(1)}, u32[]{:S(2)}) copy-start(f32[2,128,256]{2,1,0:T(8,128)S(1)} %get-tuple-element.21.g1) | copy-start | bytes 786436
  36.3 0.6 %copy-start.8 = (bf16[2,128,256]{2,1,0:T(8,128)(2,1)}, bf16[2,128,256]{2,1,0:T(8,128)(2,1)S(1)}, u32[]{:S(2)}) copy-start(bf16[2,128,256]{2,1,0:T(8,128)(2,1)S(1)} %get-tuple-element.18.q1) | copy-start | bytes 393220
  37.6 0.6 %copy-start.10 = (bf16[2,128,256]{2,1,0:T(8,128)(2,1)}, bf16[2,128,256]{2,1,0:T(8,128)(2,1)S(1)}, u32[]{:S(2)}) copy-start(bf16[2,128,256]{2,1,0:T(8,128)(2,1)S(1)} %get-tuple-element.20.v1) | copy-start | bytes 393220
  38.2 0.8 %copy-start.16 = (bf16[4,4,64,256]{3,2,1,0:T(8,128)(2,1)}, bf16[4,4,64,256]{3,2,1,0:T(8,128)(2,1)S(1)}, u32[]{:S(2)}) copy-start(bf16[4,4,64,256]{3,2,1,0:T(8,128)(2,1)S(1)} %collective-permute-done.6.other_ref) | copy-start | bytes 1572868
  (2 other events, 1.3 us)

commit v2 on v0

v2 whole, which is shorter than its diff:
```python
import functools

import jax
import jax.numpy as jnp
from jax import lax
from jax.experimental import pallas as pl
from jax.experimental.pallas import tpu as pltpu
from jax.sharding import PartitionSpec as P

WD = 2
EPS = 1e-05
MASKED = -1000000000.0
CHUNK = 256
VMEM = pl.BlockSpec(memory_space=pltpu.VMEM)
HBM = pl.BlockSpec(memory_space=pltpu.HBM)


def params(megabytes):
    return pltpu.CompilerParams(vmem_limit_bytes=megabytes * 1024 * 1024)


def for_each(count, step, unrolled):
    if unrolled:
        for index in range(count):
            step(index)
    else:
        lax.fori_loop(0, count, lambda index, carry: (step(index), carry)[1], 0)


def standardize(wide):
    center = jnp.mean(wide, -1, keepdims=True)
    away = wide - center
    spread = jnp.mean(jnp.square(away), -1, keepdims=True)
    return away * lax.rsqrt(spread + EPS)


def contract(left, right, left_dim, right_dim):
    return lax.dot_general(
        left, right, (((left_dim,), (right_dim,)), ((), ())), preferred_element_type=jnp.float32
    )


def flipped(index, flip):
    bit = 1
    while bit <= flip:
        if flip & bit:
            index = index + bit - 2 * bit * lax.rem(lax.div(index, bit), 2)
        bit *= 2
    return index


def bias_kernel(along, chips, pair_hbm, live_hbm, gain_hbm, shift_hbm, weight_hbm, out_ref, *rest):
    picks = rest[:chips]
    pair, live_row, live_each, gain, shift, weight, blocks, rows_out, wide, picked, sems, pair_sems = rest[chips:]
    rows, length, channels = pair.shape
    heads = weight.shape[1]
    lanes = out_ref.shape[1]
    small = [
        pltpu.make_async_copy(source, target, sems.at[i])
        for i, (source, target) in enumerate(
            ((live_hbm, live_row), (live_hbm, live_each), (gain_hbm, gain), (shift_hbm, shift), (weight_hbm, weight))
        )
    ]
    large = [pltpu.make_async_copy(pair_hbm.at[a], pair.at[a], pair_sems.at[a]) for a in range(rows)]
    large[0].start()
    for copy in small:
        copy.start()
    for copy in large[1:]:
        copy.start()
    device = lax.axis_index("row") * lax.axis_size("col") + lax.axis_index("col")
    for copy in small + large:
        copy.wait()
    blocks[...] = jnp.zeros_like(blocks)
    for p in range(2):
        at = slice(p * heads, (p + 1) * heads)
        blocks[at, p * channels : (p + 1) * channels] = weight[p].astype(jnp.float32)
    paired = blocks[: 2 * heads].astype(jnp.bfloat16)
    live = jnp.broadcast_to(live_row[...], (2 * heads, length))
    first = lax.broadcasted_iota(jnp.int32, live.shape, 0) < heads
    for a in range(rows):
        x = pair[a].astype(jnp.float32)
        wide[a] = x
        z = standardize(x)
        normed = jnp.concatenate(
            [(z * gain[p : p + 1, :] + shift[p : p + 1, :]).astype(jnp.bfloat16) for p in range(2)], 1
        )
        bias = contract(paired, normed, 1, 1)
        kept = jnp.where(first, live, live_each[0, device * rows + a])
        bias = jnp.where(kept > 0, bias, MASKED)
        for lane in range(length // lanes):
            part = bias[:, lane * lanes : (lane + 1) * lanes]
            rows_out[pl.ds(2 * lane * heads * rows + a, 2 * heads, stride=rows), :] = part
    out_ref[...] = rows_out[...].astype(jnp.bfloat16)
    devices = length // rows
    for a in range(rows):
        for w in range(WD):
            column = wide[a, pl.ds(w, devices, stride=rows), :]
            picked[pl.ds(w * rows + a, devices, stride=WD * rows), :] = column
    chip = lax.div(lax.axis_index("col"), 2)
    both = 2 * WD * rows
    for flip, pick in enumerate(picks):
        for shift in range(along):
            row = lax.rem(lax.axis_index("row") + shift, along)
            at = pl.multiple_of((row * chips + flipped(chip, flip)) * both, both)
            pick[shift] = picked[pl.ds(at, both), :].astype(jnp.bfloat16)


def local_bias(pair, live, gain, shift, weight, along, chips):
    rows, length, channels = pair.shape
    heads = weight.shape[1]
    pick = jax.ShapeDtypeStruct((along, 2 * WD * rows, channels), jnp.bfloat16)
    packed = 2 * heads * rows * (length // channels)
    out = pl.pallas_call(
        functools.partial(bias_kernel, along, chips),
        out_shape=(jax.ShapeDtypeStruct((packed, channels), jnp.bfloat16),) + (pick,) * chips,
        in_specs=[HBM] * 5,
        out_specs=(VMEM,) * (1 + chips),
        scratch_shapes=[
            pltpu.VMEM(pair.shape, pair.dtype),
            pltpu.VMEM(live.shape, live.dtype),
            pltpu.SMEM(live.shape, live.dtype),
            pltpu.VMEM(gain.shape, gain.dtype),
            pltpu.VMEM(shift.shape, shift.dtype),
            pltpu.VMEM(weight.shape, weight.dtype),
            pltpu.VMEM((4 * heads, 2 * channels), jnp.float32),
            pltpu.VMEM((packed, channels), jnp.float32),
            pltpu.VMEM(pair.shape, jnp.float32),
            pltpu.VMEM((length * WD, channels), jnp.float32),
            pltpu.SemaphoreType.DMA((5,)),
            pltpu.SemaphoreType.DMA((rows,)),
        ],
        compiler_params=params(60),
        name="bias",
    )(pair, live, gain, shift, weight)
    return out[0], out[1:]


def turned(row):
    return jnp.broadcast_to(row, (row.shape[1], row.shape[1])).T[:, :1]


def turned_over(index, bit):
    return lax.rem(lax.div(index, bit), 2) == 1


def to_relative(x, along, chips, rows):
    row, col = lax.axis_index("row"), lax.axis_index("col")
    cols = 2 * chips
    grid = [[x[(r * cols + c) * rows : (r * cols + c + 1) * rows] for c in range(cols)] for r in range(along)]
    bit = 1
    while bit < cols:
        swap = turned_over(col, bit)
        grid = [[jnp.where(swap, line[c ^ bit], line[c]) for c in range(cols)] for line in grid]
        bit *= 2
    grid = [grid[-t % along] for t in range(along)]
    bit = 1
    while bit < along:
        move = turned_over(row, bit)
        grid = [
            [jnp.where(move, grid[(t - bit) % along][c], grid[t][c]) for c in range(cols)] for t in range(along)
        ]
        bit *= 2
    return jnp.concatenate(
        [grid[s][2 * flip + other] for other in range(2) for flip in range(chips) for s in range(along)], 0
    )


def to_devices(x, along, chips, rows):
    row, col = lax.axis_index("row"), lax.axis_index("col")
    cols = 2 * chips
    at = lambda c, s: (((c % 2) * chips + c // 2) * along + s) * rows
    grid = [[x[at(c, s) : at(c, s) + rows] for c in range(cols)] for s in range(along)]
    bit = 1
    while bit < along:
        move = turned_over(row, bit)
        grid = [
            [jnp.where(move, grid[(s + bit) % along][c], grid[s][c]) for c in range(cols)] for s in range(along)
        ]
        bit *= 2
    grid = [grid[-r % along] for r in range(along)]
    bit = 1
    while bit < cols:
        swap = turned_over(col, bit)
        grid = [[jnp.where(swap, line[c ^ bit], line[c]) for c in range(cols)] for line in grid]
        bit *= 2
    return jnp.concatenate([block for line in grid for block in line], 0)


def queries_and_gates(normed, scale, weight, offset, q_ref, g_ref, w):
    inner = weight.shape[1] // 4
    q_ref[w] = (contract(weight[:, :inner], normed, 0, 1) * scale).astype(jnp.bfloat16)
    g_ref[w] = jax.nn.sigmoid(contract(weight[:, 3 * inner :], normed, 0, 1) + offset)


def keys_and_values(normed, weight, k_ref, v_ref, w):
    _, heads, _, size = k_ref.shape
    inner = heads * size
    for h in range(heads):
        at = inner + h * size
        k_ref[w, h] = contract(normed, weight[:, at : at + size], 1, 0).astype(jnp.bfloat16)
    v_ref[w] = contract(weight[:, 2 * inner : 3 * inner], normed, 0, 1).astype(jnp.bfloat16)


def lines_kernel(along, chips, lines_ref, gain_ref, shift_ref, weight_ref, offset_ref, q_ref, k_ref, v_ref, g_ref):
    size = k_ref.shape[-1]
    rows = lines_ref.shape[1] // (2 * chips * along)
    offset = turned(offset_ref[0:1, :])
    weight = weight_ref[0]
    for w in range(WD):
        normed = standardize(lines_ref[w].astype(jnp.float32)) * gain_ref[0:1, :] + shift_ref[0:1, :]
        keys_and_values(normed.astype(jnp.bfloat16), weight, k_ref, v_ref, w)
        near = to_relative(normed, along, chips, rows).astype(jnp.bfloat16)
        queries_and_gates(near, size ** (-0.5), weight, offset, q_ref, g_ref, w)


def projected(length, inner, heads):
    wide = (WD, inner, length)
    return (
        (wide, jnp.bfloat16),
        ((WD, heads, length, inner // heads), jnp.bfloat16),
        (wide, jnp.bfloat16),
        (wide, jnp.float32),
    )


def local_lines(pair, gain, shift, weight, offset, heads, along, chips):
    _, length, channels = pair.shape
    wide = weight.shape[2]
    shapes = projected(length, wide // 4, heads)
    whole = lambda shape: pl.BlockSpec(shape, lambda i: (0,) * len(shape))
    return pl.pallas_call(
        functools.partial(lines_kernel, along, chips),
        grid=(1,),
        out_shape=tuple(jax.ShapeDtypeStruct(shape, dtype) for shape, dtype in shapes),
        in_specs=[
            whole((WD, length, channels)), whole(gain.shape), whole(gain.shape),
            whole((1, channels, wide)), whole(gain.shape),
        ],
        out_specs=tuple(whole(shape) for shape, _ in shapes),
        compiler_params=params(8 + length // 32),
        cost_estimate=pl.CostEstimate(
            flops=2 * WD * length * channels * wide, bytes_accessed=4 * WD * length * wide, transcendentals=0
        ),
        name="lines",
    )(pair, gain, shift, weight, offset)


def unpack(source, p, pack, rows, heads, turn, into, at):
    chips, along, _, lanes = source.shape
    packed = 2 * heads * rows
    half = chips * along * rows
    slots = into.shape[0]
    for lane in range(into.shape[2 - turn] // lanes):
        first = lane * packed + (p * heads + 2 * pack) * rows
        both = [
            source[flip, shift, first : first + 2 * rows, :].astype(jnp.float32)
            for flip in range(chips)
            for shift in range(along)
        ]
        there = slice(lane * lanes, (lane + 1) * lanes)
        for i in range(2):
            slot = (2 * pack + i) % slots
            block = jnp.concatenate([part[i * rows : (i + 1) * rows] for part in both], 0)
            if turn:
                into[slot, there, at : at + half] = block.T
            else:
                into[slot, at : at + half, there] = block


def softmax_mix(keys, queries, values, added):
    scores = [contract(k, q, 1, 0) + added for k, q in zip(keys, queries)]
    tops = [jnp.max(score, 0, keepdims=True) for score in scores]
    expos = [jnp.exp(score - top) for score, top in zip(scores, tops)]
    shares = [1.0 / jnp.sum(expo, 0, keepdims=True) for expo in expos]
    weights = [(expo * share).astype(jnp.bfloat16) for expo, share in zip(expos, shares)]
    return [contract(v, weight, 1, 0) for v, weight in zip(values, weights)]


def start_half(source, other, q, k, v, mixed, bias):
    _, heads, length, size = k.shape
    half = length // 2
    rows = half // (source.shape[0] * source.shape[1])
    width = min(half, CHUNK)
    for pack in range(heads // 2):
        unpack(source, 0, pack, rows, heads, 1, bias, 0)
        for i in range(2):
            part = slice((2 * pack + i) * size, (2 * pack + i + 1) * size)

            def step(chunk):
                near = pl.ds(chunk * width if half == width else pl.multiple_of(chunk * width, width), width)
                there = pl.ds(other * half + chunk * width, width)
                if half != width:
                    there = pl.ds(pl.multiple_of(other * half + chunk * width, width), width)
                outs = softmax_mix(
                    [k[w, 2 * pack + i] for w in range(WD)],
                    [q[w, part, there] for w in range(WD)],
                    [v[w, part, :] for w in range(WD)],
                    bias[(2 * pack + i) % bias.shape[0], :, near],
                )
                for w in range(WD):
                    mixed[w, part, near] = outs[w]

            for_each(half // width, step, half == width)


def early_kernel(mine_ref, q, k, v, mixed, bias):
    start_half(mine_ref, 0, q, k, v, mixed, bias)


def attend_early(mine, q, k, v):
    _, heads, length, size = k.shape
    return pl.pallas_call(
        early_kernel,
        out_shape=jax.ShapeDtypeStruct((WD, heads * size, length // 2), jnp.float32),
        in_specs=[VMEM] * 4,
        out_specs=VMEM,
        scratch_shapes=[pltpu.VMEM((heads if length <= CHUNK else 2, length, length // 2), jnp.float32)],
        compiler_params=params(8 if length <= CHUNK else 40),
        cost_estimate=pl.CostEstimate(
            flops=4 * WD * heads * size * length * length,
            bytes_accessed=4 * WD * heads * length * length,
            transcendentals=WD * heads * length * length // 2,
        ),
        name="early",
    )(mine, q, k, v)


def attend_kernel(
    mine_ref, other_ref, early_ref, q0, k0, v0, g0,
    gain_ref, shift_ref, proj_ref, gate_ref, weight_ref, offset_ref,
    out0, out1, turned_bias, bias, late, mixed, q1, k1, v1, g1,
):
    chips, along, _, _ = mine_ref.shape
    _, heads, length, size = k0.shape
    half = length // 2
    rows = half // (chips * along)
    packed = 2 * heads * rows * (length // mine_ref.shape[3])
    first = pl.multiple_of(packed + lax.rem(lax.axis_index("col"), 2) * WD * rows, WD * rows)
    offset = turned(gate_ref[1:2, :])
    blocks = []
    for source in (mine_ref, other_ref):
        for flip in range(chips):
            for shift in range(along):
                both = source[flip, shift, pl.ds(first, WD * rows), :].astype(jnp.float32)
                blocks.append(both.reshape(WD, rows, -1))
    for w in range(WD):
        x = jnp.concatenate([block[w] for block in blocks], 0)
        normed = standardize(x) * gain_ref[1:2, :] + shift_ref[1:2, :]
        keys_and_values(normed.astype(jnp.bfloat16), proj_ref[1], k1, v1, w)
        ordered = to_devices(normed, along, chips, rows).astype(jnp.bfloat16)
        queries_and_gates(ordered, size ** (-0.5), proj_ref[1], offset, q1, g1, w)
    start_half(other_ref, 1, q0, k0, v0, late, turned_bias)
    for w in range(WD):
        gated = (jnp.concatenate([early_ref[w], late[w]], 1) * g0[w]).astype(jnp.bfloat16)
        full = contract(gated, weight_ref[0], 0, 0) + offset_ref[0:1, :]
        out0[w] = to_devices(full, along, chips, rows).astype(jnp.bfloat16)
    for pack in range(heads // 2):
        unpack(mine_ref, 1, pack, rows, heads, 0, bias, 0)
        unpack(other_ref, 1, pack, rows, heads, 0, bias, half)
        for i in range(2):
            part = slice((2 * pack + i) * size, (2 * pack + i + 1) * size)

            def step(chunk):
                there = pl.ds(chunk * CHUNK if length == CHUNK else pl.multiple_of(chunk * CHUNK, CHUNK), CHUNK)
                outs = softmax_mix(
                    [k1[w, 2 * pack + i] for w in range(WD)],
                    [q1[w, part, there] for w in range(WD)],
                    [v1[w, part, :] for w in range(WD)],
                    bias[(2 * pack + i) % bias.shape[0], :, there],
                )
                for w in range(WD):
                    mixed[w, part, there] = outs[w]

            for_each(length // CHUNK, step, length == CHUNK)
    for w in range(WD):
        gated = (mixed[w] * g1[w]).astype(jnp.bfloat16)
        full = contract(gated, weight_ref[1], 0, 0) + offset_ref[1:2, :]
        out1[w] = full.astype(jnp.bfloat16)


def attend(mine, other, early, start, gain, shift, proj, gate, weight, offset):
    _, heads, length, size = start[1].shape
    inner, channels = weight.shape[1:]
    result = jax.ShapeDtypeStruct((WD, length, channels), jnp.bfloat16)
    slots = heads if length <= CHUNK else 2
    return pl.pallas_call(
        attend_kernel,
        out_shape=(result, result),
        in_specs=[VMEM] * 13,
        out_specs=(VMEM, VMEM),
        scratch_shapes=[
            pltpu.VMEM((slots, length, length // 2), jnp.float32),
            pltpu.VMEM((slots, length, length), jnp.float32),
            pltpu.VMEM((WD, inner, length // 2), jnp.float32),
            pltpu.VMEM((WD, inner, length), jnp.float32),
        ]
        + [pltpu.VMEM(shape, dtype) for shape, dtype in projected(length, inner, heads)],
        compiler_params=params(16 if length <= CHUNK else 60),
        name="attend",
    )(mine, other, early, *start, gain, shift, proj, gate, weight, offset)


def body(pair, residue_mask, ln_gain, ln_shift, w_proj, w_bias, gate_bias, w_out, out_bias):
    rows, length, channels = pair.shape
    heads = w_bias.shape[2]
    along, cols = lax.axis_size("row"), lax.axis_size("col")
    chips = cols // 2

    def by_row(block, shift):
        return lax.ppermute(block, "row", [(i, (i + shift) % along) for i in range(along)])

    def by_col(block, flip):
        return lax.ppermute(block, "col", [(i, i ^ flip) for i in range(cols)])

    block, picks = local_bias(
        pair, residue_mask[None, :], ln_gain, ln_shift, jnp.transpose(w_bias, (0, 2, 1)), along, chips
    )
    line = jnp.stack([block] + [by_row(block, shift) for shift in range(1, along)])
    picked = jnp.stack([picks[0]] + [by_col(picks[flip], 2 * flip) for flip in range(1, chips)], 1)
    start = local_lines(pair, ln_gain, ln_shift, w_proj, gate_bias, heads, along, chips)
    shared = jnp.stack([line] + [by_col(line, 2 * flip) for flip in range(1, chips)])
    owned = jnp.stack([picked[0]] + [by_row(picked[shift], shift) for shift in range(1, along)], 1)
    mine = jnp.concatenate([shared, owned], 2)
    mine, _ = lax.optimization_barrier((mine, start))
    other = by_col(mine, 1)
    early = attend_early(mine, *start[:3])
    return attend(mine, other, early, start, ln_gain, ln_shift, w_proj, gate_bias, w_out, out_bias)


def solution(mesh):
    return jax.shard_map(
        body,
        mesh=mesh,
        in_specs=(P(("row", "col"), None, None), P(), P(), P(), P(), P(), P(), P(), P()),
        out_specs=(P(("row", "col"), None, None), P(("row", "col"), None, None)),
        check_vma=False,
    )
```

time: 111 us -> 36.3 us (0.33)
  blocking collectives: 81.4 us -> 0 us
  matrix products: 10.1 us -> 0 us
  starting transfers between devices: 7.3 us -> 17.1 us
  Pallas kernels: 0 us -> 8.67 us
  waiting for transfers between devices: 0.01 us -> 7.84 us
  local copies, waits for them, and re-layouts: 6.52 us -> 0.05 us
  other arithmetic: 4.49 us -> 1.6 us
    all_gather x2 -> x0, blocking collectives: 81.4 us -> none  [the longest x1 43.3 us: body(): lax.all_gather(bias_start, ('row', 'col'), axis=1, tiled=True)]
    ppermute x0 -> x13, starting transfers between devices: none -> 17.1 us  [the longest x6 10 us: by_row(): lax.ppermute(block, 'row', [(i, (i + shift) % along) for i in range(along)])]
    pallas_call x0 -> x4, Pallas kernels: none -> 8.67 us  [the longest x1 4.03 us: attend(): pl.pallas_call(attend_kernel, out_shape=(result, result), in_specs=[VMEM]...]
    ppermute x0 -> x13, waiting for transfers between devices: none -> 7.84 us  [the longest x6 6.86 us: by_row(): lax.ppermute(block, 'row', [(i, (i + shift) % along) for i in range(along)])]
    all_to_all x1 -> x0, starting transfers between devices: 7.3 us -> none  [body(): lax.all_to_all(picked, ('row', 'col'), split_axis=1, concat_axis=1, tiled...]
    dot_general x12 -> x0, matrix products: 5.53 us -> none  [the longest x1 1.85 us: attend_lines(): jnp.einsum('whqk,wkhd->wqhd', weights, value_rows, preferred_element_type...]
    sub x3 -> x0, matrix products: 4.55 us -> none  [the longest x1 3.43 us: attend_lines(): expo = jnp.exp(scores - top)]
    reduce_sum x4 -> x0, other arithmetic: 3.32 us -> none  [the longest x2 1.93 us: layer_norm(): spread = jnp.mean(jnp.square(wide - center), -1, keepdims=True)]
  transfers between devices with their start and end apart: 1 -> 13, of which waited for: 0 -> 6; matrix products, arithmetic and copies ran while one was open for 12% -> 4% of each run, Pallas kernels for 0% -> 5%
where the time goes in v2:
time: 36.3 us; the launch traced here: 36.1 us
  starting transfers between devices  17.1 us (47%)
  Pallas kernels  8.67 us (24%)
  waiting for transfers between devices  7.84 us (22%)
  other arithmetic  1.6 us (4%)
  between operations  0.77 us (2%)
    ppermute x6, starting transfers between devices, by_row(): lax.ppermute(block, 'row', [(i, (i + shift) % along) for i in range(along)])  10 us
    ppermute x7, starting transfers between devices, by_col(): return lax.ppermute(block, 'col', [(i, i ^ flip) for i in range(cols)])  7.11 us
    ppermute x6, waiting for transfers between devices, by_row(): lax.ppermute(block, 'row', [(i, (i + shift) % along) for i in range(along)])  6.86 us
    pallas_call x1, Pallas kernels, attend(): pl.pallas_call(attend_kernel, out_shape=(result, result), in_specs=[VMEM]...  4.03 us
    pallas_call x1, Pallas kernels, local_bias(): pl.pallas_call(functools.partial(bias_kernel, along, chips), out_shape=(j...  2.79 us
    pallas_call x1, Pallas kernels, attend_early(): pl.pallas_call(early_kernel, out_shape=jax.ShapeDtypeStruct((WD, heads *...  1.11 us
    ppermute x7, waiting for transfers between devices, by_col(): return lax.ppermute(block, 'col', [(i, i ^ flip) for i in range(cols)])  0.98 us
    another operation x1, other arithmetic, body(): jnp.stack([line] + [by_col(line, 2 * flip) for flip in range(1, chips)])  0.78 us
  transfers between devices with their start and end apart: 13, of which 6 were waited for; matrix products, arithmetic and copies ran while one was open for 4% of the time, Pallas kernels for 5%

profile of v2, /device:TPU:0, one launch (start us, length us, event | category | flops | bytes accessed | tf_op | source)
XLA Modules:
  0.0 36.1 jit_solution(2161411795089090294)
XLA Ops:
  0.7 2.8 %bias.1 = (bf16[128,128]{1,0:T(8,128)(2,1)}, bf16[4,32,128]{2,1,0:T(8,128)(2,1)}, bf16[4,32,128]{2,1,0:T(8,128)(2,1)}, bf16[4,32,128]{2,1,0:T(8,128)(2,1)}, bf16[4,32,128]{2,1,0:T(8,128)(2,1)}) custom-call(bf16[8,256,128]{2,1,0:T(8,128)(2,1)} %lines_ref.1, s32[1,256]{1,0:T(1,128)} %bitcast.47, f32[2,128]{1,0:T(2,128)} %gain_ref.3, f32[2,128]{1,0:T(2,128)} %shift_ref.3, ...), custom_call_target="tpu_custom_call" | custom-call | tf_op jit(solution)/shard_map/bias/pallas_call | solution.py:113
  3.5 5.1 %collective-permute-start.2 = (bf16[128,128]{1,0:T(8,128)(2,1)}, bf16[128,128]{1,0:T(8,128)(2,1)S(1)}, u32[]{:S(2)}, u32[]{:S(2)}) collective-permute-start(bf16[128,128]{1,0:T(8,128)(2,1)} %get-tuple-element.12), channel_id=1, source_target_pairs={{0,24},{8,0},{16,8},{24,16},{1,25},{9,1},{17,9},{25,17},{2,26},{10... | collective-permute-start | bytes 98312 | tf_op jit(solution)/shard_map/ppermute | solution.py:410
  8.6 1.0 %collective-permute-start = (bf16[128,128]{1,0:T(8,128)(2,1)}, bf16[128,128]{1,0:T(8,128)(2,1)S(1)}, u32[]{:S(2)}, u32[]{:S(2)}) collective-permute-start(bf16[128,128]{1,0:T(8,128)(2,1)} %get-tuple-element.12), channel_id=1, source_target_pairs={{0,8},{8,16},{16,24},{24,0},{1,9},{9,17},{17,25},{25,1},{2,10},{10... | collective-permute-start | bytes 98312 | tf_op jit(solution)/shard_map/ppermute | solution.py:410
  9.6 1.5 %collective-permute-start.6 = (bf16[4,32,128]{2,1,0:T(8,128)(2,1)}, bf16[4,32,128]{2,1,0:T(8,128)(2,1)S(1)}, u32[]{:S(2)}, u32[]{:S(2)}) collective-permute-start(bf16[4,32,128]{2,1,0:T(8,128)(2,1)} %get-tuple-element.14), channel_id=1, source_target_pairs={{0,2},{1,3},{2,0},{3,1},{4,6},{5,7},{6,4},{7,5},{8,10},{9,11},{10,... | collective-permute-start | bytes 98312 | tf_op jit(solution)/shard_map/ppermute | solution.py:413
  11.1 1.5 %collective-permute-start.7 = (bf16[4,32,128]{2,1,0:T(8,128)(2,1)}, bf16[4,32,128]{2,1,0:T(8,128)(2,1)S(1)}, u32[]{:S(2)}, u32[]{:S(2)}) collective-permute-start(bf16[4,32,128]{2,1,0:T(8,128)(2,1)} %get-tuple-element.15), channel_id=1, source_target_pairs={{0,4},{1,5},{2,6},{3,7},{4,0},{5,1},{6,2},{7,3},{8,12},{9,13},{10,... | collective-permute-start | bytes 98312 | tf_op jit(solution)/shard_map/ppermute | solution.py:413
  12.6 0.5 %collective-permute-start.8 = (bf16[4,32,128]{2,1,0:T(8,128)(2,1)}, bf16[4,32,128]{2,1,0:T(8,128)(2,1)S(1)}, u32[]{:S(2)}, u32[]{:S(2)}) collective-permute-start(bf16[4,32,128]{2,1,0:T(8,128)(2,1)} %get-tuple-element.16), channel_id=1, source_target_pairs={{0,6},{1,7},{2,4},{3,5},{4,2},{5,3},{6,0},{7,1},{8,14},{9,15},{10,... | collective-permute-start | bytes 98312 | tf_op jit(solution)/shard_map/ppermute | solution.py:413
  13.1 0.5 %collective-permute-done.1 = bf16[128,128]{1,0:T(8,128)(2,1)S(1)} collective-permute-done((bf16[128,128]{1,0:T(8,128)(2,1)}, bf16[128,128]{1,0:T(8,128)(2,1)S(1)}, u32[]{:S(2)}, u32[]{:S(2)}) %collective-permute-start.1) | collective-permute-done | bytes 32800 | tf_op jit(solution)/shard_map/ppermute | solution.py:410
  13.6 0.9 %collective-permute-done = bf16[128,128]{1,0:T(8,128)(2,1)S(1)} collective-permute-done((bf16[128,128]{1,0:T(8,128)(2,1)}, bf16[128,128]{1,0:T(8,128)(2,1)S(1)}, u32[]{:S(2)}, u32[]{:S(2)}) %collective-permute-start) | collective-permute-done | bytes 32800 | tf_op jit(solution)/shard_map/ppermute | solution.py:410
  14.5 0.8 %fusion = (bf16[1,4,128,128]{3,2,1,0:T(8,128)(2,1)S(1)}, bf16[4,128,128]{2,1,0:T(8,128)(2,1)S(1)}) fusion(bf16[1,128,128]{2,1,0:T(8,128)(2,1)S(1)} %bitcast.38, bf16[1,128,128]{2,1,0:T(8,128)(2,1)S(1)} %bitcast.40, bf16[1,128,128]{2,1,0:T(8,128)(2,1)S(1)} %bitcast.41, bf16[1,128,128]{2,1,0:T(8,128)(2,1)} %bitcast.36), kind=kLoop, calls=%fused_computation.7 | loop fusion | flops 196608 | bytes 393216 | tf_op jit(solution)/shard_map/stack | solution.py:421
  15.3 1.6 %collective-permute-start.4 = (bf16[4,128,128]{2,1,0:T(8,128)(2,1)S(1)}, bf16[4,128,128]{2,1,0:T(8,128)(2,1)S(1)}, u32[]{:S(2)}, u32[]{:S(2)}) collective-permute-start(bf16[4,128,128]{2,1,0:T(8,128)(2,1)S(1)} %get-tuple-element.23), channel_id=1, source_target_pairs={{0,4},{1,5},{2,6},{3,7},{4,0},{5,1},{6,2},{7,3},{8,12},{9,13},{10,... | collective-permute-start | bytes 393224 | tf_op jit(solution)/shard_map/ppermute | solution.py:413
  16.9 1.5 %collective-permute-start.3 = (bf16[4,128,128]{2,1,0:T(8,128)(2,1)S(1)}, bf16[4,128,128]{2,1,0:T(8,128)(2,1)S(1)}, u32[]{:S(2)}, u32[]{:S(2)}) collective-permute-start(bf16[4,128,128]{2,1,0:T(8,128)(2,1)S(1)} %get-tuple-element.23), channel_id=1, source_target_pairs={{0,2},{1,3},{2,0},{3,1},{4,6},{5,7},{6,4},{7,5},{8,10},{9,11},{10,... | collective-permute-start | bytes 393224 | tf_op jit(solution)/shard_map/ppermute | solution.py:413
  18.4 0.5 %collective-permute-start.5 = (bf16[4,128,128]{2,1,0:T(8,128)(2,1)S(1)}, bf16[4,128,128]{2,1,0:T(8,128)(2,1)S(1)}, u32[]{:S(2)}, u32[]{:S(2)}) collective-permute-start(bf16[4,128,128]{2,1,0:T(8,128)(2,1)S(1)} %get-tuple-element.23), channel_id=1, source_target_pairs={{0,6},{1,7},{2,4},{3,5},{4,2},{5,3},{6,0},{7,1},{8,14},{9,15},{10,... | collective-permute-start | bytes 393224 | tf_op jit(solution)/shard_map/ppermute | solution.py:413
  18.9 0.8 %pad_maximum_fusion.1 = bf16[4,4,32,128]{3,2,1,0:T(8,128)(2,1)S(1)} fusion(bf16[4,1,32,128]{3,2,1,0:T(8,128)(2,1)S(1)} %bitcast.45, bf16[4,1,32,128]{3,2,1,0:T(8,128)(2,1)S(1)} %bitcast.44, bf16[4,1,32,128]{3,2,1,0:T(8,128)(2,1)S(1)} %bitcast.43, bf16[4,1,32,128]{3,2,1,0:T(8,128)(2,1)} %bitcast.42), kind=kLoop, calls=%fused_computation.2 | loop fusion | flops 196608 | bytes 262144 | tf_op jit(solution)/shard_map/stack | solution.py:419
  19.7 2.5 %collective-permute-start.11 = (bf16[4,32,128]{2,1,0:T(8,128)(2,1)S(1)}, bf16[4,32,128]{2,1,0:T(8,128)(2,1)S(1)}, u32[]{:S(2)}, u32[]{:S(2)}) collective-permute-start(bf16[4,32,128]{2,1,0:T(8,128)(2,1)S(1)} %get-tuple-element.25), channel_id=1, source_target_pairs={{0,24},{8,0},{16,8},{24,16},{1,25},{9,1},{17,9},{25,17},{2,26},{10... | collective-permute-start | bytes 98312 | tf_op jit(solution)/shard_map/ppermute | solution.py:410
  22.2 0.3 collective-permute-start.10
  22.4 1.3 %collective-permute-done.11 = bf16[4,32,128]{2,1,0:T(8,128)(2,1)S(1)} collective-permute-done((bf16[4,32,128]{2,1,0:T(8,128)(2,1)S(1)}, bf16[4,32,128]{2,1,0:T(8,128)(2,1)S(1)}, u32[]{:S(2)}, u32[]{:S(2)}) %collective-permute-start.11) | collective-permute-done | bytes 32800 | tf_op jit(solution)/shard_map/ppermute | solution.py:410
  23.8 1.1 %collective-permute-start.9 = (bf16[4,32,128]{2,1,0:T(8,128)(2,1)S(1)}, bf16[4,32,128]{2,1,0:T(8,128)(2,1)S(1)}, u32[]{:S(2)}, u32[]{:S(2)}) collective-permute-start(bf16[4,32,128]{2,1,0:T(8,128)(2,1)S(1)} %get-tuple-element.27), channel_id=1, source_target_pairs={{0,8},{8,16},{16,24},{24,0},{1,9},{9,17},{17,25},{25,1},{2,10},{10... | collective-permute-start | bytes 98312 | tf_op jit(solution)/shard_map/ppermute | solution.py:410
  24.9 0.7 %lines.1 = (bf16[2,128,256]{2,1,0:T(8,128)(2,1)S(1)}, bf16[2,4,256,32]{3,2,1,0:T(8,128)(2,1)S(1)}, bf16[2,128,256]{2,1,0:T(8,128)(2,1)S(1)}, f32[2,128,256]{2,1,0:T(8,128)S(1)}) custom-call(bf16[8,256,128]{2,1,0:T(8,128)(2,1)S(1)} %copy-done, f32[2,128]{1,0:T(2,128)S(1)} %copy-done.3, f32[2,128]{1,0:T(2,128)S(1)} %copy-done.4, ...), custom_call_target="tpu_custom_call" | custom-call | flops 67108864 | bytes 1048576 | tf_op jit(solution)/shard_map/lines/pallas_call | solution.py:231
  25.6 1.3 %collective-permute-done.10 = bf16[4,32,128]{2,1,0:T(8,128)(2,1)S(1)} collective-permute-done((bf16[4,32,128]{2,1,0:T(8,128)(2,1)S(1)}, bf16[4,32,128]{2,1,0:T(8,128)(2,1)S(1)}, u32[]{:S(2)}, u32[]{:S(2)}) %collective-permute-start.10) | collective-permute-done | bytes 32800 | tf_op jit(solution)/shard_map/ppermute | solution.py:410
  27.0 2.8 %collective-permute-done.9 = bf16[4,32,128]{2,1,0:T(8,128)(2,1)S(1)} collective-permute-done((bf16[4,32,128]{2,1,0:T(8,128)(2,1)S(1)}, bf16[4,32,128]{2,1,0:T(8,128)(2,1)S(1)}, u32[]{:S(2)}, u32[]{:S(2)}) %collective-permute-start.9) | collective-permute-done | bytes 32800 | tf_op jit(solution)/shard_map/ppermute | solution.py:410
  29.9 0.1 collective-permute-start.12
  29.9 1.1 %early.1.early_ref = f32[2,128,128]{2,1,0:T(8,128)S(1)} custom-call(bf16[4,4,160,128]{3,2,1,0:T(8,128)(2,1)S(1)} %maximum_maximum_fusion.mine_ref, bf16[2,128,256]{2,1,0:T(8,128)(2,1)S(1)} %get-tuple-element.17.q.q0, bf16[2,4,256,32]{3,2,1,0:T(8,128)(2,1)S(1)} %get-tuple-element.18.k.k0, bf16[2,128,256]{2,1,0:T(8,128)(2,1)S(1)} %get-tuple-element.19.v.v0), custom_call_target="tpu_custom_call" | custom-call | flops 67108864 | bytes 2097152 | tf_op jit(solution)/shard_map/early/pallas_call | solution.py:312
  31.1 1.0 %collective-permute-done.12.other_ref = bf16[4,4,160,128]{3,2,1,0:T(8,128)(2,1)S(1)} collective-permute-done((bf16[4,4,160,128]{3,2,1,0:T(8,128)(2,1)S(1)}, bf16[4,4,160,128]{3,2,1,0:T(8,128)(2,1)S(1)}, u32[]{:S(2)}, u32[]{:S(2)}) %collective-permute-start.12) | collective-permute-done | bytes 655392 | tf_op jit(solution)/shard_map/ppermute | solution.py:413
  32.0 4.0 %attend.1 = (bf16[2,256,128]{2,1,0:T(8,128)(2,1)}, bf16[2,256,128]{2,1,0:T(8,128)(2,1)}) custom-call(bf16[4,4,160,128]{3,2,1,0:T(8,128)(2,1)S(1)} %maximum_maximum_fusion.mine_ref, bf16[4,4,160,128]{3,2,1,0:T(8,128)(2,1)S(1)} %collective-permute-done.12.other_ref, f32[2,128,128]{2,1,0:T(8,128)S(1)} %early.1.early_ref, ...), custom_call_target="tpu_custom_call" | custom-call | tf_op jit(solution)/shard_map/attend/pallas_call | solution.py:386
  (24 shorter events, 0.1 us)
Async XLA Ops:
  0.6 24.3 %copy-start = (bf16[8,256,128]{2,1,0:T(8,128)(2,1)S(1)}, bf16[8,256,128]{2,1,0:T(8,128)(2,1)}, u32[]{:S(2)}) copy-start(bf16[8,256,128]{2,1,0:T(8,128)(2,1)} %lines_ref.1) | copy-start | bytes 1572868
  0.6 24.2 %copy-start.1 = (bf16[2,128,512]{2,1,0:T(8,128)(2,1)S(1)}, bf16[2,128,512]{2,1,0:T(8,128)(2,1)}, u32[]{:S(2)}) copy-start(bf16[2,128,512]{2,1,0:T(8,128)(2,1)} %proj_ref.1) | copy-start | bytes 786436
  0.7 24.2 %copy-start.3 = (f32[2,128]{1,0:T(2,128)S(1)}, f32[2,128]{1,0:T(2,128)}, u32[]{:S(2)}) copy-start(f32[2,128]{1,0:T(2,128)} %gain_ref.3) | copy-start | bytes 3076
  0.7 24.2 %copy-start.4 = (f32[2,128]{1,0:T(2,128)S(1)}, f32[2,128]{1,0:T(2,128)}, u32[]{:S(2)}) copy-start(f32[2,128]{1,0:T(2,128)} %shift_ref.3) | copy-start | bytes 3076
  0.7 24.2 %copy-start.5 = (f32[2,128]{1,0:T(2,128)S(1)}, f32[2,128]{1,0:T(2,128)}, u32[]{:S(2)}) copy-start(f32[2,128]{1,0:T(2,128)} %gate_ref.1) | copy-start | bytes 3076
  3.5 9.1 %collective-permute-start.2 = (bf16[128,128]{1,0:T(8,128)(2,1)}, bf16[128,128]{1,0:T(8,128)(2,1)S(1)}, u32[]{:S(2)}, u32[]{:S(2)}) collective-permute-start(bf16[128,128]{1,0:T(8,128)(2,1)} %get-tuple-element.12), channel_id=1, source_target_pairs={{0,24},{8,0},{16,8},{24,16},{1,25},{9,1},{17,9},{25,17},{2,26},{10... | collective-permute-start | bytes 98312 | tf_op jit(solution)/shard_map/ppermute | solution.py:410
  8.6 5.0 %collective-permute-start.1 = (bf16[128,128]{1,0:T(8,128)(2,1)}, bf16[128,128]{1,0:T(8,128)(2,1)S(1)}, u32[]{:S(2)}, u32[]{:S(2)}) collective-permute-start(bf16[128,128]{1,0:T(8,128)(2,1)} %get-tuple-element.12), channel_id=1, source_target_pairs={{0,16},{8,24},{16,0},{24,8},{1,17},{9,25},{17,1},{25,9},{2,18},{10... | collective-permute-start | bytes 98312 | tf_op jit(solution)/shard_map/ppermute | solution.py:410
  8.6 5.9 %collective-permute-start = (bf16[128,128]{1,0:T(8,128)(2,1)}, bf16[128,128]{1,0:T(8,128)(2,1)S(1)}, u32[]{:S(2)}, u32[]{:S(2)}) collective-permute-start(bf16[128,128]{1,0:T(8,128)(2,1)} %get-tuple-element.12), channel_id=1, source_target_pairs={{0,8},{8,16},{16,24},{24,0},{1,9},{9,17},{17,25},{25,1},{2,10},{10... | collective-permute-start | bytes 98312 | tf_op jit(solution)/shard_map/ppermute | solution.py:410
  9.6 8.8 %collective-permute-start.6 = (bf16[4,32,128]{2,1,0:T(8,128)(2,1)}, bf16[4,32,128]{2,1,0:T(8,128)(2,1)S(1)}, u32[]{:S(2)}, u32[]{:S(2)}) collective-permute-start(bf16[4,32,128]{2,1,0:T(8,128)(2,1)} %get-tuple-element.14), channel_id=1, source_target_pairs={{0,2},{1,3},{2,0},{3,1},{4,6},{5,7},{6,4},{7,5},{8,10},{9,11},{10,... | collective-permute-start | bytes 98312 | tf_op jit(solution)/shard_map/ppermute | solution.py:413
  11.1 7.8 %collective-permute-start.7 = (bf16[4,32,128]{2,1,0:T(8,128)(2,1)}, bf16[4,32,128]{2,1,0:T(8,128)(2,1)S(1)}, u32[]{:S(2)}, u32[]{:S(2)}) collective-permute-start(bf16[4,32,128]{2,1,0:T(8,128)(2,1)} %get-tuple-element.15), channel_id=1, source_target_pairs={{0,4},{1,5},{2,6},{3,7},{4,0},{5,1},{6,2},{7,3},{8,12},{9,13},{10,... | collective-permute-start | bytes 98312 | tf_op jit(solution)/shard_map/ppermute | solution.py:413
  12.6 6.2 %collective-permute-start.8 = (bf16[4,32,128]{2,1,0:T(8,128)(2,1)}, bf16[4,32,128]{2,1,0:T(8,128)(2,1)S(1)}, u32[]{:S(2)}, u32[]{:S(2)}) collective-permute-start(bf16[4,32,128]{2,1,0:T(8,128)(2,1)} %get-tuple-element.16), channel_id=1, source_target_pairs={{0,6},{1,7},{2,4},{3,5},{4,2},{5,3},{6,0},{7,1},{8,14},{9,15},{10,... | collective-permute-start | bytes 98312 | tf_op jit(solution)/shard_map/ppermute | solution.py:413
  15.3 14.5 %collective-permute-start.4 = (bf16[4,128,128]{2,1,0:T(8,128)(2,1)S(1)}, bf16[4,128,128]{2,1,0:T(8,128)(2,1)S(1)}, u32[]{:S(2)}, u32[]{:S(2)}) collective-permute-start(bf16[4,128,128]{2,1,0:T(8,128)(2,1)S(1)} %get-tuple-element.23), channel_id=1, source_target_pairs={{0,4},{1,5},{2,6},{3,7},{4,0},{5,1},{6,2},{7,3},{8,12},{9,13},{10,... | collective-permute-start | bytes 393224 | tf_op jit(solution)/shard_map/ppermute | solution.py:413
  16.9 12.9 %collective-permute-start.3 = (bf16[4,128,128]{2,1,0:T(8,128)(2,1)S(1)}, bf16[4,128,128]{2,1,0:T(8,128)(2,1)S(1)}, u32[]{:S(2)}, u32[]{:S(2)}) collective-permute-start(bf16[4,128,128]{2,1,0:T(8,128)(2,1)S(1)} %get-tuple-element.23), channel_id=1, source_target_pairs={{0,2},{1,3},{2,0},{3,1},{4,6},{5,7},{6,4},{7,5},{8,10},{9,11},{10,... | collective-permute-start | bytes 393224 | tf_op jit(solution)/shard_map/ppermute | solution.py:413
  18.4 11.4 %collective-permute-start.5 = (bf16[4,128,128]{2,1,0:T(8,128)(2,1)S(1)}, bf16[4,128,128]{2,1,0:T(8,128)(2,1)S(1)}, u32[]{:S(2)}, u32[]{:S(2)}) collective-permute-start(bf16[4,128,128]{2,1,0:T(8,128)(2,1)S(1)} %get-tuple-element.23), channel_id=1, source_target_pairs={{0,6},{1,7},{2,4},{3,5},{4,2},{5,3},{6,0},{7,1},{8,14},{9,15},{10,... | collective-permute-start | bytes 393224 | tf_op jit(solution)/shard_map/ppermute | solution.py:413
  19.7 4.1 %collective-permute-start.11 = (bf16[4,32,128]{2,1,0:T(8,128)(2,1)S(1)}, bf16[4,32,128]{2,1,0:T(8,128)(2,1)S(1)}, u32[]{:S(2)}, u32[]{:S(2)}) collective-permute-start(bf16[4,32,128]{2,1,0:T(8,128)(2,1)S(1)} %get-tuple-element.25), channel_id=1, source_target_pairs={{0,24},{8,0},{16,8},{24,16},{1,25},{9,1},{17,9},{25,17},{2,26},{10... | collective-permute-start | bytes 98312 | tf_op jit(solution)/shard_map/ppermute | solution.py:410
  22.2 4.8 %collective-permute-start.10 = (bf16[4,32,128]{2,1,0:T(8,128)(2,1)S(1)}, bf16[4,32,128]{2,1,0:T(8,128)(2,1)S(1)}, u32[]{:S(2)}, u32[]{:S(2)}) collective-permute-start(bf16[4,32,128]{2,1,0:T(8,128)(2,1)S(1)} %get-tuple-element.26), channel_id=1, source_target_pairs={{0,16},{8,24},{16,0},{24,8},{1,17},{9,25},{17,1},{25,9},{2,18},{10... | collective-permute-start | bytes 98312 | tf_op jit(solution)/shard_map/ppermute | solution.py:410
  23.8 6.0 %collective-permute-start.9 = (bf16[4,32,128]{2,1,0:T(8,128)(2,1)S(1)}, bf16[4,32,128]{2,1,0:T(8,128)(2,1)S(1)}, u32[]{:S(2)}, u32[]{:S(2)}) collective-permute-start(bf16[4,32,128]{2,1,0:T(8,128)(2,1)S(1)} %get-tuple-element.27), channel_id=1, source_target_pairs={{0,8},{8,16},{16,24},{24,0},{1,9},{9,17},{17,25},{25,1},{2,10},{10... | collective-permute-start | bytes 98312 | tf_op jit(solution)/shard_map/ppermute | solution.py:410
  29.8 2.2 %copy-start.2 = (bf16[2,128,128]{2,1,0:T(8,128)(2,1)S(1)}, bf16[2,128,128]{2,1,0:T(8,128)(2,1)}, u32[]{:S(2)}) copy-start(bf16[2,128,128]{2,1,0:T(8,128)(2,1)} %weight_ref.3) | copy-start | bytes 196612
  29.8 2.2 %copy-start.6 = (f32[2,128]{1,0:T(2,128)S(1)}, f32[2,128]{1,0:T(2,128)}, u32[]{:S(2)}) copy-start(f32[2,128]{1,0:T(2,128)} %offset_ref.3) | copy-start | bytes 3076
  29.9 2.2 %collective-permute-start.12 = (bf16[4,4,160,128]{3,2,1,0:T(8,128)(2,1)S(1)}, bf16[4,4,160,128]{3,2,1,0:T(8,128)(2,1)S(1)}, u32[]{:S(2)}, u32[]{:S(2)}) collective-permute-start(bf16[4,4,160,128]{3,2,1,0:T(8,128)(2,1)S(1)} %maximum_maximum_fusion.mine_ref), channel_id=1, source_target_pairs={{0,1},{1,0},{2,3},{3,2},{4,5},{5,4},{6,7},{7,6},{8,9},{9,8},{10,11... | collective-permute-start | bytes 1966088 | tf_op jit(solution)/shard_map/ppermute | solution.py:413

commit v3 on v2

--- a/solution.py
+++ b/solution.py
@@ -49,12 +49,12 @@
     return index
 
 
-def bias_kernel(along, chips, pair_hbm, live_hbm, gain_hbm, shift_hbm, weight_hbm, out_ref, *rest):
-    picks = rest[:chips]
-    pair, live_row, live_each, gain, shift, weight, blocks, rows_out, wide, picked, sems, pair_sems = rest[chips:]
+def bias_kernel(along, chips, pair_hbm, live_hbm, gain_hbm, shift_hbm, weight_hbm, *rest):
+    outs = rest[:along]
+    pair, live_row, live_each, gain, shift, weight, blocks, rows_out, wide, picked, sems, pair_sems = rest[along:]
     rows, length, channels = pair.shape
     heads = weight.shape[1]
-    lanes = out_ref.shape[1]
+    lanes = outs[0].shape[1]
     small = [
         pltpu.make_async_copy(source, target, sems.at[i])
         for i, (source, target) in enumerate(
@@ -90,7 +90,6 @@
         for lane in range(length // lanes):
             part = bias[:, lane * lanes : (lane + 1) * lanes]
             rows_out[pl.ds(2 * lane * heads * rows + a, 2 * heads, stride=rows), :] = part
-    out_ref[...] = rows_out[...].astype(jnp.bfloat16)
     devices = length // rows
     for a in range(rows):
         for w in range(WD):
@@ -98,23 +97,26 @@
             picked[pl.ds(w * rows + a, devices, stride=WD * rows), :] = column
     chip = lax.div(lax.axis_index("col"), 2)
     both = 2 * WD * rows
-    for flip, pick in enumerate(picks):
-        for shift in range(along):
-            row = lax.rem(lax.axis_index("row") + shift, along)
+    packed = rows_out.shape[0]
+    sent = rows_out[...].astype(jnp.bfloat16)
+    for shift_by, out in enumerate(outs):
+        out[:packed] = sent
+        row = lax.rem(lax.axis_index("row") + shift_by, along)
+        for flip in range(chips):
             at = pl.multiple_of((row * chips + flipped(chip, flip)) * both, both)
-            pick[shift] = picked[pl.ds(at, both), :].astype(jnp.bfloat16)
+            out[packed + flip * both : packed + (flip + 1) * both] = picked[pl.ds(at, both), :].astype(jnp.bfloat16)
 
 
 def local_bias(pair, live, gain, shift, weight, along, chips):
     rows, length, channels = pair.shape
     heads = weight.shape[1]
-    pick = jax.ShapeDtypeStruct((along, 2 * WD * rows, channels), jnp.bfloat16)
     packed = 2 * heads * rows * (length // channels)
-    out = pl.pallas_call(
+    sent = jax.ShapeDtypeStruct((packed + chips * 2 * WD * rows, channels), jnp.bfloat16)
+    return pl.pallas_call(
         functools.partial(bias_kernel, along, chips),
-        out_shape=(jax.ShapeDtypeStruct((packed, channels), jnp.bfloat16),) + (pick,) * chips,
+        out_shape=(sent,) * along,
         in_specs=[HBM] * 5,
-        out_specs=(VMEM,) * (1 + chips),
+        out_specs=(VMEM,) * along,
         scratch_shapes=[
             pltpu.VMEM(pair.shape, pair.dtype),
             pltpu.VMEM(live.shape, live.dtype),
@@ -132,7 +134,6 @@
         compiler_params=params(60),
         name="bias",
     )(pair, live, gain, shift, weight)
-    return out[0], out[1:]
 
 
 def turned(row):
@@ -412,15 +413,19 @@
     def by_col(block, flip):
         return lax.ppermute(block, "col", [(i, i ^ flip) for i in range(cols)])
 
-    block, picks = local_bias(
+    sent = local_bias(
         pair, residue_mask[None, :], ln_gain, ln_shift, jnp.transpose(w_bias, (0, 2, 1)), along, chips
     )
-    line = jnp.stack([block] + [by_row(block, shift) for shift in range(1, along)])
-    picked = jnp.stack([picks[0]] + [by_col(picks[flip], 2 * flip) for flip in range(1, chips)], 1)
+    line = jnp.stack([sent[0]] + [by_row(sent[shift], shift) for shift in range(1, along)])
     start = local_lines(pair, ln_gain, ln_shift, w_proj, gate_bias, heads, along, chips)
-    shared = jnp.stack([line] + [by_col(line, 2 * flip) for flip in range(1, chips)])
-    owned = jnp.stack([picked[0]] + [by_row(picked[shift], shift) for shift in range(1, along)], 1)
-    mine = jnp.concatenate([shared, owned], 2)
+    packed = 2 * heads * rows * (length // channels)
+    both = 2 * WD * rows
+
+    def owned_by(flip):
+        at = packed + flip * both
+        return jnp.concatenate([line[:, :packed], line[:, at : at + both]], 1)
+
+    mine = jnp.stack([owned_by(0)] + [by_col(owned_by(flip), 2 * flip) for flip in range(1, chips)])
     mine, _ = lax.optimization_barrier((mine, start))
     other = by_col(mine, 1)
     early = attend_early(mine, *start[:3])

time: 36.3 us -> 31.7 us (0.87)
  starting transfers between devices: 17.1 us -> 10.6 us
  waiting for transfers between devices: 7.84 us -> 10.2 us
  other arithmetic: 1.6 us -> 0.18 us
  local copies, waits for them, and re-layouts: 0.05 us -> 1 us
    ppermute x7 -> x4, waiting for transfers between devices: 0.98 us -> 8.36 us  [by_col(): return lax.ppermute(block, 'col', [(i, i ^ flip) for i in range(cols)])]
    ppermute x6 -> x3, waiting for transfers between devices: 6.86 us -> 1.86 us  [by_row(): lax.ppermute(block, 'row', [(i, (i + shift) % along) for i in range(along)])]
    ppermute x7 -> x4, starting transfers between devices: 7.11 us -> 3.62 us  [by_col(): return lax.ppermute(block, 'col', [(i, i ^ flip) for i in range(cols)])]
    ppermute x6 -> x3, starting transfers between devices: 10 us -> 7.01 us  [by_row(): lax.ppermute(block, 'row', [(i, (i + shift) % along) for i in range(along)])]
    another operation x2, other arithmetic: 1.56 us -> 0.12 us  [the longest x1 0.08 us: body(): jnp.stack([owned_by(0)] + [by_col(owned_by(flip), 2 * flip) for flip in r...]
    unnamed x14 -> x16, local copies, waits for them, and re-layouts: 0.03 us -> 0.98 us
  transfers between devices with their start and end apart: 13 -> 7, of which waited for: 6 -> 6; matrix products, arithmetic and copies ran while one was open for 4% -> 0% of each run, Pallas kernels for 5% -> 6%
where the time goes in v3:
time: 31.7 us; the launch traced here: 31.5 us
  starting transfers between devices  10.6 us (33%)
  waiting for transfers between devices  10.2 us (32%)
  Pallas kernels  8.76 us (28%)
  local copies, waits for them, and re-layouts  1 us (3%)
  between operations  0.74 us (2%)
    ppermute x4, waiting for transfers between devices, by_col(): return lax.ppermute(block, 'col', [(i, i ^ flip) for i in range(cols)])  8.36 us
    ppermute x3, starting transfers between devices, by_row(): lax.ppermute(block, 'row', [(i, (i + shift) % along) for i in range(along)])  7.01 us
    pallas_call x1, Pallas kernels, attend(): pl.pallas_call(attend_kernel, out_shape=(result, result), in_specs=[VMEM]...  4.04 us
    ppermute x4, starting transfers between devices, by_col(): return lax.ppermute(block, 'col', [(i, i ^ flip) for i in range(cols)])  3.62 us
    pallas_call x1, Pallas kernels, local_bias(): pl.pallas_call(functools.partial(bias_kernel, along, chips), out_shape=(s...  2.89 us
    ppermute x3, waiting for transfers between devices, by_row(): lax.ppermute(block, 'row', [(i, (i + shift) % along) for i in range(along)])  1.86 us
    pallas_call x1, Pallas kernels, attend_early(): pl.pallas_call(early_kernel, out_shape=jax.ShapeDtypeStruct((WD, heads *...  1.11 us
    unnamed x16, local copies, waits for them, and re-layouts  0.98 us
  transfers between devices with their start and end apart: 7, of which 6 were waited for; matrix products, arithmetic and copies ran while one was open for 0% of the time, Pallas kernels for 6%

profile of v3, /device:TPU:0, one launch (start us, length us, event | category | flops | bytes accessed | tf_op | source)
XLA Modules:
  0.0 31.5 jit_solution(3831988340714604974)
XLA Ops:
  0.6 2.9 %bias.1 = (bf16[256,128]{1,0:T(8,128)(2,1)}, bf16[256,128]{1,0:T(8,128)(2,1)}, bf16[256,128]{1,0:T(8,128)(2,1)}, bf16[256,128]{1,0:T(8,128)(2,1)}) custom-call(bf16[8,256,128]{2,1,0:T(8,128)(2,1)} %lines_ref.1, s32[1,256]{1,0:T(1,128)} %bitcast.23, f32[2,128]{1,0:T(2,128)} %gain_ref.3, f32[2,128]{1,0:T(2,128)} %shift_ref.3, bf16[2,4,128]{2,1,0:T(4,128)(2,1)} %bitcast.22), custom_call_target="tpu_custom_call" | custom-call | tf_op jit(solution)/shard_map/bias/pallas_call | solution.py:115
  3.5 3.1 %collective-permute-start = (bf16[256,128]{1,0:T(8,128)(2,1)}, bf16[256,128]{1,0:T(8,128)(2,1)S(1)}, u32[]{:S(2)}, u32[]{:S(2)}) collective-permute-start(bf16[256,128]{1,0:T(8,128)(2,1)} %get-tuple-element.12), channel_id=1, source_target_pairs={{0,8},{8,16},{16,24},{24,0},{1,9},{9,17},{17,25},{25,1},{2,10},{10... | collective-permute-start | bytes 196616 | tf_op jit(solution)/shard_map/ppermute | solution.py:411
  6.6 2.6 %collective-permute-start.1 = (bf16[256,128]{1,0:T(8,128)(2,1)}, bf16[256,128]{1,0:T(8,128)(2,1)S(1)}, u32[]{:S(2)}, u32[]{:S(2)}) collective-permute-start(bf16[256,128]{1,0:T(8,128)(2,1)} %get-tuple-element.13), channel_id=1, source_target_pairs={{0,16},{8,24},{16,0},{24,8},{1,17},{9,25},{17,1},{25,9},{2,18},{10... | collective-permute-start | bytes 196616 | tf_op jit(solution)/shard_map/ppermute | solution.py:411
  9.2 1.3 %collective-permute-start.2 = (bf16[256,128]{1,0:T(8,128)(2,1)}, bf16[256,128]{1,0:T(8,128)(2,1)S(1)}, u32[]{:S(2)}, u32[]{:S(2)}) collective-permute-start(bf16[256,128]{1,0:T(8,128)(2,1)} %get-tuple-element.14), channel_id=1, source_target_pairs={{0,24},{8,0},{16,8},{24,16},{1,25},{9,1},{17,9},{25,17},{2,26},{10... | collective-permute-start | bytes 196616 | tf_op jit(solution)/shard_map/ppermute | solution.py:411
  10.6 0.0 copy-start.1
  10.6 0.9 %copy-done.1 = bf16[2,128,512]{2,1,0:T(8,128)(2,1)S(1)} copy-done((bf16[2,128,512]{2,1,0:T(8,128)(2,1)S(1)}, bf16[2,128,512]{2,1,0:T(8,128)(2,1)}, u32[]{:S(2)}) %copy-start.1) | copy-done | bytes 262168
  11.5 0.7 %lines.1 = (bf16[2,128,256]{2,1,0:T(8,128)(2,1)S(1)}, bf16[2,4,256,32]{3,2,1,0:T(8,128)(2,1)S(1)}, bf16[2,128,256]{2,1,0:T(8,128)(2,1)S(1)}, f32[2,128,256]{2,1,0:T(8,128)S(1)}) custom-call(bf16[8,256,128]{2,1,0:T(8,128)(2,1)S(1)} %copy-done, f32[2,128]{1,0:T(2,128)S(1)} %copy-done.3, f32[2,128]{1,0:T(2,128)S(1)} %copy-done.4, ...), custom_call_target="tpu_custom_call" | custom-call | flops 67108864 | bytes 1048576 | tf_op jit(solution)/shard_map/lines/pallas_call | solution.py:232
  12.3 0.0 collective-permute-done
  12.3 1.6 %collective-permute-done.1 = bf16[256,128]{1,0:T(8,128)(2,1)S(1)} collective-permute-done((bf16[256,128]{1,0:T(8,128)(2,1)}, bf16[256,128]{1,0:T(8,128)(2,1)S(1)}, u32[]{:S(2)}, u32[]{:S(2)}) %collective-permute-start.1) | collective-permute-done | bytes 65568 | tf_op jit(solution)/shard_map/ppermute | solution.py:411
  13.9 0.2 collective-permute-done.2
  14.2 0.1 fusion.15
  14.3 1.6 %collective-permute-start.3 = (bf16[4,160,128]{2,1,0:T(8,128)(2,1)S(1)}, bf16[4,160,128]{2,1,0:T(8,128)(2,1)S(1)}, u32[]{:S(2)}, u32[]{:S(2)}) collective-permute-start(bf16[4,160,128]{2,1,0:T(8,128)(2,1)S(1)} %get-tuple-element.20), channel_id=1, source_target_pairs={{0,2},{1,3},{2,0},{3,1},{4,6},{5,7},{6,4},{7,5},{8,10},{9,11},{10,... | collective-permute-start | bytes 491528 | tf_op jit(solution)/shard_map/ppermute | solution.py:414
  15.9 1.5 %collective-permute-start.5 = (bf16[4,160,128]{2,1,0:T(8,128)(2,1)S(1)}, bf16[4,160,128]{2,1,0:T(8,128)(2,1)S(1)}, u32[]{:S(2)}, u32[]{:S(2)}) collective-permute-start(bf16[4,160,128]{2,1,0:T(8,128)(2,1)S(1)} %get-tuple-element.21), channel_id=1, source_target_pairs={{0,6},{1,7},{2,4},{3,5},{4,2},{5,3},{6,0},{7,1},{8,14},{9,15},{10,... | collective-permute-start | bytes 491528 | tf_op jit(solution)/shard_map/ppermute | solution.py:414
  17.4 0.5 %collective-permute-start.4 = (bf16[4,160,128]{2,1,0:T(8,128)(2,1)S(1)}, bf16[4,160,128]{2,1,0:T(8,128)(2,1)S(1)}, u32[]{:S(2)}, u32[]{:S(2)}) collective-permute-start(bf16[4,160,128]{2,1,0:T(8,128)(2,1)S(1)} %get-tuple-element.22), channel_id=1, source_target_pairs={{0,4},{1,5},{2,6},{3,7},{4,0},{5,1},{6,2},{7,3},{8,12},{9,13},{10,... | collective-permute-start | bytes 491528 | tf_op jit(solution)/shard_map/ppermute | solution.py:414
  17.8 3.6 %collective-permute-done.3 = bf16[4,160,128]{2,1,0:T(8,128)(2,1)S(1)} collective-permute-done((bf16[4,160,128]{2,1,0:T(8,128)(2,1)S(1)}, bf16[4,160,128]{2,1,0:T(8,128)(2,1)S(1)}, u32[]{:S(2)}, u32[]{:S(2)}) %collective-permute-start.3) | collective-permute-done | bytes 163872 | tf_op jit(solution)/shard_map/ppermute | solution.py:414
  21.5 2.4 %collective-permute-done.5 = bf16[4,160,128]{2,1,0:T(8,128)(2,1)S(1)} collective-permute-done((bf16[4,160,128]{2,1,0:T(8,128)(2,1)S(1)}, bf16[4,160,128]{2,1,0:T(8,128)(2,1)S(1)}, u32[]{:S(2)}, u32[]{:S(2)}) %collective-permute-start.5) | collective-permute-done | bytes 163872 | tf_op jit(solution)/shard_map/ppermute | solution.py:414
  23.9 1.4 %collective-permute-done.4 = bf16[4,160,128]{2,1,0:T(8,128)(2,1)S(1)} collective-permute-done((bf16[4,160,128]{2,1,0:T(8,128)(2,1)S(1)}, bf16[4,160,128]{2,1,0:T(8,128)(2,1)S(1)}, u32[]{:S(2)}, u32[]{:S(2)}) %collective-permute-start.4) | collective-permute-done | bytes 163872 | tf_op jit(solution)/shard_map/ppermute | solution.py:414
  25.2 0.1 pad_maximum_fusion.mine_ref
  25.3 0.0 copy-start.2
  25.3 0.0 copy-start.6
  25.3 0.1 collective-permute-start.6
  25.4 1.1 %early.1.early_ref = f32[2,128,128]{2,1,0:T(8,128)S(1)} custom-call(bf16[4,4,160,128]{3,2,1,0:T(8,128)(2,1)S(1)} %pad_maximum_fusion.mine_ref, bf16[2,128,256]{2,1,0:T(8,128)(2,1)S(1)} %get-tuple-element.15.q.q0, bf16[2,4,256,32]{3,2,1,0:T(8,128)(2,1)S(1)} %get-tuple-element.16.k.k0, bf16[2,128,256]{2,1,0:T(8,128)(2,1)S(1)} %get-tuple-element.17.v.v0), custom_call_target="tpu_custom_call" | custom-call | flops 67108864 | bytes 2097152 | tf_op jit(solution)/shard_map/early/pallas_call | solution.py:313
  26.5 1.0 %collective-permute-done.6.other_ref = bf16[4,4,160,128]{3,2,1,0:T(8,128)(2,1)S(1)} collective-permute-done((bf16[4,4,160,128]{3,2,1,0:T(8,128)(2,1)S(1)}, bf16[4,4,160,128]{3,2,1,0:T(8,128)(2,1)S(1)}, u32[]{:S(2)}, u32[]{:S(2)}) %collective-permute-start.6) | collective-permute-done | bytes 655392 | tf_op jit(solution)/shard_map/ppermute | solution.py:414
  27.5 4.0 %attend.1 = (bf16[2,256,128]{2,1,0:T(8,128)(2,1)}, bf16[2,256,128]{2,1,0:T(8,128)(2,1)}) custom-call(bf16[4,4,160,128]{3,2,1,0:T(8,128)(2,1)S(1)} %pad_maximum_fusion.mine_ref, bf16[4,4,160,128]{3,2,1,0:T(8,128)(2,1)S(1)} %collective-permute-done.6.other_ref, f32[2,128,128]{2,1,0:T(8,128)S(1)} %early.1.early_ref, ...), custom_call_target="tpu_custom_call" | custom-call | tf_op jit(solution)/shard_map/attend/pallas_call | solution.py:387
  (15 shorter events, 0.1 us)
Async XLA Ops:
  0.6 9.9 %copy-start = (bf16[8,256,128]{2,1,0:T(8,128)(2,1)S(1)}, bf16[8,256,128]{2,1,0:T(8,128)(2,1)}, u32[]{:S(2)}) copy-start(bf16[8,256,128]{2,1,0:T(8,128)(2,1)} %lines_ref.1) | copy-start | bytes 1572868
  3.5 8.7 %collective-permute-start = (bf16[256,128]{1,0:T(8,128)(2,1)}, bf16[256,128]{1,0:T(8,128)(2,1)S(1)}, u32[]{:S(2)}, u32[]{:S(2)}) collective-permute-start(bf16[256,128]{1,0:T(8,128)(2,1)} %get-tuple-element.12), channel_id=1, source_target_pairs={{0,8},{8,16},{16,24},{24,0},{1,9},{9,17},{17,25},{25,1},{2,10},{10... | collective-permute-start | bytes 196616 | tf_op jit(solution)/shard_map/ppermute | solution.py:411
  6.6 3.9 %copy-start.4 = (f32[2,128]{1,0:T(2,128)S(1)}, f32[2,128]{1,0:T(2,128)}, u32[]{:S(2)}) copy-start(f32[2,128]{1,0:T(2,128)} %shift_ref.3) | copy-start | bytes 3076
  6.6 4.0 %copy-start.5 = (f32[2,128]{1,0:T(2,128)S(1)}, f32[2,128]{1,0:T(2,128)}, u32[]{:S(2)}) copy-start(f32[2,128]{1,0:T(2,128)} %gate_ref.1) | copy-start | bytes 3076
  6.6 4.0 %copy-start.3 = (f32[2,128]{1,0:T(2,128)S(1)}, f32[2,128]{1,0:T(2,128)}, u32[]{:S(2)}) copy-start(f32[2,128]{1,0:T(2,128)} %gain_ref.3) | copy-start | bytes 3076
  6.6 7.3 %collective-permute-start.1 = (bf16[256,128]{1,0:T(8,128)(2,1)}, bf16[256,128]{1,0:T(8,128)(2,1)S(1)}, u32[]{:S(2)}, u32[]{:S(2)}) collective-permute-start(bf16[256,128]{1,0:T(8,128)(2,1)} %get-tuple-element.13), channel_id=1, source_target_pairs={{0,16},{8,24},{16,0},{24,8},{1,17},{9,25},{17,1},{25,9},{2,18},{10... | collective-permute-start | bytes 196616 | tf_op jit(solution)/shard_map/ppermute | solution.py:411
  9.2 4.9 %collective-permute-start.2 = (bf16[256,128]{1,0:T(8,128)(2,1)}, bf16[256,128]{1,0:T(8,128)(2,1)S(1)}, u32[]{:S(2)}, u32[]{:S(2)}) collective-permute-start(bf16[256,128]{1,0:T(8,128)(2,1)} %get-tuple-element.14), channel_id=1, source_target_pairs={{0,24},{8,0},{16,8},{24,16},{1,25},{9,1},{17,9},{25,17},{2,26},{10... | collective-permute-start | bytes 196616 | tf_op jit(solution)/shard_map/ppermute | solution.py:411
  10.6 1.0 %copy-start.1 = (bf16[2,128,512]{2,1,0:T(8,128)(2,1)S(1)}, bf16[2,128,512]{2,1,0:T(8,128)(2,1)}, u32[]{:S(2)}) copy-start(bf16[2,128,512]{2,1,0:T(8,128)(2,1)} %proj_ref.1) | copy-start | bytes 786436
  11.5 2.6 %copy-start.7 = (bf16[256,128]{1,0:T(8,128)(2,1)S(1)}, bf16[256,128]{1,0:T(8,128)(2,1)}, u32[]{:S(2)}) copy-start(bf16[256,128]{1,0:T(8,128)(2,1)} %get-tuple-element.11) | copy-start | bytes 196612
  14.3 7.2 %collective-permute-start.3 = (bf16[4,160,128]{2,1,0:T(8,128)(2,1)S(1)}, bf16[4,160,128]{2,1,0:T(8,128)(2,1)S(1)}, u32[]{:S(2)}, u32[]{:S(2)}) collective-permute-start(bf16[4,160,128]{2,1,0:T(8,128)(2,1)S(1)} %get-tuple-element.20), channel_id=1, source_target_pairs={{0,2},{1,3},{2,0},{3,1},{4,6},{5,7},{6,4},{7,5},{8,10},{9,11},{10,... | collective-permute-start | bytes 491528 | tf_op jit(solution)/shard_map/ppermute | solution.py:414
  15.9 8.0 %collective-permute-start.5 = (bf16[4,160,128]{2,1,0:T(8,128)(2,1)S(1)}, bf16[4,160,128]{2,1,0:T(8,128)(2,1)S(1)}, u32[]{:S(2)}, u32[]{:S(2)}) collective-permute-start(bf16[4,160,128]{2,1,0:T(8,128)(2,1)S(1)} %get-tuple-element.21), channel_id=1, source_target_pairs={{0,6},{1,7},{2,4},{3,5},{4,2},{5,3},{6,0},{7,1},{8,14},{9,15},{10,... | collective-permute-start | bytes 491528 | tf_op jit(solution)/shard_map/ppermute | solution.py:414
  17.4 7.9 %collective-permute-start.4 = (bf16[4,160,128]{2,1,0:T(8,128)(2,1)S(1)}, bf16[4,160,128]{2,1,0:T(8,128)(2,1)S(1)}, u32[]{:S(2)}, u32[]{:S(2)}) collective-permute-start(bf16[4,160,128]{2,1,0:T(8,128)(2,1)S(1)} %get-tuple-element.22), channel_id=1, source_target_pairs={{0,4},{1,5},{2,6},{3,7},{4,0},{5,1},{6,2},{7,3},{8,12},{9,13},{10,... | collective-permute-start | bytes 491528 | tf_op jit(solution)/shard_map/ppermute | solution.py:414
  25.3 2.2 %copy-start.2 = (bf16[2,128,128]{2,1,0:T(8,128)(2,1)S(1)}, bf16[2,128,128]{2,1,0:T(8,128)(2,1)}, u32[]{:S(2)}) copy-start(bf16[2,128,128]{2,1,0:T(8,128)(2,1)} %weight_ref.3) | copy-start | bytes 196612
  25.3 2.2 %copy-start.6 = (f32[2,128]{1,0:T(2,128)S(1)}, f32[2,128]{1,0:T(2,128)}, u32[]{:S(2)}) copy-start(f32[2,128]{1,0:T(2,128)} %offset_ref.3) | copy-start | bytes 3076
  25.3 2.2 %collective-permute-start.6 = (bf16[4,4,160,128]{3,2,1,0:T(8,128)(2,1)S(1)}, bf16[4,4,160,128]{3,2,1,0:T(8,128)(2,1)S(1)}, u32[]{:S(2)}, u32[]{:S(2)}) collective-permute-start(bf16[4,4,160,128]{3,2,1,0:T(8,128)(2,1)S(1)} %pad_maximum_fusion.mine_ref), channel_id=1, source_target_pairs={{0,1},{1,0},{2,3},{3,2},{4,5},{5,4},{6,7},{7,6},{8,9},{9,8},{10,11... | collective-permute-start | bytes 1966088 | tf_op jit(solution)/shard_map/ppermute | solution.py:414

commit v4 on v3

--- a/solution.py
+++ b/solution.py
@@ -10,7 +10,8 @@
 WD = 2
 EPS = 1e-05
 MASKED = -1000000000.0
-CHUNK = 256
+CHUNK = 128
+WHOLE = 256
 VMEM = pl.BlockSpec(memory_space=pltpu.VMEM)
 HBM = pl.BlockSpec(memory_space=pltpu.HBM)
 
@@ -268,13 +269,11 @@
                 into[slot, at : at + half, there] = block
 
 
-def softmax_mix(keys, queries, values, added):
-    scores = [contract(k, q, 1, 0) + added for k, q in zip(keys, queries)]
-    tops = [jnp.max(score, 0, keepdims=True) for score in scores]
-    expos = [jnp.exp(score - top) for score, top in zip(scores, tops)]
-    shares = [1.0 / jnp.sum(expo, 0, keepdims=True) for expo in expos]
-    weights = [(expo * share).astype(jnp.bfloat16) for expo, share in zip(expos, shares)]
-    return [contract(v, weight, 1, 0) for v, weight in zip(values, weights)]
+def softmax_mix(key, query, value, added):
+    scores = contract(key, query, 1, 0) + added
+    expo = jnp.exp(scores - jnp.max(scores, 0, keepdims=True))
+    weights = expo * (1.0 / jnp.sum(expo, 0, keepdims=True))
+    return contract(value, weights.astype(jnp.bfloat16), 1, 0)
 
 
 def start_half(source, other, q, k, v, mixed, bias):
@@ -282,26 +281,24 @@
     half = length // 2
     rows = half // (source.shape[0] * source.shape[1])
     width = min(half, CHUNK)
+    unrolled = length <= WHOLE
     for pack in range(heads // 2):
         unpack(source, 0, pack, rows, heads, 1, bias, 0)
         for i in range(2):
             part = slice((2 * pack + i) * size, (2 * pack + i + 1) * size)
 
             def step(chunk):
-                near = pl.ds(chunk * width if half == width else pl.multiple_of(chunk * width, width), width)
+                near = pl.ds(chunk * width if unrolled else pl.multiple_of(chunk * width, width), width)
                 there = pl.ds(other * half + chunk * width, width)
-                if half != width:
+                if not unrolled:
                     there = pl.ds(pl.multiple_of(other * half + chunk * width, width), width)
-                outs = softmax_mix(
-                    [k[w, 2 * pack + i] for w in range(WD)],
-                    [q[w, part, there] for w in range(WD)],
-                    [v[w, part, :] for w in range(WD)],
-                    bias[(2 * pack + i) % bias.shape[0], :, near],
-                )
                 for w in range(WD):
-                    mixed[w, part, near] = outs[w]
-
-            for_each(half // width, step, half == width)
+                    mixed[w, part, near] = softmax_mix(
+                        k[w, 2 * pack + i], q[w, part, there], v[w, part, :],
+                        bias[(2 * pack + i) % bias.shape[0], :, near],
+                    )
+
+            for_each(half // width, step, unrolled)
 
 
 def early_kernel(mine_ref, q, k, v, mixed, bias):
@@ -315,8 +312,8 @@
         out_shape=jax.ShapeDtypeStruct((WD, heads * size, length // 2), jnp.float32),
         in_specs=[VMEM] * 4,
         out_specs=VMEM,
-        scratch_shapes=[pltpu.VMEM((heads if length <= CHUNK else 2, length, length // 2), jnp.float32)],
-        compiler_params=params(8 if length <= CHUNK else 40),
+        scratch_shapes=[pltpu.VMEM((heads if length <= WHOLE else 2, length, length // 2), jnp.float32)],
+        compiler_params=params(8 if length <= WHOLE else 40),
         cost_estimate=pl.CostEstimate(
             flops=4 * WD * heads * size * length * length,
             bytes_accessed=4 * WD * heads * length * length,
@@ -336,6 +333,7 @@
     half = length // 2
     rows = half // (chips * along)
     packed = 2 * heads * rows * (length // mine_ref.shape[3])
+    unrolled = length <= WHOLE
     first = pl.multiple_of(packed + lax.rem(lax.axis_index("col"), 2) * WD * rows, WD * rows)
     offset = turned(gate_ref[1:2, :])
     blocks = []
@@ -362,17 +360,14 @@
             part = slice((2 * pack + i) * size, (2 * pack + i + 1) * size)
 
             def step(chunk):
-                there = pl.ds(chunk * CHUNK if length == CHUNK else pl.multiple_of(chunk * CHUNK, CHUNK), CHUNK)
-                outs = softmax_mix(
-                    [k1[w, 2 * pack + i] for w in range(WD)],
-                    [q1[w, part, there] for w in range(WD)],
-                    [v1[w, part, :] for w in range(WD)],
-                    bias[(2 * pack + i) % bias.shape[0], :, there],
-                )
+                there = pl.ds(chunk * CHUNK if unrolled else pl.multiple_of(chunk * CHUNK, CHUNK), CHUNK)
                 for w in range(WD):
-                    mixed[w, part, there] = outs[w]
-
-            for_each(length // CHUNK, step, length == CHUNK)
+                    mixed[w, part, there] = softmax_mix(
+                        k1[w, 2 * pack + i], q1[w, part, there], v1[w, part, :],
+                        bias[(2 * pack + i) % bias.shape[0], :, there],
+                    )
+
+            for_each(length // CHUNK, step, unrolled)
     for w in range(WD):
         gated = (mixed[w] * g1[w]).astype(jnp.bfloat16)
         full = contract(gated, weight_ref[1], 0, 0) + offset_ref[1:2, :]
@@ -383,7 +378,7 @@
     _, heads, length, size = start[1].shape
     inner, channels = weight.shape[1:]
     result = jax.ShapeDtypeStruct((WD, length, channels), jnp.bfloat16)
-    slots = heads if length <= CHUNK else 2
+    slots = heads if length <= WHOLE else 2
     return pl.pallas_call(
         attend_kernel,
         out_shape=(result, result),
@@ -396,7 +391,7 @@
             pltpu.VMEM((WD, inner, length), jnp.float32),
         ]
         + [pltpu.VMEM(shape, dtype) for shape, dtype in projected(length, inner, heads)],
-        compiler_params=params(16 if length <= CHUNK else 60),
+        compiler_params=params(16 if length <= WHOLE else 60),
         name="attend",
     )(mine, other, early, *start, gain, shift, proj, gate, weight, offset)
 

time: 31.7 us -> 34.9 us (1.10)
  Pallas kernels: 8.76 us -> 12.9 us
  waiting for transfers between devices: 10.2 us -> 9.31 us
    pallas_call x1, Pallas kernels: 4.04 us -> 7.25 us  [attend(): pl.pallas_call(attend_kernel, out_shape=(result, result), in_specs=[VMEM]...]
    pallas_call x1, Pallas kernels: 1.11 us -> 2.02 us  [attend_early(): pl.pallas_call(early_kernel, out_shape=jax.ShapeDtypeStruct((WD, heads *...]
    ppermute x4, waiting for transfers between devices: 8.36 us -> 7.45 us  [by_col(): return lax.ppermute(block, 'col', [(i, i ^ flip) for i in range(cols)])]
  transfers between devices with their start and end apart: 7 -> 7, of which waited for: 6 -> 6; matrix products, arithmetic and copies ran while one was open for 0% -> 0% of each run, Pallas kernels for 6% -> 8%
where the time goes in v4:
time: 34.9 us; the launch traced here: 34.8 us
  Pallas kernels  12.9 us (37%)
  starting transfers between devices  10.6 us (30%)
  waiting for transfers between devices  9.31 us (27%)
  local copies, waits for them, and re-layouts  1 us (3%)
  between operations  0.74 us (2%)
    ppermute x4, waiting for transfers between devices, by_col(): return lax.ppermute(block, 'col', [(i, i ^ flip) for i in range(cols)])  7.45 us
    pallas_call x1, Pallas kernels, attend(): pl.pallas_call(attend_kernel, out_shape=(result, result), in_specs=[VMEM]...  7.25 us
    ppermute x3, starting transfers between devices, by_row(): lax.ppermute(block, 'row', [(i, (i + shift) % along) for i in range(along)])  7.01 us
    ppermute x4, starting transfers between devices, by_col(): return lax.ppermute(block, 'col', [(i, i ^ flip) for i in range(cols)])  3.62 us
    pallas_call x1, Pallas kernels, local_bias(): pl.pallas_call(functools.partial(bias_kernel, along, chips), out_shape=(s...  2.89 us
    pallas_call x1, Pallas kernels, attend_early(): pl.pallas_call(early_kernel, out_shape=jax.ShapeDtypeStruct((WD, heads *...  2.02 us
    ppermute x3, waiting for transfers between devices, by_row(): lax.ppermute(block, 'row', [(i, (i + shift) % along) for i in range(along)])  1.86 us
    unnamed x16, local copies, waits for them, and re-layouts  0.98 us
  transfers between devices with their start and end apart: 7, of which 6 were waited for; matrix products, arithmetic and copies ran while one was open for 0% of the time, Pallas kernels for 8%

profile of v4, /device:TPU:0, one launch (start us, length us, event | category | flops | bytes accessed | tf_op | source)
XLA Modules:
  0.0 34.8 jit_solution(12045431480448000400)
XLA Ops:
  0.6 2.9 %bias.1 = (bf16[256,128]{1,0:T(8,128)(2,1)}, bf16[256,128]{1,0:T(8,128)(2,1)}, bf16[256,128]{1,0:T(8,128)(2,1)}, bf16[256,128]{1,0:T(8,128)(2,1)}) custom-call(bf16[8,256,128]{2,1,0:T(8,128)(2,1)} %lines_ref.1, s32[1,256]{1,0:T(1,128)} %bitcast.23, f32[2,128]{1,0:T(2,128)} %gain_ref.3, f32[2,128]{1,0:T(2,128)} %shift_ref.3, bf16[2,4,128]{2,1,0:T(4,128)(2,1)} %bitcast.22), custom_call_target="tpu_custom_call" | custom-call | tf_op jit(solution)/shard_map/bias/pallas_call | solution.py:116
  3.5 3.1 %collective-permute-start = (bf16[256,128]{1,0:T(8,128)(2,1)}, bf16[256,128]{1,0:T(8,128)(2,1)S(1)}, u32[]{:S(2)}, u32[]{:S(2)}) collective-permute-start(bf16[256,128]{1,0:T(8,128)(2,1)} %get-tuple-element.12), channel_id=1, source_target_pairs={{0,8},{8,16},{16,24},{24,0},{1,9},{9,17},{17,25},{25,1},{2,10},{10... | collective-permute-start | bytes 196616 | tf_op jit(solution)/shard_map/ppermute | solution.py:406
  6.6 2.6 %collective-permute-start.1 = (bf16[256,128]{1,0:T(8,128)(2,1)}, bf16[256,128]{1,0:T(8,128)(2,1)S(1)}, u32[]{:S(2)}, u32[]{:S(2)}) collective-permute-start(bf16[256,128]{1,0:T(8,128)(2,1)} %get-tuple-element.13), channel_id=1, source_target_pairs={{0,16},{8,24},{16,0},{24,8},{1,17},{9,25},{17,1},{25,9},{2,18},{10... | collective-permute-start | bytes 196616 | tf_op jit(solution)/shard_map/ppermute | solution.py:406
  9.2 1.3 %collective-permute-start.2 = (bf16[256,128]{1,0:T(8,128)(2,1)}, bf16[256,128]{1,0:T(8,128)(2,1)S(1)}, u32[]{:S(2)}, u32[]{:S(2)}) collective-permute-start(bf16[256,128]{1,0:T(8,128)(2,1)} %get-tuple-element.14), channel_id=1, source_target_pairs={{0,24},{8,0},{16,8},{24,16},{1,25},{9,1},{17,9},{25,17},{2,26},{10... | collective-permute-start | bytes 196616 | tf_op jit(solution)/shard_map/ppermute | solution.py:406
  10.6 0.0 copy-start.1
  10.6 0.9 %copy-done.1 = bf16[2,128,512]{2,1,0:T(8,128)(2,1)S(1)} copy-done((bf16[2,128,512]{2,1,0:T(8,128)(2,1)S(1)}, bf16[2,128,512]{2,1,0:T(8,128)(2,1)}, u32[]{:S(2)}) %copy-start.1) | copy-done | bytes 262168
  11.5 0.7 %lines.1 = (bf16[2,128,256]{2,1,0:T(8,128)(2,1)S(1)}, bf16[2,4,256,32]{3,2,1,0:T(8,128)(2,1)S(1)}, bf16[2,128,256]{2,1,0:T(8,128)(2,1)S(1)}, f32[2,128,256]{2,1,0:T(8,128)S(1)}) custom-call(bf16[8,256,128]{2,1,0:T(8,128)(2,1)S(1)} %copy-done, f32[2,128]{1,0:T(2,128)S(1)} %copy-done.3, f32[2,128]{1,0:T(2,128)S(1)} %copy-done.4, ...), custom_call_target="tpu_custom_call" | custom-call | flops 67108864 | bytes 1048576 | tf_op jit(solution)/shard_map/lines/pallas_call | solution.py:233
  12.3 0.0 collective-permute-done
  12.3 1.6 %collective-permute-done.1 = bf16[256,128]{1,0:T(8,128)(2,1)S(1)} collective-permute-done((bf16[256,128]{1,0:T(8,128)(2,1)}, bf16[256,128]{1,0:T(8,128)(2,1)S(1)}, u32[]{:S(2)}, u32[]{:S(2)}) %collective-permute-start.1) | collective-permute-done | bytes 65568 | tf_op jit(solution)/shard_map/ppermute | solution.py:406
  13.9 0.2 collective-permute-done.2
  14.2 0.1 fusion.15
  14.3 1.6 %collective-permute-start.3 = (bf16[4,160,128]{2,1,0:T(8,128)(2,1)S(1)}, bf16[4,160,128]{2,1,0:T(8,128)(2,1)S(1)}, u32[]{:S(2)}, u32[]{:S(2)}) collective-permute-start(bf16[4,160,128]{2,1,0:T(8,128)(2,1)S(1)} %get-tuple-element.20), channel_id=1, source_target_pairs={{0,2},{1,3},{2,0},{3,1},{4,6},{5,7},{6,4},{7,5},{8,10},{9,11},{10,... | collective-permute-start | bytes 491528 | tf_op jit(solution)/shard_map/ppermute | solution.py:409
  15.9 1.5 %collective-permute-start.5 = (bf16[4,160,128]{2,1,0:T(8,128)(2,1)S(1)}, bf16[4,160,128]{2,1,0:T(8,128)(2,1)S(1)}, u32[]{:S(2)}, u32[]{:S(2)}) collective-permute-start(bf16[4,160,128]{2,1,0:T(8,128)(2,1)S(1)} %get-tuple-element.21), channel_id=1, source_target_pairs={{0,6},{1,7},{2,4},{3,5},{4,2},{5,3},{6,0},{7,1},{8,14},{9,15},{10,... | collective-permute-start | bytes 491528 | tf_op jit(solution)/shard_map/ppermute | solution.py:409
  17.4 0.5 %collective-permute-start.4 = (bf16[4,160,128]{2,1,0:T(8,128)(2,1)S(1)}, bf16[4,160,128]{2,1,0:T(8,128)(2,1)S(1)}, u32[]{:S(2)}, u32[]{:S(2)}) collective-permute-start(bf16[4,160,128]{2,1,0:T(8,128)(2,1)S(1)} %get-tuple-element.22), channel_id=1, source_target_pairs={{0,4},{1,5},{2,6},{3,7},{4,0},{5,1},{6,2},{7,3},{8,12},{9,13},{10,... | collective-permute-start | bytes 491528 | tf_op jit(solution)/shard_map/ppermute | solution.py:409
  17.8 3.6 %collective-permute-done.3 = bf16[4,160,128]{2,1,0:T(8,128)(2,1)S(1)} collective-permute-done((bf16[4,160,128]{2,1,0:T(8,128)(2,1)S(1)}, bf16[4,160,128]{2,1,0:T(8,128)(2,1)S(1)}, u32[]{:S(2)}, u32[]{:S(2)}) %collective-permute-start.3) | collective-permute-done | bytes 163872 | tf_op jit(solution)/shard_map/ppermute | solution.py:409
  21.5 2.4 %collective-permute-done.5 = bf16[4,160,128]{2,1,0:T(8,128)(2,1)S(1)} collective-permute-done((bf16[4,160,128]{2,1,0:T(8,128)(2,1)S(1)}, bf16[4,160,128]{2,1,0:T(8,128)(2,1)S(1)}, u32[]{:S(2)}, u32[]{:S(2)}) %collective-permute-start.5) | collective-permute-done | bytes 163872 | tf_op jit(solution)/shard_map/ppermute | solution.py:409
  23.9 1.4 %collective-permute-done.4 = bf16[4,160,128]{2,1,0:T(8,128)(2,1)S(1)} collective-permute-done((bf16[4,160,128]{2,1,0:T(8,128)(2,1)S(1)}, bf16[4,160,128]{2,1,0:T(8,128)(2,1)S(1)}, u32[]{:S(2)}, u32[]{:S(2)}) %collective-permute-start.4) | collective-permute-done | bytes 163872 | tf_op jit(solution)/shard_map/ppermute | solution.py:409
  25.2 0.1 pad_maximum_fusion.mine_ref
  25.3 0.0 copy-start.2
  25.3 0.0 copy-start.6
  25.3 0.1 collective-permute-start.6
  25.4 2.0 %early.1.early_ref = f32[2,128,128]{2,1,0:T(8,128)S(1)} custom-call(bf16[4,4,160,128]{3,2,1,0:T(8,128)(2,1)S(1)} %pad_maximum_fusion.mine_ref, bf16[2,128,256]{2,1,0:T(8,128)(2,1)S(1)} %get-tuple-element.15.q.q0, bf16[2,4,256,32]{3,2,1,0:T(8,128)(2,1)S(1)} %get-tuple-element.16.k.k0, bf16[2,128,256]{2,1,0:T(8,128)(2,1)S(1)} %get-tuple-element.17.v.v0), custom_call_target="tpu_custom_call" | custom-call | flops 67108864 | bytes 2097152 | tf_op jit(solution)/shard_map/early/pallas_call | solution.py:310
  27.4 0.1 collective-permute-done.6.other_ref
  27.5 7.2 %attend.1 = (bf16[2,256,128]{2,1,0:T(8,128)(2,1)}, bf16[2,256,128]{2,1,0:T(8,128)(2,1)}) custom-call(bf16[4,4,160,128]{3,2,1,0:T(8,128)(2,1)S(1)} %pad_maximum_fusion.mine_ref, bf16[4,4,160,128]{3,2,1,0:T(8,128)(2,1)S(1)} %collective-permute-done.6.other_ref, f32[2,128,128]{2,1,0:T(8,128)S(1)} %early.1.early_ref, ...), custom_call_target="tpu_custom_call" | custom-call | tf_op jit(solution)/shard_map/attend/pallas_call | solution.py:382
  (15 shorter events, 0.1 us)
Async XLA Ops:
  0.6 9.9 %copy-start = (bf16[8,256,128]{2,1,0:T(8,128)(2,1)S(1)}, bf16[8,256,128]{2,1,0:T(8,128)(2,1)}, u32[]{:S(2)}) copy-start(bf16[8,256,128]{2,1,0:T(8,128)(2,1)} %lines_ref.1) | copy-start | bytes 1572868
  3.5 8.7 %collective-permute-start = (bf16[256,128]{1,0:T(8,128)(2,1)}, bf16[256,128]{1,0:T(8,128)(2,1)S(1)}, u32[]{:S(2)}, u32[]{:S(2)}) collective-permute-start(bf16[256,128]{1,0:T(8,128)(2,1)} %get-tuple-element.12), channel_id=1, source_target_pairs={{0,8},{8,16},{16,24},{24,0},{1,9},{9,17},{17,25},{25,1},{2,10},{10... | collective-permute-start | bytes 196616 | tf_op jit(solution)/shard_map/ppermute | solution.py:406
  6.6 3.9 %copy-start.4 = (f32[2,128]{1,0:T(2,128)S(1)}, f32[2,128]{1,0:T(2,128)}, u32[]{:S(2)}) copy-start(f32[2,128]{1,0:T(2,128)} %shift_ref.3) | copy-start | bytes 3076
  6.6 4.0 %copy-start.5 = (f32[2,128]{1,0:T(2,128)S(1)}, f32[2,128]{1,0:T(2,128)}, u32[]{:S(2)}) copy-start(f32[2,128]{1,0:T(2,128)} %gate_ref.1) | copy-start | bytes 3076
  6.6 4.0 %copy-start.3 = (f32[2,128]{1,0:T(2,128)S(1)}, f32[2,128]{1,0:T(2,128)}, u32[]{:S(2)}) copy-start(f32[2,128]{1,0:T(2,128)} %gain_ref.3) | copy-start | bytes 3076
  6.6 7.3 %collective-permute-start.1 = (bf16[256,128]{1,0:T(8,128)(2,1)}, bf16[256,128]{1,0:T(8,128)(2,1)S(1)}, u32[]{:S(2)}, u32[]{:S(2)}) collective-permute-start(bf16[256,128]{1,0:T(8,128)(2,1)} %get-tuple-element.13), channel_id=1, source_target_pairs={{0,16},{8,24},{16,0},{24,8},{1,17},{9,25},{17,1},{25,9},{2,18},{10... | collective-permute-start | bytes 196616 | tf_op jit(solution)/shard_map/ppermute | solution.py:406
  9.2 4.9 %collective-permute-start.2 = (bf16[256,128]{1,0:T(8,128)(2,1)}, bf16[256,128]{1,0:T(8,128)(2,1)S(1)}, u32[]{:S(2)}, u32[]{:S(2)}) collective-permute-start(bf16[256,128]{1,0:T(8,128)(2,1)} %get-tuple-element.14), channel_id=1, source_target_pairs={{0,24},{8,0},{16,8},{24,16},{1,25},{9,1},{17,9},{25,17},{2,26},{10... | collective-permute-start | bytes 196616 | tf_op jit(solution)/shard_map/ppermute | solution.py:406
  10.6 1.0 %copy-start.1 = (bf16[2,128,512]{2,1,0:T(8,128)(2,1)S(1)}, bf16[2,128,512]{2,1,0:T(8,128)(2,1)}, u32[]{:S(2)}) copy-start(bf16[2,128,512]{2,1,0:T(8,128)(2,1)} %proj_ref.1) | copy-start | bytes 786436
  11.5 2.6 %copy-start.7 = (bf16[256,128]{1,0:T(8,128)(2,1)S(1)}, bf16[256,128]{1,0:T(8,128)(2,1)}, u32[]{:S(2)}) copy-start(bf16[256,128]{1,0:T(8,128)(2,1)} %get-tuple-element.11) | copy-start | bytes 196612
  14.3 7.2 %collective-permute-start.3 = (bf16[4,160,128]{2,1,0:T(8,128)(2,1)S(1)}, bf16[4,160,128]{2,1,0:T(8,128)(2,1)S(1)}, u32[]{:S(2)}, u32[]{:S(2)}) collective-permute-start(bf16[4,160,128]{2,1,0:T(8,128)(2,1)S(1)} %get-tuple-element.20), channel_id=1, source_target_pairs={{0,2},{1,3},{2,0},{3,1},{4,6},{5,7},{6,4},{7,5},{8,10},{9,11},{10,... | collective-permute-start | bytes 491528 | tf_op jit(solution)/shard_map/ppermute | solution.py:409
  15.9 8.0 %collective-permute-start.5 = (bf16[4,160,128]{2,1,0:T(8,128)(2,1)S(1)}, bf16[4,160,128]{2,1,0:T(8,128)(2,1)S(1)}, u32[]{:S(2)}, u32[]{:S(2)}) collective-permute-start(bf16[4,160,128]{2,1,0:T(8,128)(2,1)S(1)} %get-tuple-element.21), channel_id=1, source_target_pairs={{0,6},{1,7},{2,4},{3,5},{4,2},{5,3},{6,0},{7,1},{8,14},{9,15},{10,... | collective-permute-start | bytes 491528 | tf_op jit(solution)/shard_map/ppermute | solution.py:409
  17.4 7.9 %collective-permute-start.4 = (bf16[4,160,128]{2,1,0:T(8,128)(2,1)S(1)}, bf16[4,160,128]{2,1,0:T(8,128)(2,1)S(1)}, u32[]{:S(2)}, u32[]{:S(2)}) collective-permute-start(bf16[4,160,128]{2,1,0:T(8,128)(2,1)S(1)} %get-tuple-element.22), channel_id=1, source_target_pairs={{0,4},{1,5},{2,6},{3,7},{4,0},{5,1},{6,2},{7,3},{8,12},{9,13},{10,... | collective-permute-start | bytes 491528 | tf_op jit(solution)/shard_map/ppermute | solution.py:409
  25.3 2.2 %copy-start.2 = (bf16[2,128,128]{2,1,0:T(8,128)(2,1)S(1)}, bf16[2,128,128]{2,1,0:T(8,128)(2,1)}, u32[]{:S(2)}) copy-start(bf16[2,128,128]{2,1,0:T(8,128)(2,1)} %weight_ref.3) | copy-start | bytes 196612
  25.3 2.2 %copy-start.6 = (f32[2,128]{1,0:T(2,128)S(1)}, f32[2,128]{1,0:T(2,128)}, u32[]{:S(2)}) copy-start(f32[2,128]{1,0:T(2,128)} %offset_ref.3) | copy-start | bytes 3076
  25.3 2.2 %collective-permute-start.6 = (bf16[4,4,160,128]{3,2,1,0:T(8,128)(2,1)S(1)}, bf16[4,4,160,128]{3,2,1,0:T(8,128)(2,1)S(1)}, u32[]{:S(2)}, u32[]{:S(2)}) collective-permute-start(bf16[4,4,160,128]{3,2,1,0:T(8,128)(2,1)S(1)} %pad_maximum_fusion.mine_ref), channel_id=1, source_target_pairs={{0,1},{1,0},{2,3},{3,2},{4,5},{5,4},{6,7},{7,6},{8,9},{9,8},{10,11... | collective-permute-start | bytes 1966088 | tf_op jit(solution)/shard_map/ppermute | solution.py:409

commit v5 on v3

--- a/solution.py
+++ b/solution.py
@@ -268,13 +268,41 @@
                 into[slot, at : at + half, there] = block
 
 
-def softmax_mix(keys, queries, values, added):
-    scores = [contract(k, q, 1, 0) + added for k, q in zip(keys, queries)]
-    tops = [jnp.max(score, 0, keepdims=True) for score in scores]
-    expos = [jnp.exp(score - top) for score, top in zip(scores, tops)]
+def score(units):
+    return [contract(key, query, 1, 0) + added for key, query, added, _ in units]
+
+
+def mix(units, scores):
+    tops = [jnp.max(part, 0, keepdims=True) for part in scores]
+    expos = [jnp.exp(part - top) for part, top in zip(scores, tops)]
     shares = [1.0 / jnp.sum(expo, 0, keepdims=True) for expo in expos]
     weights = [(expo * share).astype(jnp.bfloat16) for expo, share in zip(expos, shares)]
-    return [contract(v, weight, 1, 0) for v, weight in zip(values, weights)]
+    return [contract(unit[3], weight, 1, 0) for unit, weight in zip(units, weights)]
+
+
+def attend_groups(groups):
+    ready = score(groups[0][0]())
+    for i, (units, put) in enumerate(groups):
+        ahead = score(groups[i + 1][0]()) if i + 1 < len(groups) else None
+        put(mix(units(), ready))
+        ready = ahead
+
+
+def head_group(heads, size, q, k, v, bias, mixed, there, near):
+    def units():
+        return [
+            (k[w, h], q[w, h * size : (h + 1) * size, there], bias[h % bias.shape[0], :, near],
+             v[w, h * size : (h + 1) * size, :])
+            for h in heads
+            for w in range(WD)
+        ]
+
+    def put(outs):
+        for i, h in enumerate(heads):
+            for w in range(WD):
+                mixed[w, h * size : (h + 1) * size, near] = outs[i * WD + w]
+
+    return units, put
 
 
 def start_half(source, other, q, k, v, mixed, bias):
@@ -282,26 +310,28 @@
     half = length // 2
     rows = half // (source.shape[0] * source.shape[1])
     width = min(half, CHUNK)
+    if half == width:
+        groups = []
+        for pack in range(heads // 2):
+            unpack(source, 0, pack, rows, heads, 1, bias, 0)
+            groups.append(
+                head_group(
+                    (2 * pack, 2 * pack + 1), size, q, k, v, bias, mixed,
+                    pl.ds(other * half, half), pl.ds(0, half),
+                )
+            )
+        attend_groups(groups)
+        return
     for pack in range(heads // 2):
         unpack(source, 0, pack, rows, heads, 1, bias, 0)
-        for i in range(2):
-            part = slice((2 * pack + i) * size, (2 * pack + i + 1) * size)
-
-            def step(chunk):
-                near = pl.ds(chunk * width if half == width else pl.multiple_of(chunk * width, width), width)
-                there = pl.ds(other * half + chunk * width, width)
-                if half != width:
-                    there = pl.ds(pl.multiple_of(other * half + chunk * width, width), width)
-                outs = softmax_mix(
-                    [k[w, 2 * pack + i] for w in range(WD)],
-                    [q[w, part, there] for w in range(WD)],
-                    [v[w, part, :] for w in range(WD)],
-                    bias[(2 * pack + i) % bias.shape[0], :, near],
-                )
-                for w in range(WD):
-                    mixed[w, part, near] = outs[w]
-
-            for_each(half // width, step, half == width)
+
+        def step(chunk):
+            near = pl.ds(pl.multiple_of(chunk * width, width), width)
+            there = pl.ds(pl.multiple_of(other * half + chunk * width, width), width)
+            for h in (2 * pack, 2 * pack + 1):
+                attend_groups([head_group((h,), size, q, k, v, bias, mixed, there, near)])
+
+        for_each(half // width, step, False)
 
 
 def early_kernel(mine_ref, q, k, v, mixed, bias):
@@ -355,24 +385,25 @@
         gated = (jnp.concatenate([early_ref[w], late[w]], 1) * g0[w]).astype(jnp.bfloat16)
         full = contract(gated, weight_ref[0], 0, 0) + offset_ref[0:1, :]
         out0[w] = to_devices(full, along, chips, rows).astype(jnp.bfloat16)
+    groups = []
     for pack in range(heads // 2):
         unpack(mine_ref, 1, pack, rows, heads, 0, bias, 0)
         unpack(other_ref, 1, pack, rows, heads, 0, bias, half)
-        for i in range(2):
-            part = slice((2 * pack + i) * size, (2 * pack + i + 1) * size)
-
-            def step(chunk):
-                there = pl.ds(chunk * CHUNK if length == CHUNK else pl.multiple_of(chunk * CHUNK, CHUNK), CHUNK)
-                outs = softmax_mix(
-                    [k1[w, 2 * pack + i] for w in range(WD)],
-                    [q1[w, part, there] for w in range(WD)],
-                    [v1[w, part, :] for w in range(WD)],
-                    bias[(2 * pack + i) % bias.shape[0], :, there],
-                )
-                for w in range(WD):
-                    mixed[w, part, there] = outs[w]
-
-            for_each(length // CHUNK, step, length == CHUNK)
+        pair = (2 * pack, 2 * pack + 1)
+        if length == CHUNK:
+            groups.append(
+                head_group(pair, size, q1, k1, v1, bias, mixed, pl.ds(0, length), pl.ds(0, length))
+            )
+            continue
+
+        def step(chunk):
+            there = pl.ds(pl.multiple_of(chunk * CHUNK, CHUNK), CHUNK)
+            for h in pair:
+                attend_groups([head_group((h,), size, q1, k1, v1, bias, mixed, there, there)])
+
+        for_each(length // CHUNK, step, False)
+    if groups:
+        attend_groups(groups)
     for w in range(WD):
         gated = (mixed[w] * g1[w]).astype(jnp.bfloat16)
         full = contract(gated, weight_ref[1], 0, 0) + offset_ref[1:2, :]

time: 31.7 us -> 30.8 us (0.972)
  Pallas kernels: 8.76 us -> 7.37 us
  waiting for transfers between devices: 10.2 us -> 10.7 us
    pallas_call x1, Pallas kernels: 4.04 us -> 3.13 us  [attend(): pl.pallas_call(attend_kernel, out_shape=(result, result), in_specs=[VMEM]...]
    pallas_call x1, Pallas kernels: 1.11 us -> 0.62 us  [attend_early(): pl.pallas_call(early_kernel, out_shape=jax.ShapeDtypeStruct((WD, heads *...]
    ppermute x4, waiting for transfers between devices: 8.36 us -> 8.84 us  [by_col(): return lax.ppermute(block, 'col', [(i, i ^ flip) for i in range(cols)])]
  transfers between devices with their start and end apart: 7 -> 7, of which waited for: 6 -> 6; matrix products, arithmetic and copies ran while one was open for 0% -> 0% of each run, Pallas kernels for 6% -> 4%
where the time goes in v5:
time: 30.8 us; the launch traced here: 30.6 us
  waiting for transfers between devices  10.7 us (35%)
  starting transfers between devices  10.6 us (34%)
  Pallas kernels  7.37 us (24%)
  local copies, waits for them, and re-layouts  1 us (3%)
  between operations  0.74 us (2%)
    ppermute x4, waiting for transfers between devices, by_col(): return lax.ppermute(block, 'col', [(i, i ^ flip) for i in range(cols)])  8.84 us
    ppermute x3, starting transfers between devices, by_row(): lax.ppermute(block, 'row', [(i, (i + shift) % along) for i in range(along)])  7.01 us
    ppermute x4, starting transfers between devices, by_col(): return lax.ppermute(block, 'col', [(i, i ^ flip) for i in range(cols)])  3.62 us
    pallas_call x1, Pallas kernels, attend(): pl.pallas_call(attend_kernel, out_shape=(result, result), in_specs=[VMEM]...  3.13 us
    pallas_call x1, Pallas kernels, local_bias(): pl.pallas_call(functools.partial(bias_kernel, along, chips), out_shape=(s...  2.89 us
    ppermute x3, waiting for transfers between devices, by_row(): lax.ppermute(block, 'row', [(i, (i + shift) % along) for i in range(along)])  1.86 us
    unnamed x16, local copies, waits for them, and re-layouts  0.98 us
    pallas_call x1, Pallas kernels, local_lines(): pl.pallas_call(functools.partial(lines_kernel, along, chips), grid=(1,),...  0.73 us
  transfers between devices with their start and end apart: 7, of which 6 were waited for; matrix products, arithmetic and copies ran while one was open for 0% of the time, Pallas kernels for 4%

profile of v5, /device:TPU:0, one launch (start us, length us, event | category | flops | bytes accessed | tf_op | source)
XLA Modules:
  0.0 30.6 jit_solution(16536673689797155251)
XLA Ops:
  0.6 2.9 %bias.1 = (bf16[256,128]{1,0:T(8,128)(2,1)}, bf16[256,128]{1,0:T(8,128)(2,1)}, bf16[256,128]{1,0:T(8,128)(2,1)}, bf16[256,128]{1,0:T(8,128)(2,1)}) custom-call(bf16[8,256,128]{2,1,0:T(8,128)(2,1)} %lines_ref.1, s32[1,256]{1,0:T(1,128)} %bitcast.23, f32[2,128]{1,0:T(2,128)} %gain_ref.3, f32[2,128]{1,0:T(2,128)} %shift_ref.3, bf16[2,4,128]{2,1,0:T(4,128)(2,1)} %bitcast.22), custom_call_target="tpu_custom_call" | custom-call | tf_op jit(solution)/shard_map/bias/pallas_call | solution.py:115
  3.5 3.1 %collective-permute-start = (bf16[256,128]{1,0:T(8,128)(2,1)}, bf16[256,128]{1,0:T(8,128)(2,1)S(1)}, u32[]{:S(2)}, u32[]{:S(2)}) collective-permute-start(bf16[256,128]{1,0:T(8,128)(2,1)} %get-tuple-element.12), channel_id=1, source_target_pairs={{0,8},{8,16},{16,24},{24,0},{1,9},{9,17},{17,25},{25,1},{2,10},{10... | collective-permute-start | bytes 196616 | tf_op jit(solution)/shard_map/ppermute | solution.py:442
  6.6 2.6 %collective-permute-start.1 = (bf16[256,128]{1,0:T(8,128)(2,1)}, bf16[256,128]{1,0:T(8,128)(2,1)S(1)}, u32[]{:S(2)}, u32[]{:S(2)}) collective-permute-start(bf16[256,128]{1,0:T(8,128)(2,1)} %get-tuple-element.13), channel_id=1, source_target_pairs={{0,16},{8,24},{16,0},{24,8},{1,17},{9,25},{17,1},{25,9},{2,18},{10... | collective-permute-start | bytes 196616 | tf_op jit(solution)/shard_map/ppermute | solution.py:442
  9.2 1.3 %collective-permute-start.2 = (bf16[256,128]{1,0:T(8,128)(2,1)}, bf16[256,128]{1,0:T(8,128)(2,1)S(1)}, u32[]{:S(2)}, u32[]{:S(2)}) collective-permute-start(bf16[256,128]{1,0:T(8,128)(2,1)} %get-tuple-element.14), channel_id=1, source_target_pairs={{0,24},{8,0},{16,8},{24,16},{1,25},{9,1},{17,9},{25,17},{2,26},{10... | collective-permute-start | bytes 196616 | tf_op jit(solution)/shard_map/ppermute | solution.py:442
  10.6 0.0 copy-start.1
  10.6 0.9 %copy-done.1 = bf16[2,128,512]{2,1,0:T(8,128)(2,1)S(1)} copy-done((bf16[2,128,512]{2,1,0:T(8,128)(2,1)S(1)}, bf16[2,128,512]{2,1,0:T(8,128)(2,1)}, u32[]{:S(2)}) %copy-start.1) | copy-done | bytes 262168
  11.5 0.7 %lines.1 = (bf16[2,128,256]{2,1,0:T(8,128)(2,1)S(1)}, bf16[2,4,256,32]{3,2,1,0:T(8,128)(2,1)S(1)}, bf16[2,128,256]{2,1,0:T(8,128)(2,1)S(1)}, f32[2,128,256]{2,1,0:T(8,128)S(1)}) custom-call(bf16[8,256,128]{2,1,0:T(8,128)(2,1)S(1)} %copy-done, f32[2,128]{1,0:T(2,128)S(1)} %copy-done.3, f32[2,128]{1,0:T(2,128)S(1)} %copy-done.4, ...), custom_call_target="tpu_custom_call" | custom-call | flops 67108864 | bytes 1048576 | tf_op jit(solution)/shard_map/lines/pallas_call | solution.py:232
  12.3 0.0 collective-permute-done
  12.3 1.6 %collective-permute-done.1 = bf16[256,128]{1,0:T(8,128)(2,1)S(1)} collective-permute-done((bf16[256,128]{1,0:T(8,128)(2,1)}, bf16[256,128]{1,0:T(8,128)(2,1)S(1)}, u32[]{:S(2)}, u32[]{:S(2)}) %collective-permute-start.1) | collective-permute-done | bytes 65568 | tf_op jit(solution)/shard_map/ppermute | solution.py:442
  13.9 0.2 collective-permute-done.2
  14.2 0.1 fusion.15
  14.3 1.6 %collective-permute-start.3 = (bf16[4,160,128]{2,1,0:T(8,128)(2,1)S(1)}, bf16[4,160,128]{2,1,0:T(8,128)(2,1)S(1)}, u32[]{:S(2)}, u32[]{:S(2)}) collective-permute-start(bf16[4,160,128]{2,1,0:T(8,128)(2,1)S(1)} %get-tuple-element.20), channel_id=1, source_target_pairs={{0,2},{1,3},{2,0},{3,1},{4,6},{5,7},{6,4},{7,5},{8,10},{9,11},{10,... | collective-permute-start | bytes 491528 | tf_op jit(solution)/shard_map/ppermute | solution.py:445
  15.9 1.5 %collective-permute-start.5 = (bf16[4,160,128]{2,1,0:T(8,128)(2,1)S(1)}, bf16[4,160,128]{2,1,0:T(8,128)(2,1)S(1)}, u32[]{:S(2)}, u32[]{:S(2)}) collective-permute-start(bf16[4,160,128]{2,1,0:T(8,128)(2,1)S(1)} %get-tuple-element.21), channel_id=1, source_target_pairs={{0,6},{1,7},{2,4},{3,5},{4,2},{5,3},{6,0},{7,1},{8,14},{9,15},{10,... | collective-permute-start | bytes 491528 | tf_op jit(solution)/shard_map/ppermute | solution.py:445
  17.4 0.5 %collective-permute-start.4 = (bf16[4,160,128]{2,1,0:T(8,128)(2,1)S(1)}, bf16[4,160,128]{2,1,0:T(8,128)(2,1)S(1)}, u32[]{:S(2)}, u32[]{:S(2)}) collective-permute-start(bf16[4,160,128]{2,1,0:T(8,128)(2,1)S(1)} %get-tuple-element.22), channel_id=1, source_target_pairs={{0,4},{1,5},{2,6},{3,7},{4,0},{5,1},{6,2},{7,3},{8,12},{9,13},{10,... | collective-permute-start | bytes 491528 | tf_op jit(solution)/shard_map/ppermute | solution.py:445
  17.8 3.6 %collective-permute-done.3 = bf16[4,160,128]{2,1,0:T(8,128)(2,1)S(1)} collective-permute-done((bf16[4,160,128]{2,1,0:T(8,128)(2,1)S(1)}, bf16[4,160,128]{2,1,0:T(8,128)(2,1)S(1)}, u32[]{:S(2)}, u32[]{:S(2)}) %collective-permute-start.3) | collective-permute-done | bytes 163872 | tf_op jit(solution)/shard_map/ppermute | solution.py:445
  21.5 2.4 %collective-permute-done.5 = bf16[4,160,128]{2,1,0:T(8,128)(2,1)S(1)} collective-permute-done((bf16[4,160,128]{2,1,0:T(8,128)(2,1)S(1)}, bf16[4,160,128]{2,1,0:T(8,128)(2,1)S(1)}, u32[]{:S(2)}, u32[]{:S(2)}) %collective-permute-start.5) | collective-permute-done | bytes 163872 | tf_op jit(solution)/shard_map/ppermute | solution.py:445
  23.9 1.4 %collective-permute-done.4 = bf16[4,160,128]{2,1,0:T(8,128)(2,1)S(1)} collective-permute-done((bf16[4,160,128]{2,1,0:T(8,128)(2,1)S(1)}, bf16[4,160,128]{2,1,0:T(8,128)(2,1)S(1)}, u32[]{:S(2)}, u32[]{:S(2)}) %collective-permute-start.4) | collective-permute-done | bytes 163872 | tf_op jit(solution)/shard_map/ppermute | solution.py:445
  25.2 0.1 pad_maximum_fusion.mine_ref
  25.3 0.0 copy-start.2
  25.3 0.0 copy-start.6
  25.3 0.1 collective-permute-start.6
  25.4 0.6 %early.1.early_ref = f32[2,128,128]{2,1,0:T(8,128)S(1)} custom-call(bf16[4,4,160,128]{3,2,1,0:T(8,128)(2,1)S(1)} %pad_maximum_fusion.mine_ref, bf16[2,128,256]{2,1,0:T(8,128)(2,1)S(1)} %get-tuple-element.15.q.q0, bf16[2,4,256,32]{3,2,1,0:T(8,128)(2,1)S(1)} %get-tuple-element.16.k.k0, bf16[2,128,256]{2,1,0:T(8,128)(2,1)S(1)} %get-tuple-element.17.v.v0), custom_call_target="tpu_custom_call" | custom-call | flops 67108864 | bytes 2097152 | tf_op jit(solution)/shard_map/early/pallas_call | solution.py:343
  26.0 1.5 %collective-permute-done.6.other_ref = bf16[4,4,160,128]{3,2,1,0:T(8,128)(2,1)S(1)} collective-permute-done((bf16[4,4,160,128]{3,2,1,0:T(8,128)(2,1)S(1)}, bf16[4,4,160,128]{3,2,1,0:T(8,128)(2,1)S(1)}, u32[]{:S(2)}, u32[]{:S(2)}) %collective-permute-start.6) | collective-permute-done | bytes 655392 | tf_op jit(solution)/shard_map/ppermute | solution.py:445
  27.5 3.1 %attend.1 = (bf16[2,256,128]{2,1,0:T(8,128)(2,1)}, bf16[2,256,128]{2,1,0:T(8,128)(2,1)}) custom-call(bf16[4,4,160,128]{3,2,1,0:T(8,128)(2,1)S(1)} %pad_maximum_fusion.mine_ref, bf16[4,4,160,128]{3,2,1,0:T(8,128)(2,1)S(1)} %collective-permute-done.6.other_ref, f32[2,128,128]{2,1,0:T(8,128)S(1)} %early.1.early_ref, ...), custom_call_target="tpu_custom_call" | custom-call | tf_op jit(solution)/shard_map/attend/pallas_call | solution.py:418
  (15 shorter events, 0.1 us)
Async XLA Ops:
  0.6 9.9 %copy-start = (bf16[8,256,128]{2,1,0:T(8,128)(2,1)S(1)}, bf16[8,256,128]{2,1,0:T(8,128)(2,1)}, u32[]{:S(2)}) copy-start(bf16[8,256,128]{2,1,0:T(8,128)(2,1)} %lines_ref.1) | copy-start | bytes 1572868
  3.5 8.7 %collective-permute-start = (bf16[256,128]{1,0:T(8,128)(2,1)}, bf16[256,128]{1,0:T(8,128)(2,1)S(1)}, u32[]{:S(2)}, u32[]{:S(2)}) collective-permute-start(bf16[256,128]{1,0:T(8,128)(2,1)} %get-tuple-element.12), channel_id=1, source_target_pairs={{0,8},{8,16},{16,24},{24,0},{1,9},{9,17},{17,25},{25,1},{2,10},{10... | collective-permute-start | bytes 196616 | tf_op jit(solution)/shard_map/ppermute | solution.py:442
  6.6 3.9 %copy-start.4 = (f32[2,128]{1,0:T(2,128)S(1)}, f32[2,128]{1,0:T(2,128)}, u32[]{:S(2)}) copy-start(f32[2,128]{1,0:T(2,128)} %shift_ref.3) | copy-start | bytes 3076
  6.6 4.0 %copy-start.5 = (f32[2,128]{1,0:T(2,128)S(1)}, f32[2,128]{1,0:T(2,128)}, u32[]{:S(2)}) copy-start(f32[2,128]{1,0:T(2,128)} %gate_ref.1) | copy-start | bytes 3076
  6.6 4.0 %copy-start.3 = (f32[2,128]{1,0:T(2,128)S(1)}, f32[2,128]{1,0:T(2,128)}, u32[]{:S(2)}) copy-start(f32[2,128]{1,0:T(2,128)} %gain_ref.3) | copy-start | bytes 3076
  6.6 7.3 %collective-permute-start.1 = (bf16[256,128]{1,0:T(8,128)(2,1)}, bf16[256,128]{1,0:T(8,128)(2,1)S(1)}, u32[]{:S(2)}, u32[]{:S(2)}) collective-permute-start(bf16[256,128]{1,0:T(8,128)(2,1)} %get-tuple-element.13), channel_id=1, source_target_pairs={{0,16},{8,24},{16,0},{24,8},{1,17},{9,25},{17,1},{25,9},{2,18},{10... | collective-permute-start | bytes 196616 | tf_op jit(solution)/shard_map/ppermute | solution.py:442
  9.2 4.9 %collective-permute-start.2 = (bf16[256,128]{1,0:T(8,128)(2,1)}, bf16[256,128]{1,0:T(8,128)(2,1)S(1)}, u32[]{:S(2)}, u32[]{:S(2)}) collective-permute-start(bf16[256,128]{1,0:T(8,128)(2,1)} %get-tuple-element.14), channel_id=1, source_target_pairs={{0,24},{8,0},{16,8},{24,16},{1,25},{9,1},{17,9},{25,17},{2,26},{10... | collective-permute-start | bytes 196616 | tf_op jit(solution)/shard_map/ppermute | solution.py:442
  10.6 1.0 %copy-start.1 = (bf16[2,128,512]{2,1,0:T(8,128)(2,1)S(1)}, bf16[2,128,512]{2,1,0:T(8,128)(2,1)}, u32[]{:S(2)}) copy-start(bf16[2,128,512]{2,1,0:T(8,128)(2,1)} %proj_ref.1) | copy-start | bytes 786436
  11.5 2.6 %copy-start.7 = (bf16[256,128]{1,0:T(8,128)(2,1)S(1)}, bf16[256,128]{1,0:T(8,128)(2,1)}, u32[]{:S(2)}) copy-start(bf16[256,128]{1,0:T(8,128)(2,1)} %get-tuple-element.11) | copy-start | bytes 196612
  14.3 7.2 %collective-permute-start.3 = (bf16[4,160,128]{2,1,0:T(8,128)(2,1)S(1)}, bf16[4,160,128]{2,1,0:T(8,128)(2,1)S(1)}, u32[]{:S(2)}, u32[]{:S(2)}) collective-permute-start(bf16[4,160,128]{2,1,0:T(8,128)(2,1)S(1)} %get-tuple-element.20), channel_id=1, source_target_pairs={{0,2},{1,3},{2,0},{3,1},{4,6},{5,7},{6,4},{7,5},{8,10},{9,11},{10,... | collective-permute-start | bytes 491528 | tf_op jit(solution)/shard_map/ppermute | solution.py:445
  15.9 8.0 %collective-permute-start.5 = (bf16[4,160,128]{2,1,0:T(8,128)(2,1)S(1)}, bf16[4,160,128]{2,1,0:T(8,128)(2,1)S(1)}, u32[]{:S(2)}, u32[]{:S(2)}) collective-permute-start(bf16[4,160,128]{2,1,0:T(8,128)(2,1)S(1)} %get-tuple-element.21), channel_id=1, source_target_pairs={{0,6},{1,7},{2,4},{3,5},{4,2},{5,3},{6,0},{7,1},{8,14},{9,15},{10,... | collective-permute-start | bytes 491528 | tf_op jit(solution)/shard_map/ppermute | solution.py:445
  17.4 7.9 %collective-permute-start.4 = (bf16[4,160,128]{2,1,0:T(8,128)(2,1)S(1)}, bf16[4,160,128]{2,1,0:T(8,128)(2,1)S(1)}, u32[]{:S(2)}, u32[]{:S(2)}) collective-permute-start(bf16[4,160,128]{2,1,0:T(8,128)(2,1)S(1)} %get-tuple-element.22), channel_id=1, source_target_pairs={{0,4},{1,5},{2,6},{3,7},{4,0},{5,1},{6,2},{7,3},{8,12},{9,13},{10,... | collective-permute-start | bytes 491528 | tf_op jit(solution)/shard_map/ppermute | solution.py:445
  25.3 2.2 %copy-start.2 = (bf16[2,128,128]{2,1,0:T(8,128)(2,1)S(1)}, bf16[2,128,128]{2,1,0:T(8,128)(2,1)}, u32[]{:S(2)}) copy-start(bf16[2,128,128]{2,1,0:T(8,128)(2,1)} %weight_ref.3) | copy-start | bytes 196612
  25.3 2.2 %copy-start.6 = (f32[2,128]{1,0:T(2,128)S(1)}, f32[2,128]{1,0:T(2,128)}, u32[]{:S(2)}) copy-start(f32[2,128]{1,0:T(2,128)} %offset_ref.3) | copy-start | bytes 3076
  25.3 2.2 %collective-permute-start.6 = (bf16[4,4,160,128]{3,2,1,0:T(8,128)(2,1)S(1)}, bf16[4,4,160,128]{3,2,1,0:T(8,128)(2,1)S(1)}, u32[]{:S(2)}, u32[]{:S(2)}) collective-permute-start(bf16[4,4,160,128]{3,2,1,0:T(8,128)(2,1)S(1)} %pad_maximum_fusion.mine_ref), channel_id=1, source_target_pairs={{0,1},{1,0},{2,3},{3,2},{4,5},{5,4},{6,7},{7,6},{8,9},{9,8},{10,11... | collective-permute-start | bytes 1966088 | tf_op jit(solution)/shard_map/ppermute | solution.py:445

commit v6 on v5

--- a/solution.py
+++ b/solution.py
@@ -27,11 +27,11 @@
         lax.fori_loop(0, count, lambda index, carry: (step(index), carry)[1], 0)
 
 
-def standardize(wide):
-    center = jnp.mean(wide, -1, keepdims=True)
-    away = wide - center
-    spread = jnp.mean(jnp.square(away), -1, keepdims=True)
-    return away * lax.rsqrt(spread + EPS)
+def standardize_all(lines):
+    centers = [jnp.mean(wide, -1, keepdims=True) for wide in lines]
+    aways = [wide - center for wide, center in zip(lines, centers)]
+    spreads = [jnp.mean(jnp.square(away), -1, keepdims=True) for away in aways]
+    return [away * lax.rsqrt(spread + EPS) for away, spread in zip(aways, spreads)]
 
 
 def contract(left, right, left_dim, right_dim):
@@ -77,14 +77,18 @@
     paired = blocks[: 2 * heads].astype(jnp.bfloat16)
     live = jnp.broadcast_to(live_row[...], (2 * heads, length))
     first = lax.broadcasted_iota(jnp.int32, live.shape, 0) < heads
-    for a in range(rows):
-        x = pair[a].astype(jnp.float32)
+    lines = [pair[a].astype(jnp.float32) for a in range(rows)]
+    for a, x in enumerate(lines):
         wide[a] = x
-        z = standardize(x)
-        normed = jnp.concatenate(
+    lines = standardize_all(lines)
+    normed = [
+        jnp.concatenate(
             [(z * gain[p : p + 1, :] + shift[p : p + 1, :]).astype(jnp.bfloat16) for p in range(2)], 1
         )
-        bias = contract(paired, normed, 1, 1)
+        for z in lines
+    ]
+    biases = [contract(paired, line, 1, 1) for line in normed]
+    for a, bias in enumerate(biases):
         kept = jnp.where(first, live, live_each[0, device * rows + a])
         bias = jnp.where(kept > 0, bias, MASKED)
         for lane in range(length // lanes):
@@ -187,19 +191,26 @@
     return jnp.concatenate([block for line in grid for block in line], 0)
 
 
-def queries_and_gates(normed, scale, weight, offset, q_ref, g_ref, w):
+def queries_and_gates(lines, scale, weight, offset, q_ref, g_ref):
     inner = weight.shape[1] // 4
-    q_ref[w] = (contract(weight[:, :inner], normed, 0, 1) * scale).astype(jnp.bfloat16)
-    g_ref[w] = jax.nn.sigmoid(contract(weight[:, 3 * inner :], normed, 0, 1) + offset)
-
-
-def keys_and_values(normed, weight, k_ref, v_ref, w):
+    queries = [contract(weight[:, :inner], normed, 0, 1) for normed in lines]
+    gates = [contract(weight[:, 3 * inner :], normed, 0, 1) for normed in lines]
+    for w in range(WD):
+        q_ref[w] = (queries[w] * scale).astype(jnp.bfloat16)
+        g_ref[w] = jax.nn.sigmoid(gates[w] + offset)
+
+
+def keys_and_values(lines, weight, k_ref, v_ref):
     _, heads, _, size = k_ref.shape
     inner = heads * size
     for h in range(heads):
         at = inner + h * size
-        k_ref[w, h] = contract(normed, weight[:, at : at + size], 1, 0).astype(jnp.bfloat16)
-    v_ref[w] = contract(weight[:, 2 * inner : 3 * inner], normed, 0, 1).astype(jnp.bfloat16)
+        keys = [contract(normed, weight[:, at : at + size], 1, 0) for normed in lines]
+        for w in range(WD):
+            k_ref[w, h] = keys[w].astype(jnp.bfloat16)
+    values = [contract(weight[:, 2 * inner : 3 * inner], normed, 0, 1) for normed in lines]
+    for w in range(WD):
+        v_ref[w] = values[w].astype(jnp.bfloat16)
 
 
 def lines_kernel(along, chips, lines_ref, gain_ref, shift_ref, weight_ref, offset_ref, q_ref, k_ref, v_ref, g_ref):
@@ -207,11 +218,11 @@
     rows = lines_ref.shape[1] // (2 * chips * along)
     offset = turned(offset_ref[0:1, :])
     weight = weight_ref[0]
-    for w in range(WD):
-        normed = standardize(lines_ref[w].astype(jnp.float32)) * gain_ref[0:1, :] + shift_ref[0:1, :]
-        keys_and_values(normed.astype(jnp.bfloat16), weight, k_ref, v_ref, w)
-        near = to_relative(normed, along, chips, rows).astype(jnp.bfloat16)
-        queries_and_gates(near, size ** (-0.5), weight, offset, q_ref, g_ref, w)
+    lines = standardize_all([lines_ref[w].astype(jnp.float32) for w in range(WD)])
+    lines = [line * gain_ref[0:1, :] + shift_ref[0:1, :] for line in lines]
+    keys_and_values([line.astype(jnp.bfloat16) for line in lines], weight, k_ref, v_ref)
+    near = [to_relative(line, along, chips, rows).astype(jnp.bfloat16) for line in lines]
+    queries_and_gates(near, size ** (-0.5), weight, offset, q_ref, g_ref)
 
 
 def projected(length, inner, heads):
@@ -281,6 +292,8 @@
 
 
 def attend_groups(groups):
+    if not groups:
+        return
     ready = score(groups[0][0]())
     for i, (units, put) in enumerate(groups):
         ahead = score(groups[i + 1][0]()) if i + 1 < len(groups) else None
@@ -320,8 +333,7 @@
                     pl.ds(other * half, half), pl.ds(0, half),
                 )
             )
-        attend_groups(groups)
-        return
+        return groups
     for pack in range(heads // 2):
         unpack(source, 0, pack, rows, heads, 1, bias, 0)
 
@@ -332,10 +344,11 @@
                 attend_groups([head_group((h,), size, q, k, v, bias, mixed, there, near)])
 
         for_each(half // width, step, False)
+    return []
 
 
 def early_kernel(mine_ref, q, k, v, mixed, bias):
-    start_half(mine_ref, 0, q, k, v, mixed, bias)
+    attend_groups(start_half(mine_ref, 0, q, k, v, mixed, bias))
 
 
 def attend_early(mine, q, k, v):
@@ -374,18 +387,12 @@
             for shift in range(along):
                 both = source[flip, shift, pl.ds(first, WD * rows), :].astype(jnp.float32)
                 blocks.append(both.reshape(WD, rows, -1))
-    for w in range(WD):
-        x = jnp.concatenate([block[w] for block in blocks], 0)
-        normed = standardize(x) * gain_ref[1:2, :] + shift_ref[1:2, :]
-        keys_and_values(normed.astype(jnp.bfloat16), proj_ref[1], k1, v1, w)
-        ordered = to_devices(normed, along, chips, rows).astype(jnp.bfloat16)
-        queries_and_gates(ordered, size ** (-0.5), proj_ref[1], offset, q1, g1, w)
-    start_half(other_ref, 1, q0, k0, v0, late, turned_bias)
-    for w in range(WD):
-        gated = (jnp.concatenate([early_ref[w], late[w]], 1) * g0[w]).astype(jnp.bfloat16)
-        full = contract(gated, weight_ref[0], 0, 0) + offset_ref[0:1, :]
-        out0[w] = to_devices(full, along, chips, rows).astype(jnp.bfloat16)
-    groups = []
+    lines = standardize_all([jnp.concatenate([block[w] for block in blocks], 0) for w in range(WD)])
+    lines = [line * gain_ref[1:2, :] + shift_ref[1:2, :] for line in lines]
+    keys_and_values([line.astype(jnp.bfloat16) for line in lines], proj_ref[1], k1, v1)
+    ordered = [to_devices(line, along, chips, rows).astype(jnp.bfloat16) for line in lines]
+    queries_and_gates(ordered, size ** (-0.5), proj_ref[1], offset, q1, g1)
+    groups = start_half(other_ref, 1, q0, k0, v0, late, turned_bias)
     for pack in range(heads // 2):
         unpack(mine_ref, 1, pack, rows, heads, 0, bias, 0)
         unpack(other_ref, 1, pack, rows, heads, 0, bias, half)
@@ -402,8 +409,11 @@
                 attend_groups([head_group((h,), size, q1, k1, v1, bias, mixed, there, there)])
 
         for_each(length // CHUNK, step, False)
-    if groups:
-        attend_groups(groups)
+    attend_groups(groups)
+    for w in range(WD):
+        gated = (jnp.concatenate([early_ref[w], late[w]], 1) * g0[w]).astype(jnp.bfloat16)
+        full = contract(gated, weight_ref[0], 0, 0) + offset_ref[0:1, :]
+        out0[w] = to_devices(full, along, chips, rows).astype(jnp.bfloat16)
     for w in range(WD):
         gated = (mixed[w] * g1[w]).astype(jnp.bfloat16)
         full = contract(gated, weight_ref[1], 0, 0) + offset_ref[1:2, :]

time: 30.8 us -> 30.4 us (0.987)
  Pallas kernels: 7.37 us -> 6.83 us
    pallas_call x1, Pallas kernels: 3.13 us -> 2.78 us  [attend(): pl.pallas_call(attend_kernel, out_shape=(result, result), in_specs=[VMEM]...]
where the time goes in v6:
time: 30.4 us; the launch traced here: 30.2 us
  waiting for transfers between devices  10.9 us (36%)
  starting transfers between devices  10.6 us (35%)
  Pallas kernels  6.83 us (22%)
  local copies, waits for them, and re-layouts  1 us (3%)
  between operations  0.74 us (2%)
    ppermute x4, waiting for transfers between devices, by_col(): return lax.ppermute(block, 'col', [(i, i ^ flip) for i in range(cols)])  8.85 us
    ppermute x3, starting transfers between devices, by_row(): lax.ppermute(block, 'row', [(i, (i + shift) % along) for i in range(along)])  7.01 us
    ppermute x4, starting transfers between devices, by_col(): return lax.ppermute(block, 'col', [(i, i ^ flip) for i in range(cols)])  3.62 us
    pallas_call x1, Pallas kernels, local_bias(): pl.pallas_call(functools.partial(bias_kernel, along, chips), out_shape=(s...  2.84 us
    pallas_call x1, Pallas kernels, attend(): pl.pallas_call(attend_kernel, out_shape=(result, result), in_specs=[VMEM]...  2.78 us
    ppermute x3, waiting for transfers between devices, by_row(): lax.ppermute(block, 'row', [(i, (i + shift) % along) for i in range(along)])  2.01 us
    unnamed x16, local copies, waits for them, and re-layouts  0.98 us
    pallas_call x1, Pallas kernels, attend_early(): pl.pallas_call(early_kernel, out_shape=jax.ShapeDtypeStruct((WD, heads *...  0.62 us
  transfers between devices with their start and end apart: 7, of which 6 were waited for; matrix products, arithmetic and copies ran while one was open for 0% of the time, Pallas kernels for 4%

profile of v6, /device:TPU:0, one launch (start us, length us, event | category | flops | bytes accessed | tf_op | source)
XLA Modules:
  0.0 30.2 jit_solution(7141717608090278570)
XLA Ops:
  0.6 2.8 %bias.1 = (bf16[256,128]{1,0:T(8,128)(2,1)}, bf16[256,128]{1,0:T(8,128)(2,1)}, bf16[256,128]{1,0:T(8,128)(2,1)}, bf16[256,128]{1,0:T(8,128)(2,1)}) custom-call(bf16[8,256,128]{2,1,0:T(8,128)(2,1)} %lines_ref.1, s32[1,256]{1,0:T(1,128)} %bitcast.23, f32[2,128]{1,0:T(2,128)} %gain_ref.3, f32[2,128]{1,0:T(2,128)} %shift_ref.3, bf16[2,4,128]{2,1,0:T(4,128)(2,1)} %bitcast.22), custom_call_target="tpu_custom_call" | custom-call | tf_op jit(solution)/shard_map/bias/pallas_call | solution.py:119
  3.5 3.1 %collective-permute-start = (bf16[256,128]{1,0:T(8,128)(2,1)}, bf16[256,128]{1,0:T(8,128)(2,1)S(1)}, u32[]{:S(2)}, u32[]{:S(2)}) collective-permute-start(bf16[256,128]{1,0:T(8,128)(2,1)} %get-tuple-element.12), channel_id=1, source_target_pairs={{0,8},{8,16},{16,24},{24,0},{1,9},{9,17},{17,25},{25,1},{2,10},{10... | collective-permute-start | bytes 196616 | tf_op jit(solution)/shard_map/ppermute | solution.py:452
  6.6 2.6 %collective-permute-start.1 = (bf16[256,128]{1,0:T(8,128)(2,1)}, bf16[256,128]{1,0:T(8,128)(2,1)S(1)}, u32[]{:S(2)}, u32[]{:S(2)}) collective-permute-start(bf16[256,128]{1,0:T(8,128)(2,1)} %get-tuple-element.13), channel_id=1, source_target_pairs={{0,16},{8,24},{16,0},{24,8},{1,17},{9,25},{17,1},{25,9},{2,18},{10... | collective-permute-start | bytes 196616 | tf_op jit(solution)/shard_map/ppermute | solution.py:452
  9.2 1.3 %collective-permute-start.2 = (bf16[256,128]{1,0:T(8,128)(2,1)}, bf16[256,128]{1,0:T(8,128)(2,1)S(1)}, u32[]{:S(2)}, u32[]{:S(2)}) collective-permute-start(bf16[256,128]{1,0:T(8,128)(2,1)} %get-tuple-element.14), channel_id=1, source_target_pairs={{0,24},{8,0},{16,8},{24,16},{1,25},{9,1},{17,9},{25,17},{2,26},{10... | collective-permute-start | bytes 196616 | tf_op jit(solution)/shard_map/ppermute | solution.py:452
  10.5 0.0 copy-start.1
  10.5 0.9 %copy-done.1 = bf16[2,128,512]{2,1,0:T(8,128)(2,1)S(1)} copy-done((bf16[2,128,512]{2,1,0:T(8,128)(2,1)S(1)}, bf16[2,128,512]{2,1,0:T(8,128)(2,1)}, u32[]{:S(2)}) %copy-start.1) | copy-done | bytes 262168
  11.5 0.6 %lines.1 = (bf16[2,128,256]{2,1,0:T(8,128)(2,1)S(1)}, bf16[2,4,256,32]{3,2,1,0:T(8,128)(2,1)S(1)}, bf16[2,128,256]{2,1,0:T(8,128)(2,1)S(1)}, f32[2,128,256]{2,1,0:T(8,128)S(1)}) custom-call(bf16[8,256,128]{2,1,0:T(8,128)(2,1)S(1)} %copy-done, f32[2,128]{1,0:T(2,128)S(1)} %copy-done.3, f32[2,128]{1,0:T(2,128)S(1)} %copy-done.4, ...), custom_call_target="tpu_custom_call" | custom-call | flops 67108864 | bytes 1048576 | tf_op jit(solution)/shard_map/lines/pallas_call | solution.py:243
  12.1 0.0 collective-permute-done
  12.1 1.8 %collective-permute-done.1 = bf16[256,128]{1,0:T(8,128)(2,1)S(1)} collective-permute-done((bf16[256,128]{1,0:T(8,128)(2,1)}, bf16[256,128]{1,0:T(8,128)(2,1)S(1)}, u32[]{:S(2)}, u32[]{:S(2)}) %collective-permute-start.1) | collective-permute-done | bytes 65568 | tf_op jit(solution)/shard_map/ppermute | solution.py:452
  13.8 0.2 collective-permute-done.2
  14.1 0.1 fusion.15
  14.2 1.6 %collective-permute-start.3 = (bf16[4,160,128]{2,1,0:T(8,128)(2,1)S(1)}, bf16[4,160,128]{2,1,0:T(8,128)(2,1)S(1)}, u32[]{:S(2)}, u32[]{:S(2)}) collective-permute-start(bf16[4,160,128]{2,1,0:T(8,128)(2,1)S(1)} %get-tuple-element.20), channel_id=1, source_target_pairs={{0,2},{1,3},{2,0},{3,1},{4,6},{5,7},{6,4},{7,5},{8,10},{9,11},{10,... | collective-permute-start | bytes 491528 | tf_op jit(solution)/shard_map/ppermute | solution.py:455
  15.8 1.5 %collective-permute-start.5 = (bf16[4,160,128]{2,1,0:T(8,128)(2,1)S(1)}, bf16[4,160,128]{2,1,0:T(8,128)(2,1)S(1)}, u32[]{:S(2)}, u32[]{:S(2)}) collective-permute-start(bf16[4,160,128]{2,1,0:T(8,128)(2,1)S(1)} %get-tuple-element.21), channel_id=1, source_target_pairs={{0,6},{1,7},{2,4},{3,5},{4,2},{5,3},{6,0},{7,1},{8,14},{9,15},{10,... | collective-permute-start | bytes 491528 | tf_op jit(solution)/shard_map/ppermute | solution.py:455
  17.3 0.5 %collective-permute-start.4 = (bf16[4,160,128]{2,1,0:T(8,128)(2,1)S(1)}, bf16[4,160,128]{2,1,0:T(8,128)(2,1)S(1)}, u32[]{:S(2)}, u32[]{:S(2)}) collective-permute-start(bf16[4,160,128]{2,1,0:T(8,128)(2,1)S(1)} %get-tuple-element.22), channel_id=1, source_target_pairs={{0,4},{1,5},{2,6},{3,7},{4,0},{5,1},{6,2},{7,3},{8,12},{9,13},{10,... | collective-permute-start | bytes 491528 | tf_op jit(solution)/shard_map/ppermute | solution.py:455
  17.8 3.6 %collective-permute-done.3 = bf16[4,160,128]{2,1,0:T(8,128)(2,1)S(1)} collective-permute-done((bf16[4,160,128]{2,1,0:T(8,128)(2,1)S(1)}, bf16[4,160,128]{2,1,0:T(8,128)(2,1)S(1)}, u32[]{:S(2)}, u32[]{:S(2)}) %collective-permute-start.3) | collective-permute-done | bytes 163872 | tf_op jit(solution)/shard_map/ppermute | solution.py:455
  21.4 2.4 %collective-permute-done.5 = bf16[4,160,128]{2,1,0:T(8,128)(2,1)S(1)} collective-permute-done((bf16[4,160,128]{2,1,0:T(8,128)(2,1)S(1)}, bf16[4,160,128]{2,1,0:T(8,128)(2,1)S(1)}, u32[]{:S(2)}, u32[]{:S(2)}) %collective-permute-start.5) | collective-permute-done | bytes 163872 | tf_op jit(solution)/shard_map/ppermute | solution.py:455
  23.8 1.4 %collective-permute-done.4 = bf16[4,160,128]{2,1,0:T(8,128)(2,1)S(1)} collective-permute-done((bf16[4,160,128]{2,1,0:T(8,128)(2,1)S(1)}, bf16[4,160,128]{2,1,0:T(8,128)(2,1)S(1)}, u32[]{:S(2)}, u32[]{:S(2)}) %collective-permute-start.4) | collective-permute-done | bytes 163872 | tf_op jit(solution)/shard_map/ppermute | solution.py:455
  25.2 0.1 pad_maximum_fusion.mine_ref
  25.3 0.0 copy-start.2
  25.3 0.0 copy-start.6
  25.3 0.1 collective-permute-start.6
  25.4 0.6 %early.1.early_ref = f32[2,128,128]{2,1,0:T(8,128)S(1)} custom-call(bf16[4,4,160,128]{3,2,1,0:T(8,128)(2,1)S(1)} %pad_maximum_fusion.mine_ref, bf16[2,128,256]{2,1,0:T(8,128)(2,1)S(1)} %get-tuple-element.15.q.q0, bf16[2,4,256,32]{3,2,1,0:T(8,128)(2,1)S(1)} %get-tuple-element.16.k.k0, bf16[2,128,256]{2,1,0:T(8,128)(2,1)S(1)} %get-tuple-element.17.v.v0), custom_call_target="tpu_custom_call" | custom-call | flops 67108864 | bytes 2097152 | tf_op jit(solution)/shard_map/early/pallas_call | solution.py:356
  26.0 1.5 %collective-permute-done.6.other_ref = bf16[4,4,160,128]{3,2,1,0:T(8,128)(2,1)S(1)} collective-permute-done((bf16[4,4,160,128]{3,2,1,0:T(8,128)(2,1)S(1)}, bf16[4,4,160,128]{3,2,1,0:T(8,128)(2,1)S(1)}, u32[]{:S(2)}, u32[]{:S(2)}) %collective-permute-start.6) | collective-permute-done | bytes 655392 | tf_op jit(solution)/shard_map/ppermute | solution.py:455
  27.5 2.8 %attend.1 = (bf16[2,256,128]{2,1,0:T(8,128)(2,1)}, bf16[2,256,128]{2,1,0:T(8,128)(2,1)}) custom-call(bf16[4,4,160,128]{3,2,1,0:T(8,128)(2,1)S(1)} %pad_maximum_fusion.mine_ref, bf16[4,4,160,128]{3,2,1,0:T(8,128)(2,1)S(1)} %collective-permute-done.6.other_ref, f32[2,128,128]{2,1,0:T(8,128)S(1)} %early.1.early_ref, ...), custom_call_target="tpu_custom_call" | custom-call | tf_op jit(solution)/shard_map/attend/pallas_call | solution.py:428
  (15 shorter events, 0.1 us)
Async XLA Ops:
  0.6 9.9 %copy-start = (bf16[8,256,128]{2,1,0:T(8,128)(2,1)S(1)}, bf16[8,256,128]{2,1,0:T(8,128)(2,1)}, u32[]{:S(2)}) copy-start(bf16[8,256,128]{2,1,0:T(8,128)(2,1)} %lines_ref.1) | copy-start | bytes 1572868
  3.5 8.6 %collective-permute-start = (bf16[256,128]{1,0:T(8,128)(2,1)}, bf16[256,128]{1,0:T(8,128)(2,1)S(1)}, u32[]{:S(2)}, u32[]{:S(2)}) collective-permute-start(bf16[256,128]{1,0:T(8,128)(2,1)} %get-tuple-element.12), channel_id=1, source_target_pairs={{0,8},{8,16},{16,24},{24,0},{1,9},{9,17},{17,25},{25,1},{2,10},{10... | collective-permute-start | bytes 196616 | tf_op jit(solution)/shard_map/ppermute | solution.py:452
  6.6 3.9 %copy-start.4 = (f32[2,128]{1,0:T(2,128)S(1)}, f32[2,128]{1,0:T(2,128)}, u32[]{:S(2)}) copy-start(f32[2,128]{1,0:T(2,128)} %shift_ref.3) | copy-start | bytes 3076
  6.6 4.0 %copy-start.5 = (f32[2,128]{1,0:T(2,128)S(1)}, f32[2,128]{1,0:T(2,128)}, u32[]{:S(2)}) copy-start(f32[2,128]{1,0:T(2,128)} %gate_ref.1) | copy-start | bytes 3076
  6.6 4.0 %copy-start.3 = (f32[2,128]{1,0:T(2,128)S(1)}, f32[2,128]{1,0:T(2,128)}, u32[]{:S(2)}) copy-start(f32[2,128]{1,0:T(2,128)} %gain_ref.3) | copy-start | bytes 3076
  6.6 7.3 %collective-permute-start.1 = (bf16[256,128]{1,0:T(8,128)(2,1)}, bf16[256,128]{1,0:T(8,128)(2,1)S(1)}, u32[]{:S(2)}, u32[]{:S(2)}) collective-permute-start(bf16[256,128]{1,0:T(8,128)(2,1)} %get-tuple-element.13), channel_id=1, source_target_pairs={{0,16},{8,24},{16,0},{24,8},{1,17},{9,25},{17,1},{25,9},{2,18},{10... | collective-permute-start | bytes 196616 | tf_op jit(solution)/shard_map/ppermute | solution.py:452
  9.2 4.9 %collective-permute-start.2 = (bf16[256,128]{1,0:T(8,128)(2,1)}, bf16[256,128]{1,0:T(8,128)(2,1)S(1)}, u32[]{:S(2)}, u32[]{:S(2)}) collective-permute-start(bf16[256,128]{1,0:T(8,128)(2,1)} %get-tuple-element.14), channel_id=1, source_target_pairs={{0,24},{8,0},{16,8},{24,16},{1,25},{9,1},{17,9},{25,17},{2,26},{10... | collective-permute-start | bytes 196616 | tf_op jit(solution)/shard_map/ppermute | solution.py:452
  10.5 1.0 %copy-start.1 = (bf16[2,128,512]{2,1,0:T(8,128)(2,1)S(1)}, bf16[2,128,512]{2,1,0:T(8,128)(2,1)}, u32[]{:S(2)}) copy-start(bf16[2,128,512]{2,1,0:T(8,128)(2,1)} %proj_ref.1) | copy-start | bytes 786436
  11.5 2.6 %copy-start.7 = (bf16[256,128]{1,0:T(8,128)(2,1)S(1)}, bf16[256,128]{1,0:T(8,128)(2,1)}, u32[]{:S(2)}) copy-start(bf16[256,128]{1,0:T(8,128)(2,1)} %get-tuple-element.11) | copy-start | bytes 196612
  14.2 7.2 %collective-permute-start.3 = (bf16[4,160,128]{2,1,0:T(8,128)(2,1)S(1)}, bf16[4,160,128]{2,1,0:T(8,128)(2,1)S(1)}, u32[]{:S(2)}, u32[]{:S(2)}) collective-permute-start(bf16[4,160,128]{2,1,0:T(8,128)(2,1)S(1)} %get-tuple-element.20), channel_id=1, source_target_pairs={{0,2},{1,3},{2,0},{3,1},{4,6},{5,7},{6,4},{7,5},{8,10},{9,11},{10,... | collective-permute-start | bytes 491528 | tf_op jit(solution)/shard_map/ppermute | solution.py:455
  15.8 8.0 %collective-permute-start.5 = (bf16[4,160,128]{2,1,0:T(8,128)(2,1)S(1)}, bf16[4,160,128]{2,1,0:T(8,128)(2,1)S(1)}, u32[]{:S(2)}, u32[]{:S(2)}) collective-permute-start(bf16[4,160,128]{2,1,0:T(8,128)(2,1)S(1)} %get-tuple-element.21), channel_id=1, source_target_pairs={{0,6},{1,7},{2,4},{3,5},{4,2},{5,3},{6,0},{7,1},{8,14},{9,15},{10,... | collective-permute-start | bytes 491528 | tf_op jit(solution)/shard_map/ppermute | solution.py:455
  17.3 7.9 %collective-permute-start.4 = (bf16[4,160,128]{2,1,0:T(8,128)(2,1)S(1)}, bf16[4,160,128]{2,1,0:T(8,128)(2,1)S(1)}, u32[]{:S(2)}, u32[]{:S(2)}) collective-permute-start(bf16[4,160,128]{2,1,0:T(8,128)(2,1)S(1)} %get-tuple-element.22), channel_id=1, source_target_pairs={{0,4},{1,5},{2,6},{3,7},{4,0},{5,1},{6,2},{7,3},{8,12},{9,13},{10,... | collective-permute-start | bytes 491528 | tf_op jit(solution)/shard_map/ppermute | solution.py:455
  25.3 2.2 %copy-start.2 = (bf16[2,128,128]{2,1,0:T(8,128)(2,1)S(1)}, bf16[2,128,128]{2,1,0:T(8,128)(2,1)}, u32[]{:S(2)}) copy-start(bf16[2,128,128]{2,1,0:T(8,128)(2,1)} %weight_ref.3) | copy-start | bytes 196612
  25.3 2.2 %copy-start.6 = (f32[2,128]{1,0:T(2,128)S(1)}, f32[2,128]{1,0:T(2,128)}, u32[]{:S(2)}) copy-start(f32[2,128]{1,0:T(2,128)} %offset_ref.3) | copy-start | bytes 3076
  25.3 2.2 %collective-permute-start.6 = (bf16[4,4,160,128]{3,2,1,0:T(8,128)(2,1)S(1)}, bf16[4,4,160,128]{3,2,1,0:T(8,128)(2,1)S(1)}, u32[]{:S(2)}, u32[]{:S(2)}) collective-permute-start(bf16[4,4,160,128]{3,2,1,0:T(8,128)(2,1)S(1)} %pad_maximum_fusion.mine_ref), channel_id=1, source_target_pairs={{0,1},{1,0},{2,3},{3,2},{4,5},{5,4},{6,7},{7,6},{8,9},{9,8},{10,11... | collective-permute-start | bytes 1966088 | tf_op jit(solution)/shard_map/ppermute | solution.py:455

commit v7 on v6

--- a/solution.py
+++ b/solution.py
@@ -50,11 +50,11 @@
 
 
 def bias_kernel(along, chips, pair_hbm, live_hbm, gain_hbm, shift_hbm, weight_hbm, *rest):
-    outs = rest[:along]
-    pair, live_row, live_each, gain, shift, weight, blocks, rows_out, wide, picked, sems, pair_sems = rest[along:]
+    out, owned = rest[0], rest[1 : along + 1]
+    pair, live_row, live_each, gain, shift, weight, blocks, rows_out, wide, picked, sems, pair_sems = rest[along + 1 :]
     rows, length, channels = pair.shape
     heads = weight.shape[1]
-    lanes = outs[0].shape[1]
+    lanes = out.shape[1]
     small = [
         pltpu.make_async_copy(source, target, sems.at[i])
         for i, (source, target) in enumerate(
@@ -88,39 +88,37 @@
         for z in lines
     ]
     biases = [contract(paired, line, 1, 1) for line in normed]
+    devices = length // rows
+    for a in range(rows):
+        for w in range(WD):
+            column = wide[a, pl.ds(w, devices, stride=rows), :]
+            picked[pl.ds(w * rows + a, devices, stride=WD * rows), :] = column
     for a, bias in enumerate(biases):
         kept = jnp.where(first, live, live_each[0, device * rows + a])
         bias = jnp.where(kept > 0, bias, MASKED)
         for lane in range(length // lanes):
             part = bias[:, lane * lanes : (lane + 1) * lanes]
             rows_out[pl.ds(2 * lane * heads * rows + a, 2 * heads, stride=rows), :] = part
-    devices = length // rows
-    for a in range(rows):
-        for w in range(WD):
-            column = wide[a, pl.ds(w, devices, stride=rows), :]
-            picked[pl.ds(w * rows + a, devices, stride=WD * rows), :] = column
+    out[...] = rows_out[...].astype(jnp.bfloat16)
     chip = lax.div(lax.axis_index("col"), 2)
     both = 2 * WD * rows
-    packed = rows_out.shape[0]
-    sent = rows_out[...].astype(jnp.bfloat16)
-    for shift_by, out in enumerate(outs):
-        out[:packed] = sent
+    for shift_by, pick in enumerate(owned):
         row = lax.rem(lax.axis_index("row") + shift_by, along)
         for flip in range(chips):
             at = pl.multiple_of((row * chips + flipped(chip, flip)) * both, both)
-            out[packed + flip * both : packed + (flip + 1) * both] = picked[pl.ds(at, both), :].astype(jnp.bfloat16)
+            pick[flip] = picked[pl.ds(at, both), :].astype(jnp.bfloat16)
 
 
 def local_bias(pair, live, gain, shift, weight, along, chips):
     rows, length, channels = pair.shape
     heads = weight.shape[1]
     packed = 2 * heads * rows * (length // channels)
-    sent = jax.ShapeDtypeStruct((packed + chips * 2 * WD * rows, channels), jnp.bfloat16)
-    return pl.pallas_call(
+    owned = jax.ShapeDtypeStruct((chips, 2 * WD * rows, channels), jnp.bfloat16)
+    out = pl.pallas_call(
         functools.partial(bias_kernel, along, chips),
-        out_shape=(sent,) * along,
+        out_shape=(jax.ShapeDtypeStruct((packed, channels), jnp.bfloat16),) + (owned,) * along,
         in_specs=[HBM] * 5,
-        out_specs=(VMEM,) * along,
+        out_specs=(VMEM,) * (along + 1),
         scratch_shapes=[
             pltpu.VMEM(pair.shape, pair.dtype),
             pltpu.VMEM(live.shape, live.dtype),
@@ -138,6 +136,7 @@
         compiler_params=params(60),
         name="bias",
     )(pair, live, gain, shift, weight)
+    return out[0], out[1:]
 
 
 def turned(row):
@@ -347,14 +346,14 @@
     return []
 
 
-def early_kernel(mine_ref, q, k, v, mixed, bias):
-    attend_groups(start_half(mine_ref, 0, q, k, v, mixed, bias))
-
-
-def attend_early(mine, q, k, v):
+def half_kernel(other, source_ref, q, k, v, mixed, bias):
+    attend_groups(start_half(source_ref, other, q, k, v, mixed, bias))
+
+
+def attend_half(source, other, q, k, v):
     _, heads, length, size = k.shape
     return pl.pallas_call(
-        early_kernel,
+        functools.partial(half_kernel, other),
         out_shape=jax.ShapeDtypeStruct((WD, heads * size, length // 2), jnp.float32),
         in_specs=[VMEM] * 4,
         out_specs=VMEM,
@@ -365,24 +364,23 @@
             bytes_accessed=4 * WD * heads * length * length,
             transcendentals=WD * heads * length * length // 2,
         ),
-        name="early",
-    )(mine, q, k, v)
+        name="half",
+    )(source, q, k, v)
 
 
 def attend_kernel(
-    mine_ref, other_ref, early_ref, q0, k0, v0, g0,
+    mine_ref, other_ref, near_ref, far_ref, early_ref, late_ref, g0,
     gain_ref, shift_ref, proj_ref, gate_ref, weight_ref, offset_ref,
-    out0, out1, turned_bias, bias, late, mixed, q1, k1, v1, g1,
+    out0, out1, bias, mixed, q1, k1, v1, g1,
 ):
     chips, along, _, _ = mine_ref.shape
-    _, heads, length, size = k0.shape
+    _, heads, length, size = k1.shape
     half = length // 2
     rows = half // (chips * along)
-    packed = 2 * heads * rows * (length // mine_ref.shape[3])
-    first = pl.multiple_of(packed + lax.rem(lax.axis_index("col"), 2) * WD * rows, WD * rows)
+    first = pl.multiple_of(lax.rem(lax.axis_index("col"), 2) * WD * rows, WD * rows)
     offset = turned(gate_ref[1:2, :])
     blocks = []
-    for source in (mine_ref, other_ref):
+    for source in (near_ref, far_ref):
         for flip in range(chips):
             for shift in range(along):
                 both = source[flip, shift, pl.ds(first, WD * rows), :].astype(jnp.float32)
@@ -392,7 +390,7 @@
     keys_and_values([line.astype(jnp.bfloat16) for line in lines], proj_ref[1], k1, v1)
     ordered = [to_devices(line, along, chips, rows).astype(jnp.bfloat16) for line in lines]
     queries_and_gates(ordered, size ** (-0.5), proj_ref[1], offset, q1, g1)
-    groups = start_half(other_ref, 1, q0, k0, v0, late, turned_bias)
+    groups = []
     for pack in range(heads // 2):
         unpack(mine_ref, 1, pack, rows, heads, 0, bias, 0)
         unpack(other_ref, 1, pack, rows, heads, 0, bias, half)
@@ -411,7 +409,7 @@
         for_each(length // CHUNK, step, False)
     attend_groups(groups)
     for w in range(WD):
-        gated = (jnp.concatenate([early_ref[w], late[w]], 1) * g0[w]).astype(jnp.bfloat16)
+        gated = (jnp.concatenate([early_ref[w], late_ref[w]], 1) * g0[w]).astype(jnp.bfloat16)
         full = contract(gated, weight_ref[0], 0, 0) + offset_ref[0:1, :]
         out0[w] = to_devices(full, along, chips, rows).astype(jnp.bfloat16)
     for w in range(WD):
@@ -420,7 +418,7 @@
         out1[w] = full.astype(jnp.bfloat16)
 
 
-def attend(mine, other, early, start, gain, shift, proj, gate, weight, offset):
+def attend(mine, other, near, far, early, late, start, gain, shift, proj, gate, weight, offset):
     _, heads, length, size = start[1].shape
     inner, channels = weight.shape[1:]
     result = jax.ShapeDtypeStruct((WD, length, channels), jnp.bfloat16)
@@ -431,15 +429,13 @@
         in_specs=[VMEM] * 13,
         out_specs=(VMEM, VMEM),
         scratch_shapes=[
-            pltpu.VMEM((slots, length, length // 2), jnp.float32),
             pltpu.VMEM((slots, length, length), jnp.float32),
-            pltpu.VMEM((WD, inner, length // 2), jnp.float32),
             pltpu.VMEM((WD, inner, length), jnp.float32),
         ]
         + [pltpu.VMEM(shape, dtype) for shape, dtype in projected(length, inner, heads)],
         compiler_params=params(16 if length <= CHUNK else 60),
         name="attend",
-    )(mine, other, early, *start, gain, shift, proj, gate, weight, offset)
+    )(mine, other, near, far, early, late, start[3], gain, shift, proj, gate, weight, offset)
 
 
 def body(pair, residue_mask, ln_gain, ln_shift, w_proj, w_bias, gate_bias, w_out, out_bias):
@@ -454,23 +450,24 @@
     def by_col(block, flip):
         return lax.ppermute(block, "col", [(i, i ^ flip) for i in range(cols)])
 
-    sent = local_bias(
+    block, owned = local_bias(
         pair, residue_mask[None, :], ln_gain, ln_shift, jnp.transpose(w_bias, (0, 2, 1)), along, chips
     )
-    line = jnp.stack([sent[0]] + [by_row(sent[shift], shift) for shift in range(1, along)])
+    line = jnp.stack([block] + [by_row(block, shift) for shift in range(1, along)])
     start = local_lines(pair, ln_gain, ln_shift, w_proj, gate_bias, heads, along, chips)
-    packed = 2 * heads * rows * (length // channels)
-    both = 2 * WD * rows
-
-    def owned_by(flip):
-        at = packed + flip * both
-        return jnp.concatenate([line[:, :packed], line[:, at : at + both]], 1)
-
-    mine = jnp.stack([owned_by(0)] + [by_col(owned_by(flip), 2 * flip) for flip in range(1, chips)])
+    owned, _ = lax.optimization_barrier((owned, line))
+    owned = jnp.stack([owned[0]] + [by_row(owned[shift], shift) for shift in range(1, along)], 1)
+    mine = jnp.stack([line] + [by_col(line, 2 * flip) for flip in range(1, chips)])
     mine, _ = lax.optimization_barrier((mine, start))
     other = by_col(mine, 1)
-    early = attend_early(mine, *start[:3])
-    return attend(mine, other, early, start, ln_gain, ln_shift, w_proj, gate_bias, w_out, out_bias)
+    early = attend_half(mine, 0, *start[:3])
+    owned, early = lax.optimization_barrier((owned, early))
+    near = jnp.stack([owned[0]] + [by_col(owned[flip], 2 * flip) for flip in range(1, chips)])
+    late = attend_half(other, 1, *start[:3])
+    far = by_col(near, 1)
+    return attend(
+        mine, other, near, far, early, late, start, ln_gain, ln_shift, w_proj, gate_bias, w_out, out_bias
+    )
 
 
 def solution(mesh):

time: 30.4 us -> 37.5 us (1.23)
  starting transfers between devices: 10.6 us -> 15.6 us
  waiting for transfers between devices: 10.9 us -> 12.9 us
  local copies, waits for them, and re-layouts: 1 us -> 0.07 us
  other arithmetic: 0.18 us -> 0.92 us
    ppermute x3 -> x6, waiting for transfers between devices: 2.01 us -> 7.69 us  [by_row(): lax.ppermute(block, 'row', [(i, (i + shift) % along) for i in range(along)])]
    ppermute x4 -> x8, starting transfers between devices: 3.62 us -> 7.25 us  [by_col(): return lax.ppermute(block, 'col', [(i, i ^ flip) for i in range(cols)])]
    ppermute x4 -> x8, waiting for transfers between devices: 8.85 us -> 5.24 us  [by_col(): return lax.ppermute(block, 'col', [(i, i ^ flip) for i in range(cols)])]
    ppermute x3 -> x6, starting transfers between devices: 7.01 us -> 8.32 us  [by_row(): lax.ppermute(block, 'row', [(i, (i + shift) % along) for i in range(along)])]
    unnamed x16 -> x22, local copies, waits for them, and re-layouts: 0.98 us -> 0.05 us
    another operation x2 -> x4, other arithmetic: 0.12 us -> 0.92 us  [the longest x2 0.88 us: body(): jnp.stack([line] + [by_col(line, 2 * flip) for flip in range(1, chips)])]
    pallas_call x2 -> x3, Pallas kernels: 3.46 us -> 4.01 us  [the longest x1 2.77 us: local_bias(): pl.pallas_call(functools.partial(bias_kernel, along, chips), out_shape=(j...]
  transfers between devices with their start and end apart: 7 -> 14, of which waited for: 6 -> 10; matrix products, arithmetic and copies ran while one was open for 0% -> 0% of each run, Pallas kernels for 4% -> 5%
where the time goes in v7:
time: 37.5 us; the launch traced here: 37.3 us
  starting transfers between devices  15.6 us (42%)
  waiting for transfers between devices  12.9 us (34%)
  Pallas kernels  7.02 us (19%)
  other arithmetic  0.92 us (2%)
  between operations  0.83 us (2%)
    ppermute x6, starting transfers between devices, by_row(): lax.ppermute(block, 'row', [(i, (i + shift) % along) for i in range(along)])  8.32 us
    ppermute x6, waiting for transfers between devices, by_row(): lax.ppermute(block, 'row', [(i, (i + shift) % along) for i in range(along)])  7.69 us
    ppermute x8, starting transfers between devices, by_col(): return lax.ppermute(block, 'col', [(i, i ^ flip) for i in range(cols)])  7.25 us
    ppermute x8, waiting for transfers between devices, by_col(): return lax.ppermute(block, 'col', [(i, i ^ flip) for i in range(cols)])  5.24 us
    pallas_call x1, Pallas kernels, local_bias(): pl.pallas_call(functools.partial(bias_kernel, along, chips), out_shape=(j...  2.77 us
    pallas_call x1, Pallas kernels, attend(): pl.pallas_call(attend_kernel, out_shape=(result, result), in_specs=[VMEM]...  2.41 us
    pallas_call x2, Pallas kernels, attend_half(): pl.pallas_call(functools.partial(half_kernel, other), out_shape=jax.Shape...  1.25 us
    another operation x2, other arithmetic, body(): jnp.stack([line] + [by_col(line, 2 * flip) for flip in range(1, chips)])  0.88 us
  transfers between devices with their start and end apart: 14, of which 10 were waited for; matrix products, arithmetic and copies ran while one was open for 0% of the time, Pallas kernels for 5%

profile of v7, /device:TPU:0, one launch (start us, length us, event | category | flops | bytes accessed | tf_op | source)
XLA Modules:
  0.0 37.3 jit_solution(10436528842143594094)
XLA Ops:
  0.6 2.8 %bias.1 = (bf16[128,128]{1,0:T(8,128)(2,1)}, bf16[4,32,128]{2,1,0:T(8,128)(2,1)}, bf16[4,32,128]{2,1,0:T(8,128)(2,1)}, bf16[4,32,128]{2,1,0:T(8,128)(2,1)}, bf16[4,32,128]{2,1,0:T(8,128)(2,1)}) custom-call(bf16[8,256,128]{2,1,0:T(8,128)(2,1)} %lines_ref.1, s32[1,256]{1,0:T(1,128)} %bitcast.39, f32[2,128]{1,0:T(2,128)} %gain_ref.3, f32[2,128]{1,0:T(2,128)} %shift_ref.3, ...), custom_call_target="tpu_custom_call" | custom-call | tf_op jit(solution)/shard_map/bias/pallas_call | solution.py:117
  3.4 5.1 %collective-permute-start.2 = (bf16[128,128]{1,0:T(8,128)(2,1)}, bf16[128,128]{1,0:T(8,128)(2,1)S(1)}, u32[]{:S(2)}, u32[]{:S(2)}) collective-permute-start(bf16[128,128]{1,0:T(8,128)(2,1)} %get-tuple-element.18), channel_id=1, source_target_pairs={{0,24},{8,0},{16,8},{24,16},{1,25},{9,1},{17,9},{25,17},{2,26},{10... | collective-permute-start | bytes 98312 | tf_op jit(solution)/shard_map/ppermute | solution.py:448
  8.5 1.0 %collective-permute-start = (bf16[128,128]{1,0:T(8,128)(2,1)}, bf16[128,128]{1,0:T(8,128)(2,1)S(1)}, u32[]{:S(2)}, u32[]{:S(2)}) collective-permute-start(bf16[128,128]{1,0:T(8,128)(2,1)} %get-tuple-element.18), channel_id=1, source_target_pairs={{0,8},{8,16},{16,24},{24,0},{1,9},{9,17},{17,25},{25,1},{2,10},{10... | collective-permute-start | bytes 98312 | tf_op jit(solution)/shard_map/ppermute | solution.py:448
  9.5 0.9 %collective-permute-done.2 = bf16[128,128]{1,0:T(8,128)(2,1)S(1)} collective-permute-done((bf16[128,128]{1,0:T(8,128)(2,1)}, bf16[128,128]{1,0:T(8,128)(2,1)S(1)}, u32[]{:S(2)}, u32[]{:S(2)}) %collective-permute-start.2) | collective-permute-done | bytes 32800 | tf_op jit(solution)/shard_map/ppermute | solution.py:448
  10.4 3.1 %collective-permute-done.1 = bf16[128,128]{1,0:T(8,128)(2,1)S(1)} collective-permute-done((bf16[128,128]{1,0:T(8,128)(2,1)}, bf16[128,128]{1,0:T(8,128)(2,1)S(1)}, u32[]{:S(2)}, u32[]{:S(2)}) %collective-permute-start.1) | collective-permute-done | bytes 32800 | tf_op jit(solution)/shard_map/ppermute | solution.py:448
  13.6 0.9 %collective-permute-done = bf16[128,128]{1,0:T(8,128)(2,1)S(1)} collective-permute-done((bf16[128,128]{1,0:T(8,128)(2,1)}, bf16[128,128]{1,0:T(8,128)(2,1)S(1)}, u32[]{:S(2)}, u32[]{:S(2)}) %collective-permute-start) | collective-permute-done | bytes 32800 | tf_op jit(solution)/shard_map/ppermute | solution.py:448
  14.5 0.8 %fusion = (bf16[1,4,128,128]{3,2,1,0:T(8,128)(2,1)S(1)}, bf16[4,128,128]{2,1,0:T(8,128)(2,1)S(1)}) fusion(bf16[1,128,128]{2,1,0:T(8,128)(2,1)S(1)} %bitcast.28, bf16[1,128,128]{2,1,0:T(8,128)(2,1)S(1)} %bitcast.29, bf16[1,128,128]{2,1,0:T(8,128)(2,1)S(1)} %bitcast.30, bf16[1,128,128]{2,1,0:T(8,128)(2,1)} %bitcast.27), kind=kLoop, calls=%fused_computation.7 | loop fusion | flops 196608 | bytes 393216 | tf_op jit(solution)/shard_map/stack | solution.py:460
  15.3 2.5 %collective-permute-start.5 = (bf16[4,128,128]{2,1,0:T(8,128)(2,1)S(1)}, bf16[4,128,128]{2,1,0:T(8,128)(2,1)S(1)}, u32[]{:S(2)}, u32[]{:S(2)}) collective-permute-start(bf16[4,128,128]{2,1,0:T(8,128)(2,1)S(1)} %get-tuple-element.39), channel_id=1, source_target_pairs={{0,6},{1,7},{2,4},{3,5},{4,2},{5,3},{6,0},{7,1},{8,14},{9,15},{10,... | collective-permute-start | bytes 393224 | tf_op jit(solution)/shard_map/ppermute | solution.py:451
  18.3 0.5 %collective-permute-start.3 = (bf16[4,128,128]{2,1,0:T(8,128)(2,1)S(1)}, bf16[4,128,128]{2,1,0:T(8,128)(2,1)S(1)}, u32[]{:S(2)}, u32[]{:S(2)}) collective-permute-start(bf16[4,128,128]{2,1,0:T(8,128)(2,1)S(1)} %get-tuple-element.39), channel_id=1, source_target_pairs={{0,2},{1,3},{2,0},{3,1},{4,6},{5,7},{6,4},{7,5},{8,10},{9,11},{10,... | collective-permute-start | bytes 393224 | tf_op jit(solution)/shard_map/ppermute | solution.py:451
  18.9 0.6 %lines.1 = (bf16[2,128,256]{2,1,0:T(8,128)(2,1)S(1)}, bf16[2,4,256,32]{3,2,1,0:T(8,128)(2,1)S(1)}, bf16[2,128,256]{2,1,0:T(8,128)(2,1)S(1)}, f32[2,128,256]{2,1,0:T(8,128)S(1)}) custom-call(bf16[8,256,128]{2,1,0:T(8,128)(2,1)S(1)} %copy-done, f32[2,128]{1,0:T(2,128)S(1)} %copy-done.3, f32[2,128]{1,0:T(2,128)S(1)} %copy-done.4, ...), custom_call_target="tpu_custom_call" | custom-call | flops 67108864 | bytes 1048576 | tf_op jit(solution)/shard_map/lines/pallas_call | solution.py:242
  19.6 1.2 %collective-permute-start.8 = (bf16[4,32,128]{2,1,0:T(8,128)(2,1)S(1)}, bf16[4,32,128]{2,1,0:T(8,128)(2,1)S(1)}, u32[]{:S(2)}, u32[]{:S(2)}) collective-permute-start(bf16[4,32,128]{2,1,0:T(8,128)(2,1)S(1)} %copy-done.9), channel_id=1, source_target_pairs={{0,16},{8,24},{16,0},{24,8},{1,17},{9,25},{17,1},{25,9},{2,18},{10... | collective-permute-start | bytes 98312 | tf_op jit(solution)/shard_map/ppermute | solution.py:448
  20.8 1.9 %collective-permute-done.5 = bf16[4,128,128]{2,1,0:T(8,128)(2,1)S(1)} collective-permute-done((bf16[4,128,128]{2,1,0:T(8,128)(2,1)S(1)}, bf16[4,128,128]{2,1,0:T(8,128)(2,1)S(1)}, u32[]{:S(2)}, u32[]{:S(2)}) %collective-permute-start.5) | collective-permute-done | bytes 131104 | tf_op jit(solution)/shard_map/ppermute | solution.py:451
  22.6 1.0 %collective-permute-start.9 = (bf16[4,32,128]{2,1,0:T(8,128)(2,1)S(1)}, bf16[4,32,128]{2,1,0:T(8,128)(2,1)S(1)}, u32[]{:S(2)}, u32[]{:S(2)}) collective-permute-start(bf16[4,32,128]{2,1,0:T(8,128)(2,1)S(1)} %copy-done.8), channel_id=1, source_target_pairs={{0,24},{8,0},{16,8},{24,16},{1,25},{9,1},{17,9},{25,17},{2,26},{10... | collective-permute-start | bytes 98312 | tf_op jit(solution)/shard_map/ppermute | solution.py:448
  23.8 1.5 %collective-permute-done.7 = bf16[4,32,128]{2,1,0:T(8,128)(2,1)S(1)} collective-permute-done((bf16[4,32,128]{2,1,0:T(8,128)(2,1)S(1)}, bf16[4,32,128]{2,1,0:T(8,128)(2,1)S(1)}, u32[]{:S(2)}, u32[]{:S(2)}) %collective-permute-start.7) | collective-permute-done | bytes 32800 | tf_op jit(solution)/shard_map/ppermute | solution.py:448
  25.3 1.3 %collective-permute-done.9 = bf16[4,32,128]{2,1,0:T(8,128)(2,1)S(1)} collective-permute-done((bf16[4,32,128]{2,1,0:T(8,128)(2,1)S(1)}, bf16[4,32,128]{2,1,0:T(8,128)(2,1)S(1)}, u32[]{:S(2)}, u32[]{:S(2)}) %collective-permute-start.9) | collective-permute-done | bytes 32800 | tf_op jit(solution)/shard_map/ppermute | solution.py:448
  26.6 0.6 %half.2.early_ref = f32[2,128,128]{2,1,0:T(8,128)S(1)} custom-call(bf16[4,4,128,128]{3,2,1,0:T(8,128)(2,1)S(1)} %pad_maximum_fusion.source_ref.mine_ref, bf16[2,128,256]{2,1,0:T(8,128)(2,1)S(1)} %get-tuple-element.19.q, bf16[2,4,256,32]{3,2,1,0:T(8,128)(2,1)S(1)} %get-tuple-element.20.k, bf16[2,128,256]{2,1,0:T(8,128)(2,1)S(1)} %get-tuple-element.21.v), custom_call_target="tpu_custom_call" | custom-call | flops 67108864 | bytes 2097152 | tf_op jit(solution)/shard_map/half/pallas_call | solution.py:355
  27.2 1.8 %collective-permute-start.12 = (bf16[4,32,128]{2,1,0:T(8,128)(2,1)S(1)}, bf16[4,32,128]{2,1,0:T(8,128)(2,1)S(1)}, u32[]{:S(2)}, u32[]{:S(2)}) collective-permute-start(bf16[4,32,128]{2,1,0:T(8,128)(2,1)S(1)} %get-tuple-element.35), channel_id=1, source_target_pairs={{0,6},{1,7},{2,4},{3,5},{4,2},{5,3},{6,0},{7,1},{8,14},{9,15},{10,... | collective-permute-start | bytes 98312 | tf_op jit(solution)/shard_map/ppermute | solution.py:451
  29.0 0.5 %collective-permute-start.11 = (bf16[4,32,128]{2,1,0:T(8,128)(2,1)S(1)}, bf16[4,32,128]{2,1,0:T(8,128)(2,1)S(1)}, u32[]{:S(2)}, u32[]{:S(2)}) collective-permute-start(bf16[4,32,128]{2,1,0:T(8,128)(2,1)S(1)} %get-tuple-element.36), channel_id=1, source_target_pairs={{0,4},{1,5},{2,6},{3,7},{4,0},{5,1},{6,2},{7,3},{8,12},{9,13},{10,... | collective-permute-start | bytes 98312 | tf_op jit(solution)/shard_map/ppermute | solution.py:451
  29.5 1.3 %collective-permute-start.10 = (bf16[4,32,128]{2,1,0:T(8,128)(2,1)S(1)}, bf16[4,32,128]{2,1,0:T(8,128)(2,1)S(1)}, u32[]{:S(2)}, u32[]{:S(2)}) collective-permute-start(bf16[4,32,128]{2,1,0:T(8,128)(2,1)S(1)} %get-tuple-element.37), channel_id=1, source_target_pairs={{0,2},{1,3},{2,0},{3,1},{4,6},{5,7},{6,4},{7,5},{8,10},{9,11},{10,... | collective-permute-start | bytes 98312 | tf_op jit(solution)/shard_map/ppermute | solution.py:451
  30.8 1.3 %collective-permute-done.12 = bf16[4,32,128]{2,1,0:T(8,128)(2,1)S(1)} collective-permute-done((bf16[4,32,128]{2,1,0:T(8,128)(2,1)S(1)}, bf16[4,32,128]{2,1,0:T(8,128)(2,1)S(1)}, u32[]{:S(2)}, u32[]{:S(2)}) %collective-permute-start.12) | collective-permute-done | bytes 32800 | tf_op jit(solution)/shard_map/ppermute | solution.py:451
  32.1 0.8 %collective-permute-done.11 = bf16[4,32,128]{2,1,0:T(8,128)(2,1)S(1)} collective-permute-done((bf16[4,32,128]{2,1,0:T(8,128)(2,1)S(1)}, bf16[4,32,128]{2,1,0:T(8,128)(2,1)S(1)}, u32[]{:S(2)}, u32[]{:S(2)}) %collective-permute-start.11) | collective-permute-done | bytes 32800 | tf_op jit(solution)/shard_map/ppermute | solution.py:451
  33.6 0.6 %half.3.late_ref = f32[2,128,128]{2,1,0:T(8,128)S(1)} custom-call(bf16[4,4,128,128]{3,2,1,0:T(8,128)(2,1)S(1)} %collective-permute-done.6.source_ref.other_ref, bf16[2,128,256]{2,1,0:T(8,128)(2,1)S(1)} %get-tuple-element.19.q, bf16[2,4,256,32]{3,2,1,0:T(8,128)(2,1)S(1)} %get-tuple-element.20.k, bf16[2,128,256]{2,1,0:T(8,128)(2,1)S(1)} %get-tuple-element.21.v), custom_call_target="tpu_custom_call" | custom-call | flops 67108864 | bytes 2097152 | tf_op jit(solution)/shard_map/half/pallas_call | solution.py:355
  34.2 0.7 %collective-permute-done.13.far_ref = bf16[4,4,32,128]{3,2,1,0:T(8,128)(2,1)S(1)} collective-permute-done((bf16[4,4,32,128]{3,2,1,0:T(8,128)(2,1)S(1)}, bf16[4,4,32,128]{3,2,1,0:T(8,128)(2,1)S(1)}, u32[]{:S(2)}, u32[]{:S(2)}) %collective-permute-start.13) | collective-permute-done | bytes 131104 | tf_op jit(solution)/shard_map/ppermute | solution.py:451
  34.9 2.4 %attend.1 = (bf16[2,256,128]{2,1,0:T(8,128)(2,1)}, bf16[2,256,128]{2,1,0:T(8,128)(2,1)}) custom-call(bf16[4,4,128,128]{3,2,1,0:T(8,128)(2,1)S(1)} %pad_maximum_fusion.source_ref.mine_ref, bf16[4,4,128,128]{3,2,1,0:T(8,128)(2,1)S(1)} %collective-permute-done.6.source_ref.other_ref, bf16[4,4,32,128]{3,2,1,0:T(8,128)(2,1)S(1)} %pad_maximum_fusion.3.near_ref, ...), custom_call_target="tpu_custom_call" | custom-call | tf_op jit(solution)/shard_map/attend/pallas_call | solution.py:426
  (36 shorter events, 1.4 us)
Async XLA Ops:
  0.6 18.2 %copy-start = (bf16[8,256,128]{2,1,0:T(8,128)(2,1)S(1)}, bf16[8,256,128]{2,1,0:T(8,128)(2,1)}, u32[]{:S(2)}) copy-start(bf16[8,256,128]{2,1,0:T(8,128)(2,1)} %lines_ref.1) | copy-start | bytes 1572868
  3.4 15.5 %copy-start.1 = (bf16[2,128,512]{2,1,0:T(8,128)(2,1)S(1)}, bf16[2,128,512]{2,1,0:T(8,128)(2,1)}, u32[]{:S(2)}) copy-start(bf16[2,128,512]{2,1,0:T(8,128)(2,1)} %proj_ref.1) | copy-start | bytes 786436
  3.4 7.0 %collective-permute-start.2 = (bf16[128,128]{1,0:T(8,128)(2,1)}, bf16[128,128]{1,0:T(8,128)(2,1)S(1)}, u32[]{:S(2)}, u32[]{:S(2)}) collective-permute-start(bf16[128,128]{1,0:T(8,128)(2,1)} %get-tuple-element.18), channel_id=1, source_target_pairs={{0,24},{8,0},{16,8},{24,16},{1,25},{9,1},{17,9},{25,17},{2,26},{10... | collective-permute-start | bytes 98312 | tf_op jit(solution)/shard_map/ppermute | solution.py:448
  8.5 5.0 %collective-permute-start.1 = (bf16[128,128]{1,0:T(8,128)(2,1)}, bf16[128,128]{1,0:T(8,128)(2,1)S(1)}, u32[]{:S(2)}, u32[]{:S(2)}) collective-permute-start(bf16[128,128]{1,0:T(8,128)(2,1)} %get-tuple-element.18), channel_id=1, source_target_pairs={{0,16},{8,24},{16,0},{24,8},{1,17},{9,25},{17,1},{25,9},{2,18},{10... | collective-permute-start | bytes 98312 | tf_op jit(solution)/shard_map/ppermute | solution.py:448
  8.5 5.9 %collective-permute-start = (bf16[128,128]{1,0:T(8,128)(2,1)}, bf16[128,128]{1,0:T(8,128)(2,1)S(1)}, u32[]{:S(2)}, u32[]{:S(2)}) collective-permute-start(bf16[128,128]{1,0:T(8,128)(2,1)} %get-tuple-element.18), channel_id=1, source_target_pairs={{0,8},{8,16},{16,24},{24,0},{1,9},{9,17},{17,25},{25,1},{2,10},{10... | collective-permute-start | bytes 98312 | tf_op jit(solution)/shard_map/ppermute | solution.py:448
  14.5 4.4 %copy-start.4 = (f32[2,128]{1,0:T(2,128)S(1)}, f32[2,128]{1,0:T(2,128)}, u32[]{:S(2)}) copy-start(f32[2,128]{1,0:T(2,128)} %shift_ref.3) | copy-start | bytes 3076
  14.5 4.4 %copy-start.5 = (f32[2,128]{1,0:T(2,128)S(1)}, f32[2,128]{1,0:T(2,128)}, u32[]{:S(2)}) copy-start(f32[2,128]{1,0:T(2,128)} %gate_ref.1) | copy-start | bytes 3076
  15.3 3.6 %copy-start.3 = (f32[2,128]{1,0:T(2,128)S(1)}, f32[2,128]{1,0:T(2,128)}, u32[]{:S(2)}) copy-start(f32[2,128]{1,0:T(2,128)} %gain_ref.3) | copy-start | bytes 3076
  15.3 4.2 %copy-start.10 = (bf16[4,32,128]{2,1,0:T(8,128)(2,1)S(1)}, bf16[4,32,128]{2,1,0:T(8,128)(2,1)}, u32[]{:S(2)}) copy-start(bf16[4,32,128]{2,1,0:T(8,128)(2,1)} %get-tuple-element.29) | copy-start | bytes 98308
  15.3 4.3 %copy-start.9 = (bf16[4,32,128]{2,1,0:T(8,128)(2,1)S(1)}, bf16[4,32,128]{2,1,0:T(8,128)(2,1)}, u32[]{:S(2)}) copy-start(bf16[4,32,128]{2,1,0:T(8,128)(2,1)} %get-tuple-element.30) | copy-start | bytes 98308
  15.3 7.3 %copy-start.8 = (bf16[4,32,128]{2,1,0:T(8,128)(2,1)S(1)}, bf16[4,32,128]{2,1,0:T(8,128)(2,1)}, u32[]{:S(2)}) copy-start(bf16[4,32,128]{2,1,0:T(8,128)(2,1)} %get-tuple-element.31) | copy-start | bytes 98308
  15.3 7.3 %collective-permute-start.5 = (bf16[4,128,128]{2,1,0:T(8,128)(2,1)S(1)}, bf16[4,128,128]{2,1,0:T(8,128)(2,1)S(1)}, u32[]{:S(2)}, u32[]{:S(2)}) collective-permute-start(bf16[4,128,128]{2,1,0:T(8,128)(2,1)S(1)} %get-tuple-element.39), channel_id=1, source_target_pairs={{0,6},{1,7},{2,4},{3,5},{4,2},{5,3},{6,0},{7,1},{8,14},{9,15},{10,... | collective-permute-start | bytes 393224 | tf_op jit(solution)/shard_map/ppermute | solution.py:451
  17.8 5.8 %collective-permute-start.4 = (bf16[4,128,128]{2,1,0:T(8,128)(2,1)S(1)}, bf16[4,128,128]{2,1,0:T(8,128)(2,1)S(1)}, u32[]{:S(2)}, u32[]{:S(2)}) collective-permute-start(bf16[4,128,128]{2,1,0:T(8,128)(2,1)S(1)} %get-tuple-element.39), channel_id=1, source_target_pairs={{0,4},{1,5},{2,6},{3,7},{4,0},{5,1},{6,2},{7,3},{8,12},{9,13},{10,... | collective-permute-start | bytes 393224 | tf_op jit(solution)/shard_map/ppermute | solution.py:451
  18.3 5.3 %collective-permute-start.3 = (bf16[4,128,128]{2,1,0:T(8,128)(2,1)S(1)}, bf16[4,128,128]{2,1,0:T(8,128)(2,1)S(1)}, u32[]{:S(2)}, u32[]{:S(2)}) collective-permute-start(bf16[4,128,128]{2,1,0:T(8,128)(2,1)S(1)} %get-tuple-element.39), channel_id=1, source_target_pairs={{0,2},{1,3},{2,0},{3,1},{4,6},{5,7},{6,4},{7,5},{8,10},{9,11},{10,... | collective-permute-start | bytes 393224 | tf_op jit(solution)/shard_map/ppermute | solution.py:451
  19.5 5.8 %collective-permute-start.7 = (bf16[4,32,128]{2,1,0:T(8,128)(2,1)S(1)}, bf16[4,32,128]{2,1,0:T(8,128)(2,1)S(1)}, u32[]{:S(2)}, u32[]{:S(2)}) collective-permute-start(bf16[4,32,128]{2,1,0:T(8,128)(2,1)S(1)} %copy-done.10), channel_id=1, source_target_pairs={{0,8},{8,16},{16,24},{24,0},{1,9},{9,17},{17,25},{25,1},{2,10},{10... | collective-permute-start | bytes 98312 | tf_op jit(solution)/shard_map/ppermute | solution.py:448
  19.6 5.7 %collective-permute-start.8 = (bf16[4,32,128]{2,1,0:T(8,128)(2,1)S(1)}, bf16[4,32,128]{2,1,0:T(8,128)(2,1)S(1)}, u32[]{:S(2)}, u32[]{:S(2)}) collective-permute-start(bf16[4,32,128]{2,1,0:T(8,128)(2,1)S(1)} %copy-done.9), channel_id=1, source_target_pairs={{0,16},{8,24},{16,0},{24,8},{1,17},{9,25},{17,1},{25,9},{2,18},{10... | collective-permute-start | bytes 98312 | tf_op jit(solution)/shard_map/ppermute | solution.py:448
  22.6 3.9 %collective-permute-start.9 = (bf16[4,32,128]{2,1,0:T(8,128)(2,1)S(1)}, bf16[4,32,128]{2,1,0:T(8,128)(2,1)S(1)}, u32[]{:S(2)}, u32[]{:S(2)}) collective-permute-start(bf16[4,32,128]{2,1,0:T(8,128)(2,1)S(1)} %copy-done.8), channel_id=1, source_target_pairs={{0,24},{8,0},{16,8},{24,16},{1,25},{9,1},{17,9},{25,17},{2,26},{10... | collective-permute-start | bytes 98312 | tf_op jit(solution)/shard_map/ppermute | solution.py:448
  23.6 2.9 %copy-start.7 = (bf16[4,32,128]{2,1,0:T(8,128)(2,1)S(1)}, bf16[4,32,128]{2,1,0:T(8,128)(2,1)}, u32[]{:S(2)}) copy-start(bf16[4,32,128]{2,1,0:T(8,128)(2,1)} %get-tuple-element.28) | copy-start | bytes 98308
  23.7 9.9 %collective-permute-start.6 = (bf16[4,4,128,128]{3,2,1,0:T(8,128)(2,1)S(1)}, bf16[4,4,128,128]{3,2,1,0:T(8,128)(2,1)S(1)}, u32[]{:S(2)}, u32[]{:S(2)}) collective-permute-start(bf16[4,4,128,128]{3,2,1,0:T(8,128)(2,1)S(1)} %pad_maximum_fusion.source_ref.mine_ref), channel_id=1, source_target_pairs={{0,1},{1,0},{2,3},{3,2},{4,5},{5,4},{6,7},{7,6},{8,9},{9,8},{10,11... | collective-permute-start | bytes 1572872 | tf_op jit(solution)/shard_map/ppermute | solution.py:451
  27.2 4.9 %collective-permute-start.12 = (bf16[4,32,128]{2,1,0:T(8,128)(2,1)S(1)}, bf16[4,32,128]{2,1,0:T(8,128)(2,1)S(1)}, u32[]{:S(2)}, u32[]{:S(2)}) collective-permute-start(bf16[4,32,128]{2,1,0:T(8,128)(2,1)S(1)} %get-tuple-element.35), channel_id=1, source_target_pairs={{0,6},{1,7},{2,4},{3,5},{4,2},{5,3},{6,0},{7,1},{8,14},{9,15},{10,... | collective-permute-start | bytes 98312 | tf_op jit(solution)/shard_map/ppermute | solution.py:451
  29.0 3.9 %collective-permute-start.11 = (bf16[4,32,128]{2,1,0:T(8,128)(2,1)S(1)}, bf16[4,32,128]{2,1,0:T(8,128)(2,1)S(1)}, u32[]{:S(2)}, u32[]{:S(2)}) collective-permute-start(bf16[4,32,128]{2,1,0:T(8,128)(2,1)S(1)} %get-tuple-element.36), channel_id=1, source_target_pairs={{0,4},{1,5},{2,6},{3,7},{4,0},{5,1},{6,2},{7,3},{8,12},{9,13},{10,... | collective-permute-start | bytes 98312 | tf_op jit(solution)/shard_map/ppermute | solution.py:451
  29.5 3.9 %collective-permute-start.10 = (bf16[4,32,128]{2,1,0:T(8,128)(2,1)S(1)}, bf16[4,32,128]{2,1,0:T(8,128)(2,1)S(1)}, u32[]{:S(2)}, u32[]{:S(2)}) collective-permute-start(bf16[4,32,128]{2,1,0:T(8,128)(2,1)S(1)} %get-tuple-element.37), channel_id=1, source_target_pairs={{0,2},{1,3},{2,0},{3,1},{4,6},{5,7},{6,4},{7,5},{8,10},{9,11},{10,... | collective-permute-start | bytes 98312 | tf_op jit(solution)/shard_map/ppermute | solution.py:451
  33.5 1.4 %copy-start.2 = (bf16[2,128,128]{2,1,0:T(8,128)(2,1)S(1)}, bf16[2,128,128]{2,1,0:T(8,128)(2,1)}, u32[]{:S(2)}) copy-start(bf16[2,128,128]{2,1,0:T(8,128)(2,1)} %weight_ref.3) | copy-start | bytes 196612
  33.5 1.4 %collective-permute-start.13 = (bf16[4,4,32,128]{3,2,1,0:T(8,128)(2,1)S(1)}, bf16[4,4,32,128]{3,2,1,0:T(8,128)(2,1)S(1)}, u32[]{:S(2)}, u32[]{:S(2)}) collective-permute-start(bf16[4,4,32,128]{3,2,1,0:T(8,128)(2,1)S(1)} %pad_maximum_fusion.3.near_ref), channel_id=1, source_target_pairs={{0,1},{1,0},{2,3},{3,2},{4,5},{5,4},{6,7},{7,6},{8,9},{9,8},{10,11... | collective-permute-start | bytes 393224 | tf_op jit(solution)/shard_map/ppermute | solution.py:451
  (1 other events, 1.4 us)

commit v8 on v6

--- a/solution.py
+++ b/solution.py
@@ -88,24 +88,24 @@
         for z in lines
     ]
     biases = [contract(paired, line, 1, 1) for line in normed]
+    devices = length // rows
+    for a in range(rows):
+        for w in range(WD):
+            column = wide[a, pl.ds(w, devices, stride=rows), :]
+            picked[pl.ds(w * rows + a, devices, stride=WD * rows), :] = column
     for a, bias in enumerate(biases):
         kept = jnp.where(first, live, live_each[0, device * rows + a])
         bias = jnp.where(kept > 0, bias, MASKED)
         for lane in range(length // lanes):
             part = bias[:, lane * lanes : (lane + 1) * lanes]
             rows_out[pl.ds(2 * lane * heads * rows + a, 2 * heads, stride=rows), :] = part
-    devices = length // rows
-    for a in range(rows):
-        for w in range(WD):
-            column = wide[a, pl.ds(w, devices, stride=rows), :]
-            picked[pl.ds(w * rows + a, devices, stride=WD * rows), :] = column
     chip = lax.div(lax.axis_index("col"), 2)
     both = 2 * WD * rows
     packed = rows_out.shape[0]
     sent = rows_out[...].astype(jnp.bfloat16)
     for shift_by, out in enumerate(outs):
         out[:packed] = sent
-        row = lax.rem(lax.axis_index("row") + shift_by, along)
+        row = flipped(lax.axis_index("row"), shift_by)
         for flip in range(chips):
             at = pl.multiple_of((row * chips + flipped(chip, flip)) * both, both)
             out[packed + flip * both : packed + (flip + 1) * both] = picked[pl.ds(at, both), :].astype(jnp.bfloat16)
@@ -148,46 +148,34 @@
     return lax.rem(lax.div(index, bit), 2) == 1
 
 
-def to_relative(x, along, chips, rows):
-    row, col = lax.axis_index("row"), lax.axis_index("col")
-    cols = 2 * chips
-    grid = [[x[(r * cols + c) * rows : (r * cols + c + 1) * rows] for c in range(cols)] for r in range(along)]
+def exchanged(grid, row, col):
+    along, cols = len(grid), len(grid[0])
     bit = 1
     while bit < cols:
         swap = turned_over(col, bit)
         grid = [[jnp.where(swap, line[c ^ bit], line[c]) for c in range(cols)] for line in grid]
         bit *= 2
-    grid = [grid[-t % along] for t in range(along)]
     bit = 1
     while bit < along:
-        move = turned_over(row, bit)
-        grid = [
-            [jnp.where(move, grid[(t - bit) % along][c], grid[t][c]) for c in range(cols)] for t in range(along)
-        ]
+        swap = turned_over(row, bit)
+        grid = [[jnp.where(swap, grid[r ^ bit][c], grid[r][c]) for c in range(cols)] for r in range(along)]
         bit *= 2
+    return grid
+
+
+def to_relative(x, along, chips, rows):
+    cols = 2 * chips
+    grid = [[x[(r * cols + c) * rows : (r * cols + c + 1) * rows] for c in range(cols)] for r in range(along)]
+    grid = exchanged(grid, lax.axis_index("row"), lax.axis_index("col"))
     return jnp.concatenate(
         [grid[s][2 * flip + other] for other in range(2) for flip in range(chips) for s in range(along)], 0
     )
 
 
 def to_devices(x, along, chips, rows):
-    row, col = lax.axis_index("row"), lax.axis_index("col")
-    cols = 2 * chips
     at = lambda c, s: (((c % 2) * chips + c // 2) * along + s) * rows
-    grid = [[x[at(c, s) : at(c, s) + rows] for c in range(cols)] for s in range(along)]
-    bit = 1
-    while bit < along:
-        move = turned_over(row, bit)
-        grid = [
-            [jnp.where(move, grid[(s + bit) % along][c], grid[s][c]) for c in range(cols)] for s in range(along)
-        ]
-        bit *= 2
-    grid = [grid[-r % along] for r in range(along)]
-    bit = 1
-    while bit < cols:
-        swap = turned_over(col, bit)
-        grid = [[jnp.where(swap, line[c ^ bit], line[c]) for c in range(cols)] for line in grid]
-        bit *= 2
+    grid = [[x[at(c, s) : at(c, s) + rows] for c in range(2 * chips)] for s in range(along)]
+    grid = exchanged(grid, lax.axis_index("row"), lax.axis_index("col"))
     return jnp.concatenate([block for line in grid for block in line], 0)
 
 
@@ -257,15 +245,19 @@
     )(pair, gain, shift, weight, offset)
 
 
+def by_flip(ref):
+    return [ref.at[i] for i in range(ref.shape[0])]
+
+
 def unpack(source, p, pack, rows, heads, turn, into, at):
-    chips, along, _, lanes = source.shape
+    chips, (along, _, lanes) = len(source), source[0].shape
     packed = 2 * heads * rows
     half = chips * along * rows
     slots = into.shape[0]
     for lane in range(into.shape[2 - turn] // lanes):
         first = lane * packed + (p * heads + 2 * pack) * rows
         both = [
-            source[flip, shift, first : first + 2 * rows, :].astype(jnp.float32)
+            source[flip][shift, first : first + 2 * rows, :].astype(jnp.float32)
             for flip in range(chips)
             for shift in range(along)
         ]
@@ -301,11 +293,14 @@
         ready = ahead
 
 
-def head_group(heads, size, q, k, v, bias, mixed, there, near):
+def head_group(heads, size, q, k, v, bias, mixed, there, near, own_bias=None):
+    def added(h):
+        part = bias[h % bias.shape[0], :, near]
+        return part if own_bias is None else jnp.concatenate([own_bias[h, :, near], part], 0)
+
     def units():
         return [
-            (k[w, h], q[w, h * size : (h + 1) * size, there], bias[h % bias.shape[0], :, near],
-             v[w, h * size : (h + 1) * size, :])
+            (k[w, h], q[w, h * size : (h + 1) * size, there], added(h), v[w, h * size : (h + 1) * size, :])
             for h in heads
             for w in range(WD)
         ]
@@ -321,7 +316,7 @@
 def start_half(source, other, q, k, v, mixed, bias):
     _, heads, length, size = k.shape
     half = length // 2
-    rows = half // (source.shape[0] * source.shape[1])
+    rows = half // (len(source) * source[0].shape[0])
     width = min(half, CHUNK)
     if half == width:
         groups = []
@@ -347,18 +342,55 @@
     return []
 
 
-def early_kernel(mine_ref, q, k, v, mixed, bias):
-    attend_groups(start_half(mine_ref, 0, q, k, v, mixed, bias))
-
-
-def attend_early(mine, q, k, v):
+def normed_columns(pieces, first, gain, shift, rows):
+    along = pieces[0].shape[0]
+    blocks = [
+        piece[i, pl.ds(first, WD * rows), :].astype(jnp.float32).reshape(WD, rows, -1)
+        for piece in pieces
+        for i in range(along)
+    ]
+    lines = standardize_all([jnp.concatenate([block[w] for block in blocks], 0) for w in range(WD)])
+    return [line * gain + shift for line in lines]
+
+
+def first_column(packed, rows):
+    at = packed + lax.rem(lax.axis_index("col"), 2) * WD * rows
+    return pl.multiple_of(at, WD * rows)
+
+
+def early_kernel(
+    mine_ref, q, k, v, gain_ref, shift_ref, proj_ref, mixed, own_bias, own_lines, own_k, own_v, bias
+):
+    mine = by_flip(mine_ref)
+    _, heads, half, _ = own_k.shape
+    length = k.shape[2]
+    rows = half // (len(mine) * mine[0].shape[0])
+    packed = 2 * heads * rows * (length // mine_ref.shape[3])
+    lines = normed_columns(mine, first_column(packed, rows), gain_ref[1:2, :], shift_ref[1:2, :], rows)
+    groups = start_half(mine, 0, q, k, v, mixed, bias)
+    for w in range(WD):
+        own_lines[w] = lines[w]
+    keys_and_values([line.astype(jnp.bfloat16) for line in lines], proj_ref[1], own_k, own_v)
+    attend_groups(groups)
+    for pack in range(heads // 2):
+        unpack(mine, 1, pack, rows, heads, 0, own_bias, 0)
+
+
+def attend_early(mine, q, k, v, gain, shift, proj):
     _, heads, length, size = k.shape
+    inner, half, channels = heads * size, length // 2, proj.shape[1]
     return pl.pallas_call(
         early_kernel,
-        out_shape=jax.ShapeDtypeStruct((WD, heads * size, length // 2), jnp.float32),
-        in_specs=[VMEM] * 4,
-        out_specs=VMEM,
-        scratch_shapes=[pltpu.VMEM((heads if length <= CHUNK else 2, length, length // 2), jnp.float32)],
+        out_shape=(
+            jax.ShapeDtypeStruct((WD, inner, half), jnp.float32),
+            jax.ShapeDtypeStruct((heads, half, length), jnp.float32),
+            jax.ShapeDtypeStruct((WD, half, channels), jnp.float32),
+            jax.ShapeDtypeStruct((WD, heads, half, size), jnp.bfloat16),
+            jax.ShapeDtypeStruct((WD, inner, half), jnp.bfloat16),
+        ),
+        in_specs=[VMEM] * 7,
+        out_specs=(VMEM,) * 5,
+        scratch_shapes=[pltpu.VMEM((heads if length <= CHUNK else 2, length, half), jnp.float32)],
         compiler_params=params(8 if length <= CHUNK else 40),
         cost_estimate=pl.CostEstimate(
             flops=4 * WD * heads * size * length * length,
@@ -366,47 +398,44 @@
             transcendentals=WD * heads * length * length // 2,
         ),
         name="early",
-    )(mine, q, k, v)
+    )(mine, q, k, v, gain, shift, proj)
 
 
 def attend_kernel(
-    mine_ref, other_ref, early_ref, q0, k0, v0, g0,
+    other_ref, early_ref, own_bias, own_lines, own_k, own_v, q0, k0, v0, g0,
     gain_ref, shift_ref, proj_ref, gate_ref, weight_ref, offset_ref,
     out0, out1, turned_bias, bias, late, mixed, q1, k1, v1, g1,
 ):
-    chips, along, _, _ = mine_ref.shape
+    others = by_flip(other_ref)
+    chips, (along, _, lanes) = len(others), others[0].shape
     _, heads, length, size = k0.shape
     half = length // 2
     rows = half // (chips * along)
-    packed = 2 * heads * rows * (length // mine_ref.shape[3])
-    first = pl.multiple_of(packed + lax.rem(lax.axis_index("col"), 2) * WD * rows, WD * rows)
+    packed = 2 * heads * rows * (length // lanes)
     offset = turned(gate_ref[1:2, :])
-    blocks = []
-    for source in (mine_ref, other_ref):
-        for flip in range(chips):
-            for shift in range(along):
-                both = source[flip, shift, pl.ds(first, WD * rows), :].astype(jnp.float32)
-                blocks.append(both.reshape(WD, rows, -1))
-    lines = standardize_all([jnp.concatenate([block[w] for block in blocks], 0) for w in range(WD)])
-    lines = [line * gain_ref[1:2, :] + shift_ref[1:2, :] for line in lines]
-    keys_and_values([line.astype(jnp.bfloat16) for line in lines], proj_ref[1], k1, v1)
-    ordered = [to_devices(line, along, chips, rows).astype(jnp.bfloat16) for line in lines]
+    far = normed_columns(others, first_column(packed, rows), gain_ref[1:2, :], shift_ref[1:2, :], rows)
+    keys_and_values([line.astype(jnp.bfloat16) for line in far], proj_ref[1], k1.at[:, :, half:], v1.at[:, :, half:])
+    for w in range(WD):
+        k1[w, :, :half] = own_k[w]
+        v1[w, :, :half] = own_v[w]
+    ordered = [
+        to_devices(jnp.concatenate([own_lines[w], far[w]], 0), along, chips, rows).astype(jnp.bfloat16)
+        for w in range(WD)
+    ]
     queries_and_gates(ordered, size ** (-0.5), proj_ref[1], offset, q1, g1)
-    groups = start_half(other_ref, 1, q0, k0, v0, late, turned_bias)
+    groups = start_half(others, 1, q0, k0, v0, late, turned_bias)
     for pack in range(heads // 2):
-        unpack(mine_ref, 1, pack, rows, heads, 0, bias, 0)
-        unpack(other_ref, 1, pack, rows, heads, 0, bias, half)
+        unpack(others, 1, pack, rows, heads, 0, bias, 0)
         pair = (2 * pack, 2 * pack + 1)
         if length == CHUNK:
-            groups.append(
-                head_group(pair, size, q1, k1, v1, bias, mixed, pl.ds(0, length), pl.ds(0, length))
-            )
+            whole = pl.ds(0, length)
+            groups.append(head_group(pair, size, q1, k1, v1, bias, mixed, whole, whole, own_bias))
             continue
 
         def step(chunk):
             there = pl.ds(pl.multiple_of(chunk * CHUNK, CHUNK), CHUNK)
             for h in pair:
-                attend_groups([head_group((h,), size, q1, k1, v1, bias, mixed, there, there)])
+                attend_groups([head_group((h,), size, q1, k1, v1, bias, mixed, there, there, own_bias)])
 
         for_each(length // CHUNK, step, False)
     attend_groups(groups)
@@ -420,7 +449,7 @@
         out1[w] = full.astype(jnp.bfloat16)
 
 
-def attend(mine, other, early, start, gain, shift, proj, gate, weight, offset):
+def attend(other, early, start, gain, shift, proj, gate, weight, offset):
     _, heads, length, size = start[1].shape
     inner, channels = weight.shape[1:]
     result = jax.ShapeDtypeStruct((WD, length, channels), jnp.bfloat16)
@@ -428,18 +457,18 @@
     return pl.pallas_call(
         attend_kernel,
         out_shape=(result, result),
-        in_specs=[VMEM] * 13,
+        in_specs=[VMEM] * 16,
         out_specs=(VMEM, VMEM),
         scratch_shapes=[
             pltpu.VMEM((slots, length, length // 2), jnp.float32),
-            pltpu.VMEM((slots, length, length), jnp.float32),
+            pltpu.VMEM((slots, length // 2, length), jnp.float32),
             pltpu.VMEM((WD, inner, length // 2), jnp.float32),
             pltpu.VMEM((WD, inner, length), jnp.float32),
         ]
         + [pltpu.VMEM(shape, dtype) for shape, dtype in projected(length, inner, heads)],
         compiler_params=params(16 if length <= CHUNK else 60),
         name="attend",
-    )(mine, other, early, *start, gain, shift, proj, gate, weight, offset)
+    )(other, *early, *start, gain, shift, proj, gate, weight, offset)
 
 
 def body(pair, residue_mask, ln_gain, ln_shift, w_proj, w_bias, gate_bias, w_out, out_bias):
@@ -449,7 +478,7 @@
     chips = cols // 2
 
     def by_row(block, shift):
-        return lax.ppermute(block, "row", [(i, (i + shift) % along) for i in range(along)])
+        return lax.ppermute(block, "row", [(i, i ^ shift) for i in range(along)])
 
     def by_col(block, flip):
         return lax.ppermute(block, "col", [(i, i ^ flip) for i in range(cols)])
@@ -459,6 +488,7 @@
     )
     line = jnp.stack([sent[0]] + [by_row(sent[shift], shift) for shift in range(1, along)])
     start = local_lines(pair, ln_gain, ln_shift, w_proj, gate_bias, heads, along, chips)
+    line, _ = lax.optimization_barrier((line, start))
     packed = 2 * heads * rows * (length // channels)
     both = 2 * WD * rows
 
@@ -467,10 +497,9 @@
         return jnp.concatenate([line[:, :packed], line[:, at : at + both]], 1)
 
     mine = jnp.stack([owned_by(0)] + [by_col(owned_by(flip), 2 * flip) for flip in range(1, chips)])
-    mine, _ = lax.optimization_barrier((mine, start))
     other = by_col(mine, 1)
-    early = attend_early(mine, *start[:3])
-    return attend(mine, other, early, start, ln_gain, ln_shift, w_proj, gate_bias, w_out, out_bias)
+    early = attend_early(mine, *start[:3], ln_gain, ln_shift, w_proj)
+    return attend(other, early, start, ln_gain, ln_shift, w_proj, gate_bias, w_out, out_bias)
 
 
 def solution(mesh):

time: 30.4 us -> 31.3 us (1.030)
  starting transfers between devices: 10.6 us -> 9.3 us
  waiting for transfers between devices: 10.9 us -> 12 us
  local copies, waits for them, and re-layouts: 1 us -> 1.77 us
    ppermute x3, waiting for transfers between devices: 2.01 us -> 4.61 us  [by_row(): return lax.ppermute(block, 'row', [(i, i ^ shift) for i in range(along)])]
    ppermute x4, waiting for transfers between devices: 8.85 us -> 7.37 us  [by_col(): return lax.ppermute(block, 'col', [(i, i ^ flip) for i in range(cols)])]
    ppermute x3, starting transfers between devices: 7.01 us -> 5.68 us  [by_row(): return lax.ppermute(block, 'row', [(i, i ^ shift) for i in range(along)])]
    unnamed x16, local copies, waits for them, and re-layouts: 0.98 us -> 1.74 us
    pallas_call x1, Pallas kernels: 0.62 us -> 0.95 us  [attend_early(): pl.pallas_call(early_kernel, out_shape=(jax.ShapeDtypeStruct((WD, inner,...]
  transfers between devices with their start and end apart: 7 -> 7, of which waited for: 6 -> 5; matrix products, arithmetic and copies ran while one was open for 0% -> 0% of each run, Pallas kernels for 4% -> 5%
where the time goes in v8:
time: 31.3 us; the launch traced here: 31.1 us
  waiting for transfers between devices  12 us (38%)
  starting transfers between devices  9.3 us (30%)
  Pallas kernels  7.14 us (23%)
  local copies, waits for them, and re-layouts  1.77 us (6%)
  between operations  0.76 us (2%)
    ppermute x4, waiting for transfers between devices, by_col(): return lax.ppermute(block, 'col', [(i, i ^ flip) for i in range(cols)])  7.37 us
    ppermute x3, starting transfers between devices, by_row(): return lax.ppermute(block, 'row', [(i, i ^ shift) for i in range(along)])  5.68 us
    ppermute x3, waiting for transfers between devices, by_row(): return lax.ppermute(block, 'row', [(i, i ^ shift) for i in range(along)])  4.61 us
    ppermute x4, starting transfers between devices, by_col(): return lax.ppermute(block, 'col', [(i, i ^ flip) for i in range(cols)])  3.62 us
    pallas_call x1, Pallas kernels, local_bias(): pl.pallas_call(functools.partial(bias_kernel, along, chips), out_shape=(s...  2.82 us
    pallas_call x1, Pallas kernels, attend(): pl.pallas_call(attend_kernel, out_shape=(result, result), in_specs=[VMEM]...  2.79 us
    unnamed x16, local copies, waits for them, and re-layouts  1.74 us
    pallas_call x1, Pallas kernels, attend_early(): pl.pallas_call(early_kernel, out_shape=(jax.ShapeDtypeStruct((WD, inner,...  0.95 us
  transfers between devices with their start and end apart: 7, of which 5 were waited for; matrix products, arithmetic and copies ran while one was open for 0% of the time, Pallas kernels for 5%

profile of v8, /device:TPU:0, one launch (start us, length us, event | category | flops | bytes accessed | tf_op | source)
XLA Modules:
  0.0 31.1 jit_solution(8371211002609122792)
XLA Ops:
  0.6 2.8 %bias.1 = (bf16[256,128]{1,0:T(8,128)(2,1)}, bf16[256,128]{1,0:T(8,128)(2,1)}, bf16[256,128]{1,0:T(8,128)(2,1)}, bf16[256,128]{1,0:T(8,128)(2,1)}) custom-call(bf16[8,256,128]{2,1,0:T(8,128)(2,1)} %lines_ref.1, s32[1,256]{1,0:T(1,128)} %bitcast.19, f32[2,128]{1,0:T(2,128)} %gain_ref.5, f32[2,128]{1,0:T(2,128)} %shift_ref.5, bf16[2,4,128]{2,1,0:T(4,128)(2,1)} %bitcast.18), custom_call_target="tpu_custom_call" | custom-call | tf_op jit(solution)/shard_map/bias/pallas_call | solution.py:119
  3.5 3.1 %collective-permute-start = (bf16[256,128]{1,0:T(8,128)(2,1)}, bf16[256,128]{1,0:T(8,128)(2,1)S(1)}, u32[]{:S(2)}, u32[]{:S(2)}) collective-permute-start(bf16[256,128]{1,0:T(8,128)(2,1)} %get-tuple-element.17), channel_id=1, source_target_pairs={{0,8},{8,0},{16,24},{24,16},{1,9},{9,1},{17,25},{25,17},{2,10},{10... | collective-permute-start | bytes 196616 | tf_op jit(solution)/shard_map/ppermute | solution.py:481
  6.6 2.6 %collective-permute-start.1 = (bf16[256,128]{1,0:T(8,128)(2,1)}, bf16[256,128]{1,0:T(8,128)(2,1)S(1)}, u32[]{:S(2)}, u32[]{:S(2)}) collective-permute-start(bf16[256,128]{1,0:T(8,128)(2,1)} %get-tuple-element.18), channel_id=1, source_target_pairs={{0,16},{8,24},{16,0},{24,8},{1,17},{9,25},{17,1},{25,9},{2,18},{10... | collective-permute-start | bytes 196616 | tf_op jit(solution)/shard_map/ppermute | solution.py:481
  9.2 0.0 collective-permute-start.2
  9.2 0.0 copy-start.1
  9.2 1.0 %copy-done.1 = bf16[8,256,128]{2,1,0:T(8,128)(2,1)S(1)} copy-done((bf16[8,256,128]{2,1,0:T(8,128)(2,1)S(1)}, bf16[8,256,128]{2,1,0:T(8,128)(2,1)}, u32[]{:S(2)}) %copy-start.1) | copy-done | bytes 524312
  10.2 0.6 %lines.1 = (bf16[2,128,256]{2,1,0:T(8,128)(2,1)S(1)}, bf16[2,4,256,32]{3,2,1,0:T(8,128)(2,1)S(1)}, bf16[2,128,256]{2,1,0:T(8,128)(2,1)S(1)}, f32[2,128,256]{2,1,0:T(8,128)S(1)}) custom-call(bf16[8,256,128]{2,1,0:T(8,128)(2,1)S(1)} %copy-done.1, f32[2,128]{1,0:T(2,128)S(1)} %copy-done.3, f32[2,128]{1,0:T(2,128)S(1)} %copy-done.4, ...), custom_call_target="tpu_custom_call" | custom-call | flops 67108864 | bytes 1048576 | tf_op jit(solution)/shard_map/lines/pallas_call | solution.py:231
  10.8 0.0 collective-permute-done
  10.8 3.2 %collective-permute-done.1 = bf16[256,128]{1,0:T(8,128)(2,1)S(1)} collective-permute-done((bf16[256,128]{1,0:T(8,128)(2,1)}, bf16[256,128]{1,0:T(8,128)(2,1)S(1)}, u32[]{:S(2)}, u32[]{:S(2)}) %collective-permute-start.1) | collective-permute-done | bytes 65568 | tf_op jit(solution)/shard_map/ppermute | solution.py:481
  14.0 1.4 %collective-permute-done.2 = bf16[256,128]{1,0:T(8,128)(2,1)S(1)} collective-permute-done((bf16[256,128]{1,0:T(8,128)(2,1)}, bf16[256,128]{1,0:T(8,128)(2,1)S(1)}, u32[]{:S(2)}, u32[]{:S(2)}) %collective-permute-start.2) | collective-permute-done | bytes 65568 | tf_op jit(solution)/shard_map/ppermute | solution.py:481
  15.5 0.1 pad_maximum_fusion.2
  15.6 1.6 %collective-permute-start.3 = (bf16[4,160,128]{2,1,0:T(8,128)(2,1)S(1)}, bf16[4,160,128]{2,1,0:T(8,128)(2,1)S(1)}, u32[]{:S(2)}, u32[]{:S(2)}) collective-permute-start(bf16[4,160,128]{2,1,0:T(8,128)(2,1)S(1)} %get-tuple-element.33), channel_id=1, source_target_pairs={{0,2},{1,3},{2,0},{3,1},{4,6},{5,7},{6,4},{7,5},{8,10},{9,11},{10,... | collective-permute-start | bytes 491528 | tf_op jit(solution)/shard_map/ppermute | solution.py:484
  17.1 1.5 %collective-permute-start.4 = (bf16[4,160,128]{2,1,0:T(8,128)(2,1)S(1)}, bf16[4,160,128]{2,1,0:T(8,128)(2,1)S(1)}, u32[]{:S(2)}, u32[]{:S(2)}) collective-permute-start(bf16[4,160,128]{2,1,0:T(8,128)(2,1)S(1)} %get-tuple-element.34), channel_id=1, source_target_pairs={{0,4},{1,5},{2,6},{3,7},{4,0},{5,1},{6,2},{7,3},{8,12},{9,13},{10,... | collective-permute-start | bytes 491528 | tf_op jit(solution)/shard_map/ppermute | solution.py:484
  18.7 0.5 %collective-permute-start.5 = (bf16[4,160,128]{2,1,0:T(8,128)(2,1)S(1)}, bf16[4,160,128]{2,1,0:T(8,128)(2,1)S(1)}, u32[]{:S(2)}, u32[]{:S(2)}) collective-permute-start(bf16[4,160,128]{2,1,0:T(8,128)(2,1)S(1)} %get-tuple-element.35), channel_id=1, source_target_pairs={{0,6},{1,7},{2,4},{3,5},{4,2},{5,3},{6,0},{7,1},{8,14},{9,15},{10,... | collective-permute-start | bytes 491528 | tf_op jit(solution)/shard_map/ppermute | solution.py:484
  19.2 3.2 %collective-permute-done.3 = bf16[4,160,128]{2,1,0:T(8,128)(2,1)S(1)} collective-permute-done((bf16[4,160,128]{2,1,0:T(8,128)(2,1)S(1)}, bf16[4,160,128]{2,1,0:T(8,128)(2,1)S(1)}, u32[]{:S(2)}, u32[]{:S(2)}) %collective-permute-start.3) | collective-permute-done | bytes 163872 | tf_op jit(solution)/shard_map/ppermute | solution.py:484
  22.4 3.0 %collective-permute-done.4 = bf16[4,160,128]{2,1,0:T(8,128)(2,1)S(1)} collective-permute-done((bf16[4,160,128]{2,1,0:T(8,128)(2,1)S(1)}, bf16[4,160,128]{2,1,0:T(8,128)(2,1)S(1)}, u32[]{:S(2)}, u32[]{:S(2)}) %collective-permute-start.4) | collective-permute-done | bytes 163872 | tf_op jit(solution)/shard_map/ppermute | solution.py:484
  25.4 0.0 collective-permute-done.5
  25.4 0.1 pad_maximum_fusion.mine_ref
  25.5 0.0 copy-start.2
  25.5 0.1 collective-permute-start.6
  25.6 0.9 %early.1 = (f32[2,128,128]{2,1,0:T(8,128)S(1)}, f32[4,128,256]{2,1,0:T(8,128)S(1)}, f32[2,128,128]{2,1,0:T(8,128)S(1)}, bf16[2,4,128,32]{3,2,1,0:T(8,128)(2,1)S(1)}, bf16[2,128,128]{2,1,0:T(8,128)(2,1)S(1)}) custom-call(bf16[4,4,160,128]{3,2,1,0:T(8,128)(2,1)S(1)} %pad_maximum_fusion.mine_ref, bf16[2,128,256]{2,1,0:T(8,128)(2,1)S(1)} %get-tuple-element.20.q.q0, ...), custom_call_target="tpu_custom_call" | custom-call | flops 67108864 | bytes 2097152 | tf_op jit(solution)/shard_map/early/pallas_call | solution.py:382
  26.5 1.1 %collective-permute-done.6.other_ref = bf16[4,4,160,128]{3,2,1,0:T(8,128)(2,1)S(1)} collective-permute-done((bf16[4,4,160,128]{3,2,1,0:T(8,128)(2,1)S(1)}, bf16[4,4,160,128]{3,2,1,0:T(8,128)(2,1)S(1)}, u32[]{:S(2)}, u32[]{:S(2)}) %collective-permute-start.6) | collective-permute-done | bytes 655392 | tf_op jit(solution)/shard_map/ppermute | solution.py:484
  27.7 0.7 %copy-done.6 = f32[2,128]{1,0:T(2,128)S(1)} copy-done((f32[2,128]{1,0:T(2,128)S(1)}, f32[2,128]{1,0:T(2,128)}, u32[]{:S(2)}) %copy-start.6) | copy-done | bytes 1048
  28.3 2.8 %attend.1 = (bf16[2,256,128]{2,1,0:T(8,128)(2,1)}, bf16[2,256,128]{2,1,0:T(8,128)(2,1)}) custom-call(bf16[4,4,160,128]{3,2,1,0:T(8,128)(2,1)S(1)} %collective-permute-done.6.other_ref, f32[2,128,128]{2,1,0:T(8,128)S(1)} %get-tuple-element.25.early_ref, f32[4,128,256]{2,1,0:T(8,128)S(1)} %get-tuple-element.26.own_bias, ...), custom_call_target="tpu_custom_call" | custom-call | tf_op jit(solution)/shard_map/attend/pallas_call | solution.py:457
  (16 shorter events, 0.1 us)
Async XLA Ops:
  0.6 8.5 %copy-start = (bf16[2,128,512]{2,1,0:T(8,128)(2,1)S(1)}, bf16[2,128,512]{2,1,0:T(8,128)(2,1)}, u32[]{:S(2)}) copy-start(bf16[2,128,512]{2,1,0:T(8,128)(2,1)} %proj_ref.3) | copy-start | bytes 786436
  3.5 7.4 %collective-permute-start = (bf16[256,128]{1,0:T(8,128)(2,1)}, bf16[256,128]{1,0:T(8,128)(2,1)S(1)}, u32[]{:S(2)}, u32[]{:S(2)}) collective-permute-start(bf16[256,128]{1,0:T(8,128)(2,1)} %get-tuple-element.17), channel_id=1, source_target_pairs={{0,8},{8,0},{16,24},{24,16},{1,9},{9,1},{17,25},{25,17},{2,10},{10... | collective-permute-start | bytes 196616 | tf_op jit(solution)/shard_map/ppermute | solution.py:481
  6.6 2.6 %copy-start.4 = (f32[2,128]{1,0:T(2,128)S(1)}, f32[2,128]{1,0:T(2,128)}, u32[]{:S(2)}) copy-start(f32[2,128]{1,0:T(2,128)} %shift_ref.5) | copy-start | bytes 3076
  6.6 2.6 %copy-start.5 = (f32[2,128]{1,0:T(2,128)S(1)}, f32[2,128]{1,0:T(2,128)}, u32[]{:S(2)}) copy-start(f32[2,128]{1,0:T(2,128)} %gate_ref.1) | copy-start | bytes 3076
  6.6 2.6 %copy-start.3 = (f32[2,128]{1,0:T(2,128)S(1)}, f32[2,128]{1,0:T(2,128)}, u32[]{:S(2)}) copy-start(f32[2,128]{1,0:T(2,128)} %gain_ref.5) | copy-start | bytes 3076
  6.6 7.5 %collective-permute-start.1 = (bf16[256,128]{1,0:T(8,128)(2,1)}, bf16[256,128]{1,0:T(8,128)(2,1)S(1)}, u32[]{:S(2)}, u32[]{:S(2)}) collective-permute-start(bf16[256,128]{1,0:T(8,128)(2,1)} %get-tuple-element.18), channel_id=1, source_target_pairs={{0,16},{8,24},{16,0},{24,8},{1,17},{9,25},{17,1},{25,9},{2,18},{10... | collective-permute-start | bytes 196616 | tf_op jit(solution)/shard_map/ppermute | solution.py:481
  9.2 6.3 %collective-permute-start.2 = (bf16[256,128]{1,0:T(8,128)(2,1)}, bf16[256,128]{1,0:T(8,128)(2,1)S(1)}, u32[]{:S(2)}, u32[]{:S(2)}) collective-permute-start(bf16[256,128]{1,0:T(8,128)(2,1)} %get-tuple-element.19), channel_id=1, source_target_pairs={{0,24},{8,16},{16,8},{24,0},{1,25},{9,17},{17,9},{25,1},{2,26},{10... | collective-permute-start | bytes 196616 | tf_op jit(solution)/shard_map/ppermute | solution.py:481
  9.2 1.0 %copy-start.1 = (bf16[8,256,128]{2,1,0:T(8,128)(2,1)S(1)}, bf16[8,256,128]{2,1,0:T(8,128)(2,1)}, u32[]{:S(2)}) copy-start(bf16[8,256,128]{2,1,0:T(8,128)(2,1)} %lines_ref.1) | copy-start | bytes 1572868
  10.2 5.2 %copy-start.7 = (bf16[256,128]{1,0:T(8,128)(2,1)S(1)}, bf16[256,128]{1,0:T(8,128)(2,1)}, u32[]{:S(2)}) copy-start(bf16[256,128]{1,0:T(8,128)(2,1)} %get-tuple-element.16) | copy-start | bytes 196612
  15.6 6.8 %collective-permute-start.3 = (bf16[4,160,128]{2,1,0:T(8,128)(2,1)S(1)}, bf16[4,160,128]{2,1,0:T(8,128)(2,1)S(1)}, u32[]{:S(2)}, u32[]{:S(2)}) collective-permute-start(bf16[4,160,128]{2,1,0:T(8,128)(2,1)S(1)} %get-tuple-element.33), channel_id=1, source_target_pairs={{0,2},{1,3},{2,0},{3,1},{4,6},{5,7},{6,4},{7,5},{8,10},{9,11},{10,... | collective-permute-start | bytes 491528 | tf_op jit(solution)/shard_map/ppermute | solution.py:484
  17.1 8.2 %collective-permute-start.4 = (bf16[4,160,128]{2,1,0:T(8,128)(2,1)S(1)}, bf16[4,160,128]{2,1,0:T(8,128)(2,1)S(1)}, u32[]{:S(2)}, u32[]{:S(2)}) collective-permute-start(bf16[4,160,128]{2,1,0:T(8,128)(2,1)S(1)} %get-tuple-element.34), channel_id=1, source_target_pairs={{0,4},{1,5},{2,6},{3,7},{4,0},{5,1},{6,2},{7,3},{8,12},{9,13},{10,... | collective-permute-start | bytes 491528 | tf_op jit(solution)/shard_map/ppermute | solution.py:484
  18.7 6.7 %collective-permute-start.5 = (bf16[4,160,128]{2,1,0:T(8,128)(2,1)S(1)}, bf16[4,160,128]{2,1,0:T(8,128)(2,1)S(1)}, u32[]{:S(2)}, u32[]{:S(2)}) collective-permute-start(bf16[4,160,128]{2,1,0:T(8,128)(2,1)S(1)} %get-tuple-element.35), channel_id=1, source_target_pairs={{0,6},{1,7},{2,4},{3,5},{4,2},{5,3},{6,0},{7,1},{8,14},{9,15},{10,... | collective-permute-start | bytes 491528 | tf_op jit(solution)/shard_map/ppermute | solution.py:484
  25.5 2.2 %copy-start.2 = (bf16[2,128,128]{2,1,0:T(8,128)(2,1)S(1)}, bf16[2,128,128]{2,1,0:T(8,128)(2,1)}, u32[]{:S(2)}) copy-start(bf16[2,128,128]{2,1,0:T(8,128)(2,1)} %weight_ref.3) | copy-start | bytes 196612
  25.5 2.2 %collective-permute-start.6 = (bf16[4,4,160,128]{3,2,1,0:T(8,128)(2,1)S(1)}, bf16[4,4,160,128]{3,2,1,0:T(8,128)(2,1)S(1)}, u32[]{:S(2)}, u32[]{:S(2)}) collective-permute-start(bf16[4,4,160,128]{3,2,1,0:T(8,128)(2,1)S(1)} %pad_maximum_fusion.mine_ref), channel_id=1, source_target_pairs={{0,1},{1,0},{2,3},{3,2},{4,5},{5,4},{6,7},{7,6},{8,9},{9,8},{10,11... | collective-permute-start | bytes 1966088 | tf_op jit(solution)/shard_map/ppermute | solution.py:484
  27.7 0.7 %copy-start.6 = (f32[2,128]{1,0:T(2,128)S(1)}, f32[2,128]{1,0:T(2,128)}, u32[]{:S(2)}) copy-start(f32[2,128]{1,0:T(2,128)} %offset_ref.3) | copy-start | bytes 3076

commit v9 on v6

--- a/solution.py
+++ b/solution.py
@@ -88,24 +88,24 @@
         for z in lines
     ]
     biases = [contract(paired, line, 1, 1) for line in normed]
+    devices = length // rows
+    for a in range(rows):
+        for w in range(WD):
+            column = wide[a, pl.ds(w, devices, stride=rows), :]
+            picked[pl.ds(w * rows + a, devices, stride=WD * rows), :] = column
     for a, bias in enumerate(biases):
         kept = jnp.where(first, live, live_each[0, device * rows + a])
         bias = jnp.where(kept > 0, bias, MASKED)
         for lane in range(length // lanes):
             part = bias[:, lane * lanes : (lane + 1) * lanes]
             rows_out[pl.ds(2 * lane * heads * rows + a, 2 * heads, stride=rows), :] = part
-    devices = length // rows
-    for a in range(rows):
-        for w in range(WD):
-            column = wide[a, pl.ds(w, devices, stride=rows), :]
-            picked[pl.ds(w * rows + a, devices, stride=WD * rows), :] = column
     chip = lax.div(lax.axis_index("col"), 2)
     both = 2 * WD * rows
     packed = rows_out.shape[0]
     sent = rows_out[...].astype(jnp.bfloat16)
     for shift_by, out in enumerate(outs):
         out[:packed] = sent
-        row = lax.rem(lax.axis_index("row") + shift_by, along)
+        row = flipped(lax.axis_index("row"), shift_by)
         for flip in range(chips):
             at = pl.multiple_of((row * chips + flipped(chip, flip)) * both, both)
             out[packed + flip * both : packed + (flip + 1) * both] = picked[pl.ds(at, both), :].astype(jnp.bfloat16)
@@ -148,46 +148,34 @@
     return lax.rem(lax.div(index, bit), 2) == 1
 
 
-def to_relative(x, along, chips, rows):
-    row, col = lax.axis_index("row"), lax.axis_index("col")
-    cols = 2 * chips
-    grid = [[x[(r * cols + c) * rows : (r * cols + c + 1) * rows] for c in range(cols)] for r in range(along)]
+def exchanged(grid, row, col):
+    along, cols = len(grid), len(grid[0])
     bit = 1
     while bit < cols:
         swap = turned_over(col, bit)
         grid = [[jnp.where(swap, line[c ^ bit], line[c]) for c in range(cols)] for line in grid]
         bit *= 2
-    grid = [grid[-t % along] for t in range(along)]
     bit = 1
     while bit < along:
-        move = turned_over(row, bit)
-        grid = [
-            [jnp.where(move, grid[(t - bit) % along][c], grid[t][c]) for c in range(cols)] for t in range(along)
-        ]
+        swap = turned_over(row, bit)
+        grid = [[jnp.where(swap, grid[r ^ bit][c], grid[r][c]) for c in range(cols)] for r in range(along)]
         bit *= 2
+    return grid
+
+
+def to_relative(x, along, chips, rows):
+    cols = 2 * chips
+    grid = [[x[(r * cols + c) * rows : (r * cols + c + 1) * rows] for c in range(cols)] for r in range(along)]
+    grid = exchanged(grid, lax.axis_index("row"), lax.axis_index("col"))
     return jnp.concatenate(
-        [grid[s][2 * flip + other] for other in range(2) for flip in range(chips) for s in range(along)], 0
+        [grid[s][2 * flip + other] for other in range(2) for flip in range(chips) for s in reversed(range(along))], 0
     )
 
 
 def to_devices(x, along, chips, rows):
-    row, col = lax.axis_index("row"), lax.axis_index("col")
-    cols = 2 * chips
-    at = lambda c, s: (((c % 2) * chips + c // 2) * along + s) * rows
-    grid = [[x[at(c, s) : at(c, s) + rows] for c in range(cols)] for s in range(along)]
-    bit = 1
-    while bit < along:
-        move = turned_over(row, bit)
-        grid = [
-            [jnp.where(move, grid[(s + bit) % along][c], grid[s][c]) for c in range(cols)] for s in range(along)
-        ]
-        bit *= 2
-    grid = [grid[-r % along] for r in range(along)]
-    bit = 1
-    while bit < cols:
-        swap = turned_over(col, bit)
-        grid = [[jnp.where(swap, line[c ^ bit], line[c]) for c in range(cols)] for line in grid]
-        bit *= 2
+    at = lambda c, s: (((c % 2) * chips + c // 2) * along + along - 1 - s) * rows
+    grid = [[x[at(c, s) : at(c, s) + rows] for c in range(2 * chips)] for s in range(along)]
+    grid = exchanged(grid, lax.axis_index("row"), lax.axis_index("col"))
     return jnp.concatenate([block for line in grid for block in line], 0)
 
 
@@ -449,7 +437,7 @@
     chips = cols // 2
 
     def by_row(block, shift):
-        return lax.ppermute(block, "row", [(i, (i + shift) % along) for i in range(along)])
+        return lax.ppermute(block, "row", [(i, i ^ shift) for i in range(along)])
 
     def by_col(block, flip):
         return lax.ppermute(block, "col", [(i, i ^ flip) for i in range(cols)])
@@ -457,8 +445,10 @@
     sent = local_bias(
         pair, residue_mask[None, :], ln_gain, ln_shift, jnp.transpose(w_bias, (0, 2, 1)), along, chips
     )
-    line = jnp.stack([sent[0]] + [by_row(sent[shift], shift) for shift in range(1, along)])
+    far_first = [by_row(sent[flip], flip) for flip in reversed(range(1, along))]
+    line = jnp.stack(far_first + [sent[0]])
     start = local_lines(pair, ln_gain, ln_shift, w_proj, gate_bias, heads, along, chips)
+    line, _ = lax.optimization_barrier((line, start))
     packed = 2 * heads * rows * (length // channels)
     both = 2 * WD * rows
 
@@ -467,7 +457,6 @@
         return jnp.concatenate([line[:, :packed], line[:, at : at + both]], 1)
 
     mine = jnp.stack([owned_by(0)] + [by_col(owned_by(flip), 2 * flip) for flip in range(1, chips)])
-    mine, _ = lax.optimization_barrier((mine, start))
     other = by_col(mine, 1)
     early = attend_early(mine, *start[:3])
     return attend(mine, other, early, start, ln_gain, ln_shift, w_proj, gate_bias, w_out, out_bias)

time: 30.4 us -> 30.6 us (level)
  waiting for transfers between devices: 10.9 us -> 12.2 us
  starting transfers between devices: 10.6 us -> 9.4 us
    ppermute x3, waiting for transfers between devices: 2.01 us -> 3.56 us  [by_row(): return lax.ppermute(block, 'row', [(i, i ^ shift) for i in range(along)])]
    ppermute x3, starting transfers between devices: 7.01 us -> 5.78 us  [by_row(): return lax.ppermute(block, 'row', [(i, i ^ shift) for i in range(along)])]
  transfers between devices with their start and end apart: 7 -> 7, of which waited for: 6 -> 5; matrix products, arithmetic and copies ran while one was open for 0% -> 0% of each run, Pallas kernels for 4% -> 4%
where the time goes in v9:
time: 30.6 us; the launch traced here: 30.4 us
  waiting for transfers between devices  12.2 us (40%)
  starting transfers between devices  9.4 us (31%)
  Pallas kernels  6.83 us (22%)
  local copies, waits for them, and re-layouts  1.03 us (3%)
  between operations  0.74 us (2%)
    ppermute x4, waiting for transfers between devices, by_col(): return lax.ppermute(block, 'col', [(i, i ^ flip) for i in range(cols)])  8.62 us
    ppermute x3, starting transfers between devices, by_row(): return lax.ppermute(block, 'row', [(i, i ^ shift) for i in range(along)])  5.78 us
    ppermute x4, starting transfers between devices, by_col(): return lax.ppermute(block, 'col', [(i, i ^ flip) for i in range(cols)])  3.62 us
    ppermute x3, waiting for transfers between devices, by_row(): return lax.ppermute(block, 'row', [(i, i ^ shift) for i in range(along)])  3.56 us
    pallas_call x1, Pallas kernels, local_bias(): pl.pallas_call(functools.partial(bias_kernel, along, chips), out_shape=(s...  2.84 us
    pallas_call x1, Pallas kernels, attend(): pl.pallas_call(attend_kernel, out_shape=(result, result), in_specs=[VMEM]...  2.79 us
    unnamed x16, local copies, waits for them, and re-layouts  1 us
    pallas_call x1, Pallas kernels, attend_early(): pl.pallas_call(early_kernel, out_shape=jax.ShapeDtypeStruct((WD, heads *...  0.62 us
  transfers between devices with their start and end apart: 7, of which 5 were waited for; matrix products, arithmetic and copies ran while one was open for 0% of the time, Pallas kernels for 4%

profile of v9, /device:TPU:0, one launch (start us, length us, event | category | flops | bytes accessed | tf_op | source)
XLA Modules:
  0.0 30.4 jit_solution(3877188655509467903)
XLA Ops:
  0.6 2.8 %bias.1 = (bf16[256,128]{1,0:T(8,128)(2,1)}, bf16[256,128]{1,0:T(8,128)(2,1)}, bf16[256,128]{1,0:T(8,128)(2,1)}, bf16[256,128]{1,0:T(8,128)(2,1)}) custom-call(bf16[8,256,128]{2,1,0:T(8,128)(2,1)} %lines_ref.1, s32[1,256]{1,0:T(1,128)} %bitcast.19, f32[2,128]{1,0:T(2,128)} %gain_ref.3, f32[2,128]{1,0:T(2,128)} %shift_ref.3, bf16[2,4,128]{2,1,0:T(4,128)(2,1)} %bitcast.18), custom_call_target="tpu_custom_call" | custom-call | tf_op jit(solution)/shard_map/bias/pallas_call | solution.py:119
  3.5 5.1 %collective-permute-start = (bf16[256,128]{1,0:T(8,128)(2,1)}, bf16[256,128]{1,0:T(8,128)(2,1)S(1)}, u32[]{:S(2)}, u32[]{:S(2)}) collective-permute-start(bf16[256,128]{1,0:T(8,128)(2,1)} %get-tuple-element.11), channel_id=1, source_target_pairs={{0,24},{8,16},{16,8},{24,0},{1,25},{9,17},{17,9},{25,1},{2,26},{10... | collective-permute-start | bytes 196616 | tf_op jit(solution)/shard_map/ppermute | solution.py:440
  8.6 0.0 collective-permute-start.1
  8.6 0.7 %collective-permute-start.2 = (bf16[256,128]{1,0:T(8,128)(2,1)}, bf16[256,128]{1,0:T(8,128)(2,1)S(1)}, u32[]{:S(2)}, u32[]{:S(2)}) collective-permute-start(bf16[256,128]{1,0:T(8,128)(2,1)} %get-tuple-element.13), channel_id=1, source_target_pairs={{0,8},{8,0},{16,24},{24,16},{1,9},{9,1},{17,25},{25,17},{2,10},{10... | collective-permute-start | bytes 196616 | tf_op jit(solution)/shard_map/ppermute | solution.py:440
  9.3 0.0 copy-done.5
  9.3 0.0 copy-done.3
  9.3 0.9 %copy-done.1 = bf16[2,128,512]{2,1,0:T(8,128)(2,1)S(1)} copy-done((bf16[2,128,512]{2,1,0:T(8,128)(2,1)S(1)}, bf16[2,128,512]{2,1,0:T(8,128)(2,1)}, u32[]{:S(2)}) %copy-start.1) | copy-done | bytes 262168
  10.3 0.6 %lines.1 = (bf16[2,128,256]{2,1,0:T(8,128)(2,1)S(1)}, bf16[2,4,256,32]{3,2,1,0:T(8,128)(2,1)S(1)}, bf16[2,128,256]{2,1,0:T(8,128)(2,1)S(1)}, f32[2,128,256]{2,1,0:T(8,128)S(1)}) custom-call(bf16[8,256,128]{2,1,0:T(8,128)(2,1)S(1)} %copy-done, f32[2,128]{1,0:T(2,128)S(1)} %copy-done.3, f32[2,128]{1,0:T(2,128)S(1)} %copy-done.4, ...), custom_call_target="tpu_custom_call" | custom-call | flops 67108864 | bytes 1048576 | tf_op jit(solution)/shard_map/lines/pallas_call | solution.py:231
  10.9 0.6 %collective-permute-done = bf16[256,128]{1,0:T(8,128)(2,1)S(1)} collective-permute-done((bf16[256,128]{1,0:T(8,128)(2,1)}, bf16[256,128]{1,0:T(8,128)(2,1)S(1)}, u32[]{:S(2)}, u32[]{:S(2)}) %collective-permute-start) | collective-permute-done | bytes 65568 | tf_op jit(solution)/shard_map/ppermute | solution.py:440
  11.4 3.0 %collective-permute-done.1 = bf16[256,128]{1,0:T(8,128)(2,1)S(1)} collective-permute-done((bf16[256,128]{1,0:T(8,128)(2,1)}, bf16[256,128]{1,0:T(8,128)(2,1)S(1)}, u32[]{:S(2)}, u32[]{:S(2)}) %collective-permute-start.1) | collective-permute-done | bytes 65568 | tf_op jit(solution)/shard_map/ppermute | solution.py:440
  14.4 0.0 collective-permute-done.2
  14.5 0.1 pad_maximum_fusion.2
  14.6 1.6 %collective-permute-start.3 = (bf16[4,160,128]{2,1,0:T(8,128)(2,1)S(1)}, bf16[4,160,128]{2,1,0:T(8,128)(2,1)S(1)}, u32[]{:S(2)}, u32[]{:S(2)}) collective-permute-start(bf16[4,160,128]{2,1,0:T(8,128)(2,1)S(1)} %get-tuple-element.23), channel_id=1, source_target_pairs={{0,2},{1,3},{2,0},{3,1},{4,6},{5,7},{6,4},{7,5},{8,10},{9,11},{10,... | collective-permute-start | bytes 491528 | tf_op jit(solution)/shard_map/ppermute | solution.py:443
  16.2 1.5 %collective-permute-start.4 = (bf16[4,160,128]{2,1,0:T(8,128)(2,1)S(1)}, bf16[4,160,128]{2,1,0:T(8,128)(2,1)S(1)}, u32[]{:S(2)}, u32[]{:S(2)}) collective-permute-start(bf16[4,160,128]{2,1,0:T(8,128)(2,1)S(1)} %get-tuple-element.24), channel_id=1, source_target_pairs={{0,4},{1,5},{2,6},{3,7},{4,0},{5,1},{6,2},{7,3},{8,12},{9,13},{10,... | collective-permute-start | bytes 491528 | tf_op jit(solution)/shard_map/ppermute | solution.py:443
  17.7 0.4 %collective-permute-start.5 = (bf16[4,160,128]{2,1,0:T(8,128)(2,1)S(1)}, bf16[4,160,128]{2,1,0:T(8,128)(2,1)S(1)}, u32[]{:S(2)}, u32[]{:S(2)}) collective-permute-start(bf16[4,160,128]{2,1,0:T(8,128)(2,1)S(1)} %get-tuple-element.25), channel_id=1, source_target_pairs={{0,6},{1,7},{2,4},{3,5},{4,2},{5,3},{6,0},{7,1},{8,14},{9,15},{10,... | collective-permute-start | bytes 491528 | tf_op jit(solution)/shard_map/ppermute | solution.py:443
  18.1 3.2 %collective-permute-done.3 = bf16[4,160,128]{2,1,0:T(8,128)(2,1)S(1)} collective-permute-done((bf16[4,160,128]{2,1,0:T(8,128)(2,1)S(1)}, bf16[4,160,128]{2,1,0:T(8,128)(2,1)S(1)}, u32[]{:S(2)}, u32[]{:S(2)}) %collective-permute-start.3) | collective-permute-done | bytes 163872 | tf_op jit(solution)/shard_map/ppermute | solution.py:443
  21.3 4.0 %collective-permute-done.4 = bf16[4,160,128]{2,1,0:T(8,128)(2,1)S(1)} collective-permute-done((bf16[4,160,128]{2,1,0:T(8,128)(2,1)S(1)}, bf16[4,160,128]{2,1,0:T(8,128)(2,1)S(1)}, u32[]{:S(2)}, u32[]{:S(2)}) %collective-permute-start.4) | collective-permute-done | bytes 163872 | tf_op jit(solution)/shard_map/ppermute | solution.py:443
  25.3 0.1 pad_maximum_fusion.mine_ref
  25.4 0.0 copy-start.2
  25.4 0.0 copy-start.6
  25.4 0.1 collective-permute-start.6
  25.5 0.6 %early.1.early_ref = f32[2,128,128]{2,1,0:T(8,128)S(1)} custom-call(bf16[4,4,160,128]{3,2,1,0:T(8,128)(2,1)S(1)} %pad_maximum_fusion.mine_ref, bf16[2,128,256]{2,1,0:T(8,128)(2,1)S(1)} %get-tuple-element.15.q.q0, bf16[2,4,256,32]{3,2,1,0:T(8,128)(2,1)S(1)} %get-tuple-element.16.k.k0, bf16[2,128,256]{2,1,0:T(8,128)(2,1)S(1)} %get-tuple-element.17.v.v0), custom_call_target="tpu_custom_call" | custom-call | flops 67108864 | bytes 2097152 | tf_op jit(solution)/shard_map/early/pallas_call | solution.py:344
  26.1 1.5 %collective-permute-done.6.other_ref = bf16[4,4,160,128]{3,2,1,0:T(8,128)(2,1)S(1)} collective-permute-done((bf16[4,4,160,128]{3,2,1,0:T(8,128)(2,1)S(1)}, bf16[4,4,160,128]{3,2,1,0:T(8,128)(2,1)S(1)}, u32[]{:S(2)}, u32[]{:S(2)}) %collective-permute-start.6) | collective-permute-done | bytes 655392 | tf_op jit(solution)/shard_map/ppermute | solution.py:443
  27.6 2.8 %attend.1 = (bf16[2,256,128]{2,1,0:T(8,128)(2,1)}, bf16[2,256,128]{2,1,0:T(8,128)(2,1)}) custom-call(bf16[4,4,160,128]{3,2,1,0:T(8,128)(2,1)S(1)} %pad_maximum_fusion.mine_ref, bf16[4,4,160,128]{3,2,1,0:T(8,128)(2,1)S(1)} %collective-permute-done.6.other_ref, f32[2,128,128]{2,1,0:T(8,128)S(1)} %early.1.early_ref, ...), custom_call_target="tpu_custom_call" | custom-call | tf_op jit(solution)/shard_map/attend/pallas_call | solution.py:416
  (16 shorter events, 0.1 us)
Async XLA Ops:
  0.6 8.7 %copy-start = (bf16[8,256,128]{2,1,0:T(8,128)(2,1)S(1)}, bf16[8,256,128]{2,1,0:T(8,128)(2,1)}, u32[]{:S(2)}) copy-start(bf16[8,256,128]{2,1,0:T(8,128)(2,1)} %lines_ref.1) | copy-start | bytes 1572868
  3.5 7.9 %collective-permute-start = (bf16[256,128]{1,0:T(8,128)(2,1)}, bf16[256,128]{1,0:T(8,128)(2,1)S(1)}, u32[]{:S(2)}, u32[]{:S(2)}) collective-permute-start(bf16[256,128]{1,0:T(8,128)(2,1)} %get-tuple-element.11), channel_id=1, source_target_pairs={{0,24},{8,16},{16,8},{24,0},{1,25},{9,17},{17,9},{25,1},{2,26},{10... | collective-permute-start | bytes 196616 | tf_op jit(solution)/shard_map/ppermute | solution.py:440
  8.6 0.7 %copy-start.4 = (f32[2,128]{1,0:T(2,128)S(1)}, f32[2,128]{1,0:T(2,128)}, u32[]{:S(2)}) copy-start(f32[2,128]{1,0:T(2,128)} %shift_ref.3) | copy-start | bytes 3076
  8.6 0.7 %copy-start.5 = (f32[2,128]{1,0:T(2,128)S(1)}, f32[2,128]{1,0:T(2,128)}, u32[]{:S(2)}) copy-start(f32[2,128]{1,0:T(2,128)} %gate_ref.1) | copy-start | bytes 3076
  8.6 0.7 %copy-start.3 = (f32[2,128]{1,0:T(2,128)S(1)}, f32[2,128]{1,0:T(2,128)}, u32[]{:S(2)}) copy-start(f32[2,128]{1,0:T(2,128)} %gain_ref.3) | copy-start | bytes 3076
  8.6 5.8 %collective-permute-start.1 = (bf16[256,128]{1,0:T(8,128)(2,1)}, bf16[256,128]{1,0:T(8,128)(2,1)S(1)}, u32[]{:S(2)}, u32[]{:S(2)}) collective-permute-start(bf16[256,128]{1,0:T(8,128)(2,1)} %get-tuple-element.12), channel_id=1, source_target_pairs={{0,16},{8,24},{16,0},{24,8},{1,17},{9,25},{17,1},{25,9},{2,18},{10... | collective-permute-start | bytes 196616 | tf_op jit(solution)/shard_map/ppermute | solution.py:440
  8.6 5.8 %collective-permute-start.2 = (bf16[256,128]{1,0:T(8,128)(2,1)}, bf16[256,128]{1,0:T(8,128)(2,1)S(1)}, u32[]{:S(2)}, u32[]{:S(2)}) collective-permute-start(bf16[256,128]{1,0:T(8,128)(2,1)} %get-tuple-element.13), channel_id=1, source_target_pairs={{0,8},{8,0},{16,24},{24,16},{1,9},{9,1},{17,25},{25,17},{2,10},{10... | collective-permute-start | bytes 196616 | tf_op jit(solution)/shard_map/ppermute | solution.py:440
  9.3 0.9 %copy-start.1 = (bf16[2,128,512]{2,1,0:T(8,128)(2,1)S(1)}, bf16[2,128,512]{2,1,0:T(8,128)(2,1)}, u32[]{:S(2)}) copy-start(bf16[2,128,512]{2,1,0:T(8,128)(2,1)} %proj_ref.1) | copy-start | bytes 786436
  10.3 4.2 %copy-start.7 = (bf16[256,128]{1,0:T(8,128)(2,1)S(1)}, bf16[256,128]{1,0:T(8,128)(2,1)}, u32[]{:S(2)}) copy-start(bf16[256,128]{1,0:T(8,128)(2,1)} %get-tuple-element.14) | copy-start | bytes 196612
  14.6 6.8 %collective-permute-start.3 = (bf16[4,160,128]{2,1,0:T(8,128)(2,1)S(1)}, bf16[4,160,128]{2,1,0:T(8,128)(2,1)S(1)}, u32[]{:S(2)}, u32[]{:S(2)}) collective-permute-start(bf16[4,160,128]{2,1,0:T(8,128)(2,1)S(1)} %get-tuple-element.23), channel_id=1, source_target_pairs={{0,2},{1,3},{2,0},{3,1},{4,6},{5,7},{6,4},{7,5},{8,10},{9,11},{10,... | collective-permute-start | bytes 491528 | tf_op jit(solution)/shard_map/ppermute | solution.py:443
  16.2 9.1 %collective-permute-start.4 = (bf16[4,160,128]{2,1,0:T(8,128)(2,1)S(1)}, bf16[4,160,128]{2,1,0:T(8,128)(2,1)S(1)}, u32[]{:S(2)}, u32[]{:S(2)}) collective-permute-start(bf16[4,160,128]{2,1,0:T(8,128)(2,1)S(1)} %get-tuple-element.24), channel_id=1, source_target_pairs={{0,4},{1,5},{2,6},{3,7},{4,0},{5,1},{6,2},{7,3},{8,12},{9,13},{10,... | collective-permute-start | bytes 491528 | tf_op jit(solution)/shard_map/ppermute | solution.py:443
  17.7 7.6 %collective-permute-start.5 = (bf16[4,160,128]{2,1,0:T(8,128)(2,1)S(1)}, bf16[4,160,128]{2,1,0:T(8,128)(2,1)S(1)}, u32[]{:S(2)}, u32[]{:S(2)}) collective-permute-start(bf16[4,160,128]{2,1,0:T(8,128)(2,1)S(1)} %get-tuple-element.25), channel_id=1, source_target_pairs={{0,6},{1,7},{2,4},{3,5},{4,2},{5,3},{6,0},{7,1},{8,14},{9,15},{10,... | collective-permute-start | bytes 491528 | tf_op jit(solution)/shard_map/ppermute | solution.py:443
  25.4 2.2 %copy-start.2 = (bf16[2,128,128]{2,1,0:T(8,128)(2,1)S(1)}, bf16[2,128,128]{2,1,0:T(8,128)(2,1)}, u32[]{:S(2)}) copy-start(bf16[2,128,128]{2,1,0:T(8,128)(2,1)} %weight_ref.3) | copy-start | bytes 196612
  25.4 2.2 %copy-start.6 = (f32[2,128]{1,0:T(2,128)S(1)}, f32[2,128]{1,0:T(2,128)}, u32[]{:S(2)}) copy-start(f32[2,128]{1,0:T(2,128)} %offset_ref.3) | copy-start | bytes 3076
  25.4 2.2 %collective-permute-start.6 = (bf16[4,4,160,128]{3,2,1,0:T(8,128)(2,1)S(1)}, bf16[4,4,160,128]{3,2,1,0:T(8,128)(2,1)S(1)}, u32[]{:S(2)}, u32[]{:S(2)}) collective-permute-start(bf16[4,4,160,128]{3,2,1,0:T(8,128)(2,1)S(1)} %pad_maximum_fusion.mine_ref), channel_id=1, source_target_pairs={{0,1},{1,0},{2,3},{3,2},{4,5},{5,4},{6,7},{7,6},{8,9},{9,8},{10,11... | collective-permute-start | bytes 1966088 | tf_op jit(solution)/shard_map/ppermute | solution.py:443

commit v10 on v9

--- a/solution.py
+++ b/solution.py
@@ -51,32 +51,32 @@
 
 def bias_kernel(along, chips, pair_hbm, live_hbm, gain_hbm, shift_hbm, weight_hbm, *rest):
     outs = rest[:along]
-    pair, live_row, live_each, gain, shift, weight, blocks, rows_out, wide, picked, sems, pair_sems = rest[along:]
+    pair, live_row, gain, shift, weight, blocks, rows_out, wide, picked, sems = rest[along:]
     rows, length, channels = pair.shape
     heads = weight.shape[1]
     lanes = outs[0].shape[1]
-    small = [
+    copies = [
         pltpu.make_async_copy(source, target, sems.at[i])
         for i, (source, target) in enumerate(
-            ((live_hbm, live_row), (live_hbm, live_each), (gain_hbm, gain), (shift_hbm, shift), (weight_hbm, weight))
+            ((pair_hbm, pair), (live_hbm, live_row), (gain_hbm, gain), (shift_hbm, shift), (weight_hbm, weight))
         )
     ]
-    large = [pltpu.make_async_copy(pair_hbm.at[a], pair.at[a], pair_sems.at[a]) for a in range(rows)]
-    large[0].start()
-    for copy in small:
-        copy.start()
-    for copy in large[1:]:
+    for copy in copies:
         copy.start()
     device = lax.axis_index("row") * lax.axis_size("col") + lax.axis_index("col")
-    for copy in small + large:
+    for copy in copies:
         copy.wait()
     blocks[...] = jnp.zeros_like(blocks)
     for p in range(2):
         at = slice(p * heads, (p + 1) * heads)
         blocks[at, p * channels : (p + 1) * channels] = weight[p].astype(jnp.float32)
     paired = blocks[: 2 * heads].astype(jnp.bfloat16)
-    live = jnp.broadcast_to(live_row[...], (2 * heads, length))
+    live = jnp.broadcast_to(live_row[...], (2 * heads, length)).astype(jnp.float32)
     first = lax.broadcasted_iota(jnp.int32, live.shape, 0) < heads
+    token = lax.broadcasted_iota(jnp.int32, (rows, length), 1)
+    mine = device * rows + lax.broadcasted_iota(jnp.int32, (rows, length), 0)
+    here = jnp.where(token == mine, live_row[...], 0).astype(jnp.float32)
+    here = jnp.sum(here, 1, keepdims=True)
     lines = [pair[a].astype(jnp.float32) for a in range(rows)]
     for a, x in enumerate(lines):
         wide[a] = x
@@ -94,7 +94,7 @@
             column = wide[a, pl.ds(w, devices, stride=rows), :]
             picked[pl.ds(w * rows + a, devices, stride=WD * rows), :] = column
     for a, bias in enumerate(biases):
-        kept = jnp.where(first, live, live_each[0, device * rows + a])
+        kept = jnp.where(first, live, here[a : a + 1])
         bias = jnp.where(kept > 0, bias, MASKED)
         for lane in range(length // lanes):
             part = bias[:, lane * lanes : (lane + 1) * lanes]
@@ -124,7 +124,6 @@
         scratch_shapes=[
             pltpu.VMEM(pair.shape, pair.dtype),
             pltpu.VMEM(live.shape, live.dtype),
-            pltpu.SMEM(live.shape, live.dtype),
             pltpu.VMEM(gain.shape, gain.dtype),
             pltpu.VMEM(shift.shape, shift.dtype),
             pltpu.VMEM(weight.shape, weight.dtype),
@@ -133,7 +132,6 @@
             pltpu.VMEM(pair.shape, jnp.float32),
             pltpu.VMEM((length * WD, channels), jnp.float32),
             pltpu.SemaphoreType.DMA((5,)),
-            pltpu.SemaphoreType.DMA((rows,)),
         ],
         compiler_params=params(60),
         name="bias",
@@ -360,7 +358,7 @@
 def attend_kernel(
     mine_ref, other_ref, early_ref, q0, k0, v0, g0,
     gain_ref, shift_ref, proj_ref, gate_ref, weight_ref, offset_ref,
-    out0, out1, turned_bias, bias, late, mixed, q1, k1, v1, g1,
+    out0, out1, turned_bias, bias, late, mixed, kept, sem, q1, k1, v1, g1,
 ):
     chips, along, _, _ = mine_ref.shape
     _, heads, length, size = k0.shape
@@ -381,6 +379,19 @@
     ordered = [to_devices(line, along, chips, rows).astype(jnp.bfloat16) for line in lines]
     queries_and_gates(ordered, size ** (-0.5), proj_ref[1], offset, q1, g1)
     groups = start_half(other_ref, 1, q0, k0, v0, late, turned_bias)
+    leaving = pltpu.make_async_copy(kept, out0, sem)
+
+    def finish_start():
+        for w in range(WD):
+            gated = (jnp.concatenate([early_ref[w], late[w]], 1) * g0[w]).astype(jnp.bfloat16)
+            full = contract(gated, weight_ref[0], 0, 0) + offset_ref[0:1, :]
+            kept[w] = to_devices(full, along, chips, rows).astype(jnp.bfloat16)
+        leaving.start()
+
+    if groups:
+        groups[-1] = (groups[-1][0], lambda outs, put=groups[-1][1]: (put(outs), finish_start()))
+    else:
+        finish_start()
     for pack in range(heads // 2):
         unpack(mine_ref, 1, pack, rows, heads, 0, bias, 0)
         unpack(other_ref, 1, pack, rows, heads, 0, bias, half)
@@ -399,13 +410,10 @@
         for_each(length // CHUNK, step, False)
     attend_groups(groups)
     for w in range(WD):
-        gated = (jnp.concatenate([early_ref[w], late[w]], 1) * g0[w]).astype(jnp.bfloat16)
-        full = contract(gated, weight_ref[0], 0, 0) + offset_ref[0:1, :]
-        out0[w] = to_devices(full, along, chips, rows).astype(jnp.bfloat16)
-    for w in range(WD):
         gated = (mixed[w] * g1[w]).astype(jnp.bfloat16)
         full = contract(gated, weight_ref[1], 0, 0) + offset_ref[1:2, :]
         out1[w] = full.astype(jnp.bfloat16)
+    leaving.wait()
 
 
 def attend(mine, other, early, start, gain, shift, proj, gate, weight, offset):
@@ -417,12 +425,14 @@
         attend_kernel,
         out_shape=(result, result),
         in_specs=[VMEM] * 13,
-        out_specs=(VMEM, VMEM),
+        out_specs=(HBM, VMEM),
         scratch_shapes=[
             pltpu.VMEM((slots, length, length // 2), jnp.float32),
             pltpu.VMEM((slots, length, length), jnp.float32),
             pltpu.VMEM((WD, inner, length // 2), jnp.float32),
             pltpu.VMEM((WD, inner, length), jnp.float32),
+            pltpu.VMEM((WD, length, channels), jnp.bfloat16),
+            pltpu.SemaphoreType.DMA(()),
         ]
         + [pltpu.VMEM(shape, dtype) for shape, dtype in projected(length, inner, heads)],
         compiler_params=params(16 if length <= CHUNK else 60),

time: 30.6 us -> 31 us (1.013)
  Pallas kernels: 6.83 us -> 7.26 us
    pallas_call x1, Pallas kernels: 2.79 us -> 3.33 us  [attend(): pl.pallas_call(attend_kernel, out_shape=(result, result), in_specs=[VMEM]...]
where the time goes in v10:
time: 31 us; the launch traced here: 30.8 us
  waiting for transfers between devices  12.2 us (39%)
  starting transfers between devices  9.4 us (30%)
  Pallas kernels  7.26 us (23%)
  local copies, waits for them, and re-layouts  1.03 us (3%)
  between operations  0.74 us (2%)
    ppermute x4, waiting for transfers between devices, by_col(): return lax.ppermute(block, 'col', [(i, i ^ flip) for i in range(cols)])  8.62 us
    ppermute x3, starting transfers between devices, by_row(): return lax.ppermute(block, 'row', [(i, i ^ shift) for i in range(along)])  5.78 us
    ppermute x4, starting transfers between devices, by_col(): return lax.ppermute(block, 'col', [(i, i ^ flip) for i in range(cols)])  3.62 us
    ppermute x3, waiting for transfers between devices, by_row(): return lax.ppermute(block, 'row', [(i, i ^ shift) for i in range(along)])  3.56 us
    pallas_call x1, Pallas kernels, attend(): pl.pallas_call(attend_kernel, out_shape=(result, result), in_specs=[VMEM]...  3.33 us
    pallas_call x1, Pallas kernels, local_bias(): pl.pallas_call(functools.partial(bias_kernel, along, chips), out_shape=(s...  2.73 us
    unnamed x16, local copies, waits for them, and re-layouts  1 us
    pallas_call x1, Pallas kernels, attend_early(): pl.pallas_call(early_kernel, out_shape=jax.ShapeDtypeStruct((WD, heads *...  0.62 us
  transfers between devices with their start and end apart: 7, of which 5 were waited for; matrix products, arithmetic and copies ran while one was open for 0% of the time, Pallas kernels for 4%

profile of v10, /device:TPU:0, one launch (start us, length us, event | category | flops | bytes accessed | tf_op | source)
XLA Modules:
  0.0 30.8 jit_solution(2221045672741577185)
XLA Ops:
  0.6 2.7 %bias.1 = (bf16[256,128]{1,0:T(8,128)(2,1)}, bf16[256,128]{1,0:T(8,128)(2,1)}, bf16[256,128]{1,0:T(8,128)(2,1)}, bf16[256,128]{1,0:T(8,128)(2,1)}) custom-call(bf16[8,256,128]{2,1,0:T(8,128)(2,1)} %lines_ref.1, s32[1,256]{1,0:T(1,128)} %bitcast.19, f32[2,128]{1,0:T(2,128)} %gain_ref.3, f32[2,128]{1,0:T(2,128)} %shift_ref.3, bf16[2,4,128]{2,1,0:T(4,128)(2,1)} %bitcast.18), custom_call_target="tpu_custom_call" | custom-call | tf_op jit(solution)/shard_map/bias/pallas_call | solution.py:119
  3.4 5.1 %collective-permute-start = (bf16[256,128]{1,0:T(8,128)(2,1)}, bf16[256,128]{1,0:T(8,128)(2,1)S(1)}, u32[]{:S(2)}, u32[]{:S(2)}) collective-permute-start(bf16[256,128]{1,0:T(8,128)(2,1)} %get-tuple-element.11), channel_id=1, source_target_pairs={{0,24},{8,16},{16,8},{24,0},{1,25},{9,17},{17,9},{25,1},{2,26},{10... | collective-permute-start | bytes 196616 | tf_op jit(solution)/shard_map/ppermute | solution.py:450
  8.5 0.0 collective-permute-start.1
  8.5 0.7 %collective-permute-start.2 = (bf16[256,128]{1,0:T(8,128)(2,1)}, bf16[256,128]{1,0:T(8,128)(2,1)S(1)}, u32[]{:S(2)}, u32[]{:S(2)}) collective-permute-start(bf16[256,128]{1,0:T(8,128)(2,1)} %get-tuple-element.13), channel_id=1, source_target_pairs={{0,8},{8,0},{16,24},{24,16},{1,9},{9,1},{17,25},{25,17},{2,10},{10... | collective-permute-start | bytes 196616 | tf_op jit(solution)/shard_map/ppermute | solution.py:450
  9.2 0.0 copy-done.5
  9.2 0.0 copy-done.3
  9.2 0.9 %copy-done.1 = bf16[2,128,512]{2,1,0:T(8,128)(2,1)S(1)} copy-done((bf16[2,128,512]{2,1,0:T(8,128)(2,1)S(1)}, bf16[2,128,512]{2,1,0:T(8,128)(2,1)}, u32[]{:S(2)}) %copy-start.1) | copy-done | bytes 262168
  10.2 0.6 %lines.1 = (bf16[2,128,256]{2,1,0:T(8,128)(2,1)S(1)}, bf16[2,4,256,32]{3,2,1,0:T(8,128)(2,1)S(1)}, bf16[2,128,256]{2,1,0:T(8,128)(2,1)S(1)}, f32[2,128,256]{2,1,0:T(8,128)S(1)}) custom-call(bf16[8,256,128]{2,1,0:T(8,128)(2,1)S(1)} %copy-done, f32[2,128]{1,0:T(2,128)S(1)} %copy-done.3, f32[2,128]{1,0:T(2,128)S(1)} %copy-done.4, ...), custom_call_target="tpu_custom_call" | custom-call | flops 67108864 | bytes 1048576 | tf_op jit(solution)/shard_map/lines/pallas_call | solution.py:229
  10.7 0.6 %collective-permute-done = bf16[256,128]{1,0:T(8,128)(2,1)S(1)} collective-permute-done((bf16[256,128]{1,0:T(8,128)(2,1)}, bf16[256,128]{1,0:T(8,128)(2,1)S(1)}, u32[]{:S(2)}, u32[]{:S(2)}) %collective-permute-start) | collective-permute-done | bytes 65568 | tf_op jit(solution)/shard_map/ppermute | solution.py:450
  11.3 3.0 %collective-permute-done.1 = bf16[256,128]{1,0:T(8,128)(2,1)S(1)} collective-permute-done((bf16[256,128]{1,0:T(8,128)(2,1)}, bf16[256,128]{1,0:T(8,128)(2,1)S(1)}, u32[]{:S(2)}, u32[]{:S(2)}) %collective-permute-start.1) | collective-permute-done | bytes 65568 | tf_op jit(solution)/shard_map/ppermute | solution.py:450
  14.4 0.1 pad_maximum_fusion.2
  14.5 1.6 %collective-permute-start.3 = (bf16[4,160,128]{2,1,0:T(8,128)(2,1)S(1)}, bf16[4,160,128]{2,1,0:T(8,128)(2,1)S(1)}, u32[]{:S(2)}, u32[]{:S(2)}) collective-permute-start(bf16[4,160,128]{2,1,0:T(8,128)(2,1)S(1)} %get-tuple-element.23), channel_id=1, source_target_pairs={{0,2},{1,3},{2,0},{3,1},{4,6},{5,7},{6,4},{7,5},{8,10},{9,11},{10,... | collective-permute-start | bytes 491528 | tf_op jit(solution)/shard_map/ppermute | solution.py:453
  16.1 1.5 %collective-permute-start.4 = (bf16[4,160,128]{2,1,0:T(8,128)(2,1)S(1)}, bf16[4,160,128]{2,1,0:T(8,128)(2,1)S(1)}, u32[]{:S(2)}, u32[]{:S(2)}) collective-permute-start(bf16[4,160,128]{2,1,0:T(8,128)(2,1)S(1)} %get-tuple-element.24), channel_id=1, source_target_pairs={{0,4},{1,5},{2,6},{3,7},{4,0},{5,1},{6,2},{7,3},{8,12},{9,13},{10,... | collective-permute-start | bytes 491528 | tf_op jit(solution)/shard_map/ppermute | solution.py:453
  17.6 0.4 %collective-permute-start.5 = (bf16[4,160,128]{2,1,0:T(8,128)(2,1)S(1)}, bf16[4,160,128]{2,1,0:T(8,128)(2,1)S(1)}, u32[]{:S(2)}, u32[]{:S(2)}) collective-permute-start(bf16[4,160,128]{2,1,0:T(8,128)(2,1)S(1)} %get-tuple-element.25), channel_id=1, source_target_pairs={{0,6},{1,7},{2,4},{3,5},{4,2},{5,3},{6,0},{7,1},{8,14},{9,15},{10,... | collective-permute-start | bytes 491528 | tf_op jit(solution)/shard_map/ppermute | solution.py:453
  18.0 3.2 %collective-permute-done.3 = bf16[4,160,128]{2,1,0:T(8,128)(2,1)S(1)} collective-permute-done((bf16[4,160,128]{2,1,0:T(8,128)(2,1)S(1)}, bf16[4,160,128]{2,1,0:T(8,128)(2,1)S(1)}, u32[]{:S(2)}, u32[]{:S(2)}) %collective-permute-start.3) | collective-permute-done | bytes 163872 | tf_op jit(solution)/shard_map/ppermute | solution.py:453
  21.2 4.0 %collective-permute-done.4 = bf16[4,160,128]{2,1,0:T(8,128)(2,1)S(1)} collective-permute-done((bf16[4,160,128]{2,1,0:T(8,128)(2,1)S(1)}, bf16[4,160,128]{2,1,0:T(8,128)(2,1)S(1)}, u32[]{:S(2)}, u32[]{:S(2)}) %collective-permute-start.4) | collective-permute-done | bytes 163872 | tf_op jit(solution)/shard_map/ppermute | solution.py:453
  25.2 0.0 collective-permute-done.5
  25.2 0.1 pad_maximum_fusion.mine_ref
  25.3 0.0 copy-start.2
  25.3 0.0 copy-start.6
  25.3 0.1 collective-permute-start.6
  25.4 0.6 %early.1.early_ref = f32[2,128,128]{2,1,0:T(8,128)S(1)} custom-call(bf16[4,4,160,128]{3,2,1,0:T(8,128)(2,1)S(1)} %pad_maximum_fusion.mine_ref, bf16[2,128,256]{2,1,0:T(8,128)(2,1)S(1)} %get-tuple-element.15.q.q0, bf16[2,4,256,32]{3,2,1,0:T(8,128)(2,1)S(1)} %get-tuple-element.16.k.k0, bf16[2,128,256]{2,1,0:T(8,128)(2,1)S(1)} %get-tuple-element.17.v.v0), custom_call_target="tpu_custom_call" | custom-call | flops 67108864 | bytes 2097152 | tf_op jit(solution)/shard_map/early/pallas_call | solution.py:342
  26.0 1.5 %collective-permute-done.6.other_ref = bf16[4,4,160,128]{3,2,1,0:T(8,128)(2,1)S(1)} collective-permute-done((bf16[4,4,160,128]{3,2,1,0:T(8,128)(2,1)S(1)}, bf16[4,4,160,128]{3,2,1,0:T(8,128)(2,1)S(1)}, u32[]{:S(2)}, u32[]{:S(2)}) %collective-permute-start.6) | collective-permute-done | bytes 655392 | tf_op jit(solution)/shard_map/ppermute | solution.py:453
  27.5 3.3 %attend.1 = (bf16[2,256,128]{2,1,0:T(8,128)(2,1)}, bf16[2,256,128]{2,1,0:T(8,128)(2,1)}) custom-call(bf16[4,4,160,128]{3,2,1,0:T(8,128)(2,1)S(1)} %pad_maximum_fusion.mine_ref, bf16[4,4,160,128]{3,2,1,0:T(8,128)(2,1)S(1)} %collective-permute-done.6.other_ref, f32[2,128,128]{2,1,0:T(8,128)S(1)} %early.1.early_ref, ...), custom_call_target="tpu_custom_call" | custom-call | tf_op jit(solution)/shard_map/attend/pallas_call | solution.py:424
  (16 shorter events, 0.1 us)
Async XLA Ops:
  0.6 8.5 %copy-start = (bf16[8,256,128]{2,1,0:T(8,128)(2,1)S(1)}, bf16[8,256,128]{2,1,0:T(8,128)(2,1)}, u32[]{:S(2)}) copy-start(bf16[8,256,128]{2,1,0:T(8,128)(2,1)} %lines_ref.1) | copy-start | bytes 1572868
  3.4 7.9 %collective-permute-start = (bf16[256,128]{1,0:T(8,128)(2,1)}, bf16[256,128]{1,0:T(8,128)(2,1)S(1)}, u32[]{:S(2)}, u32[]{:S(2)}) collective-permute-start(bf16[256,128]{1,0:T(8,128)(2,1)} %get-tuple-element.11), channel_id=1, source_target_pairs={{0,24},{8,16},{16,8},{24,0},{1,25},{9,17},{17,9},{25,1},{2,26},{10... | collective-permute-start | bytes 196616 | tf_op jit(solution)/shard_map/ppermute | solution.py:450
  8.5 0.7 %copy-start.4 = (f32[2,128]{1,0:T(2,128)S(1)}, f32[2,128]{1,0:T(2,128)}, u32[]{:S(2)}) copy-start(f32[2,128]{1,0:T(2,128)} %shift_ref.3) | copy-start | bytes 3076
  8.5 0.7 %copy-start.5 = (f32[2,128]{1,0:T(2,128)S(1)}, f32[2,128]{1,0:T(2,128)}, u32[]{:S(2)}) copy-start(f32[2,128]{1,0:T(2,128)} %gate_ref.1) | copy-start | bytes 3076
  8.5 0.7 %copy-start.3 = (f32[2,128]{1,0:T(2,128)S(1)}, f32[2,128]{1,0:T(2,128)}, u32[]{:S(2)}) copy-start(f32[2,128]{1,0:T(2,128)} %gain_ref.3) | copy-start | bytes 3076
  8.5 5.8 %collective-permute-start.1 = (bf16[256,128]{1,0:T(8,128)(2,1)}, bf16[256,128]{1,0:T(8,128)(2,1)S(1)}, u32[]{:S(2)}, u32[]{:S(2)}) collective-permute-start(bf16[256,128]{1,0:T(8,128)(2,1)} %get-tuple-element.12), channel_id=1, source_target_pairs={{0,16},{8,24},{16,0},{24,8},{1,17},{9,25},{17,1},{25,9},{2,18},{10... | collective-permute-start | bytes 196616 | tf_op jit(solution)/shard_map/ppermute | solution.py:450
  8.5 5.8 %collective-permute-start.2 = (bf16[256,128]{1,0:T(8,128)(2,1)}, bf16[256,128]{1,0:T(8,128)(2,1)S(1)}, u32[]{:S(2)}, u32[]{:S(2)}) collective-permute-start(bf16[256,128]{1,0:T(8,128)(2,1)} %get-tuple-element.13), channel_id=1, source_target_pairs={{0,8},{8,0},{16,24},{24,16},{1,9},{9,1},{17,25},{25,17},{2,10},{10... | collective-permute-start | bytes 196616 | tf_op jit(solution)/shard_map/ppermute | solution.py:450
  9.2 0.9 %copy-start.1 = (bf16[2,128,512]{2,1,0:T(8,128)(2,1)S(1)}, bf16[2,128,512]{2,1,0:T(8,128)(2,1)}, u32[]{:S(2)}) copy-start(bf16[2,128,512]{2,1,0:T(8,128)(2,1)} %proj_ref.1) | copy-start | bytes 786436
  10.1 4.2 %copy-start.7 = (bf16[256,128]{1,0:T(8,128)(2,1)S(1)}, bf16[256,128]{1,0:T(8,128)(2,1)}, u32[]{:S(2)}) copy-start(bf16[256,128]{1,0:T(8,128)(2,1)} %get-tuple-element.14) | copy-start | bytes 196612
  14.5 6.8 %collective-permute-start.3 = (bf16[4,160,128]{2,1,0:T(8,128)(2,1)S(1)}, bf16[4,160,128]{2,1,0:T(8,128)(2,1)S(1)}, u32[]{:S(2)}, u32[]{:S(2)}) collective-permute-start(bf16[4,160,128]{2,1,0:T(8,128)(2,1)S(1)} %get-tuple-element.23), channel_id=1, source_target_pairs={{0,2},{1,3},{2,0},{3,1},{4,6},{5,7},{6,4},{7,5},{8,10},{9,11},{10,... | collective-permute-start | bytes 491528 | tf_op jit(solution)/shard_map/ppermute | solution.py:453
  16.1 9.1 %collective-permute-start.4 = (bf16[4,160,128]{2,1,0:T(8,128)(2,1)S(1)}, bf16[4,160,128]{2,1,0:T(8,128)(2,1)S(1)}, u32[]{:S(2)}, u32[]{:S(2)}) collective-permute-start(bf16[4,160,128]{2,1,0:T(8,128)(2,1)S(1)} %get-tuple-element.24), channel_id=1, source_target_pairs={{0,4},{1,5},{2,6},{3,7},{4,0},{5,1},{6,2},{7,3},{8,12},{9,13},{10,... | collective-permute-start | bytes 491528 | tf_op jit(solution)/shard_map/ppermute | solution.py:453
  17.6 7.6 %collective-permute-start.5 = (bf16[4,160,128]{2,1,0:T(8,128)(2,1)S(1)}, bf16[4,160,128]{2,1,0:T(8,128)(2,1)S(1)}, u32[]{:S(2)}, u32[]{:S(2)}) collective-permute-start(bf16[4,160,128]{2,1,0:T(8,128)(2,1)S(1)} %get-tuple-element.25), channel_id=1, source_target_pairs={{0,6},{1,7},{2,4},{3,5},{4,2},{5,3},{6,0},{7,1},{8,14},{9,15},{10,... | collective-permute-start | bytes 491528 | tf_op jit(solution)/shard_map/ppermute | solution.py:453
  25.3 2.2 %copy-start.2 = (bf16[2,128,128]{2,1,0:T(8,128)(2,1)S(1)}, bf16[2,128,128]{2,1,0:T(8,128)(2,1)}, u32[]{:S(2)}) copy-start(bf16[2,128,128]{2,1,0:T(8,128)(2,1)} %weight_ref.3) | copy-start | bytes 196612
  25.3 2.2 %copy-start.6 = (f32[2,128]{1,0:T(2,128)S(1)}, f32[2,128]{1,0:T(2,128)}, u32[]{:S(2)}) copy-start(f32[2,128]{1,0:T(2,128)} %offset_ref.3) | copy-start | bytes 3076
  25.3 2.2 %collective-permute-start.6 = (bf16[4,4,160,128]{3,2,1,0:T(8,128)(2,1)S(1)}, bf16[4,4,160,128]{3,2,1,0:T(8,128)(2,1)S(1)}, u32[]{:S(2)}, u32[]{:S(2)}) collective-permute-start(bf16[4,4,160,128]{3,2,1,0:T(8,128)(2,1)S(1)} %pad_maximum_fusion.mine_ref), channel_id=1, source_target_pairs={{0,1},{1,0},{2,3},{3,2},{4,5},{5,4},{6,7},{7,6},{8,9},{9,8},{10,11... | collective-permute-start | bytes 1966088 | tf_op jit(solution)/shard_map/ppermute | solution.py:453

commit v11 on v10

--- a/solution.py
+++ b/solution.py
@@ -277,10 +277,11 @@
     return [contract(unit[3], weight, 1, 0) for unit, weight in zip(units, weights)]
 
 
-def attend_groups(groups):
+def attend_groups(groups, ready=None):
     if not groups:
         return
-    ready = score(groups[0][0]())
+    if ready is None:
+        ready = score(groups[0][0]())
     for i, (units, put) in enumerate(groups):
         ahead = score(groups[i + 1][0]()) if i + 1 < len(groups) else None
         put(mix(units(), ready))
@@ -358,7 +359,7 @@
 def attend_kernel(
     mine_ref, other_ref, early_ref, q0, k0, v0, g0,
     gain_ref, shift_ref, proj_ref, gate_ref, weight_ref, offset_ref,
-    out0, out1, turned_bias, bias, late, mixed, kept, sem, q1, k1, v1, g1,
+    out0, out1, turned_bias, bias, late, mixed, q1, k1, v1, g1,
 ):
     chips, along, _, _ = mine_ref.shape
     _, heads, length, size = k0.shape
@@ -366,6 +367,8 @@
     rows = half // (chips * along)
     packed = 2 * heads * rows * (length // mine_ref.shape[3])
     first = pl.multiple_of(packed + lax.rem(lax.axis_index("col"), 2) * WD * rows, WD * rows)
+    groups = start_half(other_ref, 1, q0, k0, v0, late, turned_bias)
+    ready = score(groups[0][0]()) if groups else None
     offset = turned(gate_ref[1:2, :])
     blocks = []
     for source in (mine_ref, other_ref):
@@ -378,20 +381,6 @@
     keys_and_values([line.astype(jnp.bfloat16) for line in lines], proj_ref[1], k1, v1)
     ordered = [to_devices(line, along, chips, rows).astype(jnp.bfloat16) for line in lines]
     queries_and_gates(ordered, size ** (-0.5), proj_ref[1], offset, q1, g1)
-    groups = start_half(other_ref, 1, q0, k0, v0, late, turned_bias)
-    leaving = pltpu.make_async_copy(kept, out0, sem)
-
-    def finish_start():
-        for w in range(WD):
-            gated = (jnp.concatenate([early_ref[w], late[w]], 1) * g0[w]).astype(jnp.bfloat16)
-            full = contract(gated, weight_ref[0], 0, 0) + offset_ref[0:1, :]
-            kept[w] = to_devices(full, along, chips, rows).astype(jnp.bfloat16)
-        leaving.start()
-
-    if groups:
-        groups[-1] = (groups[-1][0], lambda outs, put=groups[-1][1]: (put(outs), finish_start()))
-    else:
-        finish_start()
     for pack in range(heads // 2):
         unpack(mine_ref, 1, pack, rows, heads, 0, bias, 0)
         unpack(other_ref, 1, pack, rows, heads, 0, bias, half)
@@ -408,12 +397,15 @@
                 attend_groups([head_group((h,), size, q1, k1, v1, bias, mixed, there, there)])
 
         for_each(length // CHUNK, step, False)
-    attend_groups(groups)
+    attend_groups(groups, ready)
+    for w in range(WD):
+        gated = (jnp.concatenate([early_ref[w], late[w]], 1) * g0[w]).astype(jnp.bfloat16)
+        full = contract(gated, weight_ref[0], 0, 0) + offset_ref[0:1, :]
+        out0[w] = to_devices(full, along, chips, rows).astype(jnp.bfloat16)
     for w in range(WD):
         gated = (mixed[w] * g1[w]).astype(jnp.bfloat16)
         full = contract(gated, weight_ref[1], 0, 0) + offset_ref[1:2, :]
         out1[w] = full.astype(jnp.bfloat16)
-    leaving.wait()
 
 
 def attend(mine, other, early, start, gain, shift, proj, gate, weight, offset):
@@ -425,14 +417,12 @@
         attend_kernel,
         out_shape=(result, result),
         in_specs=[VMEM] * 13,
-        out_specs=(HBM, VMEM),
+        out_specs=(VMEM, VMEM),
         scratch_shapes=[
             pltpu.VMEM((slots, length, length // 2), jnp.float32),
             pltpu.VMEM((slots, length, length), jnp.float32),
             pltpu.VMEM((WD, inner, length // 2), jnp.float32),
             pltpu.VMEM((WD, inner, length), jnp.float32),
-            pltpu.VMEM((WD, length, channels), jnp.bfloat16),
-            pltpu.SemaphoreType.DMA(()),
         ]
         + [pltpu.VMEM(shape, dtype) for shape, dtype in projected(length, inner, heads)],
         compiler_params=params(16 if length <= CHUNK else 60),

time: 31 us -> 30.4 us (0.981)
  Pallas kernels: 7.26 us -> 6.63 us
    pallas_call x1, Pallas kernels: 3.33 us -> 2.7 us  [attend(): pl.pallas_call(attend_kernel, out_shape=(result, result), in_specs=[VMEM]...]
where the time goes in v11:
time: 30.4 us; the launch traced here: 30.2 us
  waiting for transfers between devices  12.2 us (40%)
  starting transfers between devices  9.4 us (31%)
  Pallas kernels  6.63 us (22%)
  local copies, waits for them, and re-layouts  1.03 us (3%)
  between operations  0.74 us (2%)
    ppermute x4, waiting for transfers between devices, by_col(): return lax.ppermute(block, 'col', [(i, i ^ flip) for i in range(cols)])  8.62 us
    ppermute x3, starting transfers between devices, by_row(): return lax.ppermute(block, 'row', [(i, i ^ shift) for i in range(along)])  5.78 us
    ppermute x4, starting transfers between devices, by_col(): return lax.ppermute(block, 'col', [(i, i ^ flip) for i in range(cols)])  3.62 us
    ppermute x3, waiting for transfers between devices, by_row(): return lax.ppermute(block, 'row', [(i, i ^ shift) for i in range(along)])  3.56 us
    pallas_call x1, Pallas kernels, local_bias(): pl.pallas_call(functools.partial(bias_kernel, along, chips), out_shape=(s...  2.73 us
    pallas_call x1, Pallas kernels, attend(): pl.pallas_call(attend_kernel, out_shape=(result, result), in_specs=[VMEM]...  2.7 us
    unnamed x16, local copies, waits for them, and re-layouts  1 us
    pallas_call x1, Pallas kernels, attend_early(): pl.pallas_call(early_kernel, out_shape=jax.ShapeDtypeStruct((WD, heads *...  0.62 us
  transfers between devices with their start and end apart: 7, of which 5 were waited for; matrix products, arithmetic and copies ran while one was open for 0% of the time, Pallas kernels for 4%

profile of v11, /device:TPU:0, one launch (start us, length us, event | category | flops | bytes accessed | tf_op | source)
XLA Modules:
  0.0 30.2 jit_solution(5679392995826115751)
XLA Ops:
  0.6 2.7 %bias.1 = (bf16[256,128]{1,0:T(8,128)(2,1)}, bf16[256,128]{1,0:T(8,128)(2,1)}, bf16[256,128]{1,0:T(8,128)(2,1)}, bf16[256,128]{1,0:T(8,128)(2,1)}) custom-call(bf16[8,256,128]{2,1,0:T(8,128)(2,1)} %lines_ref.1, s32[1,256]{1,0:T(1,128)} %bitcast.19, f32[2,128]{1,0:T(2,128)} %gain_ref.3, f32[2,128]{1,0:T(2,128)} %shift_ref.3, bf16[2,4,128]{2,1,0:T(4,128)(2,1)} %bitcast.18), custom_call_target="tpu_custom_call" | custom-call | tf_op jit(solution)/shard_map/bias/pallas_call | solution.py:119
  3.4 5.1 %collective-permute-start = (bf16[256,128]{1,0:T(8,128)(2,1)}, bf16[256,128]{1,0:T(8,128)(2,1)S(1)}, u32[]{:S(2)}, u32[]{:S(2)}) collective-permute-start(bf16[256,128]{1,0:T(8,128)(2,1)} %get-tuple-element.11), channel_id=1, source_target_pairs={{0,24},{8,16},{16,8},{24,0},{1,25},{9,17},{17,9},{25,1},{2,26},{10... | collective-permute-start | bytes 196616 | tf_op jit(solution)/shard_map/ppermute | solution.py:440
  8.5 0.0 collective-permute-start.1
  8.5 0.7 %collective-permute-start.2 = (bf16[256,128]{1,0:T(8,128)(2,1)}, bf16[256,128]{1,0:T(8,128)(2,1)S(1)}, u32[]{:S(2)}, u32[]{:S(2)}) collective-permute-start(bf16[256,128]{1,0:T(8,128)(2,1)} %get-tuple-element.13), channel_id=1, source_target_pairs={{0,8},{8,0},{16,24},{24,16},{1,9},{9,1},{17,25},{25,17},{2,10},{10... | collective-permute-start | bytes 196616 | tf_op jit(solution)/shard_map/ppermute | solution.py:440
  9.2 0.0 copy-done.5
  9.2 0.0 copy-done.3
  9.2 0.9 %copy-done.1 = bf16[2,128,512]{2,1,0:T(8,128)(2,1)S(1)} copy-done((bf16[2,128,512]{2,1,0:T(8,128)(2,1)S(1)}, bf16[2,128,512]{2,1,0:T(8,128)(2,1)}, u32[]{:S(2)}) %copy-start.1) | copy-done | bytes 262168
  10.2 0.6 %lines.1 = (bf16[2,128,256]{2,1,0:T(8,128)(2,1)S(1)}, bf16[2,4,256,32]{3,2,1,0:T(8,128)(2,1)S(1)}, bf16[2,128,256]{2,1,0:T(8,128)(2,1)S(1)}, f32[2,128,256]{2,1,0:T(8,128)S(1)}) custom-call(bf16[8,256,128]{2,1,0:T(8,128)(2,1)S(1)} %copy-done, f32[2,128]{1,0:T(2,128)S(1)} %copy-done.3, f32[2,128]{1,0:T(2,128)S(1)} %copy-done.4, ...), custom_call_target="tpu_custom_call" | custom-call | flops 67108864 | bytes 1048576 | tf_op jit(solution)/shard_map/lines/pallas_call | solution.py:229
  10.7 0.6 %collective-permute-done = bf16[256,128]{1,0:T(8,128)(2,1)S(1)} collective-permute-done((bf16[256,128]{1,0:T(8,128)(2,1)}, bf16[256,128]{1,0:T(8,128)(2,1)S(1)}, u32[]{:S(2)}, u32[]{:S(2)}) %collective-permute-start) | collective-permute-done | bytes 65568 | tf_op jit(solution)/shard_map/ppermute | solution.py:440
  11.3 3.0 %collective-permute-done.1 = bf16[256,128]{1,0:T(8,128)(2,1)S(1)} collective-permute-done((bf16[256,128]{1,0:T(8,128)(2,1)}, bf16[256,128]{1,0:T(8,128)(2,1)S(1)}, u32[]{:S(2)}, u32[]{:S(2)}) %collective-permute-start.1) | collective-permute-done | bytes 65568 | tf_op jit(solution)/shard_map/ppermute | solution.py:440
  14.3 0.0 collective-permute-done.2
  14.4 0.1 pad_maximum_fusion.2
  14.5 1.6 %collective-permute-start.3 = (bf16[4,160,128]{2,1,0:T(8,128)(2,1)S(1)}, bf16[4,160,128]{2,1,0:T(8,128)(2,1)S(1)}, u32[]{:S(2)}, u32[]{:S(2)}) collective-permute-start(bf16[4,160,128]{2,1,0:T(8,128)(2,1)S(1)} %get-tuple-element.23), channel_id=1, source_target_pairs={{0,2},{1,3},{2,0},{3,1},{4,6},{5,7},{6,4},{7,5},{8,10},{9,11},{10,... | collective-permute-start | bytes 491528 | tf_op jit(solution)/shard_map/ppermute | solution.py:443
  16.1 1.5 %collective-permute-start.4 = (bf16[4,160,128]{2,1,0:T(8,128)(2,1)S(1)}, bf16[4,160,128]{2,1,0:T(8,128)(2,1)S(1)}, u32[]{:S(2)}, u32[]{:S(2)}) collective-permute-start(bf16[4,160,128]{2,1,0:T(8,128)(2,1)S(1)} %get-tuple-element.24), channel_id=1, source_target_pairs={{0,4},{1,5},{2,6},{3,7},{4,0},{5,1},{6,2},{7,3},{8,12},{9,13},{10,... | collective-permute-start | bytes 491528 | tf_op jit(solution)/shard_map/ppermute | solution.py:443
  17.6 0.4 %collective-permute-start.5 = (bf16[4,160,128]{2,1,0:T(8,128)(2,1)S(1)}, bf16[4,160,128]{2,1,0:T(8,128)(2,1)S(1)}, u32[]{:S(2)}, u32[]{:S(2)}) collective-permute-start(bf16[4,160,128]{2,1,0:T(8,128)(2,1)S(1)} %get-tuple-element.25), channel_id=1, source_target_pairs={{0,6},{1,7},{2,4},{3,5},{4,2},{5,3},{6,0},{7,1},{8,14},{9,15},{10,... | collective-permute-start | bytes 491528 | tf_op jit(solution)/shard_map/ppermute | solution.py:443
  18.0 3.2 %collective-permute-done.3 = bf16[4,160,128]{2,1,0:T(8,128)(2,1)S(1)} collective-permute-done((bf16[4,160,128]{2,1,0:T(8,128)(2,1)S(1)}, bf16[4,160,128]{2,1,0:T(8,128)(2,1)S(1)}, u32[]{:S(2)}, u32[]{:S(2)}) %collective-permute-start.3) | collective-permute-done | bytes 163872 | tf_op jit(solution)/shard_map/ppermute | solution.py:443
  21.2 4.0 %collective-permute-done.4 = bf16[4,160,128]{2,1,0:T(8,128)(2,1)S(1)} collective-permute-done((bf16[4,160,128]{2,1,0:T(8,128)(2,1)S(1)}, bf16[4,160,128]{2,1,0:T(8,128)(2,1)S(1)}, u32[]{:S(2)}, u32[]{:S(2)}) %collective-permute-start.4) | collective-permute-done | bytes 163872 | tf_op jit(solution)/shard_map/ppermute | solution.py:443
  25.2 0.1 pad_maximum_fusion.mine_ref
  25.3 0.0 copy-start.2
  25.3 0.0 copy-start.6
  25.3 0.1 collective-permute-start.6
  25.4 0.6 %early.1.early_ref = f32[2,128,128]{2,1,0:T(8,128)S(1)} custom-call(bf16[4,4,160,128]{3,2,1,0:T(8,128)(2,1)S(1)} %pad_maximum_fusion.mine_ref, bf16[2,128,256]{2,1,0:T(8,128)(2,1)S(1)} %get-tuple-element.15.q.q0, bf16[2,4,256,32]{3,2,1,0:T(8,128)(2,1)S(1)} %get-tuple-element.16.k.k0, bf16[2,128,256]{2,1,0:T(8,128)(2,1)S(1)} %get-tuple-element.17.v.v0), custom_call_target="tpu_custom_call" | custom-call | flops 67108864 | bytes 2097152 | tf_op jit(solution)/shard_map/early/pallas_call | solution.py:343
  26.0 1.5 %collective-permute-done.6.other_ref = bf16[4,4,160,128]{3,2,1,0:T(8,128)(2,1)S(1)} collective-permute-done((bf16[4,4,160,128]{3,2,1,0:T(8,128)(2,1)S(1)}, bf16[4,4,160,128]{3,2,1,0:T(8,128)(2,1)S(1)}, u32[]{:S(2)}, u32[]{:S(2)}) %collective-permute-start.6) | collective-permute-done | bytes 655392 | tf_op jit(solution)/shard_map/ppermute | solution.py:443
  27.5 2.7 %attend.1 = (bf16[2,256,128]{2,1,0:T(8,128)(2,1)}, bf16[2,256,128]{2,1,0:T(8,128)(2,1)}) custom-call(bf16[4,4,160,128]{3,2,1,0:T(8,128)(2,1)S(1)} %pad_maximum_fusion.mine_ref, bf16[4,4,160,128]{3,2,1,0:T(8,128)(2,1)S(1)} %collective-permute-done.6.other_ref, f32[2,128,128]{2,1,0:T(8,128)S(1)} %early.1.early_ref, ...), custom_call_target="tpu_custom_call" | custom-call | tf_op jit(solution)/shard_map/attend/pallas_call | solution.py:416
  (16 shorter events, 0.1 us)
Async XLA Ops:
  0.6 8.5 %copy-start = (bf16[8,256,128]{2,1,0:T(8,128)(2,1)S(1)}, bf16[8,256,128]{2,1,0:T(8,128)(2,1)}, u32[]{:S(2)}) copy-start(bf16[8,256,128]{2,1,0:T(8,128)(2,1)} %lines_ref.1) | copy-start | bytes 1572868
  3.4 7.9 %collective-permute-start = (bf16[256,128]{1,0:T(8,128)(2,1)}, bf16[256,128]{1,0:T(8,128)(2,1)S(1)}, u32[]{:S(2)}, u32[]{:S(2)}) collective-permute-start(bf16[256,128]{1,0:T(8,128)(2,1)} %get-tuple-element.11), channel_id=1, source_target_pairs={{0,24},{8,16},{16,8},{24,0},{1,25},{9,17},{17,9},{25,1},{2,26},{10... | collective-permute-start | bytes 196616 | tf_op jit(solution)/shard_map/ppermute | solution.py:440
  8.5 0.7 %copy-start.4 = (f32[2,128]{1,0:T(2,128)S(1)}, f32[2,128]{1,0:T(2,128)}, u32[]{:S(2)}) copy-start(f32[2,128]{1,0:T(2,128)} %shift_ref.3) | copy-start | bytes 3076
  8.5 0.7 %copy-start.5 = (f32[2,128]{1,0:T(2,128)S(1)}, f32[2,128]{1,0:T(2,128)}, u32[]{:S(2)}) copy-start(f32[2,128]{1,0:T(2,128)} %gate_ref.1) | copy-start | bytes 3076
  8.5 0.7 %copy-start.3 = (f32[2,128]{1,0:T(2,128)S(1)}, f32[2,128]{1,0:T(2,128)}, u32[]{:S(2)}) copy-start(f32[2,128]{1,0:T(2,128)} %gain_ref.3) | copy-start | bytes 3076
  8.5 5.8 %collective-permute-start.1 = (bf16[256,128]{1,0:T(8,128)(2,1)}, bf16[256,128]{1,0:T(8,128)(2,1)S(1)}, u32[]{:S(2)}, u32[]{:S(2)}) collective-permute-start(bf16[256,128]{1,0:T(8,128)(2,1)} %get-tuple-element.12), channel_id=1, source_target_pairs={{0,16},{8,24},{16,0},{24,8},{1,17},{9,25},{17,1},{25,9},{2,18},{10... | collective-permute-start | bytes 196616 | tf_op jit(solution)/shard_map/ppermute | solution.py:440
  8.5 5.8 %collective-permute-start.2 = (bf16[256,128]{1,0:T(8,128)(2,1)}, bf16[256,128]{1,0:T(8,128)(2,1)S(1)}, u32[]{:S(2)}, u32[]{:S(2)}) collective-permute-start(bf16[256,128]{1,0:T(8,128)(2,1)} %get-tuple-element.13), channel_id=1, source_target_pairs={{0,8},{8,0},{16,24},{24,16},{1,9},{9,1},{17,25},{25,17},{2,10},{10... | collective-permute-start | bytes 196616 | tf_op jit(solution)/shard_map/ppermute | solution.py:440
  9.2 0.9 %copy-start.1 = (bf16[2,128,512]{2,1,0:T(8,128)(2,1)S(1)}, bf16[2,128,512]{2,1,0:T(8,128)(2,1)}, u32[]{:S(2)}) copy-start(bf16[2,128,512]{2,1,0:T(8,128)(2,1)} %proj_ref.1) | copy-start | bytes 786436
  10.1 4.2 %copy-start.7 = (bf16[256,128]{1,0:T(8,128)(2,1)S(1)}, bf16[256,128]{1,0:T(8,128)(2,1)}, u32[]{:S(2)}) copy-start(bf16[256,128]{1,0:T(8,128)(2,1)} %get-tuple-element.14) | copy-start | bytes 196612
  14.5 6.8 %collective-permute-start.3 = (bf16[4,160,128]{2,1,0:T(8,128)(2,1)S(1)}, bf16[4,160,128]{2,1,0:T(8,128)(2,1)S(1)}, u32[]{:S(2)}, u32[]{:S(2)}) collective-permute-start(bf16[4,160,128]{2,1,0:T(8,128)(2,1)S(1)} %get-tuple-element.23), channel_id=1, source_target_pairs={{0,2},{1,3},{2,0},{3,1},{4,6},{5,7},{6,4},{7,5},{8,10},{9,11},{10,... | collective-permute-start | bytes 491528 | tf_op jit(solution)/shard_map/ppermute | solution.py:443
  16.1 9.1 %collective-permute-start.4 = (bf16[4,160,128]{2,1,0:T(8,128)(2,1)S(1)}, bf16[4,160,128]{2,1,0:T(8,128)(2,1)S(1)}, u32[]{:S(2)}, u32[]{:S(2)}) collective-permute-start(bf16[4,160,128]{2,1,0:T(8,128)(2,1)S(1)} %get-tuple-element.24), channel_id=1, source_target_pairs={{0,4},{1,5},{2,6},{3,7},{4,0},{5,1},{6,2},{7,3},{8,12},{9,13},{10,... | collective-permute-start | bytes 491528 | tf_op jit(solution)/shard_map/ppermute | solution.py:443
  17.6 7.6 %collective-permute-start.5 = (bf16[4,160,128]{2,1,0:T(8,128)(2,1)S(1)}, bf16[4,160,128]{2,1,0:T(8,128)(2,1)S(1)}, u32[]{:S(2)}, u32[]{:S(2)}) collective-permute-start(bf16[4,160,128]{2,1,0:T(8,128)(2,1)S(1)} %get-tuple-element.25), channel_id=1, source_target_pairs={{0,6},{1,7},{2,4},{3,5},{4,2},{5,3},{6,0},{7,1},{8,14},{9,15},{10,... | collective-permute-start | bytes 491528 | tf_op jit(solution)/shard_map/ppermute | solution.py:443
  25.3 2.2 %copy-start.2 = (bf16[2,128,128]{2,1,0:T(8,128)(2,1)S(1)}, bf16[2,128,128]{2,1,0:T(8,128)(2,1)}, u32[]{:S(2)}) copy-start(bf16[2,128,128]{2,1,0:T(8,128)(2,1)} %weight_ref.3) | copy-start | bytes 196612
  25.3 2.2 %copy-start.6 = (f32[2,128]{1,0:T(2,128)S(1)}, f32[2,128]{1,0:T(2,128)}, u32[]{:S(2)}) copy-start(f32[2,128]{1,0:T(2,128)} %offset_ref.3) | copy-start | bytes 3076
  25.3 2.2 %collective-permute-start.6 = (bf16[4,4,160,128]{3,2,1,0:T(8,128)(2,1)S(1)}, bf16[4,4,160,128]{3,2,1,0:T(8,128)(2,1)S(1)}, u32[]{:S(2)}, u32[]{:S(2)}) collective-permute-start(bf16[4,4,160,128]{3,2,1,0:T(8,128)(2,1)S(1)} %pad_maximum_fusion.mine_ref), channel_id=1, source_target_pairs={{0,1},{1,0},{2,3},{3,2},{4,5},{5,4},{6,7},{7,6},{8,9},{9,8},{10,11... | collective-permute-start | bytes 1966088 | tf_op jit(solution)/shard_map/ppermute | solution.py:443

commit v12 on v10

--- a/solution.py
+++ b/solution.py
@@ -366,6 +366,16 @@
     rows = half // (chips * along)
     packed = 2 * heads * rows * (length // mine_ref.shape[3])
     first = pl.multiple_of(packed + lax.rem(lax.axis_index("col"), 2) * WD * rows, WD * rows)
+    attend_groups(start_half(other_ref, 1, q0, k0, v0, late, turned_bias))
+    gated = [
+        (jnp.concatenate([early_ref[w], late[w]], 1) * g0[w]).astype(jnp.bfloat16) for w in range(WD)
+    ]
+    full = [contract(line, weight_ref[0], 0, 0) + offset_ref[0:1, :] for line in gated]
+    for w in range(WD):
+        kept[w] = to_devices(full[w], along, chips, rows).astype(jnp.bfloat16)
+    leaving = pltpu.make_async_copy(kept, out0, sem)
+    leaving.start()
+    groups = []
     offset = turned(gate_ref[1:2, :])
     blocks = []
     for source in (mine_ref, other_ref):
@@ -378,20 +388,6 @@
     keys_and_values([line.astype(jnp.bfloat16) for line in lines], proj_ref[1], k1, v1)
     ordered = [to_devices(line, along, chips, rows).astype(jnp.bfloat16) for line in lines]
     queries_and_gates(ordered, size ** (-0.5), proj_ref[1], offset, q1, g1)
-    groups = start_half(other_ref, 1, q0, k0, v0, late, turned_bias)
-    leaving = pltpu.make_async_copy(kept, out0, sem)
-
-    def finish_start():
-        for w in range(WD):
-            gated = (jnp.concatenate([early_ref[w], late[w]], 1) * g0[w]).astype(jnp.bfloat16)
-            full = contract(gated, weight_ref[0], 0, 0) + offset_ref[0:1, :]
-            kept[w] = to_devices(full, along, chips, rows).astype(jnp.bfloat16)
-        leaving.start()
-
-    if groups:
-        groups[-1] = (groups[-1][0], lambda outs, put=groups[-1][1]: (put(outs), finish_start()))
-    else:
-        finish_start()
     for pack in range(heads // 2):
         unpack(mine_ref, 1, pack, rows, heads, 0, bias, 0)
         unpack(other_ref, 1, pack, rows, heads, 0, bias, half)
@@ -409,10 +405,10 @@
 
         for_each(length // CHUNK, step, False)
     attend_groups(groups)
+    gated = [(mixed[w] * g1[w]).astype(jnp.bfloat16) for w in range(WD)]
+    full = [contract(line, weight_ref[1], 0, 0) + offset_ref[1:2, :] for line in gated]
     for w in range(WD):
-        gated = (mixed[w] * g1[w]).astype(jnp.bfloat16)
-        full = contract(gated, weight_ref[1], 0, 0) + offset_ref[1:2, :]
-        out1[w] = full.astype(jnp.bfloat16)
+        out1[w] = full[w].astype(jnp.bfloat16)
     leaving.wait()
 
 

time: 31 us -> 31 us (level)
  no operation moved by 1% of the time
where the time goes in v12:
time: 31 us; the launch traced here: 30.8 us
  waiting for transfers between devices  12.2 us (39%)
  starting transfers between devices  9.4 us (30%)
  Pallas kernels  7.31 us (24%)
  local copies, waits for them, and re-layouts  1.03 us (3%)
  between operations  0.74 us (2%)
    ppermute x4, waiting for transfers between devices, by_col(): return lax.ppermute(block, 'col', [(i, i ^ flip) for i in range(cols)])  8.62 us
    ppermute x3, starting transfers between devices, by_row(): return lax.ppermute(block, 'row', [(i, i ^ shift) for i in range(along)])  5.78 us
    ppermute x4, starting transfers between devices, by_col(): return lax.ppermute(block, 'col', [(i, i ^ flip) for i in range(cols)])  3.62 us
    ppermute x3, waiting for transfers between devices, by_row(): return lax.ppermute(block, 'row', [(i, i ^ shift) for i in range(along)])  3.56 us
    pallas_call x1, Pallas kernels, attend(): pl.pallas_call(attend_kernel, out_shape=(result, result), in_specs=[VMEM]...  3.38 us
    pallas_call x1, Pallas kernels, local_bias(): pl.pallas_call(functools.partial(bias_kernel, along, chips), out_shape=(s...  2.73 us
    unnamed x16, local copies, waits for them, and re-layouts  1 us
    pallas_call x1, Pallas kernels, attend_early(): pl.pallas_call(early_kernel, out_shape=jax.ShapeDtypeStruct((WD, heads *...  0.62 us
  transfers between devices with their start and end apart: 7, of which 5 were waited for; matrix products, arithmetic and copies ran while one was open for 0% of the time, Pallas kernels for 4%

profile of v12, /device:TPU:0, one launch (start us, length us, event | category | flops | bytes accessed | tf_op | source)
XLA Modules:
  0.0 30.8 jit_solution(12700460861519618260)
XLA Ops:
  0.6 2.7 %bias.1 = (bf16[256,128]{1,0:T(8,128)(2,1)}, bf16[256,128]{1,0:T(8,128)(2,1)}, bf16[256,128]{1,0:T(8,128)(2,1)}, bf16[256,128]{1,0:T(8,128)(2,1)}) custom-call(bf16[8,256,128]{2,1,0:T(8,128)(2,1)} %lines_ref.1, s32[1,256]{1,0:T(1,128)} %bitcast.19, f32[2,128]{1,0:T(2,128)} %gain_ref.3, f32[2,128]{1,0:T(2,128)} %shift_ref.3, bf16[2,4,128]{2,1,0:T(4,128)(2,1)} %bitcast.18), custom_call_target="tpu_custom_call" | custom-call | tf_op jit(solution)/shard_map/bias/pallas_call | solution.py:119
  3.4 5.1 %collective-permute-start = (bf16[256,128]{1,0:T(8,128)(2,1)}, bf16[256,128]{1,0:T(8,128)(2,1)S(1)}, u32[]{:S(2)}, u32[]{:S(2)}) collective-permute-start(bf16[256,128]{1,0:T(8,128)(2,1)} %get-tuple-element.11), channel_id=1, source_target_pairs={{0,24},{8,16},{16,8},{24,0},{1,25},{9,17},{17,9},{25,1},{2,26},{10... | collective-permute-start | bytes 196616 | tf_op jit(solution)/shard_map/ppermute | solution.py:446
  8.5 0.0 collective-permute-start.1
  8.5 0.7 %collective-permute-start.2 = (bf16[256,128]{1,0:T(8,128)(2,1)}, bf16[256,128]{1,0:T(8,128)(2,1)S(1)}, u32[]{:S(2)}, u32[]{:S(2)}) collective-permute-start(bf16[256,128]{1,0:T(8,128)(2,1)} %get-tuple-element.13), channel_id=1, source_target_pairs={{0,8},{8,0},{16,24},{24,16},{1,9},{9,1},{17,25},{25,17},{2,10},{10... | collective-permute-start | bytes 196616 | tf_op jit(solution)/shard_map/ppermute | solution.py:446
  9.2 0.0 copy-done.5
  9.2 0.0 copy-done.3
  9.2 0.9 %copy-done.1 = bf16[2,128,512]{2,1,0:T(8,128)(2,1)S(1)} copy-done((bf16[2,128,512]{2,1,0:T(8,128)(2,1)S(1)}, bf16[2,128,512]{2,1,0:T(8,128)(2,1)}, u32[]{:S(2)}) %copy-start.1) | copy-done | bytes 262168
  10.2 0.6 %lines.1 = (bf16[2,128,256]{2,1,0:T(8,128)(2,1)S(1)}, bf16[2,4,256,32]{3,2,1,0:T(8,128)(2,1)S(1)}, bf16[2,128,256]{2,1,0:T(8,128)(2,1)S(1)}, f32[2,128,256]{2,1,0:T(8,128)S(1)}) custom-call(bf16[8,256,128]{2,1,0:T(8,128)(2,1)S(1)} %copy-done, f32[2,128]{1,0:T(2,128)S(1)} %copy-done.3, f32[2,128]{1,0:T(2,128)S(1)} %copy-done.4, ...), custom_call_target="tpu_custom_call" | custom-call | flops 67108864 | bytes 1048576 | tf_op jit(solution)/shard_map/lines/pallas_call | solution.py:229
  10.7 0.6 %collective-permute-done = bf16[256,128]{1,0:T(8,128)(2,1)S(1)} collective-permute-done((bf16[256,128]{1,0:T(8,128)(2,1)}, bf16[256,128]{1,0:T(8,128)(2,1)S(1)}, u32[]{:S(2)}, u32[]{:S(2)}) %collective-permute-start) | collective-permute-done | bytes 65568 | tf_op jit(solution)/shard_map/ppermute | solution.py:446
  11.3 3.0 %collective-permute-done.1 = bf16[256,128]{1,0:T(8,128)(2,1)S(1)} collective-permute-done((bf16[256,128]{1,0:T(8,128)(2,1)}, bf16[256,128]{1,0:T(8,128)(2,1)S(1)}, u32[]{:S(2)}, u32[]{:S(2)}) %collective-permute-start.1) | collective-permute-done | bytes 65568 | tf_op jit(solution)/shard_map/ppermute | solution.py:446
  14.3 0.0 collective-permute-done.2
  14.4 0.1 pad_maximum_fusion.2
  14.5 1.6 %collective-permute-start.3 = (bf16[4,160,128]{2,1,0:T(8,128)(2,1)S(1)}, bf16[4,160,128]{2,1,0:T(8,128)(2,1)S(1)}, u32[]{:S(2)}, u32[]{:S(2)}) collective-permute-start(bf16[4,160,128]{2,1,0:T(8,128)(2,1)S(1)} %get-tuple-element.23), channel_id=1, source_target_pairs={{0,2},{1,3},{2,0},{3,1},{4,6},{5,7},{6,4},{7,5},{8,10},{9,11},{10,... | collective-permute-start | bytes 491528 | tf_op jit(solution)/shard_map/ppermute | solution.py:449
  16.1 1.5 %collective-permute-start.4 = (bf16[4,160,128]{2,1,0:T(8,128)(2,1)S(1)}, bf16[4,160,128]{2,1,0:T(8,128)(2,1)S(1)}, u32[]{:S(2)}, u32[]{:S(2)}) collective-permute-start(bf16[4,160,128]{2,1,0:T(8,128)(2,1)S(1)} %get-tuple-element.24), channel_id=1, source_target_pairs={{0,4},{1,5},{2,6},{3,7},{4,0},{5,1},{6,2},{7,3},{8,12},{9,13},{10,... | collective-permute-start | bytes 491528 | tf_op jit(solution)/shard_map/ppermute | solution.py:449
  17.6 0.4 %collective-permute-start.5 = (bf16[4,160,128]{2,1,0:T(8,128)(2,1)S(1)}, bf16[4,160,128]{2,1,0:T(8,128)(2,1)S(1)}, u32[]{:S(2)}, u32[]{:S(2)}) collective-permute-start(bf16[4,160,128]{2,1,0:T(8,128)(2,1)S(1)} %get-tuple-element.25), channel_id=1, source_target_pairs={{0,6},{1,7},{2,4},{3,5},{4,2},{5,3},{6,0},{7,1},{8,14},{9,15},{10,... | collective-permute-start | bytes 491528 | tf_op jit(solution)/shard_map/ppermute | solution.py:449
  18.0 3.2 %collective-permute-done.3 = bf16[4,160,128]{2,1,0:T(8,128)(2,1)S(1)} collective-permute-done((bf16[4,160,128]{2,1,0:T(8,128)(2,1)S(1)}, bf16[4,160,128]{2,1,0:T(8,128)(2,1)S(1)}, u32[]{:S(2)}, u32[]{:S(2)}) %collective-permute-start.3) | collective-permute-done | bytes 163872 | tf_op jit(solution)/shard_map/ppermute | solution.py:449
  21.2 4.0 %collective-permute-done.4 = bf16[4,160,128]{2,1,0:T(8,128)(2,1)S(1)} collective-permute-done((bf16[4,160,128]{2,1,0:T(8,128)(2,1)S(1)}, bf16[4,160,128]{2,1,0:T(8,128)(2,1)S(1)}, u32[]{:S(2)}, u32[]{:S(2)}) %collective-permute-start.4) | collective-permute-done | bytes 163872 | tf_op jit(solution)/shard_map/ppermute | solution.py:449
  25.2 0.1 pad_maximum_fusion.mine_ref
  25.3 0.0 copy-start.2
  25.3 0.0 copy-start.6
  25.3 0.1 collective-permute-start.6
  25.4 0.6 %early.1.early_ref = f32[2,128,128]{2,1,0:T(8,128)S(1)} custom-call(bf16[4,4,160,128]{3,2,1,0:T(8,128)(2,1)S(1)} %pad_maximum_fusion.mine_ref, bf16[2,128,256]{2,1,0:T(8,128)(2,1)S(1)} %get-tuple-element.15.q.q0, bf16[2,4,256,32]{3,2,1,0:T(8,128)(2,1)S(1)} %get-tuple-element.16.k.k0, bf16[2,128,256]{2,1,0:T(8,128)(2,1)S(1)} %get-tuple-element.17.v.v0), custom_call_target="tpu_custom_call" | custom-call | flops 67108864 | bytes 2097152 | tf_op jit(solution)/shard_map/early/pallas_call | solution.py:342
  26.0 1.5 %collective-permute-done.6.other_ref = bf16[4,4,160,128]{3,2,1,0:T(8,128)(2,1)S(1)} collective-permute-done((bf16[4,4,160,128]{3,2,1,0:T(8,128)(2,1)S(1)}, bf16[4,4,160,128]{3,2,1,0:T(8,128)(2,1)S(1)}, u32[]{:S(2)}, u32[]{:S(2)}) %collective-permute-start.6) | collective-permute-done | bytes 655392 | tf_op jit(solution)/shard_map/ppermute | solution.py:449
  27.5 3.4 %attend.1 = (bf16[2,256,128]{2,1,0:T(8,128)(2,1)}, bf16[2,256,128]{2,1,0:T(8,128)(2,1)}) custom-call(bf16[4,4,160,128]{3,2,1,0:T(8,128)(2,1)S(1)} %pad_maximum_fusion.mine_ref, bf16[4,4,160,128]{3,2,1,0:T(8,128)(2,1)S(1)} %collective-permute-done.6.other_ref, f32[2,128,128]{2,1,0:T(8,128)S(1)} %early.1.early_ref, ...), custom_call_target="tpu_custom_call" | custom-call | tf_op jit(solution)/shard_map/attend/pallas_call | solution.py:420
  (16 shorter events, 0.1 us)
Async XLA Ops:
  0.6 8.5 %copy-start = (bf16[8,256,128]{2,1,0:T(8,128)(2,1)S(1)}, bf16[8,256,128]{2,1,0:T(8,128)(2,1)}, u32[]{:S(2)}) copy-start(bf16[8,256,128]{2,1,0:T(8,128)(2,1)} %lines_ref.1) | copy-start | bytes 1572868
  3.4 7.9 %collective-permute-start = (bf16[256,128]{1,0:T(8,128)(2,1)}, bf16[256,128]{1,0:T(8,128)(2,1)S(1)}, u32[]{:S(2)}, u32[]{:S(2)}) collective-permute-start(bf16[256,128]{1,0:T(8,128)(2,1)} %get-tuple-element.11), channel_id=1, source_target_pairs={{0,24},{8,16},{16,8},{24,0},{1,25},{9,17},{17,9},{25,1},{2,26},{10... | collective-permute-start | bytes 196616 | tf_op jit(solution)/shard_map/ppermute | solution.py:446
  8.5 0.7 %copy-start.4 = (f32[2,128]{1,0:T(2,128)S(1)}, f32[2,128]{1,0:T(2,128)}, u32[]{:S(2)}) copy-start(f32[2,128]{1,0:T(2,128)} %shift_ref.3) | copy-start | bytes 3076
  8.5 0.7 %copy-start.5 = (f32[2,128]{1,0:T(2,128)S(1)}, f32[2,128]{1,0:T(2,128)}, u32[]{:S(2)}) copy-start(f32[2,128]{1,0:T(2,128)} %gate_ref.1) | copy-start | bytes 3076
  8.5 0.7 %copy-start.3 = (f32[2,128]{1,0:T(2,128)S(1)}, f32[2,128]{1,0:T(2,128)}, u32[]{:S(2)}) copy-start(f32[2,128]{1,0:T(2,128)} %gain_ref.3) | copy-start | bytes 3076
  8.5 5.8 %collective-permute-start.1 = (bf16[256,128]{1,0:T(8,128)(2,1)}, bf16[256,128]{1,0:T(8,128)(2,1)S(1)}, u32[]{:S(2)}, u32[]{:S(2)}) collective-permute-start(bf16[256,128]{1,0:T(8,128)(2,1)} %get-tuple-element.12), channel_id=1, source_target_pairs={{0,16},{8,24},{16,0},{24,8},{1,17},{9,25},{17,1},{25,9},{2,18},{10... | collective-permute-start | bytes 196616 | tf_op jit(solution)/shard_map/ppermute | solution.py:446
  8.5 5.8 %collective-permute-start.2 = (bf16[256,128]{1,0:T(8,128)(2,1)}, bf16[256,128]{1,0:T(8,128)(2,1)S(1)}, u32[]{:S(2)}, u32[]{:S(2)}) collective-permute-start(bf16[256,128]{1,0:T(8,128)(2,1)} %get-tuple-element.13), channel_id=1, source_target_pairs={{0,8},{8,0},{16,24},{24,16},{1,9},{9,1},{17,25},{25,17},{2,10},{10... | collective-permute-start | bytes 196616 | tf_op jit(solution)/shard_map/ppermute | solution.py:446
  9.2 0.9 %copy-start.1 = (bf16[2,128,512]{2,1,0:T(8,128)(2,1)S(1)}, bf16[2,128,512]{2,1,0:T(8,128)(2,1)}, u32[]{:S(2)}) copy-start(bf16[2,128,512]{2,1,0:T(8,128)(2,1)} %proj_ref.1) | copy-start | bytes 786436
  10.1 4.2 %copy-start.7 = (bf16[256,128]{1,0:T(8,128)(2,1)S(1)}, bf16[256,128]{1,0:T(8,128)(2,1)}, u32[]{:S(2)}) copy-start(bf16[256,128]{1,0:T(8,128)(2,1)} %get-tuple-element.14) | copy-start | bytes 196612
  14.5 6.8 %collective-permute-start.3 = (bf16[4,160,128]{2,1,0:T(8,128)(2,1)S(1)}, bf16[4,160,128]{2,1,0:T(8,128)(2,1)S(1)}, u32[]{:S(2)}, u32[]{:S(2)}) collective-permute-start(bf16[4,160,128]{2,1,0:T(8,128)(2,1)S(1)} %get-tuple-element.23), channel_id=1, source_target_pairs={{0,2},{1,3},{2,0},{3,1},{4,6},{5,7},{6,4},{7,5},{8,10},{9,11},{10,... | collective-permute-start | bytes 491528 | tf_op jit(solution)/shard_map/ppermute | solution.py:449
  16.1 9.1 %collective-permute-start.4 = (bf16[4,160,128]{2,1,0:T(8,128)(2,1)S(1)}, bf16[4,160,128]{2,1,0:T(8,128)(2,1)S(1)}, u32[]{:S(2)}, u32[]{:S(2)}) collective-permute-start(bf16[4,160,128]{2,1,0:T(8,128)(2,1)S(1)} %get-tuple-element.24), channel_id=1, source_target_pairs={{0,4},{1,5},{2,6},{3,7},{4,0},{5,1},{6,2},{7,3},{8,12},{9,13},{10,... | collective-permute-start | bytes 491528 | tf_op jit(solution)/shard_map/ppermute | solution.py:449
  17.6 7.6 %collective-permute-start.5 = (bf16[4,160,128]{2,1,0:T(8,128)(2,1)S(1)}, bf16[4,160,128]{2,1,0:T(8,128)(2,1)S(1)}, u32[]{:S(2)}, u32[]{:S(2)}) collective-permute-start(bf16[4,160,128]{2,1,0:T(8,128)(2,1)S(1)} %get-tuple-element.25), channel_id=1, source_target_pairs={{0,6},{1,7},{2,4},{3,5},{4,2},{5,3},{6,0},{7,1},{8,14},{9,15},{10,... | collective-permute-start | bytes 491528 | tf_op jit(solution)/shard_map/ppermute | solution.py:449
  25.3 2.2 %copy-start.2 = (bf16[2,128,128]{2,1,0:T(8,128)(2,1)S(1)}, bf16[2,128,128]{2,1,0:T(8,128)(2,1)}, u32[]{:S(2)}) copy-start(bf16[2,128,128]{2,1,0:T(8,128)(2,1)} %weight_ref.3) | copy-start | bytes 196612
  25.3 2.2 %copy-start.6 = (f32[2,128]{1,0:T(2,128)S(1)}, f32[2,128]{1,0:T(2,128)}, u32[]{:S(2)}) copy-start(f32[2,128]{1,0:T(2,128)} %offset_ref.3) | copy-start | bytes 3076
  25.3 2.2 %collective-permute-start.6 = (bf16[4,4,160,128]{3,2,1,0:T(8,128)(2,1)S(1)}, bf16[4,4,160,128]{3,2,1,0:T(8,128)(2,1)S(1)}, u32[]{:S(2)}, u32[]{:S(2)}) collective-permute-start(bf16[4,4,160,128]{3,2,1,0:T(8,128)(2,1)S(1)} %pad_maximum_fusion.mine_ref), channel_id=1, source_target_pairs={{0,1},{1,0},{2,3},{3,2},{4,5},{5,4},{6,7},{7,6},{8,9},{9,8},{10,11... | collective-permute-start | bytes 1966088 | tf_op jit(solution)/shard_map/ppermute | solution.py:449

commit v13 on v11

--- a/solution.py
+++ b/solution.py
@@ -265,27 +265,26 @@
                 into[slot, at : at + half, there] = block
 
 
-def score(units):
-    return [contract(key, query, 1, 0) + added for key, query, added, _ in units]
-
-
-def mix(units, scores):
-    tops = [jnp.max(part, 0, keepdims=True) for part in scores]
-    expos = [jnp.exp(part - top) for part, top in zip(scores, tops)]
-    shares = [1.0 / jnp.sum(expo, 0, keepdims=True) for expo in expos]
-    weights = [(expo * share).astype(jnp.bfloat16) for expo, share in zip(expos, shares)]
-    return [contract(unit[3], weight, 1, 0) for unit, weight in zip(units, weights)]
-
-
-def attend_groups(groups, ready=None):
-    if not groups:
-        return
-    if ready is None:
-        ready = score(groups[0][0]())
-    for i, (units, put) in enumerate(groups):
-        ahead = score(groups[i + 1][0]()) if i + 1 < len(groups) else None
-        put(mix(units(), ready))
-        ready = ahead
+def stages(units, put):
+    return (
+        lambda _: [contract(key, query, 1, 0) + added for key, query, added, _ in units()],
+        lambda scores: [(part, jnp.max(part, 0, keepdims=True)) for part in scores],
+        lambda pairs: [jnp.exp(part - top) for part, top in pairs],
+        lambda expos: [(expo, 1.0 / jnp.sum(expo, 0, keepdims=True)) for expo in expos],
+        lambda pairs: [(expo * share).astype(jnp.bfloat16) for expo, share in pairs],
+        lambda weights: put(
+            [contract(unit[3], weight, 1, 0) for unit, weight in zip(units(), weights)]
+        ),
+    )
+
+
+def attend_groups(groups):
+    steps = [stages(*group) for group in groups]
+    held = [None] * len(groups)
+    for t in range(len(groups) + 5 if groups else 0):
+        for g in range(len(groups)):
+            if 0 <= t - g < 6:
+                held[g] = steps[g][t - g](held[g])
 
 
 def head_group(heads, size, q, k, v, bias, mixed, there, near):
@@ -314,12 +313,10 @@
         groups = []
         for pack in range(heads // 2):
             unpack(source, 0, pack, rows, heads, 1, bias, 0)
-            groups.append(
-                head_group(
-                    (2 * pack, 2 * pack + 1), size, q, k, v, bias, mixed,
-                    pl.ds(other * half, half), pl.ds(0, half),
+            for h in (2 * pack, 2 * pack + 1):
+                groups.append(
+                    head_group((h,), size, q, k, v, bias, mixed, pl.ds(other * half, half), pl.ds(0, half))
                 )
-            )
         return groups
     for pack in range(heads // 2):
         unpack(source, 0, pack, rows, heads, 1, bias, 0)
@@ -368,7 +365,6 @@
     packed = 2 * heads * rows * (length // mine_ref.shape[3])
     first = pl.multiple_of(packed + lax.rem(lax.axis_index("col"), 2) * WD * rows, WD * rows)
     groups = start_half(other_ref, 1, q0, k0, v0, late, turned_bias)
-    ready = score(groups[0][0]()) if groups else None
     offset = turned(gate_ref[1:2, :])
     blocks = []
     for source in (mine_ref, other_ref):
@@ -386,9 +382,10 @@
         unpack(other_ref, 1, pack, rows, heads, 0, bias, half)
         pair = (2 * pack, 2 * pack + 1)
         if length == CHUNK:
-            groups.append(
-                head_group(pair, size, q1, k1, v1, bias, mixed, pl.ds(0, length), pl.ds(0, length))
-            )
+            for h in pair:
+                groups.append(
+                    head_group((h,), size, q1, k1, v1, bias, mixed, pl.ds(0, length), pl.ds(0, length))
+                )
             continue
 
         def step(chunk):
@@ -397,7 +394,7 @@
                 attend_groups([head_group((h,), size, q1, k1, v1, bias, mixed, there, there)])
 
         for_each(length // CHUNK, step, False)
-    attend_groups(groups, ready)
+    attend_groups(groups)
     for w in range(WD):
         gated = (jnp.concatenate([early_ref[w], late[w]], 1) * g0[w]).astype(jnp.bfloat16)
         full = contract(gated, weight_ref[0], 0, 0) + offset_ref[0:1, :]

time: 30.4 us -> 30.4 us (level)
  no operation moved by 1% of the time
where the time goes in v13:
time: 30.4 us; the launch traced here: 30.2 us
  waiting for transfers between devices  12.2 us (40%)
  starting transfers between devices  9.4 us (31%)
  Pallas kernels  6.67 us (22%)
  local copies, waits for them, and re-layouts  1.03 us (3%)
  between operations  0.74 us (2%)
    ppermute x4, waiting for transfers between devices, by_col(): return lax.ppermute(block, 'col', [(i, i ^ flip) for i in range(cols)])  8.62 us
    ppermute x3, starting transfers between devices, by_row(): return lax.ppermute(block, 'row', [(i, i ^ shift) for i in range(along)])  5.78 us
    ppermute x4, starting transfers between devices, by_col(): return lax.ppermute(block, 'col', [(i, i ^ flip) for i in range(cols)])  3.62 us
    ppermute x3, waiting for transfers between devices, by_row(): return lax.ppermute(block, 'row', [(i, i ^ shift) for i in range(along)])  3.56 us
    pallas_call x1, Pallas kernels, attend(): pl.pallas_call(attend_kernel, out_shape=(result, result), in_specs=[VMEM]...  2.74 us
    pallas_call x1, Pallas kernels, local_bias(): pl.pallas_call(functools.partial(bias_kernel, along, chips), out_shape=(s...  2.73 us
    unnamed x16, local copies, waits for them, and re-layouts  1 us
    pallas_call x1, Pallas kernels, attend_early(): pl.pallas_call(early_kernel, out_shape=jax.ShapeDtypeStruct((WD, heads *...  0.62 us
  transfers between devices with their start and end apart: 7, of which 5 were waited for; matrix products, arithmetic and copies ran while one was open for 0% of the time, Pallas kernels for 4%

profile of v13, /device:TPU:0, one launch (start us, length us, event | category | flops | bytes accessed | tf_op | source)
XLA Modules:
  0.0 30.2 jit_solution(7331152917372126631)
XLA Ops:
  0.6 2.7 %bias.1 = (bf16[256,128]{1,0:T(8,128)(2,1)}, bf16[256,128]{1,0:T(8,128)(2,1)}, bf16[256,128]{1,0:T(8,128)(2,1)}, bf16[256,128]{1,0:T(8,128)(2,1)}) custom-call(bf16[8,256,128]{2,1,0:T(8,128)(2,1)} %lines_ref.1, s32[1,256]{1,0:T(1,128)} %bitcast.19, f32[2,128]{1,0:T(2,128)} %gain_ref.3, f32[2,128]{1,0:T(2,128)} %shift_ref.3, bf16[2,4,128]{2,1,0:T(4,128)(2,1)} %bitcast.18), custom_call_target="tpu_custom_call" | custom-call | tf_op jit(solution)/shard_map/bias/pallas_call | solution.py:119
  3.4 5.1 %collective-permute-start = (bf16[256,128]{1,0:T(8,128)(2,1)}, bf16[256,128]{1,0:T(8,128)(2,1)S(1)}, u32[]{:S(2)}, u32[]{:S(2)}) collective-permute-start(bf16[256,128]{1,0:T(8,128)(2,1)} %get-tuple-element.11), channel_id=1, source_target_pairs={{0,24},{8,16},{16,8},{24,0},{1,25},{9,17},{17,9},{25,1},{2,26},{10... | collective-permute-start | bytes 196616 | tf_op jit(solution)/shard_map/ppermute | solution.py:437
  8.5 0.0 collective-permute-start.1
  8.5 0.7 %collective-permute-start.2 = (bf16[256,128]{1,0:T(8,128)(2,1)}, bf16[256,128]{1,0:T(8,128)(2,1)S(1)}, u32[]{:S(2)}, u32[]{:S(2)}) collective-permute-start(bf16[256,128]{1,0:T(8,128)(2,1)} %get-tuple-element.13), channel_id=1, source_target_pairs={{0,8},{8,0},{16,24},{24,16},{1,9},{9,1},{17,25},{25,17},{2,10},{10... | collective-permute-start | bytes 196616 | tf_op jit(solution)/shard_map/ppermute | solution.py:437
  9.2 0.0 copy-done.5
  9.2 0.0 copy-done.3
  9.2 0.9 %copy-done.1 = bf16[2,128,512]{2,1,0:T(8,128)(2,1)S(1)} copy-done((bf16[2,128,512]{2,1,0:T(8,128)(2,1)S(1)}, bf16[2,128,512]{2,1,0:T(8,128)(2,1)}, u32[]{:S(2)}) %copy-start.1) | copy-done | bytes 262168
  10.2 0.6 %lines.1 = (bf16[2,128,256]{2,1,0:T(8,128)(2,1)S(1)}, bf16[2,4,256,32]{3,2,1,0:T(8,128)(2,1)S(1)}, bf16[2,128,256]{2,1,0:T(8,128)(2,1)S(1)}, f32[2,128,256]{2,1,0:T(8,128)S(1)}) custom-call(bf16[8,256,128]{2,1,0:T(8,128)(2,1)S(1)} %copy-done, f32[2,128]{1,0:T(2,128)S(1)} %copy-done.3, f32[2,128]{1,0:T(2,128)S(1)} %copy-done.4, ...), custom_call_target="tpu_custom_call" | custom-call | flops 67108864 | bytes 1048576 | tf_op jit(solution)/shard_map/lines/pallas_call | solution.py:229
  10.7 0.6 %collective-permute-done = bf16[256,128]{1,0:T(8,128)(2,1)S(1)} collective-permute-done((bf16[256,128]{1,0:T(8,128)(2,1)}, bf16[256,128]{1,0:T(8,128)(2,1)S(1)}, u32[]{:S(2)}, u32[]{:S(2)}) %collective-permute-start) | collective-permute-done | bytes 65568 | tf_op jit(solution)/shard_map/ppermute | solution.py:437
  11.3 3.0 %collective-permute-done.1 = bf16[256,128]{1,0:T(8,128)(2,1)S(1)} collective-permute-done((bf16[256,128]{1,0:T(8,128)(2,1)}, bf16[256,128]{1,0:T(8,128)(2,1)S(1)}, u32[]{:S(2)}, u32[]{:S(2)}) %collective-permute-start.1) | collective-permute-done | bytes 65568 | tf_op jit(solution)/shard_map/ppermute | solution.py:437
  14.3 0.0 collective-permute-done.2
  14.4 0.1 pad_maximum_fusion.2
  14.5 1.6 %collective-permute-start.3 = (bf16[4,160,128]{2,1,0:T(8,128)(2,1)S(1)}, bf16[4,160,128]{2,1,0:T(8,128)(2,1)S(1)}, u32[]{:S(2)}, u32[]{:S(2)}) collective-permute-start(bf16[4,160,128]{2,1,0:T(8,128)(2,1)S(1)} %get-tuple-element.23), channel_id=1, source_target_pairs={{0,2},{1,3},{2,0},{3,1},{4,6},{5,7},{6,4},{7,5},{8,10},{9,11},{10,... | collective-permute-start | bytes 491528 | tf_op jit(solution)/shard_map/ppermute | solution.py:440
  16.1 1.5 %collective-permute-start.4 = (bf16[4,160,128]{2,1,0:T(8,128)(2,1)S(1)}, bf16[4,160,128]{2,1,0:T(8,128)(2,1)S(1)}, u32[]{:S(2)}, u32[]{:S(2)}) collective-permute-start(bf16[4,160,128]{2,1,0:T(8,128)(2,1)S(1)} %get-tuple-element.24), channel_id=1, source_target_pairs={{0,4},{1,5},{2,6},{3,7},{4,0},{5,1},{6,2},{7,3},{8,12},{9,13},{10,... | collective-permute-start | bytes 491528 | tf_op jit(solution)/shard_map/ppermute | solution.py:440
  17.6 0.4 %collective-permute-start.5 = (bf16[4,160,128]{2,1,0:T(8,128)(2,1)S(1)}, bf16[4,160,128]{2,1,0:T(8,128)(2,1)S(1)}, u32[]{:S(2)}, u32[]{:S(2)}) collective-permute-start(bf16[4,160,128]{2,1,0:T(8,128)(2,1)S(1)} %get-tuple-element.25), channel_id=1, source_target_pairs={{0,6},{1,7},{2,4},{3,5},{4,2},{5,3},{6,0},{7,1},{8,14},{9,15},{10,... | collective-permute-start | bytes 491528 | tf_op jit(solution)/shard_map/ppermute | solution.py:440
  18.0 3.2 %collective-permute-done.3 = bf16[4,160,128]{2,1,0:T(8,128)(2,1)S(1)} collective-permute-done((bf16[4,160,128]{2,1,0:T(8,128)(2,1)S(1)}, bf16[4,160,128]{2,1,0:T(8,128)(2,1)S(1)}, u32[]{:S(2)}, u32[]{:S(2)}) %collective-permute-start.3) | collective-permute-done | bytes 163872 | tf_op jit(solution)/shard_map/ppermute | solution.py:440
  21.2 4.0 %collective-permute-done.4 = bf16[4,160,128]{2,1,0:T(8,128)(2,1)S(1)} collective-permute-done((bf16[4,160,128]{2,1,0:T(8,128)(2,1)S(1)}, bf16[4,160,128]{2,1,0:T(8,128)(2,1)S(1)}, u32[]{:S(2)}, u32[]{:S(2)}) %collective-permute-start.4) | collective-permute-done | bytes 163872 | tf_op jit(solution)/shard_map/ppermute | solution.py:440
  25.2 0.1 pad_maximum_fusion.mine_ref
  25.3 0.0 copy-start.2
  25.3 0.0 copy-start.6
  25.3 0.1 collective-permute-start.6
  25.4 0.6 %early.1.early_ref = f32[2,128,128]{2,1,0:T(8,128)S(1)} custom-call(bf16[4,4,160,128]{3,2,1,0:T(8,128)(2,1)S(1)} %pad_maximum_fusion.mine_ref, bf16[2,128,256]{2,1,0:T(8,128)(2,1)S(1)} %get-tuple-element.15.q.q0, bf16[2,4,256,32]{3,2,1,0:T(8,128)(2,1)S(1)} %get-tuple-element.16.k.k0, bf16[2,128,256]{2,1,0:T(8,128)(2,1)S(1)} %get-tuple-element.17.v.v0), custom_call_target="tpu_custom_call" | custom-call | flops 67108864 | bytes 2097152 | tf_op jit(solution)/shard_map/early/pallas_call | solution.py:340
  26.0 1.5 %collective-permute-done.6.other_ref = bf16[4,4,160,128]{3,2,1,0:T(8,128)(2,1)S(1)} collective-permute-done((bf16[4,4,160,128]{3,2,1,0:T(8,128)(2,1)S(1)}, bf16[4,4,160,128]{3,2,1,0:T(8,128)(2,1)S(1)}, u32[]{:S(2)}, u32[]{:S(2)}) %collective-permute-start.6) | collective-permute-done | bytes 655392 | tf_op jit(solution)/shard_map/ppermute | solution.py:440
  27.5 2.7 %attend.1 = (bf16[2,256,128]{2,1,0:T(8,128)(2,1)}, bf16[2,256,128]{2,1,0:T(8,128)(2,1)}) custom-call(bf16[4,4,160,128]{3,2,1,0:T(8,128)(2,1)S(1)} %pad_maximum_fusion.mine_ref, bf16[4,4,160,128]{3,2,1,0:T(8,128)(2,1)S(1)} %collective-permute-done.6.other_ref, f32[2,128,128]{2,1,0:T(8,128)S(1)} %early.1.early_ref, ...), custom_call_target="tpu_custom_call" | custom-call | tf_op jit(solution)/shard_map/attend/pallas_call | solution.py:413
  (16 shorter events, 0.1 us)
Async XLA Ops:
  0.6 8.5 %copy-start = (bf16[8,256,128]{2,1,0:T(8,128)(2,1)S(1)}, bf16[8,256,128]{2,1,0:T(8,128)(2,1)}, u32[]{:S(2)}) copy-start(bf16[8,256,128]{2,1,0:T(8,128)(2,1)} %lines_ref.1) | copy-start | bytes 1572868
  3.4 7.9 %collective-permute-start = (bf16[256,128]{1,0:T(8,128)(2,1)}, bf16[256,128]{1,0:T(8,128)(2,1)S(1)}, u32[]{:S(2)}, u32[]{:S(2)}) collective-permute-start(bf16[256,128]{1,0:T(8,128)(2,1)} %get-tuple-element.11), channel_id=1, source_target_pairs={{0,24},{8,16},{16,8},{24,0},{1,25},{9,17},{17,9},{25,1},{2,26},{10... | collective-permute-start | bytes 196616 | tf_op jit(solution)/shard_map/ppermute | solution.py:437
  8.5 0.7 %copy-start.4 = (f32[2,128]{1,0:T(2,128)S(1)}, f32[2,128]{1,0:T(2,128)}, u32[]{:S(2)}) copy-start(f32[2,128]{1,0:T(2,128)} %shift_ref.3) | copy-start | bytes 3076
  8.5 0.7 %copy-start.5 = (f32[2,128]{1,0:T(2,128)S(1)}, f32[2,128]{1,0:T(2,128)}, u32[]{:S(2)}) copy-start(f32[2,128]{1,0:T(2,128)} %gate_ref.1) | copy-start | bytes 3076
  8.5 0.7 %copy-start.3 = (f32[2,128]{1,0:T(2,128)S(1)}, f32[2,128]{1,0:T(2,128)}, u32[]{:S(2)}) copy-start(f32[2,128]{1,0:T(2,128)} %gain_ref.3) | copy-start | bytes 3076
  8.5 5.8 %collective-permute-start.1 = (bf16[256,128]{1,0:T(8,128)(2,1)}, bf16[256,128]{1,0:T(8,128)(2,1)S(1)}, u32[]{:S(2)}, u32[]{:S(2)}) collective-permute-start(bf16[256,128]{1,0:T(8,128)(2,1)} %get-tuple-element.12), channel_id=1, source_target_pairs={{0,16},{8,24},{16,0},{24,8},{1,17},{9,25},{17,1},{25,9},{2,18},{10... | collective-permute-start | bytes 196616 | tf_op jit(solution)/shard_map/ppermute | solution.py:437
  8.5 5.8 %collective-permute-start.2 = (bf16[256,128]{1,0:T(8,128)(2,1)}, bf16[256,128]{1,0:T(8,128)(2,1)S(1)}, u32[]{:S(2)}, u32[]{:S(2)}) collective-permute-start(bf16[256,128]{1,0:T(8,128)(2,1)} %get-tuple-element.13), channel_id=1, source_target_pairs={{0,8},{8,0},{16,24},{24,16},{1,9},{9,1},{17,25},{25,17},{2,10},{10... | collective-permute-start | bytes 196616 | tf_op jit(solution)/shard_map/ppermute | solution.py:437
  9.2 0.9 %copy-start.1 = (bf16[2,128,512]{2,1,0:T(8,128)(2,1)S(1)}, bf16[2,128,512]{2,1,0:T(8,128)(2,1)}, u32[]{:S(2)}) copy-start(bf16[2,128,512]{2,1,0:T(8,128)(2,1)} %proj_ref.1) | copy-start | bytes 786436
  10.1 4.2 %copy-start.7 = (bf16[256,128]{1,0:T(8,128)(2,1)S(1)}, bf16[256,128]{1,0:T(8,128)(2,1)}, u32[]{:S(2)}) copy-start(bf16[256,128]{1,0:T(8,128)(2,1)} %get-tuple-element.14) | copy-start | bytes 196612
  14.5 6.8 %collective-permute-start.3 = (bf16[4,160,128]{2,1,0:T(8,128)(2,1)S(1)}, bf16[4,160,128]{2,1,0:T(8,128)(2,1)S(1)}, u32[]{:S(2)}, u32[]{:S(2)}) collective-permute-start(bf16[4,160,128]{2,1,0:T(8,128)(2,1)S(1)} %get-tuple-element.23), channel_id=1, source_target_pairs={{0,2},{1,3},{2,0},{3,1},{4,6},{5,7},{6,4},{7,5},{8,10},{9,11},{10,... | collective-permute-start | bytes 491528 | tf_op jit(solution)/shard_map/ppermute | solution.py:440
  16.1 9.1 %collective-permute-start.4 = (bf16[4,160,128]{2,1,0:T(8,128)(2,1)S(1)}, bf16[4,160,128]{2,1,0:T(8,128)(2,1)S(1)}, u32[]{:S(2)}, u32[]{:S(2)}) collective-permute-start(bf16[4,160,128]{2,1,0:T(8,128)(2,1)S(1)} %get-tuple-element.24), channel_id=1, source_target_pairs={{0,4},{1,5},{2,6},{3,7},{4,0},{5,1},{6,2},{7,3},{8,12},{9,13},{10,... | collective-permute-start | bytes 491528 | tf_op jit(solution)/shard_map/ppermute | solution.py:440
  17.6 7.6 %collective-permute-start.5 = (bf16[4,160,128]{2,1,0:T(8,128)(2,1)S(1)}, bf16[4,160,128]{2,1,0:T(8,128)(2,1)S(1)}, u32[]{:S(2)}, u32[]{:S(2)}) collective-permute-start(bf16[4,160,128]{2,1,0:T(8,128)(2,1)S(1)} %get-tuple-element.25), channel_id=1, source_target_pairs={{0,6},{1,7},{2,4},{3,5},{4,2},{5,3},{6,0},{7,1},{8,14},{9,15},{10,... | collective-permute-start | bytes 491528 | tf_op jit(solution)/shard_map/ppermute | solution.py:440
  25.3 2.2 %copy-start.2 = (bf16[2,128,128]{2,1,0:T(8,128)(2,1)S(1)}, bf16[2,128,128]{2,1,0:T(8,128)(2,1)}, u32[]{:S(2)}) copy-start(bf16[2,128,128]{2,1,0:T(8,128)(2,1)} %weight_ref.3) | copy-start | bytes 196612
  25.3 2.2 %copy-start.6 = (f32[2,128]{1,0:T(2,128)S(1)}, f32[2,128]{1,0:T(2,128)}, u32[]{:S(2)}) copy-start(f32[2,128]{1,0:T(2,128)} %offset_ref.3) | copy-start | bytes 3076
  25.3 2.2 %collective-permute-start.6 = (bf16[4,4,160,128]{3,2,1,0:T(8,128)(2,1)S(1)}, bf16[4,4,160,128]{3,2,1,0:T(8,128)(2,1)S(1)}, u32[]{:S(2)}, u32[]{:S(2)}) collective-permute-start(bf16[4,4,160,128]{3,2,1,0:T(8,128)(2,1)S(1)} %pad_maximum_fusion.mine_ref), channel_id=1, source_target_pairs={{0,1},{1,0},{2,3},{3,2},{4,5},{5,4},{6,7},{7,6},{8,9},{9,8},{10,11... | collective-permute-start | bytes 1966088 | tf_op jit(solution)/shard_map/ppermute | solution.py:440

commit v14 on v13

--- a/solution.py
+++ b/solution.py
@@ -166,12 +166,18 @@
     grid = [[x[(r * cols + c) * rows : (r * cols + c + 1) * rows] for c in range(cols)] for r in range(along)]
     grid = exchanged(grid, lax.axis_index("row"), lax.axis_index("col"))
     return jnp.concatenate(
-        [grid[s][2 * flip + other] for other in range(2) for flip in range(chips) for s in reversed(range(along))], 0
+        [
+            grid[s][2 * flip + other]
+            for other in range(2)
+            for flip in reversed(range(chips))
+            for s in reversed(range(along))
+        ],
+        0,
     )
 
 
 def to_devices(x, along, chips, rows):
-    at = lambda c, s: (((c % 2) * chips + c // 2) * along + along - 1 - s) * rows
+    at = lambda c, s: (((c % 2) * chips + chips - 1 - c // 2) * along + along - 1 - s) * rows
     grid = [[x[at(c, s) : at(c, s) + rows] for c in range(2 * chips)] for s in range(along)]
     grid = exchanged(grid, lax.axis_index("row"), lax.axis_index("col"))
     return jnp.concatenate([block for line in grid for block in line], 0)
@@ -453,7 +459,8 @@
         at = packed + flip * both
         return jnp.concatenate([line[:, :packed], line[:, at : at + both]], 1)
 
-    mine = jnp.stack([owned_by(0)] + [by_col(owned_by(flip), 2 * flip) for flip in range(1, chips)])
+    far_first = [by_col(owned_by(flip), 2 * flip) for flip in reversed(range(1, chips))]
+    mine = jnp.stack(far_first + [owned_by(0)])
     other = by_col(mine, 1)
     early = attend_early(mine, *start[:3])
     return attend(mine, other, early, start, ln_gain, ln_shift, w_proj, gate_bias, w_out, out_bias)

time: 30.4 us -> 30.2 us (level)
  transfers between devices with their start and end apart: 7 -> 7, of which waited for: 5 -> 6; matrix products, arithmetic and copies ran while one was open for 0% -> 0% of each run, Pallas kernels for 4% -> 4%
where the time goes in v14:
time: 30.2 us; the launch traced here: 30 us
  waiting for transfers between devices  12 us (40%)
  starting transfers between devices  9.41 us (31%)
  Pallas kernels  6.68 us (22%)
  local copies, waits for them, and re-layouts  1.03 us (3%)
  between operations  0.74 us (2%)
    ppermute x4, waiting for transfers between devices, by_col(): return lax.ppermute(block, 'col', [(i, i ^ flip) for i in range(cols)])  8.41 us
    ppermute x3, starting transfers between devices, by_row(): return lax.ppermute(block, 'row', [(i, i ^ shift) for i in range(along)])  5.78 us
    ppermute x4, starting transfers between devices, by_col(): return lax.ppermute(block, 'col', [(i, i ^ flip) for i in range(cols)])  3.62 us
    ppermute x3, waiting for transfers between devices, by_row(): return lax.ppermute(block, 'row', [(i, i ^ shift) for i in range(along)])  3.55 us
    pallas_call x1, Pallas kernels, attend(): pl.pallas_call(attend_kernel, out_shape=(result, result), in_specs=[VMEM]...  2.74 us
    pallas_call x1, Pallas kernels, local_bias(): pl.pallas_call(functools.partial(bias_kernel, along, chips), out_shape=(s...  2.73 us
    unnamed x16, local copies, waits for them, and re-layouts  1 us
    pallas_call x1, Pallas kernels, attend_early(): pl.pallas_call(early_kernel, out_shape=jax.ShapeDtypeStruct((WD, heads *...  0.62 us
  transfers between devices with their start and end apart: 7, of which 6 were waited for; matrix products, arithmetic and copies ran while one was open for 0% of the time, Pallas kernels for 4%

profile of v14, /device:TPU:0, one launch (start us, length us, event | category | flops | bytes accessed | tf_op | source)
XLA Modules:
  0.0 30.0 jit_solution(4292685495518670438)
XLA Ops:
  0.6 2.7 %bias.1 = (bf16[256,128]{1,0:T(8,128)(2,1)}, bf16[256,128]{1,0:T(8,128)(2,1)}, bf16[256,128]{1,0:T(8,128)(2,1)}, bf16[256,128]{1,0:T(8,128)(2,1)}) custom-call(bf16[8,256,128]{2,1,0:T(8,128)(2,1)} %lines_ref.1, s32[1,256]{1,0:T(1,128)} %bitcast.19, f32[2,128]{1,0:T(2,128)} %gain_ref.3, f32[2,128]{1,0:T(2,128)} %shift_ref.3, bf16[2,4,128]{2,1,0:T(4,128)(2,1)} %bitcast.18), custom_call_target="tpu_custom_call" | custom-call | tf_op jit(solution)/shard_map/bias/pallas_call | solution.py:119
  3.4 5.1 %collective-permute-start = (bf16[256,128]{1,0:T(8,128)(2,1)}, bf16[256,128]{1,0:T(8,128)(2,1)S(1)}, u32[]{:S(2)}, u32[]{:S(2)}) collective-permute-start(bf16[256,128]{1,0:T(8,128)(2,1)} %get-tuple-element.11), channel_id=1, source_target_pairs={{0,24},{8,16},{16,8},{24,0},{1,25},{9,17},{17,9},{25,1},{2,26},{10... | collective-permute-start | bytes 196616 | tf_op jit(solution)/shard_map/ppermute | solution.py:443
  8.5 0.0 collective-permute-start.1
  8.5 0.7 %collective-permute-start.2 = (bf16[256,128]{1,0:T(8,128)(2,1)}, bf16[256,128]{1,0:T(8,128)(2,1)S(1)}, u32[]{:S(2)}, u32[]{:S(2)}) collective-permute-start(bf16[256,128]{1,0:T(8,128)(2,1)} %get-tuple-element.13), channel_id=1, source_target_pairs={{0,8},{8,0},{16,24},{24,16},{1,9},{9,1},{17,25},{25,17},{2,10},{10... | collective-permute-start | bytes 196616 | tf_op jit(solution)/shard_map/ppermute | solution.py:443
  9.2 0.0 copy-done.5
  9.2 0.0 copy-done.3
  9.2 0.9 %copy-done.1 = bf16[2,128,512]{2,1,0:T(8,128)(2,1)S(1)} copy-done((bf16[2,128,512]{2,1,0:T(8,128)(2,1)S(1)}, bf16[2,128,512]{2,1,0:T(8,128)(2,1)}, u32[]{:S(2)}) %copy-start.1) | copy-done | bytes 262168
  10.2 0.6 %lines.1 = (bf16[2,128,256]{2,1,0:T(8,128)(2,1)S(1)}, bf16[2,4,256,32]{3,2,1,0:T(8,128)(2,1)S(1)}, bf16[2,128,256]{2,1,0:T(8,128)(2,1)S(1)}, f32[2,128,256]{2,1,0:T(8,128)S(1)}) custom-call(bf16[8,256,128]{2,1,0:T(8,128)(2,1)S(1)} %copy-done, f32[2,128]{1,0:T(2,128)S(1)} %copy-done.3, f32[2,128]{1,0:T(2,128)S(1)} %copy-done.4, ...), custom_call_target="tpu_custom_call" | custom-call | flops 67108864 | bytes 1048576 | tf_op jit(solution)/shard_map/lines/pallas_call | solution.py:235
  10.8 0.6 %collective-permute-done = bf16[256,128]{1,0:T(8,128)(2,1)S(1)} collective-permute-done((bf16[256,128]{1,0:T(8,128)(2,1)}, bf16[256,128]{1,0:T(8,128)(2,1)S(1)}, u32[]{:S(2)}, u32[]{:S(2)}) %collective-permute-start) | collective-permute-done | bytes 65568 | tf_op jit(solution)/shard_map/ppermute | solution.py:443
  11.3 3.0 %collective-permute-done.1 = bf16[256,128]{1,0:T(8,128)(2,1)S(1)} collective-permute-done((bf16[256,128]{1,0:T(8,128)(2,1)}, bf16[256,128]{1,0:T(8,128)(2,1)S(1)}, u32[]{:S(2)}, u32[]{:S(2)}) %collective-permute-start.1) | collective-permute-done | bytes 65568 | tf_op jit(solution)/shard_map/ppermute | solution.py:443
  14.4 0.1 pad_maximum_fusion.2
  14.5 2.6 %collective-permute-start.3 = (bf16[4,160,128]{2,1,0:T(8,128)(2,1)S(1)}, bf16[4,160,128]{2,1,0:T(8,128)(2,1)S(1)}, u32[]{:S(2)}, u32[]{:S(2)}) collective-permute-start(bf16[4,160,128]{2,1,0:T(8,128)(2,1)S(1)} %get-tuple-element.23), channel_id=1, source_target_pairs={{0,6},{1,7},{2,4},{3,5},{4,2},{5,3},{6,0},{7,1},{8,14},{9,15},{10,... | collective-permute-start | bytes 491528 | tf_op jit(solution)/shard_map/ppermute | solution.py:446
  17.0 0.5 %collective-permute-start.4 = (bf16[4,160,128]{2,1,0:T(8,128)(2,1)S(1)}, bf16[4,160,128]{2,1,0:T(8,128)(2,1)S(1)}, u32[]{:S(2)}, u32[]{:S(2)}) collective-permute-start(bf16[4,160,128]{2,1,0:T(8,128)(2,1)S(1)} %get-tuple-element.24), channel_id=1, source_target_pairs={{0,4},{1,5},{2,6},{3,7},{4,0},{5,1},{6,2},{7,3},{8,12},{9,13},{10,... | collective-permute-start | bytes 491528 | tf_op jit(solution)/shard_map/ppermute | solution.py:446
  17.5 0.5 %collective-permute-start.5 = (bf16[4,160,128]{2,1,0:T(8,128)(2,1)S(1)}, bf16[4,160,128]{2,1,0:T(8,128)(2,1)S(1)}, u32[]{:S(2)}, u32[]{:S(2)}) collective-permute-start(bf16[4,160,128]{2,1,0:T(8,128)(2,1)S(1)} %get-tuple-element.25), channel_id=1, source_target_pairs={{0,2},{1,3},{2,0},{3,1},{4,6},{5,7},{6,4},{7,5},{8,10},{9,11},{10,... | collective-permute-start | bytes 491528 | tf_op jit(solution)/shard_map/ppermute | solution.py:446
  18.0 4.0 %collective-permute-done.3 = bf16[4,160,128]{2,1,0:T(8,128)(2,1)S(1)} collective-permute-done((bf16[4,160,128]{2,1,0:T(8,128)(2,1)S(1)}, bf16[4,160,128]{2,1,0:T(8,128)(2,1)S(1)}, u32[]{:S(2)}, u32[]{:S(2)}) %collective-permute-start.3) | collective-permute-done | bytes 163872 | tf_op jit(solution)/shard_map/ppermute | solution.py:446
  22.0 2.7 %collective-permute-done.4 = bf16[4,160,128]{2,1,0:T(8,128)(2,1)S(1)} collective-permute-done((bf16[4,160,128]{2,1,0:T(8,128)(2,1)S(1)}, bf16[4,160,128]{2,1,0:T(8,128)(2,1)S(1)}, u32[]{:S(2)}, u32[]{:S(2)}) %collective-permute-start.4) | collective-permute-done | bytes 163872 | tf_op jit(solution)/shard_map/ppermute | solution.py:446
  24.7 0.3 collective-permute-done.5
  25.0 0.1 pad_maximum_fusion.mine_ref
  25.1 0.0 copy-start.2
  25.1 0.0 copy-start.6
  25.1 0.1 collective-permute-start.6
  25.2 0.6 %early.1.early_ref = f32[2,128,128]{2,1,0:T(8,128)S(1)} custom-call(bf16[4,4,160,128]{3,2,1,0:T(8,128)(2,1)S(1)} %pad_maximum_fusion.mine_ref, bf16[2,128,256]{2,1,0:T(8,128)(2,1)S(1)} %get-tuple-element.15.q.q0, bf16[2,4,256,32]{3,2,1,0:T(8,128)(2,1)S(1)} %get-tuple-element.16.k.k0, bf16[2,128,256]{2,1,0:T(8,128)(2,1)S(1)} %get-tuple-element.17.v.v0), custom_call_target="tpu_custom_call" | custom-call | flops 67108864 | bytes 2097152 | tf_op jit(solution)/shard_map/early/pallas_call | solution.py:346
  25.8 1.5 %collective-permute-done.6.other_ref = bf16[4,4,160,128]{3,2,1,0:T(8,128)(2,1)S(1)} collective-permute-done((bf16[4,4,160,128]{3,2,1,0:T(8,128)(2,1)S(1)}, bf16[4,4,160,128]{3,2,1,0:T(8,128)(2,1)S(1)}, u32[]{:S(2)}, u32[]{:S(2)}) %collective-permute-start.6) | collective-permute-done | bytes 655392 | tf_op jit(solution)/shard_map/ppermute | solution.py:446
  27.3 2.7 %attend.1 = (bf16[2,256,128]{2,1,0:T(8,128)(2,1)}, bf16[2,256,128]{2,1,0:T(8,128)(2,1)}) custom-call(bf16[4,4,160,128]{3,2,1,0:T(8,128)(2,1)S(1)} %pad_maximum_fusion.mine_ref, bf16[4,4,160,128]{3,2,1,0:T(8,128)(2,1)S(1)} %collective-permute-done.6.other_ref, f32[2,128,128]{2,1,0:T(8,128)S(1)} %early.1.early_ref, ...), custom_call_target="tpu_custom_call" | custom-call | tf_op jit(solution)/shard_map/attend/pallas_call | solution.py:419
  (16 shorter events, 0.1 us)
Async XLA Ops:
  0.6 8.5 %copy-start = (bf16[8,256,128]{2,1,0:T(8,128)(2,1)S(1)}, bf16[8,256,128]{2,1,0:T(8,128)(2,1)}, u32[]{:S(2)}) copy-start(bf16[8,256,128]{2,1,0:T(8,128)(2,1)} %lines_ref.1) | copy-start | bytes 1572868
  3.4 7.9 %collective-permute-start = (bf16[256,128]{1,0:T(8,128)(2,1)}, bf16[256,128]{1,0:T(8,128)(2,1)S(1)}, u32[]{:S(2)}, u32[]{:S(2)}) collective-permute-start(bf16[256,128]{1,0:T(8,128)(2,1)} %get-tuple-element.11), channel_id=1, source_target_pairs={{0,24},{8,16},{16,8},{24,0},{1,25},{9,17},{17,9},{25,1},{2,26},{10... | collective-permute-start | bytes 196616 | tf_op jit(solution)/shard_map/ppermute | solution.py:443
  8.5 0.7 %copy-start.4 = (f32[2,128]{1,0:T(2,128)S(1)}, f32[2,128]{1,0:T(2,128)}, u32[]{:S(2)}) copy-start(f32[2,128]{1,0:T(2,128)} %shift_ref.3) | copy-start | bytes 3076
  8.5 0.7 %copy-start.5 = (f32[2,128]{1,0:T(2,128)S(1)}, f32[2,128]{1,0:T(2,128)}, u32[]{:S(2)}) copy-start(f32[2,128]{1,0:T(2,128)} %gate_ref.1) | copy-start | bytes 3076
  8.5 0.7 %copy-start.3 = (f32[2,128]{1,0:T(2,128)S(1)}, f32[2,128]{1,0:T(2,128)}, u32[]{:S(2)}) copy-start(f32[2,128]{1,0:T(2,128)} %gain_ref.3) | copy-start | bytes 3076
  8.5 5.8 %collective-permute-start.1 = (bf16[256,128]{1,0:T(8,128)(2,1)}, bf16[256,128]{1,0:T(8,128)(2,1)S(1)}, u32[]{:S(2)}, u32[]{:S(2)}) collective-permute-start(bf16[256,128]{1,0:T(8,128)(2,1)} %get-tuple-element.12), channel_id=1, source_target_pairs={{0,16},{8,24},{16,0},{24,8},{1,17},{9,25},{17,1},{25,9},{2,18},{10... | collective-permute-start | bytes 196616 | tf_op jit(solution)/shard_map/ppermute | solution.py:443
  8.5 5.8 %collective-permute-start.2 = (bf16[256,128]{1,0:T(8,128)(2,1)}, bf16[256,128]{1,0:T(8,128)(2,1)S(1)}, u32[]{:S(2)}, u32[]{:S(2)}) collective-permute-start(bf16[256,128]{1,0:T(8,128)(2,1)} %get-tuple-element.13), channel_id=1, source_target_pairs={{0,8},{8,0},{16,24},{24,16},{1,9},{9,1},{17,25},{25,17},{2,10},{10... | collective-permute-start | bytes 196616 | tf_op jit(solution)/shard_map/ppermute | solution.py:443
  9.2 0.9 %copy-start.1 = (bf16[2,128,512]{2,1,0:T(8,128)(2,1)S(1)}, bf16[2,128,512]{2,1,0:T(8,128)(2,1)}, u32[]{:S(2)}) copy-start(bf16[2,128,512]{2,1,0:T(8,128)(2,1)} %proj_ref.1) | copy-start | bytes 786436
  10.1 4.2 %copy-start.7 = (bf16[256,128]{1,0:T(8,128)(2,1)S(1)}, bf16[256,128]{1,0:T(8,128)(2,1)}, u32[]{:S(2)}) copy-start(bf16[256,128]{1,0:T(8,128)(2,1)} %get-tuple-element.14) | copy-start | bytes 196612
  14.5 7.6 %collective-permute-start.3 = (bf16[4,160,128]{2,1,0:T(8,128)(2,1)S(1)}, bf16[4,160,128]{2,1,0:T(8,128)(2,1)S(1)}, u32[]{:S(2)}, u32[]{:S(2)}) collective-permute-start(bf16[4,160,128]{2,1,0:T(8,128)(2,1)S(1)} %get-tuple-element.23), channel_id=1, source_target_pairs={{0,6},{1,7},{2,4},{3,5},{4,2},{5,3},{6,0},{7,1},{8,14},{9,15},{10,... | collective-permute-start | bytes 491528 | tf_op jit(solution)/shard_map/ppermute | solution.py:446
  17.0 7.7 %collective-permute-start.4 = (bf16[4,160,128]{2,1,0:T(8,128)(2,1)S(1)}, bf16[4,160,128]{2,1,0:T(8,128)(2,1)S(1)}, u32[]{:S(2)}, u32[]{:S(2)}) collective-permute-start(bf16[4,160,128]{2,1,0:T(8,128)(2,1)S(1)} %get-tuple-element.24), channel_id=1, source_target_pairs={{0,4},{1,5},{2,6},{3,7},{4,0},{5,1},{6,2},{7,3},{8,12},{9,13},{10,... | collective-permute-start | bytes 491528 | tf_op jit(solution)/shard_map/ppermute | solution.py:446
  17.5 7.4 %collective-permute-start.5 = (bf16[4,160,128]{2,1,0:T(8,128)(2,1)S(1)}, bf16[4,160,128]{2,1,0:T(8,128)(2,1)S(1)}, u32[]{:S(2)}, u32[]{:S(2)}) collective-permute-start(bf16[4,160,128]{2,1,0:T(8,128)(2,1)S(1)} %get-tuple-element.25), channel_id=1, source_target_pairs={{0,2},{1,3},{2,0},{3,1},{4,6},{5,7},{6,4},{7,5},{8,10},{9,11},{10,... | collective-permute-start | bytes 491528 | tf_op jit(solution)/shard_map/ppermute | solution.py:446
  25.1 2.2 %copy-start.2 = (bf16[2,128,128]{2,1,0:T(8,128)(2,1)S(1)}, bf16[2,128,128]{2,1,0:T(8,128)(2,1)}, u32[]{:S(2)}) copy-start(bf16[2,128,128]{2,1,0:T(8,128)(2,1)} %weight_ref.3) | copy-start | bytes 196612
  25.1 2.2 %copy-start.6 = (f32[2,128]{1,0:T(2,128)S(1)}, f32[2,128]{1,0:T(2,128)}, u32[]{:S(2)}) copy-start(f32[2,128]{1,0:T(2,128)} %offset_ref.3) | copy-start | bytes 3076
  25.1 2.2 %collective-permute-start.6 = (bf16[4,4,160,128]{3,2,1,0:T(8,128)(2,1)S(1)}, bf16[4,4,160,128]{3,2,1,0:T(8,128)(2,1)S(1)}, u32[]{:S(2)}, u32[]{:S(2)}) collective-permute-start(bf16[4,4,160,128]{3,2,1,0:T(8,128)(2,1)S(1)} %pad_maximum_fusion.mine_ref), channel_id=1, source_target_pairs={{0,1},{1,0},{2,3},{3,2},{4,5},{5,4},{6,7},{7,6},{8,9},{9,8},{10,11... | collective-permute-start | bytes 1966088 | tf_op jit(solution)/shard_map/ppermute | solution.py:446

commit v15 on v14

--- a/solution.py
+++ b/solution.py
@@ -371,6 +371,19 @@
     packed = 2 * heads * rows * (length // mine_ref.shape[3])
     first = pl.multiple_of(packed + lax.rem(lax.axis_index("col"), 2) * WD * rows, WD * rows)
     groups = start_half(other_ref, 1, q0, k0, v0, late, turned_bias)
+
+    def finish_start():
+        gated = [
+            (jnp.concatenate([early_ref[w], late[w]], 1) * g0[w]).astype(jnp.bfloat16) for w in range(WD)
+        ]
+        full = [contract(line, weight_ref[0], 0, 0) + offset_ref[0:1, :] for line in gated]
+        for w in range(WD):
+            out0[w] = to_devices(full[w], along, chips, rows).astype(jnp.bfloat16)
+
+    if groups:
+        groups[-1] = (groups[-1][0], lambda outs, put=groups[-1][1]: (put(outs), finish_start()))
+    else:
+        finish_start()
     offset = turned(gate_ref[1:2, :])
     blocks = []
     for source in (mine_ref, other_ref):
@@ -401,14 +414,10 @@
 
         for_each(length // CHUNK, step, False)
     attend_groups(groups)
+    gated = [(mixed[w] * g1[w]).astype(jnp.bfloat16) for w in range(WD)]
+    full = [contract(line, weight_ref[1], 0, 0) + offset_ref[1:2, :] for line in gated]
     for w in range(WD):
-        gated = (jnp.concatenate([early_ref[w], late[w]], 1) * g0[w]).astype(jnp.bfloat16)
-        full = contract(gated, weight_ref[0], 0, 0) + offset_ref[0:1, :]
-        out0[w] = to_devices(full, along, chips, rows).astype(jnp.bfloat16)
-    for w in range(WD):
-        gated = (mixed[w] * g1[w]).astype(jnp.bfloat16)
-        full = contract(gated, weight_ref[1], 0, 0) + offset_ref[1:2, :]
-        out1[w] = full.astype(jnp.bfloat16)
+        out1[w] = full[w].astype(jnp.bfloat16)
 
 
 def attend(mine, other, early, start, gain, shift, proj, gate, weight, offset):

time: 30.2 us -> 30.2 us (level)
  no operation moved by 1% of the time
where the time goes in v15:
time: 30.2 us; the launch traced here: 30.1 us
  waiting for transfers between devices  12 us (40%)
  starting transfers between devices  9.41 us (31%)
  Pallas kernels  6.75 us (22%)
  local copies, waits for them, and re-layouts  1.03 us (3%)
  between operations  0.74 us (2%)
    ppermute x4, waiting for transfers between devices, by_col(): return lax.ppermute(block, 'col', [(i, i ^ flip) for i in range(cols)])  8.41 us
    ppermute x3, starting transfers between devices, by_row(): return lax.ppermute(block, 'row', [(i, i ^ shift) for i in range(along)])  5.78 us
    ppermute x4, starting transfers between devices, by_col(): return lax.ppermute(block, 'col', [(i, i ^ flip) for i in range(cols)])  3.62 us
    ppermute x3, waiting for transfers between devices, by_row(): return lax.ppermute(block, 'row', [(i, i ^ shift) for i in range(along)])  3.55 us
    pallas_call x1, Pallas kernels, attend(): pl.pallas_call(attend_kernel, out_shape=(result, result), in_specs=[VMEM]...  2.81 us
    pallas_call x1, Pallas kernels, local_bias(): pl.pallas_call(functools.partial(bias_kernel, along, chips), out_shape=(s...  2.73 us
    unnamed x16, local copies, waits for them, and re-layouts  1 us
    pallas_call x1, Pallas kernels, attend_early(): pl.pallas_call(early_kernel, out_shape=jax.ShapeDtypeStruct((WD, heads *...  0.62 us
  transfers between devices with their start and end apart: 7, of which 6 were waited for; matrix products, arithmetic and copies ran while one was open for 0% of the time, Pallas kernels for 4%

profile of v15, /device:TPU:0, one launch (start us, length us, event | category | flops | bytes accessed | tf_op | source)
XLA Modules:
  0.0 30.1 jit_solution(16727971102892400443)
XLA Ops:
  0.6 2.7 %bias.1 = (bf16[256,128]{1,0:T(8,128)(2,1)}, bf16[256,128]{1,0:T(8,128)(2,1)}, bf16[256,128]{1,0:T(8,128)(2,1)}, bf16[256,128]{1,0:T(8,128)(2,1)}) custom-call(bf16[8,256,128]{2,1,0:T(8,128)(2,1)} %lines_ref.1, s32[1,256]{1,0:T(1,128)} %bitcast.19, f32[2,128]{1,0:T(2,128)} %gain_ref.3, f32[2,128]{1,0:T(2,128)} %shift_ref.3, bf16[2,4,128]{2,1,0:T(4,128)(2,1)} %bitcast.18), custom_call_target="tpu_custom_call" | custom-call | tf_op jit(solution)/shard_map/bias/pallas_call | solution.py:119
  3.4 5.1 %collective-permute-start = (bf16[256,128]{1,0:T(8,128)(2,1)}, bf16[256,128]{1,0:T(8,128)(2,1)S(1)}, u32[]{:S(2)}, u32[]{:S(2)}) collective-permute-start(bf16[256,128]{1,0:T(8,128)(2,1)} %get-tuple-element.11), channel_id=1, source_target_pairs={{0,24},{8,16},{16,8},{24,0},{1,25},{9,17},{17,9},{25,1},{2,26},{10... | collective-permute-start | bytes 196616 | tf_op jit(solution)/shard_map/ppermute | solution.py:452
  8.5 0.7 %collective-permute-start.2 = (bf16[256,128]{1,0:T(8,128)(2,1)}, bf16[256,128]{1,0:T(8,128)(2,1)S(1)}, u32[]{:S(2)}, u32[]{:S(2)}) collective-permute-start(bf16[256,128]{1,0:T(8,128)(2,1)} %get-tuple-element.13), channel_id=1, source_target_pairs={{0,8},{8,0},{16,24},{24,16},{1,9},{9,1},{17,25},{25,17},{2,10},{10... | collective-permute-start | bytes 196616 | tf_op jit(solution)/shard_map/ppermute | solution.py:452
  9.2 0.0 copy-done.5
  9.2 0.0 copy-done.3
  9.2 0.9 %copy-done.1 = bf16[2,128,512]{2,1,0:T(8,128)(2,1)S(1)} copy-done((bf16[2,128,512]{2,1,0:T(8,128)(2,1)S(1)}, bf16[2,128,512]{2,1,0:T(8,128)(2,1)}, u32[]{:S(2)}) %copy-start.1) | copy-done | bytes 262168
  10.2 0.6 %lines.1 = (bf16[2,128,256]{2,1,0:T(8,128)(2,1)S(1)}, bf16[2,4,256,32]{3,2,1,0:T(8,128)(2,1)S(1)}, bf16[2,128,256]{2,1,0:T(8,128)(2,1)S(1)}, f32[2,128,256]{2,1,0:T(8,128)S(1)}) custom-call(bf16[8,256,128]{2,1,0:T(8,128)(2,1)S(1)} %copy-done, f32[2,128]{1,0:T(2,128)S(1)} %copy-done.3, f32[2,128]{1,0:T(2,128)S(1)} %copy-done.4, ...), custom_call_target="tpu_custom_call" | custom-call | flops 67108864 | bytes 1048576 | tf_op jit(solution)/shard_map/lines/pallas_call | solution.py:235
  10.8 0.6 %collective-permute-done = bf16[256,128]{1,0:T(8,128)(2,1)S(1)} collective-permute-done((bf16[256,128]{1,0:T(8,128)(2,1)}, bf16[256,128]{1,0:T(8,128)(2,1)S(1)}, u32[]{:S(2)}, u32[]{:S(2)}) %collective-permute-start) | collective-permute-done | bytes 65568 | tf_op jit(solution)/shard_map/ppermute | solution.py:452
  11.3 3.0 %collective-permute-done.1 = bf16[256,128]{1,0:T(8,128)(2,1)S(1)} collective-permute-done((bf16[256,128]{1,0:T(8,128)(2,1)}, bf16[256,128]{1,0:T(8,128)(2,1)S(1)}, u32[]{:S(2)}, u32[]{:S(2)}) %collective-permute-start.1) | collective-permute-done | bytes 65568 | tf_op jit(solution)/shard_map/ppermute | solution.py:452
  14.3 0.0 collective-permute-done.2
  14.4 0.1 pad_maximum_fusion.2
  14.5 2.6 %collective-permute-start.3 = (bf16[4,160,128]{2,1,0:T(8,128)(2,1)S(1)}, bf16[4,160,128]{2,1,0:T(8,128)(2,1)S(1)}, u32[]{:S(2)}, u32[]{:S(2)}) collective-permute-start(bf16[4,160,128]{2,1,0:T(8,128)(2,1)S(1)} %get-tuple-element.23), channel_id=1, source_target_pairs={{0,6},{1,7},{2,4},{3,5},{4,2},{5,3},{6,0},{7,1},{8,14},{9,15},{10,... | collective-permute-start | bytes 491528 | tf_op jit(solution)/shard_map/ppermute | solution.py:455
  17.0 0.5 %collective-permute-start.4 = (bf16[4,160,128]{2,1,0:T(8,128)(2,1)S(1)}, bf16[4,160,128]{2,1,0:T(8,128)(2,1)S(1)}, u32[]{:S(2)}, u32[]{:S(2)}) collective-permute-start(bf16[4,160,128]{2,1,0:T(8,128)(2,1)S(1)} %get-tuple-element.24), channel_id=1, source_target_pairs={{0,4},{1,5},{2,6},{3,7},{4,0},{5,1},{6,2},{7,3},{8,12},{9,13},{10,... | collective-permute-start | bytes 491528 | tf_op jit(solution)/shard_map/ppermute | solution.py:455
  17.5 0.5 %collective-permute-start.5 = (bf16[4,160,128]{2,1,0:T(8,128)(2,1)S(1)}, bf16[4,160,128]{2,1,0:T(8,128)(2,1)S(1)}, u32[]{:S(2)}, u32[]{:S(2)}) collective-permute-start(bf16[4,160,128]{2,1,0:T(8,128)(2,1)S(1)} %get-tuple-element.25), channel_id=1, source_target_pairs={{0,2},{1,3},{2,0},{3,1},{4,6},{5,7},{6,4},{7,5},{8,10},{9,11},{10,... | collective-permute-start | bytes 491528 | tf_op jit(solution)/shard_map/ppermute | solution.py:455
  18.0 4.0 %collective-permute-done.3 = bf16[4,160,128]{2,1,0:T(8,128)(2,1)S(1)} collective-permute-done((bf16[4,160,128]{2,1,0:T(8,128)(2,1)S(1)}, bf16[4,160,128]{2,1,0:T(8,128)(2,1)S(1)}, u32[]{:S(2)}, u32[]{:S(2)}) %collective-permute-start.3) | collective-permute-done | bytes 163872 | tf_op jit(solution)/shard_map/ppermute | solution.py:455
  22.0 2.7 %collective-permute-done.4 = bf16[4,160,128]{2,1,0:T(8,128)(2,1)S(1)} collective-permute-done((bf16[4,160,128]{2,1,0:T(8,128)(2,1)S(1)}, bf16[4,160,128]{2,1,0:T(8,128)(2,1)S(1)}, u32[]{:S(2)}, u32[]{:S(2)}) %collective-permute-start.4) | collective-permute-done | bytes 163872 | tf_op jit(solution)/shard_map/ppermute | solution.py:455
  24.7 0.3 collective-permute-done.5
  25.0 0.1 pad_maximum_fusion.mine_ref
  25.1 0.0 copy-start.2
  25.1 0.0 copy-start.6
  25.1 0.1 collective-permute-start.6
  25.2 0.6 %early.1.early_ref = f32[2,128,128]{2,1,0:T(8,128)S(1)} custom-call(bf16[4,4,160,128]{3,2,1,0:T(8,128)(2,1)S(1)} %pad_maximum_fusion.mine_ref, bf16[2,128,256]{2,1,0:T(8,128)(2,1)S(1)} %get-tuple-element.15.q.q0, bf16[2,4,256,32]{3,2,1,0:T(8,128)(2,1)S(1)} %get-tuple-element.16.k.k0, bf16[2,128,256]{2,1,0:T(8,128)(2,1)S(1)} %get-tuple-element.17.v.v0), custom_call_target="tpu_custom_call" | custom-call | flops 67108864 | bytes 2097152 | tf_op jit(solution)/shard_map/early/pallas_call | solution.py:346
  25.8 1.5 %collective-permute-done.6.other_ref = bf16[4,4,160,128]{3,2,1,0:T(8,128)(2,1)S(1)} collective-permute-done((bf16[4,4,160,128]{3,2,1,0:T(8,128)(2,1)S(1)}, bf16[4,4,160,128]{3,2,1,0:T(8,128)(2,1)S(1)}, u32[]{:S(2)}, u32[]{:S(2)}) %collective-permute-start.6) | collective-permute-done | bytes 655392 | tf_op jit(solution)/shard_map/ppermute | solution.py:455
  27.3 2.8 %attend.1 = (bf16[2,256,128]{2,1,0:T(8,128)(2,1)}, bf16[2,256,128]{2,1,0:T(8,128)(2,1)}) custom-call(bf16[4,4,160,128]{3,2,1,0:T(8,128)(2,1)S(1)} %pad_maximum_fusion.mine_ref, bf16[4,4,160,128]{3,2,1,0:T(8,128)(2,1)S(1)} %collective-permute-done.6.other_ref, f32[2,128,128]{2,1,0:T(8,128)S(1)} %early.1.early_ref, ...), custom_call_target="tpu_custom_call" | custom-call | tf_op jit(solution)/shard_map/attend/pallas_call | solution.py:428
  (16 shorter events, 0.1 us)
Async XLA Ops:
  0.6 8.5 %copy-start = (bf16[8,256,128]{2,1,0:T(8,128)(2,1)S(1)}, bf16[8,256,128]{2,1,0:T(8,128)(2,1)}, u32[]{:S(2)}) copy-start(bf16[8,256,128]{2,1,0:T(8,128)(2,1)} %lines_ref.1) | copy-start | bytes 1572868
  3.4 7.9 %collective-permute-start = (bf16[256,128]{1,0:T(8,128)(2,1)}, bf16[256,128]{1,0:T(8,128)(2,1)S(1)}, u32[]{:S(2)}, u32[]{:S(2)}) collective-permute-start(bf16[256,128]{1,0:T(8,128)(2,1)} %get-tuple-element.11), channel_id=1, source_target_pairs={{0,24},{8,16},{16,8},{24,0},{1,25},{9,17},{17,9},{25,1},{2,26},{10... | collective-permute-start | bytes 196616 | tf_op jit(solution)/shard_map/ppermute | solution.py:452
  8.5 0.7 %copy-start.4 = (f32[2,128]{1,0:T(2,128)S(1)}, f32[2,128]{1,0:T(2,128)}, u32[]{:S(2)}) copy-start(f32[2,128]{1,0:T(2,128)} %shift_ref.3) | copy-start | bytes 3076
  8.5 0.7 %copy-start.5 = (f32[2,128]{1,0:T(2,128)S(1)}, f32[2,128]{1,0:T(2,128)}, u32[]{:S(2)}) copy-start(f32[2,128]{1,0:T(2,128)} %gate_ref.1) | copy-start | bytes 3076
  8.5 0.7 %copy-start.3 = (f32[2,128]{1,0:T(2,128)S(1)}, f32[2,128]{1,0:T(2,128)}, u32[]{:S(2)}) copy-start(f32[2,128]{1,0:T(2,128)} %gain_ref.3) | copy-start | bytes 3076
  8.5 5.8 %collective-permute-start.1 = (bf16[256,128]{1,0:T(8,128)(2,1)}, bf16[256,128]{1,0:T(8,128)(2,1)S(1)}, u32[]{:S(2)}, u32[]{:S(2)}) collective-permute-start(bf16[256,128]{1,0:T(8,128)(2,1)} %get-tuple-element.12), channel_id=1, source_target_pairs={{0,16},{8,24},{16,0},{24,8},{1,17},{9,25},{17,1},{25,9},{2,18},{10... | collective-permute-start | bytes 196616 | tf_op jit(solution)/shard_map/ppermute | solution.py:452
  8.5 5.8 %collective-permute-start.2 = (bf16[256,128]{1,0:T(8,128)(2,1)}, bf16[256,128]{1,0:T(8,128)(2,1)S(1)}, u32[]{:S(2)}, u32[]{:S(2)}) collective-permute-start(bf16[256,128]{1,0:T(8,128)(2,1)} %get-tuple-element.13), channel_id=1, source_target_pairs={{0,8},{8,0},{16,24},{24,16},{1,9},{9,1},{17,25},{25,17},{2,10},{10... | collective-permute-start | bytes 196616 | tf_op jit(solution)/shard_map/ppermute | solution.py:452
  9.2 0.9 %copy-start.1 = (bf16[2,128,512]{2,1,0:T(8,128)(2,1)S(1)}, bf16[2,128,512]{2,1,0:T(8,128)(2,1)}, u32[]{:S(2)}) copy-start(bf16[2,128,512]{2,1,0:T(8,128)(2,1)} %proj_ref.1) | copy-start | bytes 786436
  10.1 4.2 %copy-start.7 = (bf16[256,128]{1,0:T(8,128)(2,1)S(1)}, bf16[256,128]{1,0:T(8,128)(2,1)}, u32[]{:S(2)}) copy-start(bf16[256,128]{1,0:T(8,128)(2,1)} %get-tuple-element.14) | copy-start | bytes 196612
  14.5 7.6 %collective-permute-start.3 = (bf16[4,160,128]{2,1,0:T(8,128)(2,1)S(1)}, bf16[4,160,128]{2,1,0:T(8,128)(2,1)S(1)}, u32[]{:S(2)}, u32[]{:S(2)}) collective-permute-start(bf16[4,160,128]{2,1,0:T(8,128)(2,1)S(1)} %get-tuple-element.23), channel_id=1, source_target_pairs={{0,6},{1,7},{2,4},{3,5},{4,2},{5,3},{6,0},{7,1},{8,14},{9,15},{10,... | collective-permute-start | bytes 491528 | tf_op jit(solution)/shard_map/ppermute | solution.py:455
  17.0 7.7 %collective-permute-start.4 = (bf16[4,160,128]{2,1,0:T(8,128)(2,1)S(1)}, bf16[4,160,128]{2,1,0:T(8,128)(2,1)S(1)}, u32[]{:S(2)}, u32[]{:S(2)}) collective-permute-start(bf16[4,160,128]{2,1,0:T(8,128)(2,1)S(1)} %get-tuple-element.24), channel_id=1, source_target_pairs={{0,4},{1,5},{2,6},{3,7},{4,0},{5,1},{6,2},{7,3},{8,12},{9,13},{10,... | collective-permute-start | bytes 491528 | tf_op jit(solution)/shard_map/ppermute | solution.py:455
  17.5 7.4 %collective-permute-start.5 = (bf16[4,160,128]{2,1,0:T(8,128)(2,1)S(1)}, bf16[4,160,128]{2,1,0:T(8,128)(2,1)S(1)}, u32[]{:S(2)}, u32[]{:S(2)}) collective-permute-start(bf16[4,160,128]{2,1,0:T(8,128)(2,1)S(1)} %get-tuple-element.25), channel_id=1, source_target_pairs={{0,2},{1,3},{2,0},{3,1},{4,6},{5,7},{6,4},{7,5},{8,10},{9,11},{10,... | collective-permute-start | bytes 491528 | tf_op jit(solution)/shard_map/ppermute | solution.py:455
  25.1 2.2 %copy-start.2 = (bf16[2,128,128]{2,1,0:T(8,128)(2,1)S(1)}, bf16[2,128,128]{2,1,0:T(8,128)(2,1)}, u32[]{:S(2)}) copy-start(bf16[2,128,128]{2,1,0:T(8,128)(2,1)} %weight_ref.3) | copy-start | bytes 196612
  25.1 2.2 %copy-start.6 = (f32[2,128]{1,0:T(2,128)S(1)}, f32[2,128]{1,0:T(2,128)}, u32[]{:S(2)}) copy-start(f32[2,128]{1,0:T(2,128)} %offset_ref.3) | copy-start | bytes 3076
  25.1 2.2 %collective-permute-start.6 = (bf16[4,4,160,128]{3,2,1,0:T(8,128)(2,1)S(1)}, bf16[4,4,160,128]{3,2,1,0:T(8,128)(2,1)S(1)}, u32[]{:S(2)}, u32[]{:S(2)}) collective-permute-start(bf16[4,4,160,128]{3,2,1,0:T(8,128)(2,1)S(1)} %pad_maximum_fusion.mine_ref), channel_id=1, source_target_pairs={{0,1},{1,0},{2,3},{3,2},{4,5},{5,4},{6,7},{7,6},{8,9},{9,8},{10,11... | collective-permute-start | bytes 1966088 | tf_op jit(solution)/shard_map/ppermute | solution.py:455

commit v16 on v14

--- a/solution.py
+++ b/solution.py
@@ -28,7 +28,9 @@
 
 
 def standardize_all(lines):
-    centers = [jnp.mean(wide, -1, keepdims=True) for wide in lines]
+    channels = lines[0].shape[-1]
+    ones = jnp.ones((channels, channels), jnp.bfloat16)
+    centers = [contract(wide.astype(jnp.bfloat16), ones, 1, 0) * (1.0 / channels) for wide in lines]
     aways = [wide - center for wide, center in zip(lines, centers)]
     spreads = [jnp.mean(jnp.square(away), -1, keepdims=True) for away in aways]
     return [away * lax.rsqrt(spread + EPS) for away, spread in zip(aways, spreads)]

time: 30.2 us -> 30.2 us (level)
  no operation moved by 1% of the time
where the time goes in v16:
time: 30.2 us; the launch traced here: 30 us
  waiting for transfers between devices  11.9 us (39%)
  starting transfers between devices  9.4 us (31%)
  Pallas kernels  6.7 us (22%)
  local copies, waits for them, and re-layouts  1.03 us (3%)
  between operations  0.74 us (2%)
    ppermute x4, waiting for transfers between devices, by_col(): return lax.ppermute(block, 'col', [(i, i ^ flip) for i in range(cols)])  8.4 us
    ppermute x3, starting transfers between devices, by_row(): return lax.ppermute(block, 'row', [(i, i ^ shift) for i in range(along)])  5.78 us
    ppermute x4, starting transfers between devices, by_col(): return lax.ppermute(block, 'col', [(i, i ^ flip) for i in range(cols)])  3.62 us
    ppermute x3, waiting for transfers between devices, by_row(): return lax.ppermute(block, 'row', [(i, i ^ shift) for i in range(along)])  3.5 us
    pallas_call x1, Pallas kernels, attend(): pl.pallas_call(attend_kernel, out_shape=(result, result), in_specs=[VMEM]...  2.76 us
    pallas_call x1, Pallas kernels, local_bias(): pl.pallas_call(functools.partial(bias_kernel, along, chips), out_shape=(s...  2.68 us
    unnamed x16, local copies, waits for them, and re-layouts  1 us
    pallas_call x1, Pallas kernels, local_lines(): pl.pallas_call(functools.partial(lines_kernel, along, chips), grid=(1,),...  0.64 us
  transfers between devices with their start and end apart: 7, of which 6 were waited for; matrix products, arithmetic and copies ran while one was open for 0% of the time, Pallas kernels for 4%

profile of v16, /device:TPU:0, one launch (start us, length us, event | category | flops | bytes accessed | tf_op | source)
XLA Modules:
  0.0 30.0 jit_solution(8486464612916313248)
XLA Ops:
  0.6 2.7 %bias.1 = (bf16[256,128]{1,0:T(8,128)(2,1)}, bf16[256,128]{1,0:T(8,128)(2,1)}, bf16[256,128]{1,0:T(8,128)(2,1)}, bf16[256,128]{1,0:T(8,128)(2,1)}) custom-call(bf16[8,256,128]{2,1,0:T(8,128)(2,1)} %lines_ref.1, s32[1,256]{1,0:T(1,128)} %bitcast.19, f32[2,128]{1,0:T(2,128)} %gain_ref.3, f32[2,128]{1,0:T(2,128)} %shift_ref.3, bf16[2,4,128]{2,1,0:T(4,128)(2,1)} %bitcast.18), custom_call_target="tpu_custom_call" | custom-call | tf_op jit(solution)/shard_map/bias/pallas_call | solution.py:121
  3.3 5.1 %collective-permute-start = (bf16[256,128]{1,0:T(8,128)(2,1)}, bf16[256,128]{1,0:T(8,128)(2,1)S(1)}, u32[]{:S(2)}, u32[]{:S(2)}) collective-permute-start(bf16[256,128]{1,0:T(8,128)(2,1)} %get-tuple-element.11), channel_id=1, source_target_pairs={{0,24},{8,16},{16,8},{24,0},{1,25},{9,17},{17,9},{25,1},{2,26},{10... | collective-permute-start | bytes 196616 | tf_op jit(solution)/shard_map/ppermute | solution.py:445
  8.4 0.0 collective-permute-start.1
  8.5 0.7 %collective-permute-start.2 = (bf16[256,128]{1,0:T(8,128)(2,1)}, bf16[256,128]{1,0:T(8,128)(2,1)S(1)}, u32[]{:S(2)}, u32[]{:S(2)}) collective-permute-start(bf16[256,128]{1,0:T(8,128)(2,1)} %get-tuple-element.13), channel_id=1, source_target_pairs={{0,8},{8,0},{16,24},{24,16},{1,9},{9,1},{17,25},{25,17},{2,10},{10... | collective-permute-start | bytes 196616 | tf_op jit(solution)/shard_map/ppermute | solution.py:445
  9.1 0.0 copy-done.5
  9.1 0.0 copy-done.3
  9.2 0.9 %copy-done.1 = bf16[2,128,512]{2,1,0:T(8,128)(2,1)S(1)} copy-done((bf16[2,128,512]{2,1,0:T(8,128)(2,1)S(1)}, bf16[2,128,512]{2,1,0:T(8,128)(2,1)}, u32[]{:S(2)}) %copy-start.1) | copy-done | bytes 262168
  10.1 0.6 %lines.1 = (bf16[2,128,256]{2,1,0:T(8,128)(2,1)S(1)}, bf16[2,4,256,32]{3,2,1,0:T(8,128)(2,1)S(1)}, bf16[2,128,256]{2,1,0:T(8,128)(2,1)S(1)}, f32[2,128,256]{2,1,0:T(8,128)S(1)}) custom-call(bf16[8,256,128]{2,1,0:T(8,128)(2,1)S(1)} %copy-done, f32[2,128]{1,0:T(2,128)S(1)} %copy-done.3, f32[2,128]{1,0:T(2,128)S(1)} %copy-done.4, ...), custom_call_target="tpu_custom_call" | custom-call | flops 67108864 | bytes 1048576 | tf_op jit(solution)/shard_map/lines/pallas_call | solution.py:237
  10.8 0.5 %collective-permute-done = bf16[256,128]{1,0:T(8,128)(2,1)S(1)} collective-permute-done((bf16[256,128]{1,0:T(8,128)(2,1)}, bf16[256,128]{1,0:T(8,128)(2,1)S(1)}, u32[]{:S(2)}, u32[]{:S(2)}) %collective-permute-start) | collective-permute-done | bytes 65568 | tf_op jit(solution)/shard_map/ppermute | solution.py:445
  11.3 3.0 %collective-permute-done.1 = bf16[256,128]{1,0:T(8,128)(2,1)S(1)} collective-permute-done((bf16[256,128]{1,0:T(8,128)(2,1)}, bf16[256,128]{1,0:T(8,128)(2,1)S(1)}, u32[]{:S(2)}, u32[]{:S(2)}) %collective-permute-start.1) | collective-permute-done | bytes 65568 | tf_op jit(solution)/shard_map/ppermute | solution.py:445
  14.3 0.1 pad_maximum_fusion.2
  14.4 2.6 %collective-permute-start.3 = (bf16[4,160,128]{2,1,0:T(8,128)(2,1)S(1)}, bf16[4,160,128]{2,1,0:T(8,128)(2,1)S(1)}, u32[]{:S(2)}, u32[]{:S(2)}) collective-permute-start(bf16[4,160,128]{2,1,0:T(8,128)(2,1)S(1)} %get-tuple-element.23), channel_id=1, source_target_pairs={{0,6},{1,7},{2,4},{3,5},{4,2},{5,3},{6,0},{7,1},{8,14},{9,15},{10,... | collective-permute-start | bytes 491528 | tf_op jit(solution)/shard_map/ppermute | solution.py:448
  17.0 0.5 %collective-permute-start.4 = (bf16[4,160,128]{2,1,0:T(8,128)(2,1)S(1)}, bf16[4,160,128]{2,1,0:T(8,128)(2,1)S(1)}, u32[]{:S(2)}, u32[]{:S(2)}) collective-permute-start(bf16[4,160,128]{2,1,0:T(8,128)(2,1)S(1)} %get-tuple-element.24), channel_id=1, source_target_pairs={{0,4},{1,5},{2,6},{3,7},{4,0},{5,1},{6,2},{7,3},{8,12},{9,13},{10,... | collective-permute-start | bytes 491528 | tf_op jit(solution)/shard_map/ppermute | solution.py:448
  17.5 0.5 %collective-permute-start.5 = (bf16[4,160,128]{2,1,0:T(8,128)(2,1)S(1)}, bf16[4,160,128]{2,1,0:T(8,128)(2,1)S(1)}, u32[]{:S(2)}, u32[]{:S(2)}) collective-permute-start(bf16[4,160,128]{2,1,0:T(8,128)(2,1)S(1)} %get-tuple-element.25), channel_id=1, source_target_pairs={{0,2},{1,3},{2,0},{3,1},{4,6},{5,7},{6,4},{7,5},{8,10},{9,11},{10,... | collective-permute-start | bytes 491528 | tf_op jit(solution)/shard_map/ppermute | solution.py:448
  18.0 4.0 %collective-permute-done.3 = bf16[4,160,128]{2,1,0:T(8,128)(2,1)S(1)} collective-permute-done((bf16[4,160,128]{2,1,0:T(8,128)(2,1)S(1)}, bf16[4,160,128]{2,1,0:T(8,128)(2,1)S(1)}, u32[]{:S(2)}, u32[]{:S(2)}) %collective-permute-start.3) | collective-permute-done | bytes 163872 | tf_op jit(solution)/shard_map/ppermute | solution.py:448
  22.0 2.7 %collective-permute-done.4 = bf16[4,160,128]{2,1,0:T(8,128)(2,1)S(1)} collective-permute-done((bf16[4,160,128]{2,1,0:T(8,128)(2,1)S(1)}, bf16[4,160,128]{2,1,0:T(8,128)(2,1)S(1)}, u32[]{:S(2)}, u32[]{:S(2)}) %collective-permute-start.4) | collective-permute-done | bytes 163872 | tf_op jit(solution)/shard_map/ppermute | solution.py:448
  24.7 0.3 collective-permute-done.5
  24.9 0.1 pad_maximum_fusion.mine_ref
  25.0 0.0 copy-start.2
  25.0 0.0 copy-start.6
  25.0 0.1 collective-permute-start.6
  25.1 0.6 %early.1.early_ref = f32[2,128,128]{2,1,0:T(8,128)S(1)} custom-call(bf16[4,4,160,128]{3,2,1,0:T(8,128)(2,1)S(1)} %pad_maximum_fusion.mine_ref, bf16[2,128,256]{2,1,0:T(8,128)(2,1)S(1)} %get-tuple-element.15.q.q0, bf16[2,4,256,32]{3,2,1,0:T(8,128)(2,1)S(1)} %get-tuple-element.16.k.k0, bf16[2,128,256]{2,1,0:T(8,128)(2,1)S(1)} %get-tuple-element.17.v.v0), custom_call_target="tpu_custom_call" | custom-call | flops 67108864 | bytes 2097152 | tf_op jit(solution)/shard_map/early/pallas_call | solution.py:348
  25.7 1.5 %collective-permute-done.6.other_ref = bf16[4,4,160,128]{3,2,1,0:T(8,128)(2,1)S(1)} collective-permute-done((bf16[4,4,160,128]{3,2,1,0:T(8,128)(2,1)S(1)}, bf16[4,4,160,128]{3,2,1,0:T(8,128)(2,1)S(1)}, u32[]{:S(2)}, u32[]{:S(2)}) %collective-permute-start.6) | collective-permute-done | bytes 655392 | tf_op jit(solution)/shard_map/ppermute | solution.py:448
  27.2 2.8 %attend.1 = (bf16[2,256,128]{2,1,0:T(8,128)(2,1)}, bf16[2,256,128]{2,1,0:T(8,128)(2,1)}) custom-call(bf16[4,4,160,128]{3,2,1,0:T(8,128)(2,1)S(1)} %pad_maximum_fusion.mine_ref, bf16[4,4,160,128]{3,2,1,0:T(8,128)(2,1)S(1)} %collective-permute-done.6.other_ref, f32[2,128,128]{2,1,0:T(8,128)S(1)} %early.1.early_ref, ...), custom_call_target="tpu_custom_call" | custom-call | tf_op jit(solution)/shard_map/attend/pallas_call | solution.py:421
  (16 shorter events, 0.1 us)
Async XLA Ops:
  0.6 8.5 %copy-start = (bf16[8,256,128]{2,1,0:T(8,128)(2,1)S(1)}, bf16[8,256,128]{2,1,0:T(8,128)(2,1)}, u32[]{:S(2)}) copy-start(bf16[8,256,128]{2,1,0:T(8,128)(2,1)} %lines_ref.1) | copy-start | bytes 1572868
  3.3 7.9 %collective-permute-start = (bf16[256,128]{1,0:T(8,128)(2,1)}, bf16[256,128]{1,0:T(8,128)(2,1)S(1)}, u32[]{:S(2)}, u32[]{:S(2)}) collective-permute-start(bf16[256,128]{1,0:T(8,128)(2,1)} %get-tuple-element.11), channel_id=1, source_target_pairs={{0,24},{8,16},{16,8},{24,0},{1,25},{9,17},{17,9},{25,1},{2,26},{10... | collective-permute-start | bytes 196616 | tf_op jit(solution)/shard_map/ppermute | solution.py:445
  8.4 0.7 %copy-start.4 = (f32[2,128]{1,0:T(2,128)S(1)}, f32[2,128]{1,0:T(2,128)}, u32[]{:S(2)}) copy-start(f32[2,128]{1,0:T(2,128)} %shift_ref.3) | copy-start | bytes 3076
  8.4 0.7 %copy-start.5 = (f32[2,128]{1,0:T(2,128)S(1)}, f32[2,128]{1,0:T(2,128)}, u32[]{:S(2)}) copy-start(f32[2,128]{1,0:T(2,128)} %gate_ref.1) | copy-start | bytes 3076
  8.4 0.7 %copy-start.3 = (f32[2,128]{1,0:T(2,128)S(1)}, f32[2,128]{1,0:T(2,128)}, u32[]{:S(2)}) copy-start(f32[2,128]{1,0:T(2,128)} %gain_ref.3) | copy-start | bytes 3076
  8.4 5.8 %collective-permute-start.1 = (bf16[256,128]{1,0:T(8,128)(2,1)}, bf16[256,128]{1,0:T(8,128)(2,1)S(1)}, u32[]{:S(2)}, u32[]{:S(2)}) collective-permute-start(bf16[256,128]{1,0:T(8,128)(2,1)} %get-tuple-element.12), channel_id=1, source_target_pairs={{0,16},{8,24},{16,0},{24,8},{1,17},{9,25},{17,1},{25,9},{2,18},{10... | collective-permute-start | bytes 196616 | tf_op jit(solution)/shard_map/ppermute | solution.py:445
  8.5 5.8 %collective-permute-start.2 = (bf16[256,128]{1,0:T(8,128)(2,1)}, bf16[256,128]{1,0:T(8,128)(2,1)S(1)}, u32[]{:S(2)}, u32[]{:S(2)}) collective-permute-start(bf16[256,128]{1,0:T(8,128)(2,1)} %get-tuple-element.13), channel_id=1, source_target_pairs={{0,8},{8,0},{16,24},{24,16},{1,9},{9,1},{17,25},{25,17},{2,10},{10... | collective-permute-start | bytes 196616 | tf_op jit(solution)/shard_map/ppermute | solution.py:445
  9.2 0.9 %copy-start.1 = (bf16[2,128,512]{2,1,0:T(8,128)(2,1)S(1)}, bf16[2,128,512]{2,1,0:T(8,128)(2,1)}, u32[]{:S(2)}) copy-start(bf16[2,128,512]{2,1,0:T(8,128)(2,1)} %proj_ref.1) | copy-start | bytes 786436
  10.1 4.2 %copy-start.7 = (bf16[256,128]{1,0:T(8,128)(2,1)S(1)}, bf16[256,128]{1,0:T(8,128)(2,1)}, u32[]{:S(2)}) copy-start(bf16[256,128]{1,0:T(8,128)(2,1)} %get-tuple-element.14) | copy-start | bytes 196612
  14.4 7.6 %collective-permute-start.3 = (bf16[4,160,128]{2,1,0:T(8,128)(2,1)S(1)}, bf16[4,160,128]{2,1,0:T(8,128)(2,1)S(1)}, u32[]{:S(2)}, u32[]{:S(2)}) collective-permute-start(bf16[4,160,128]{2,1,0:T(8,128)(2,1)S(1)} %get-tuple-element.23), channel_id=1, source_target_pairs={{0,6},{1,7},{2,4},{3,5},{4,2},{5,3},{6,0},{7,1},{8,14},{9,15},{10,... | collective-permute-start | bytes 491528 | tf_op jit(solution)/shard_map/ppermute | solution.py:448
  17.0 7.7 %collective-permute-start.4 = (bf16[4,160,128]{2,1,0:T(8,128)(2,1)S(1)}, bf16[4,160,128]{2,1,0:T(8,128)(2,1)S(1)}, u32[]{:S(2)}, u32[]{:S(2)}) collective-permute-start(bf16[4,160,128]{2,1,0:T(8,128)(2,1)S(1)} %get-tuple-element.24), channel_id=1, source_target_pairs={{0,4},{1,5},{2,6},{3,7},{4,0},{5,1},{6,2},{7,3},{8,12},{9,13},{10,... | collective-permute-start | bytes 491528 | tf_op jit(solution)/shard_map/ppermute | solution.py:448
  17.5 7.4 %collective-permute-start.5 = (bf16[4,160,128]{2,1,0:T(8,128)(2,1)S(1)}, bf16[4,160,128]{2,1,0:T(8,128)(2,1)S(1)}, u32[]{:S(2)}, u32[]{:S(2)}) collective-permute-start(bf16[4,160,128]{2,1,0:T(8,128)(2,1)S(1)} %get-tuple-element.25), channel_id=1, source_target_pairs={{0,2},{1,3},{2,0},{3,1},{4,6},{5,7},{6,4},{7,5},{8,10},{9,11},{10,... | collective-permute-start | bytes 491528 | tf_op jit(solution)/shard_map/ppermute | solution.py:448
  25.0 2.2 %copy-start.2 = (bf16[2,128,128]{2,1,0:T(8,128)(2,1)S(1)}, bf16[2,128,128]{2,1,0:T(8,128)(2,1)}, u32[]{:S(2)}) copy-start(bf16[2,128,128]{2,1,0:T(8,128)(2,1)} %weight_ref.3) | copy-start | bytes 196612
  25.0 2.2 %copy-start.6 = (f32[2,128]{1,0:T(2,128)S(1)}, f32[2,128]{1,0:T(2,128)}, u32[]{:S(2)}) copy-start(f32[2,128]{1,0:T(2,128)} %offset_ref.3) | copy-start | bytes 3076
  25.0 2.2 %collective-permute-start.6 = (bf16[4,4,160,128]{3,2,1,0:T(8,128)(2,1)S(1)}, bf16[4,4,160,128]{3,2,1,0:T(8,128)(2,1)S(1)}, u32[]{:S(2)}, u32[]{:S(2)}) collective-permute-start(bf16[4,4,160,128]{3,2,1,0:T(8,128)(2,1)S(1)} %pad_maximum_fusion.mine_ref), channel_id=1, source_target_pairs={{0,1},{1,0},{2,3},{3,2},{4,5},{5,4},{6,7},{7,6},{8,9},{9,8},{10,11... | collective-permute-start | bytes 1966088 | tf_op jit(solution)/shard_map/ppermute | solution.py:448
